TPU v7x, 256 devices: a whole 4x4x8 slice. The times are simulated.
256 devices in a mesh: rot: 16 (over x, y_hi, core), az: 16 (over y_lo, z).
Axes of the slice: x: 4, y: 4 (y_hi: 2, y_lo: 2; y = y_hi * 2 + y_lo), z: 8, core: 2. Of those that a mesh axis runs over, the one named last changes fastest.
Arguments:
- inputs: bfloat16 [16, 4, 512, 128], P('rot', None, 'az'), may hold values from -6 to 6
- pre_one: bfloat16 [16, 4, 512, 128], P('rot', None, 'az'), may hold values from -8 to 8
- pre_two: bfloat16 [16, 4, 512, 128], P('rot', None, 'az'), may hold values from -8 to 8
- cotangent: bfloat16 [16, 4, 512, 128], P('rot', None, 'az'), may hold values from -6 to 6
- filt_one: bfloat16 [16, 3, 3, 128, 128], P('rot'), may hold values from -0.046875 to 0.046875
- filt_two: bfloat16 [16, 3, 3, 128, 128], P('rot'), may hold values from -0.046875 to 0.046875
Outputs:
- input_grad: bfloat16 [16, 4, 512, 128], P('rot', None, 'az')
- filt_grad_one: float32 [16, 3, 3, 128, 128], P('rot')
- filt_grad_two: float32 [16, 3, 3, 128, 128], P('rot')
All inputs are finite; a program needn't handle non-finite values.
Results may differ from a plain program's by a relative error of at most 0.018.
Values may be sent and summed in bfloat16 or wider, within the bound.
No kernel may reach another device: no remote copies, remote signals or barrier semaphores. Data moves between devices by JAX's collectives and lax.ppermute only.
A program may use at most 64 MiB of HBM per device.

v0:
```python
import jax
import jax.numpy as jnp
from jax import lax
from jax.sharding import Mesh
from jax.sharding import PartitionSpec as P

ROT = ("rot_0", "rot_1", "rot_2")


def with_halo(block, sides, width):
    for axis, dim in sides:
        count = lax.axis_size(axis)
        forward = [(i, i + 1) for i in range(count - 1)]
        forward.append((count - 1, 0))
        backward = [(target, source) for source, target in forward]
        low = lax.ppermute(
            lax.slice_in_dim(block, block.shape[dim] - width, None, axis=dim), axis, forward
        )
        high = lax.ppermute(lax.slice_in_dim(block, 0, width, axis=dim), axis, backward)
        block = jnp.concatenate([low, block, high], axis=dim)
    return block


def from_everyone(array, axis):
    length = lax.axis_size(axis)
    return lax.all_to_all(
        jnp.broadcast_to(array[None], (length, *array.shape)), axis, 0, 0, tiled=True
    )


def laid_out(parts, dim):
    lengths = list(parts.shape[1:])
    lengths[dim] *= parts.shape[0]
    return jnp.moveaxis(parts, 0, dim).reshape(lengths)


def gathered_by_axis(array, axes, dim):
    far, near = axes
    first = from_everyone(array, far)
    parts = jnp.swapaxes(from_everyone(first, near), 0, 1)
    return laid_out(parts.reshape(-1, *array.shape), dim)


def sent_together(arrays, axis, dim, along):
    ends, at = ([], 0)
    for a in arrays[:-1]:
        at += a.shape[along]
        ends.append(at)
    both = jnp.concatenate(arrays, axis=along)
    return tuple(jnp.split(gathered_by_axis(both, axis, dim), ends, axis=along))


def split_up(array, dim, length):
    lengths = array.shape
    parts = array.reshape(*lengths[:dim], length, lengths[dim] // length, *lengths[dim + 1 :])
    return jnp.moveaxis(parts, dim, 0)


def sum_at_owner(array, axis, dim):
    length = lax.axis_size(axis)
    parts = lax.all_to_all(split_up(array, dim, length), axis, 0, 0, tiled=True)
    return jnp.sum(parts, axis=0)


def collect(array, axis, dim):
    parts = from_everyone(array, axis)
    return laid_out(parts, dim)


def summed_on_arrival(array, axis, dim):
    parts = split_up(array, dim, lax.axis_size(axis))
    arrived = lax.all_to_all(parts, axis, split_axis=0, concat_axis=0, tiled=True)
    return arrived.astype(jnp.float32).sum(axis=0)


def filled_up(lines, length):
    spare = -lines.shape[0] % length
    if not spare:
        return lines
    return jnp.concatenate([lines, jnp.zeros((spare, *lines.shape[1:]), lines.dtype)])


def nested_sum(array, axes):
    lines = array.reshape(-1, array.shape[-1])
    padded = filled_up(lines, lax.axis_size(axes))
    whole = collect(summed_on_arrival(padded, axes, 0).astype(jnp.bfloat16), axes, 0)
    return lax.slice_in_dim(whole, 0, len(lines)).reshape(array.shape).astype(jnp.float32)


def slope(pre):
    widened = pre.astype(jnp.float32)
    logistic = jax.nn.sigmoid(widened)
    return logistic * (1.0 + widened * (1.0 - logistic))


def pad_rows(field):
    return jnp.pad(field, ((0, 0), (1, 1), (0, 0), (0, 0)))


def doubled_rows(field):
    padded = pad_rows(field)
    return jnp.concatenate([padded, padded], axis=0)


def filter_terms(features, gradient, my_rank, per_dev):
    doubled = doubled_rows(features)
    orient_count = gradient.shape[0]
    row_count = gradient.shape[1]
    col_count = gradient.shape[2]
    channels = gradient.shape[3]
    shifted = lax.dynamic_slice_in_dim(doubled, my_rank * per_dev + 0, orient_count, 0)
    pieces = []
    for row_tap in range(3):
        for col_tap in range(3):
            window = shifted[:, row_tap : row_tap + row_count, col_tap : col_tap + col_count, :]
            pieces.append(
                lax.dot_general(
                    window,
                    gradient,
                    (((0, 1, 2), (0, 1, 2)), ((), ())),
                    preferred_element_type=jnp.float32,
                )
            )
    results = [jnp.stack(pieces).reshape(3, 3, channels, channels)]
    return jnp.stack(results)


def make_terms(doubled, my_rank, filt_local, row_count, col_count, first_row, row_span):
    orient_count = doubled.shape[0] // 2
    channels = doubled.shape[3]
    per_dev = filt_local.shape[0]
    summed = jnp.zeros((row_span, row_count, col_count, channels), jnp.float32)
    relative = my_rank * per_dev + 0
    offset = (first_row - relative) % orient_count
    chosen = lax.dynamic_slice_in_dim(doubled, offset, row_span, 0)
    for row_tap in range(3):
        for col_tap in range(3):
            window = chosen[
                :, 2 - row_tap : 2 - row_tap + row_count, 2 - col_tap : 2 - col_tap + col_count, :
            ]
            summed = summed + lax.dot_general(
                window,
                filt_local[0, row_tap, col_tap],
                (((3,), (1,)), ((), ())),
                preferred_element_type=jnp.float32,
            )
    return summed


def shards(inputs, pre_one, pre_two, cotangent, filt_one, filt_two):
    per_dev = inputs.shape[0]
    row_count = inputs.shape[1]
    col_count = inputs.shape[2]
    my_rank = lax.axis_index(ROT)
    cell_count = per_dev * lax.axis_size(ROT) * row_count * col_count * lax.axis_size("az")
    norm_scale = cell_count ** (-0.5)
    act_one = jax.nn.silu(pre_one.astype(jnp.float32)).astype(jnp.bfloat16)
    grad_two = (cotangent.astype(jnp.float32) * slope(pre_two)).astype(jnp.bfloat16)
    stacked = jnp.concatenate([inputs, act_one, grad_two], axis=0)
    widened = with_halo(stacked, (("az", 2),), 1)
    inputs_rim = widened[0:per_dev]
    act_rim = widened[per_dev : 2 * per_dev]
    grad_rim = widened[2 * per_dev : 3 * per_dev]
    all_inputs, all_act, all_grad = sent_together(
        (inputs_rim, act_rim, grad_rim), (("rot_0", "rot_1"), "rot_2"), 0, 1
    )
    out_cols = all_grad.shape[2] - 2
    margin = (all_grad.shape[2] - col_count) // 2
    doubled_two = doubled_rows(all_grad)
    delta_one = sum_at_owner(
        make_terms(
            doubled_two,
            my_rank,
            filt_two,
            row_count,
            out_cols,
            jnp.int32(0),
            per_dev * lax.axis_size(ROT),
        ),
        ROT,
        0,
    )
    grad_inner = all_grad[:, :, margin : margin + col_count]
    filt_part_two = filter_terms(all_act, grad_inner, my_rank, per_dev)
    grad_one = (delta_one * slope(pre_one)).astype(jnp.bfloat16)
    grad_one_rim = with_halo(grad_one, (("az", 2),), 1)
    all_grad_one = collect(grad_one_rim, ROT, 0)
    doubled_one = doubled_rows(all_grad_one)
    input_sum = summed_on_arrival(
        make_terms(
            doubled_one,
            my_rank,
            filt_one,
            row_count,
            col_count,
            jnp.int32(0),
            per_dev * lax.axis_size(ROT),
        ).astype(jnp.bfloat16),
        ROT,
        0,
    )
    filt_part_one = filter_terms(all_inputs, all_grad_one[:, :, 1:-1], my_rank, per_dev)
    summed_one, summed_two = (
        nested_sum(filt_part_one.astype(jnp.bfloat16), "az"),
        nested_sum(filt_part_two.astype(jnp.bfloat16), "az"),
    )
    return (input_sum.astype(jnp.bfloat16), summed_one * norm_scale, summed_two * norm_scale)


def solution(mesh):
    finer = Mesh(mesh.devices.reshape(4, 2, 2, mesh.shape["az"]), ("rot_0", "rot_1", "rot_2", "az"))
    placed = (
        P(ROT, None, "az", None),
        P(ROT, None, "az", None),
        P(ROT, None, "az", None),
        P(ROT, None, "az", None),
        P(ROT, None, None, None, None),
        P(ROT, None, None, None, None),
    )
    return jax.shard_map(
        shards,
        mesh=finer,
        in_specs=placed,
        out_specs=(
            P(ROT, None, "az", None),
            P(ROT, None, None, None, None),
            P(ROT, None, None, None, None),
        ),
        check_vma=False,
    )
```

profile of v0, /device:TPU:32, one launch (start us, length us, event | category | flops | bytes accessed | tf_op | source)
XLA Modules:
  0.0 170.2 jit_solution(18357428729939991045)
XLA Ops:
  2.2 2.0 %collective-permute-start = (bf16[3,4,1,128]{3,2,1,0:T(2,128)(2,1)S(1)}, bf16[3,4,1,128]{3,2,1,0:T(2,128)(2,1)S(1)}, u32[]{:S(2)}, u32[]{:S(2)}) collective-permute-start(bf16[3,4,1,128]{3,2,1,0:T(2,128)(2,1)S(1)} %get-tuple-element.9), channel_id=1, source_target_pairs={{0,1},{1,2},{2,3},{3,4},{4,5},{5,6},{6,7},{7,8},{8,9},{9,10},{10,1... | collective-permute-start | bytes 9224 | tf_op jit(solution)/shard_map/ppermute | solution.py:16
  4.3 1.6 collective-permute-done
  5.9 1.9 %collective-permute-done.1 = bf16[3,4,1,128]{3,2,1,0:T(2,128)(2,1)S(1)} collective-permute-done((bf16[3,4,1,128]{3,2,1,0:T(2,128)(2,1)S(1)}, bf16[3,4,1,128]{3,2,1,0:T(2,128)(2,1)S(1)}, u32[]{:S(2)}, u32[]{:S(2)}) %collective-permute-start.1) | collective-permute-done | bytes 3104 | tf_op jit(solution)/shard_map/ppermute | solution.py:19
  9.8 6.9 %all-to-all-start = ((bf16[8,1,12,34,128]{4,3,2,1,0:T(8,128)(2,1)}), bf16[8,1,12,34,128]{4,3,2,1,0:T(8,128)(2,1)S(1)}, u32[]{:S(2)}, u32[]{:S(2)}) async-start(bf16[8,1,12,34,128]{4,3,2,1,0:T(8,128)(2,1)} %broadcast_in_dim.17), calls=%async_computation | async-start | bytes 1966080 | tf_op jit(solution)/shard_map/all_to_all | solution.py:26
  16.7 14.3 %all-to-all-done = bf16[8,1,12,34,128]{4,3,2,1,0:T(8,128)(2,1)S(1)} async-done(((bf16[8,1,12,34,128]{4,3,2,1,0:T(8,128)(2,1)}), bf16[8,1,12,34,128]{4,3,2,1,0:T(8,128)(2,1)S(1)}, u32[]{:S(2)}, u32[]{:S(2)}) %all-to-all-start) | async-done | bytes 835616 | tf_op jit(solution)/shard_map/all_to_all | solution.py:26
  31.6 5.1 %all_to_all.45 = bf16[2,8,1,12,34,128]{5,1,4,3,2,0:T(8,128)(2,1)S(1)} all-to-all(bf16[2,8,1,12,34,128]{5,1,4,3,2,0:T(8,128)(2,1)S(1)} %broadcast_in_dim.19), channel_id=1, replica_groups=mesh['rot_0'=4,'rot_1'=2,'rot_2'=2,'az'=16] {'rot_2'}, dimensions={0} | all-to-all | bytes 3342336 | tf_op jit(solution)/shard_map/all_to_all | solution.py:26
  48.5 3.8 %all-to-all-start.2 = ((f32[16,1,4,32,128]{4,3,2,1,0:T(8,128)}), f32[16,1,4,32,128]{4,3,2,1,0:T(8,128)S(1)}, u32[]{:S(2)}, u32[]{:S(2)}) async-start(f32[16,1,4,32,128]{4,3,2,1,0:T(8,128)} %fusion), calls=%async_computation.2 | async-start | bytes 2097152 | tf_op jit(solution)/shard_map/all_to_all | solution.py:61
  52.3 2.2 %fusion.28 = bf16[9,128,128]{2,1,0:T(8,128)(2,1)} fusion(bf16[9,128,128]{2,1,0:T(8,128)(2,1)} %fusion.30, bf16[16,6,34,128]{3,2,1,0:T(8,128)(2,1)} %copy-done.1, bf16[16,12,34,128]{3,2,1,0:T(8,128)(2,1)S(1)} %bitcast.409), kind=kOutput, calls=%fused_computation.70 | convolution fusion | flops 67125248 | bytes 1081344 | tf_op jit(solution)/shard_map/dot_general | solution.py:117
  57.6 12.7 %all-to-all-done.2 = f32[16,1,4,32,128]{4,3,2,1,0:T(8,128)S(1)} async-done(((f32[16,1,4,32,128]{4,3,2,1,0:T(8,128)}), f32[16,1,4,32,128]{4,3,2,1,0:T(8,128)S(1)}, u32[]{:S(2)}, u32[]{:S(2)}) %all-to-all-start.2) | async-done | bytes 1048608 | tf_op jit(solution)/shard_map/all_to_all | solution.py:61
  70.3 8.4 %all-to-all-start.7 = ((bf16[16,72,128]{2,1,0:T(8,128)(2,1)}), bf16[16,72,128]{2,1,0:T(8,128)(2,1)S(1)}, u32[]{:S(2)}, u32[]{:S(2)}) async-start(bf16[16,72,128]{2,1,0:T(8,128)(2,1)} %bitcast.122), calls=%async_computation.7 | async-start | bytes 589824 | tf_op jit(solution)/shard_map/all_to_all | solution.py:72
  80.9 3.0 %collective-permute-done.2 = bf16[1,4,1,128]{3,2,1,0:T(2,128)(2,1)S(1)} collective-permute-done((bf16[1,4,1,128]{3,2,1,0:T(2,128)(2,1)S(1)}, bf16[1,4,1,128]{3,2,1,0:T(2,128)(2,1)S(1)}, u32[]{:S(2)}, u32[]{:S(2)}) %collective-permute-start.2) | collective-permute-done | bytes 1056 | tf_op jit(solution)/shard_map/ppermute | solution.py:16
  83.9 1.7 collective-permute-done.3
  85.6 3.4 %all-to-all-done.7 = bf16[16,72,128]{2,1,0:T(8,128)(2,1)S(1)} async-done(((bf16[16,72,128]{2,1,0:T(8,128)(2,1)}), bf16[16,72,128]{2,1,0:T(8,128)(2,1)S(1)}, u32[]{:S(2)}, u32[]{:S(2)}) %all-to-all-start.7) | async-done | bytes 294944 | tf_op jit(solution)/shard_map/all_to_all | solution.py:72
  90.0 4.7 %all-to-all-start.3 = ((bf16[16,1,4,34,128]{4,2,3,1,0:T(4,128)(2,1)}), bf16[16,1,4,34,128]{4,2,3,1,0:T(4,128)(2,1)S(1)}, u32[]{:S(2)}, u32[]{:S(2)}) async-start(bf16[16,1,4,34,128]{4,2,3,1,0:T(4,128)(2,1)} %broadcast_in_dim.41), calls=%async_computation.3 | async-start | bytes 1114112 | tf_op jit(solution)/shard_map/all_to_all | solution.py:26
  95.2 12.1 %all-to-all-done.3 = bf16[16,1,4,34,128]{4,2,3,1,0:T(4,128)(2,1)S(1)} async-done(((bf16[16,1,4,34,128]{4,2,3,1,0:T(4,128)(2,1)}), bf16[16,1,4,34,128]{4,2,3,1,0:T(4,128)(2,1)S(1)}, u32[]{:S(2)}, u32[]{:S(2)}) %all-to-all-start.3) | async-done | bytes 557088 | tf_op jit(solution)/shard_map/all_to_all | solution.py:26
  108.1 4.5 %all-to-all-start.8 = ((bf16[16,72,128]{2,1,0:T(8,128)(2,1)}), bf16[16,72,128]{2,1,0:T(8,128)(2,1)S(1)}, u32[]{:S(2)}, u32[]{:S(2)}) async-start(bf16[16,72,128]{2,1,0:T(8,128)(2,1)} %broadcast_in_dim.43), calls=%async_computation.8 | async-start | bytes 589824 | tf_op jit(solution)/shard_map/all_to_all | solution.py:26
  119.7 3.0 %all-to-all-done.8 = bf16[16,72,128]{2,1,0:T(8,128)(2,1)S(1)} async-done(((bf16[16,72,128]{2,1,0:T(8,128)(2,1)}), bf16[16,72,128]{2,1,0:T(8,128)(2,1)S(1)}, u32[]{:S(2)}, u32[]{:S(2)}) %all-to-all-start.8) | async-done | bytes 294944 | tf_op jit(solution)/shard_map/all_to_all | solution.py:26
  122.8 5.1 %all-to-all-start.5 = ((bf16[16,72,128]{2,1,0:T(8,128)(2,1)}), bf16[16,72,128]{2,1,0:T(8,128)(2,1)S(1)}, u32[]{:S(2)}, u32[]{:S(2)}) async-start(bf16[16,72,128]{2,1,0:T(8,128)(2,1)} %bitcast.427), calls=%async_computation.5 | async-start | bytes 589824 | tf_op jit(solution)/shard_map/all_to_all | solution.py:72
  130.0 1.8 %fusion.2 = bf16[16,1,4,32,128]{4,3,2,1,0:T(8,128)(2,1)} fusion(f32[16,4,32,128]{3,2,1,0:T(8,128)S(1)} %convolution_add_fusion.1, bf16[16,6,34,128]{3,2,1,0:T(8,128)(2,1)S(1)} %fusion.59, bf16[1,3,3,128,128]{4,3,2,1,0:T(8,128)(2,1)} %param.10), kind=kOutput, calls=%fused_computation.26 | convolution fusion | flops 67633152 | bytes 2129920 | tf_op jit(solution)/shard_map/dot_general | solution.py:141
  131.9 5.6 %all-to-all-done.5 = bf16[16,72,128]{2,1,0:T(8,128)(2,1)S(1)} async-done(((bf16[16,72,128]{2,1,0:T(8,128)(2,1)}), bf16[16,72,128]{2,1,0:T(8,128)(2,1)S(1)}, u32[]{:S(2)}, u32[]{:S(2)}) %all-to-all-start.5) | async-done | bytes 294944 | tf_op jit(solution)/shard_map/all_to_all | solution.py:72
  137.4 4.0 %all-to-all-start.4 = ((bf16[16,1,4,32,128]{4,3,2,1,0:T(8,128)(2,1)}), bf16[16,1,4,32,128]{4,3,2,1,0:T(8,128)(2,1)S(1)}, u32[]{:S(2)}, u32[]{:S(2)}) async-start(bf16[16,1,4,32,128]{4,3,2,1,0:T(8,128)(2,1)} %fusion.2), calls=%async_computation.4 | async-start | bytes 1048576 | tf_op jit(solution)/shard_map/all_to_all | solution.py:72
  141.5 12.3 %all-to-all-done.4 = bf16[16,1,4,32,128]{4,3,2,1,0:T(8,128)(2,1)S(1)} async-done(((bf16[16,1,4,32,128]{4,3,2,1,0:T(8,128)(2,1)}), bf16[16,1,4,32,128]{4,3,2,1,0:T(8,128)(2,1)S(1)}, u32[]{:S(2)}, u32[]{:S(2)}) %all-to-all-start.4) | async-done | bytes 524320 | tf_op jit(solution)/shard_map/all_to_all | solution.py:72
  154.6 4.6 %all-to-all-start.6 = ((bf16[16,72,128]{2,1,0:T(8,128)(2,1)}), bf16[16,72,128]{2,1,0:T(8,128)(2,1)S(1)}, u32[]{:S(2)}, u32[]{:S(2)}) async-start(bf16[16,72,128]{2,1,0:T(8,128)(2,1)} %broadcast_in_dim.42), calls=%async_computation.6 | async-start | bytes 589824 | tf_op jit(solution)/shard_map/all_to_all | solution.py:26
  160.7 8.6 %all-to-all-done.6 = bf16[16,72,128]{2,1,0:T(8,128)(2,1)S(1)} async-done(((bf16[16,72,128]{2,1,0:T(8,128)(2,1)}), bf16[16,72,128]{2,1,0:T(8,128)(2,1)S(1)}, u32[]{:S(2)}, u32[]{:S(2)}) %all-to-all-start.6) | async-done | bytes 294944 | tf_op jit(solution)/shard_map/all_to_all | solution.py:26
  (83 shorter events, 35.9 us)
Async XLA Ops:
  2.2 3.7 %collective-permute-start = (bf16[3,4,1,128]{3,2,1,0:T(2,128)(2,1)S(1)}, bf16[3,4,1,128]{3,2,1,0:T(2,128)(2,1)S(1)}, u32[]{:S(2)}, u32[]{:S(2)}) collective-permute-start(bf16[3,4,1,128]{3,2,1,0:T(2,128)(2,1)S(1)} %get-tuple-element.9), channel_id=1, source_target_pairs={{0,1},{1,2},{2,3},{3,4},{4,5},{5,6},{6,7},{7,8},{8,9},{9,10},{10,1... | collective-permute-start | bytes 9224 | tf_op jit(solution)/shard_map/ppermute | solution.py:16
  4.2 3.6 %collective-permute-start.1 = (bf16[3,4,1,128]{3,2,1,0:T(2,128)(2,1)S(1)}, bf16[3,4,1,128]{3,2,1,0:T(2,128)(2,1)S(1)}, u32[]{:S(2)}, u32[]{:S(2)}) collective-permute-start(bf16[3,4,1,128]{3,2,1,0:T(2,128)(2,1)S(1)} %get-tuple-element.10), channel_id=1, source_target_pairs={{1,0},{2,1},{3,2},{4,3},{5,4},{6,5},{7,6},{8,7},{9,8},{10,9},{11,1... | collective-permute-start | bytes 9224 | tf_op jit(solution)/shard_map/ppermute | solution.py:19
  9.8 21.3 %all-to-all-start = ((bf16[8,1,12,34,128]{4,3,2,1,0:T(8,128)(2,1)}), bf16[8,1,12,34,128]{4,3,2,1,0:T(8,128)(2,1)S(1)}, u32[]{:S(2)}, u32[]{:S(2)}) async-start(bf16[8,1,12,34,128]{4,3,2,1,0:T(8,128)(2,1)} %broadcast_in_dim.17), calls=%async_computation | async-start | bytes 1966080 | tf_op jit(solution)/shard_map/all_to_all | solution.py:26
  38.6 4.0 %copy-start.1 = (bf16[16,6,34,128]{3,2,1,0:T(8,128)(2,1)}, bf16[16,6,34,128]{3,2,1,0:T(8,128)(2,1)S(1)}, u32[]{:S(2)}) copy-start(bf16[16,6,34,128]{3,2,1,0:T(8,128)(2,1)S(1)} %fusion.57) | copy-start | bytes 2506756
  43.7 1.0 copy-start.5
  48.5 21.8 %all-to-all-start.2 = ((f32[16,1,4,32,128]{4,3,2,1,0:T(8,128)}), f32[16,1,4,32,128]{4,3,2,1,0:T(8,128)S(1)}, u32[]{:S(2)}, u32[]{:S(2)}) async-start(f32[16,1,4,32,128]{4,3,2,1,0:T(8,128)} %fusion), calls=%async_computation.2 | async-start | bytes 2097152 | tf_op jit(solution)/shard_map/all_to_all | solution.py:61
  52.3 2.2 %copy-start.2 = (bf16[16,6,34,128]{3,2,1,0:T(8,128)(2,1)S(1)}, bf16[16,6,34,128]{3,2,1,0:T(8,128)(2,1)}, u32[]{:S(2)}) copy-start(bf16[16,6,34,128]{3,2,1,0:T(8,128)(2,1)} %copy-done.1) | copy-start | bytes 2506756
  56.5 22.2 %copy-start.6 = (bf16[1,4,32,128]{3,2,1,0:T(8,128)(2,1)S(1)}, bf16[1,4,32,128]{3,2,1,0:T(8,128)(2,1)}, u32[]{:S(2)}) copy-start(bf16[1,4,32,128]{3,2,1,0:T(8,128)(2,1)} %param.7) | copy-start | bytes 98308
  57.6 37.1 %copy-start = (bf16[16,4,34,128]{3,2,1,0:T(8,128)(2,1)S(1)}, bf16[16,4,34,128]{3,2,1,0:T(8,128)(2,1)}, u32[]{:S(2)}) copy-start(bf16[16,4,34,128]{3,2,1,0:T(8,128)(2,1)} %get-tuple-element.4) | copy-start | bytes 1671172
  70.3 18.7 %all-to-all-start.7 = ((bf16[16,72,128]{2,1,0:T(8,128)(2,1)}), bf16[16,72,128]{2,1,0:T(8,128)(2,1)S(1)}, u32[]{:S(2)}, u32[]{:S(2)}) async-start(bf16[16,72,128]{2,1,0:T(8,128)(2,1)} %bitcast.122), calls=%async_computation.7 | async-start | bytes 589824 | tf_op jit(solution)/shard_map/all_to_all | solution.py:72
  78.8 5.1 %collective-permute-start.2 = (bf16[1,4,1,128]{3,2,1,0:T(2,128)(2,1)S(1)}, bf16[1,4,1,128]{3,2,1,0:T(2,128)(2,1)S(1)}, u32[]{:S(2)}, u32[]{:S(2)}) collective-permute-start(bf16[1,4,1,128]{3,2,1,0:T(2,128)(2,1)S(1)} %get-tuple-element.11), channel_id=1, source_target_pairs={{0,1},{1,2},{2,3},{3,4},{4,5},{5,6},{6,7},{7,8},{8,9},{9,10},{10,1... | collective-permute-start | bytes 3080 | tf_op jit(solution)/shard_map/ppermute | solution.py:16
  80.4 5.2 %collective-permute-start.3 = (bf16[1,4,1,128]{3,2,1,0:T(2,128)(2,1)S(1)}, bf16[1,4,1,128]{3,2,1,0:T(2,128)(2,1)S(1)}, u32[]{:S(2)}, u32[]{:S(2)}) collective-permute-start(bf16[1,4,1,128]{3,2,1,0:T(2,128)(2,1)S(1)} %get-tuple-element.12), channel_id=1, source_target_pairs={{1,0},{2,1},{3,2},{4,3},{5,4},{6,5},{7,6},{8,7},{9,8},{10,9},{11,1... | collective-permute-start | bytes 3080 | tf_op jit(solution)/shard_map/ppermute | solution.py:19
  90.0 17.4 %all-to-all-start.3 = ((bf16[16,1,4,34,128]{4,2,3,1,0:T(4,128)(2,1)}), bf16[16,1,4,34,128]{4,2,3,1,0:T(4,128)(2,1)S(1)}, u32[]{:S(2)}, u32[]{:S(2)}) async-start(bf16[16,1,4,34,128]{4,2,3,1,0:T(4,128)(2,1)} %broadcast_in_dim.41), calls=%async_computation.3 | async-start | bytes 1114112 | tf_op jit(solution)/shard_map/all_to_all | solution.py:26
  108.1 14.6 %all-to-all-start.8 = ((bf16[16,72,128]{2,1,0:T(8,128)(2,1)}), bf16[16,72,128]{2,1,0:T(8,128)(2,1)S(1)}, u32[]{:S(2)}, u32[]{:S(2)}) async-start(bf16[16,72,128]{2,1,0:T(8,128)(2,1)} %broadcast_in_dim.43), calls=%async_computation.8 | async-start | bytes 589824 | tf_op jit(solution)/shard_map/all_to_all | solution.py:26
  115.2 1.0 copy-start.4
  118.7 0.7 copy-start.3
  122.8 14.7 %all-to-all-start.5 = ((bf16[16,72,128]{2,1,0:T(8,128)(2,1)}), bf16[16,72,128]{2,1,0:T(8,128)(2,1)S(1)}, u32[]{:S(2)}, u32[]{:S(2)}) async-start(bf16[16,72,128]{2,1,0:T(8,128)(2,1)} %bitcast.427), calls=%async_computation.5 | async-start | bytes 589824 | tf_op jit(solution)/shard_map/all_to_all | solution.py:72
  137.4 16.4 %all-to-all-start.4 = ((bf16[16,1,4,32,128]{4,3,2,1,0:T(8,128)(2,1)}), bf16[16,1,4,32,128]{4,3,2,1,0:T(8,128)(2,1)S(1)}, u32[]{:S(2)}, u32[]{:S(2)}) async-start(bf16[16,1,4,32,128]{4,3,2,1,0:T(8,128)(2,1)} %fusion.2), calls=%async_computation.4 | async-start | bytes 1048576 | tf_op jit(solution)/shard_map/all_to_all | solution.py:72
  154.6 14.8 %all-to-all-start.6 = ((bf16[16,72,128]{2,1,0:T(8,128)(2,1)}), bf16[16,72,128]{2,1,0:T(8,128)(2,1)S(1)}, u32[]{:S(2)}, u32[]{:S(2)}) async-start(bf16[16,72,128]{2,1,0:T(8,128)(2,1)} %broadcast_in_dim.42), calls=%async_computation.6 | async-start | bytes 589824 | tf_op jit(solution)/shard_map/all_to_all | solution.py:26
where the time goes:
time: 172 us; the launch traced here: 170 us
  waiting for transfers between devices  80.3 us (47%)
  starting transfers between devices  46.2 us (27%)
  matrix products  23.6 us (14%)
  local copies, waits for them, and re-layouts  7.42 us (4%)
  other arithmetic  6.65 us (4%)
  blocking collectives  5.06 us (3%)
    all_to_all x4, waiting for transfers between devices, from_everyone(): lax.all_to_all(jnp.broadcast_to(array[None], (length, *array.shape)), axi...  38.1 us
    all_to_all x3, waiting for transfers between devices, summed_on_arrival(): lax.all_to_all(parts, axis, split_axis=0, concat_axis=0, tiled=True)  21.3 us
    all_to_all x4, starting transfers between devices, from_everyone(): lax.all_to_all(jnp.broadcast_to(array[None], (length, *array.shape)), axi...  20.6 us
    all_to_all x3, starting transfers between devices, summed_on_arrival(): lax.all_to_all(parts, axis, split_axis=0, concat_axis=0, tiled=True)  17.5 us
    dot_general x18, matrix products, filter_terms(): lax.dot_general(window, gradient, (((0, 1, 2), (0, 1, 2)), ((), ())), pre...  13.9 us
    all_to_all x1, waiting for transfers between devices, sum_at_owner(): parts = lax.all_to_all(split_up(array, dim, length), axis, 0, 0, tiled=True)  12.7 us
    dot_general x18, matrix products, make_terms(): lax.dot_general(window, filt_local[0, row_tap, col_tap], (((3,), (1,)), (...  9.68 us
    all_to_all x1, blocking collectives, from_everyone(): lax.all_to_all(jnp.broadcast_to(array[None], (length, *array.shape)), axi...  5.06 us
  transfers between devices with their start and end apart: 12, of which 12 were waited for; matrix products, arithmetic and copies ran while one was open for 10% of the time, Pallas kernels for 0%

commit v1 on v0

v1 whole, which is shorter than its diff:
```python
import functools

import jax
import jax.numpy as jnp
from jax import lax
from jax.experimental import pallas as pl
from jax.experimental.pallas import tpu as pltpu
from jax.sharding import Mesh
from jax.sharding import PartitionSpec as P

CHIPS = ("rot_x", "rot_y")
CORE = "rot_c"
ROT = (*CHIPS, CORE)
AZ = "az"

ROWS = 4
CHAN = 128
WIDE = ROWS * CHAN
SWAP = [(0, 1), (1, 0)]
VMEM = pl.BlockSpec(memory_space=pltpu.VMEM)
SMEM = pl.BlockSpec(memory_space=pltpu.SMEM)


def slope(pre):
    logistic = 1.0 / (1.0 + jnp.exp(-pre))
    return logistic * (1.0 + pre * (1.0 - logistic))


def params():
    return pltpu.CompilerParams(vmem_limit_bytes=40 * 1024 * 1024)


def call(kernel, out_shape, scratch, flops, *operands):
    n_bytes = sum(a.size * a.dtype.itemsize for a in operands)
    in_specs = [SMEM if a.dtype == jnp.int32 else VMEM for a in operands]
    out_specs = jax.tree.map(lambda _: VMEM, out_shape)
    return pl.pallas_call(
        kernel,
        out_shape=out_shape,
        in_specs=in_specs,
        out_specs=out_specs,
        scratch_shapes=scratch,
        compiler_params=params(),
        cost_estimate=pl.CostEstimate(flops=flops, bytes_accessed=2 * n_bytes, transcendentals=0),
    )(*operands)


def interleave(blocks_ref, rows_ref, orients, width, shift):
    per_block = blocks_ref.shape[2] // WIDE
    for g in range(orients):
        s = (g - shift) % orients
        lanes = slice((s % per_block) * WIDE, (s % per_block + 1) * WIDE)
        rows_ref[:, g, :] = blocks_ref[s // per_block, :width, lanes].astype(jnp.float32)


def band_weights(filt_ref, band_ref, slot):
    zero = jnp.zeros((CHAN, CHAN), jnp.bfloat16)
    for j in range(3):
        for out_row in range(ROWS):
            for in_row in range(ROWS):
                i = out_row - in_row + 1
                piece = filt_ref[i, j] if 0 <= i < 3 else zero
                band_ref[
                    slot,
                    j,
                    out_row * CHAN : (out_row + 1) * CHAN,
                    in_row * CHAN : (in_row + 1) * CHAN,
                ] = piece


def conv_kernel(
    orients, width, place_ref, blocks_ref, mine_ref, other_ref, out_ref, rows_0, rows_1, band, sums
):
    chip, core = place_ref[0], place_ref[1]
    in_width = rows_0.shape[0]
    band_weights(mine_ref, band, core)
    band_weights(other_ref, band, 1 - core)
    interleave(blocks_ref, rows_0, orients, in_width, 0)
    interleave(blocks_ref, rows_1, orients, in_width, 1)
    total = None
    for slot, rows in ((0, rows_0), (1, rows_1)):
        flat = rows[...].reshape(in_width * orients, WIDE).astype(jnp.bfloat16)
        for j in range(3):
            window = flat[(2 - j) * orients : (2 - j + width) * orients]
            term = lax.dot_general(
                window,
                band[slot, j],
                (((1,), (1,)), ((), ())),
                preferred_element_type=jnp.float32,
            )
            total = term if total is None else total + term
    sums[...] = jnp.zeros_like(sums)
    sums[:width] = total.reshape(width, orients, WIDE)
    chips = orients // 2
    for pair in range(chips):
        to = lax.rem(pair + chip, chips)
        for half in range(2):
            out_ref[to, :, half * WIDE : (half + 1) * WIDE] = sums[:, 2 * pair + half, :].astype(
                jnp.bfloat16
            )


def conv(place, blocks, mine, other, width, out_width):
    orients = 16
    in_width = blocks.shape[1]
    return call(
        functools.partial(conv_kernel, orients, width),
        jax.ShapeDtypeStruct((orients // 2, out_width, 2 * WIDE), jnp.bfloat16),
        [
            pltpu.VMEM((in_width, orients, WIDE), jnp.float32),
            pltpu.VMEM((in_width, orients, WIDE), jnp.float32),
            pltpu.VMEM((2, 3, WIDE, WIDE), jnp.bfloat16),
            pltpu.VMEM((out_width, orients, WIDE), jnp.float32),
        ],
        2 * 6 * width * orients * WIDE * WIDE,
        place,
        blocks,
        mine,
        other,
    )


def filter_kernel(
    orients, width, first, place_ref, feat_ref, grad_ref, mine_ref, other_ref, feat_rows, grad_rows
):
    chip, core = place_ref[0], place_ref[1]
    in_width = grad_rows.shape[0]
    interleave(grad_ref, grad_rows, orients, in_width, 0)
    grads = grad_rows[...].reshape(in_width * orients, WIDE).astype(jnp.bfloat16)
    for out_ref, slot in ((other_ref, 1 - core), (mine_ref, core)):
        for g in range(orients):
            feat_rows[:, g, :] = feat_ref[lax.rem(g + 2 * chip + slot, orients)].astype(jnp.float32)
        feats = feat_rows[...].reshape(width * orients, WIDE).astype(jnp.bfloat16)
        for j in range(3):
            window = grads[(first - j) * orients : (first - j + width) * orients]
            product = lax.dot_general(
                feats,
                window,
                (((0,), (0,)), ((), ())),
                preferred_element_type=jnp.float32,
            )
            for i in range(3):
                total = None
                for row in range(ROWS):
                    grad_row = row - i + 1
                    if not 0 <= grad_row < ROWS:
                        continue
                    piece = product[
                        row * CHAN : (row + 1) * CHAN, grad_row * CHAN : (grad_row + 1) * CHAN
                    ]
                    total = piece if total is None else total + piece
                out_ref[i, j] = total.astype(jnp.bfloat16)


def filter_terms(place, feats, grads, first):
    orients = feats.shape[0]
    width = feats.shape[1]
    in_width = grads.shape[1]
    bank = jax.ShapeDtypeStruct((3, 3, CHAN, CHAN), jnp.bfloat16)
    mine, other = call(
        functools.partial(filter_kernel, orients, width, first),
        (bank, bank),
        [
            pltpu.VMEM((width, orients, WIDE), jnp.float32),
            pltpu.VMEM((in_width, orients, WIDE), jnp.float32),
        ],
        2 * 6 * width * orients * WIDE * WIDE,
        place,
        feats,
        grads,
    )
    theirs = lax.ppermute(other, CORE, SWAP)
    both = mine.astype(jnp.float32) + theirs.astype(jnp.float32)
    return both.astype(jnp.bfloat16)


def point_kernel(parts_ref, pre_ref, out_ref):
    total = parts_ref[0].astype(jnp.float32)
    for n in range(1, parts_ref.shape[0]):
        total = total + parts_ref[n].astype(jnp.float32)
    grad = (total * slope(pre_ref[...].astype(jnp.float32))).astype(jnp.bfloat16)
    for n in range(out_ref.shape[0]):
        out_ref[n] = grad


def to_everyone(array, axes):
    count = lax.axis_size(axes)
    return jnp.broadcast_to(array[None], (count, *array.shape))


def exchange(parts, axes):
    return lax.all_to_all(parts, axes, 0, 0, tiled=True)


def reduce_kernel(parts_ref, out_ref):
    total = parts_ref[0].astype(jnp.float32)
    for n in range(1, parts_ref.shape[0]):
        total = total + parts_ref[n].astype(jnp.float32)
    total = total.astype(jnp.bfloat16)
    for n in range(out_ref.shape[0]):
        out_ref[n] = total


def summed_over_az(bank, scale):
    count = lax.axis_size(AZ)
    lines = bank.reshape(count, -1, CHAN)
    arrived = exchange(lines, AZ)
    copies = call(
        reduce_kernel, jax.ShapeDtypeStruct(lines.shape, jnp.bfloat16), [], lines.size, arrived
    )
    whole = exchange(copies, AZ).reshape(bank.shape)
    return whole.astype(jnp.float32)[None] * scale


def shards(inputs, pre_one, pre_two, cotangent, filt_one, filt_two):
    columns = inputs.shape[2]
    half = columns // 2
    chip = lax.axis_index(CHIPS)
    core = lax.axis_index(CORE)
    place = jnp.stack([chip, core]).astype(jnp.int32)
    az_count = lax.axis_size(AZ)
    cell_count = lax.axis_size(ROT) * inputs.shape[1] * columns * az_count
    scale = cell_count ** (-0.5)

    def lines(field):
        return jnp.moveaxis(field[0], 0, 1).reshape(columns, WIDE)

    grad_two = lines((cotangent.astype(jnp.float32) * slope(pre_two.astype(jnp.float32))).astype(jnp.bfloat16))
    pre = lines(pre_one)
    forward = [(i, (i + 1) % az_count) for i in range(az_count)]
    backward = [(target, source) for source, target in forward]
    low = lax.ppermute(jnp.concatenate([grad_two[-2:], pre[-1:]]), AZ, forward)
    high = lax.ppermute(jnp.concatenate([grad_two[:2], pre[:1]]), AZ, backward)
    grad_rim = jnp.concatenate([low[:2], grad_two, high[:2]])
    halves = jnp.stack([jnp.pad(grad_rim[n * half : n * half + half + 4], ((0, 4), (0, 0))) for n in range(2)])
    chips = lax.axis_size(CHIPS)
    sent = jnp.broadcast_to(halves[None], (chips, *halves.shape)).reshape(2 * chips, *halves.shape[1:])
    all_grad_two = exchange(sent, ROT)

    other_two = lax.ppermute(filt_two[0], CORE, SWAP)
    other_one = lax.ppermute(filt_one[0], CORE, SWAP)
    act = lines(jax.nn.silu(pre_one.astype(jnp.float32)).astype(jnp.bfloat16))
    feats = jnp.concatenate([act, lines(inputs)], axis=1).reshape(2, half, 2 * WIDE)
    sent = jnp.broadcast_to(feats[None], (chips, *feats.shape)).reshape(2 * chips, *feats.shape[1:])
    all_feats = exchange(sent, ROT)
    all_act, all_inputs = all_feats[:, :, :WIDE], all_feats[:, :, WIDE:]
    pre_rim = jnp.concatenate([low[2:], pre, high[2:]])
    pre_halves = jnp.stack([pre_rim[: half + 2], pre_rim[half:]])
    pre_mine = lax.dynamic_index_in_dim(pre_halves, core, 0, keepdims=False)
    pre_other = lax.ppermute(lax.dynamic_index_in_dim(pre_halves, 1 - core, 0, keepdims=False), CORE, SWAP)
    pre_pair = jnp.where(
        core == 0,
        jnp.concatenate([pre_mine, pre_other], axis=1),
        jnp.concatenate([pre_other, pre_mine], axis=1),
    )
    pre_pair = jnp.pad(pre_pair, ((0, 6), (0, 0)))

    parts = exchange(conv(place, all_grad_two, filt_two[0], other_two, half + 2, half + 8), CHIPS)
    copies = call(
        point_kernel, jax.ShapeDtypeStruct(parts.shape, jnp.bfloat16), [], parts.size, parts, pre_pair
    )
    bank_two = filter_terms(place, all_act, all_grad_two, 3)
    all_grad_one = exchange(copies, CHIPS)
    bank_one = filter_terms(place, all_inputs, all_grad_one, 2)
    filt_grad_two = summed_over_az(bank_two, scale)
    filt_grad_one = summed_over_az(bank_one, scale)

    parts = exchange(conv(place, all_grad_one, filt_one[0], other_one, half, half), CHIPS)
    total = jnp.sum(parts.astype(jnp.float32), axis=0).astype(jnp.bfloat16)
    pair = total.reshape(half, 2, WIDE)
    mine = lax.dynamic_index_in_dim(pair, core, 1, keepdims=False)
    theirs = lax.ppermute(lax.dynamic_index_in_dim(pair, 1 - core, 1, keepdims=False), CORE, SWAP)
    whole = jnp.where(core == 0, jnp.concatenate([mine, theirs]), jnp.concatenate([theirs, mine]))
    input_grad = jnp.moveaxis(whole.reshape(columns, ROWS, CHAN), 1, 0)[None]
    return input_grad, filt_grad_one, filt_grad_two


def solution(mesh):
    finer = Mesh(mesh.devices.reshape(4, 2, 2, mesh.shape["az"]), (*ROT, AZ))
    field = P(ROT, None, AZ, None)
    bank = P(ROT, None, None, None, None)
    return jax.shard_map(
        shards,
        mesh=finer,
        in_specs=(field, field, field, field, bank, bank),
        out_specs=(field, bank, bank),
        check_vma=False,
    )
```

time: 172 us -> 155 us (0.901)
  matrix products: 23.6 us -> 0 us
  Pallas kernels: 0 us -> 13.4 us
  blocking collectives: 5.06 us -> 0 us
  waiting for transfers between devices: 80.3 us -> 83.6 us
  local copies, waits for them, and re-layouts: 7.42 us -> 5.35 us
  other arithmetic: 6.65 us -> 4.59 us
    dot_general x36 -> x0, matrix products: 23.6 us -> none  [the longest x18 13.9 us: filter_terms(): lax.dot_general(window, gradient, (((0, 1, 2), (0, 1, 2)), ((), ())), pre...]
    pallas_call x0 -> x7, Pallas kernels: none -> 13.4 us  [call(): pl.pallas_call(kernel, out_shape=out_shape, in_specs=in_specs, out_specs=...]
    all_to_all x1 -> x0, blocking collectives: 5.06 us -> none  [from_everyone(): lax.all_to_all(jnp.broadcast_to(array[None], (length, *array.shape)), axi...]
    ppermute x4 -> x8, waiting for transfers between devices: 8.14 us -> 10.7 us  [the longest x1 4.45 us: shards(): low = lax.ppermute(jnp.concatenate([grad_two[-2:], pre[-1:]]), AZ, forward)]
    broadcast_in_dim x7 -> x2, local copies, waits for them, and re-layouts: 4.09 us -> 1.63 us  [the longest x1 0.85 us: shards(): jnp.broadcast_to(feats[None], (chips, *feats.shape))]
    concatenate x5 -> x2, other arithmetic: 2.41 us -> 0.02 us  [the longest x1 0.01 us: shards(): high = lax.ppermute(jnp.concatenate([grad_two[:2], pre[:1]]), AZ, backward)]
    all_to_all x8 -> x9, waiting for transfers between devices: 72.2 us -> 73 us  [exchange(): return lax.all_to_all(parts, axes, 0, 0, tiled=True)]
    ppermute x4 -> x8, starting transfers between devices: 4.21 us -> 3.7 us  [the longest x1 1.92 us: shards(): high = lax.ppermute(jnp.concatenate([grad_two[:2], pre[:1]]), AZ, backward)]
  transfers between devices with their start and end apart: 12 -> 17, of which waited for: 12 -> 15; matrix products, arithmetic and copies ran while one was open for 10% -> 2% of each run, Pallas kernels for 0% -> 6%
where the time goes in v1:
time: 155 us; the launch traced here: 153 us
  waiting for transfers between devices  83.6 us (54%)
  starting transfers between devices  45.4 us (29%)
  Pallas kernels  13.4 us (9%)
  local copies, waits for them, and re-layouts  5.35 us (3%)
  other arithmetic  4.59 us (3%)
    all_to_all x9, waiting for transfers between devices, exchange(): return lax.all_to_all(parts, axes, 0, 0, tiled=True)  73 us
    all_to_all x9, starting transfers between devices, exchange(): return lax.all_to_all(parts, axes, 0, 0, tiled=True)  41.7 us
    pallas_call x7, Pallas kernels, call(): pl.pallas_call(kernel, out_shape=out_shape, in_specs=in_specs, out_specs=...  13.4 us
    ppermute x1, waiting for transfers between devices, shards(): low = lax.ppermute(jnp.concatenate([grad_two[-2:], pre[-1:]]), AZ, forward)  4.45 us
  transfers between devices with their start and end apart: 17, of which 15 were waited for; matrix products, arithmetic and copies ran while one was open for 2% of the time, Pallas kernels for 6%

profile of v1, /device:TPU:32, one launch (start us, length us, event | category | flops | bytes accessed | tf_op | source)
XLA Modules:
  0.0 153.3 jit_solution(11862129592900901229)
XLA Ops:
  2.3 1.9 %collective-permute-start.1 = (bf16[3,512]{1,0:T(4,128)(2,1)S(1)}, bf16[3,512]{1,0:T(4,128)(2,1)S(1)}, u32[]{:S(2)}, u32[]{:S(2)}) collective-permute-start(bf16[3,512]{1,0:T(4,128)(2,1)S(1)} %pad_maximum_fusion.5), channel_id=1, source_target_pairs={{1,0},{2,1},{3,2},{4,3},{5,4},{6,5},{7,6},{8,7},{9,8},{10,9},{11,1... | collective-permute-start | bytes 9224 | tf_op jit(solution)/shard_map/ppermute | solution.py:233
  6.5 4.5 %collective-permute-done = bf16[3,512]{1,0:T(4,128)(2,1)S(1)} collective-permute-done((bf16[3,512]{1,0:T(4,128)(2,1)S(1)}, bf16[3,512]{1,0:T(4,128)(2,1)S(1)}, u32[]{:S(2)}, u32[]{:S(2)}) %collective-permute-start) | collective-permute-done | bytes 3104 | tf_op jit(solution)/shard_map/ppermute | solution.py:232
  12.5 6.9 %all-to-all-start = ((bf16[16,24,512]{2,1,0:T(8,128)(2,1)}), bf16[16,24,512]{2,1,0:T(8,128)(2,1)S(1)}, u32[]{:S(2)}, u32[]{:S(2)}) async-start(bf16[16,24,512]{2,1,0:T(8,128)(2,1)} %bitcast.14), calls=%async_computation | async-start | bytes 786432 | tf_op jit(solution)/shard_map/all_to_all | solution.py:192
  21.1 9.0 %all-to-all-done.blocks_ref.grad_ref = bf16[16,24,512]{2,1,0:T(8,128)(2,1)S(1)} async-done(((bf16[16,24,512]{2,1,0:T(8,128)(2,1)}), bf16[16,24,512]{2,1,0:T(8,128)(2,1)S(1)}, u32[]{:S(2)}, u32[]{:S(2)}) %all-to-all-start) | async-done | bytes 393248 | tf_op jit(solution)/shard_map/all_to_all | solution.py:192
  30.1 3.7 %shard_map.85 = bf16[8,24,1024]{2,1,0:T(8,128)(2,1)} custom-call(s32[2]{0:T(128)S(1)} %pad_add_fusion.place_ref, bf16[16,24,512]{2,1,0:T(8,128)(2,1)S(1)} %all-to-all-done.blocks_ref.grad_ref, bf16[3,3,128,128]{3,2,1,0:T(8,128)(2,1)S(1)} %bitcast.64, bf16[3,3,128,128]{3,2,1,0:T(8,128)(2,1)S(1)} %collective-permute-done.2.other_ref), custom_call_target="tpu_custom_call" | custom-call | flops 905969664 | bytes 1966096 | tf_op jit(solution)/shard_map/pallas_call | solution.py:37
  33.9 3.6 %all-to-all-start.1 = ((bf16[8,24,1024]{2,1,0:T(8,128)(2,1)}), bf16[8,24,1024]{2,1,0:T(8,128)(2,1)S(1)}, u32[]{:S(2)}, u32[]{:S(2)}) async-start(bf16[8,24,1024]{2,1,0:T(8,128)(2,1)} %shard_map.85), calls=%async_computation.1 | async-start | bytes 786432 | tf_op jit(solution)/shard_map/all_to_all | solution.py:192
  38.4 8.9 %all-to-all-done.1.parts_ref = bf16[8,24,1024]{2,1,0:T(8,128)(2,1)S(1)} async-done(((bf16[8,24,1024]{2,1,0:T(8,128)(2,1)}), bf16[8,24,1024]{2,1,0:T(8,128)(2,1)S(1)}, u32[]{:S(2)}, u32[]{:S(2)}) %all-to-all-start.1) | async-done | bytes 393248 | tf_op jit(solution)/shard_map/all_to_all | solution.py:192
  48.1 3.7 %all-to-all-start.4 = ((bf16[16,16,1024]{2,1,0:T(8,128)(2,1)}), bf16[16,16,1024]{2,1,0:T(8,128)(2,1)S(1)}, u32[]{:S(2)}, u32[]{:S(2)}) async-start(bf16[16,16,1024]{2,1,0:T(8,128)(2,1)} %bitcast.28), calls=%async_computation.4 | async-start | bytes 1048576 | tf_op jit(solution)/shard_map/all_to_all | solution.py:192
  54.5 9.6 %all-to-all-done.4 = bf16[16,16,1024]{2,1,0:T(8,128)(2,1)S(1)} async-done(((bf16[16,16,1024]{2,1,0:T(8,128)(2,1)}), bf16[16,16,1024]{2,1,0:T(8,128)(2,1)S(1)}, u32[]{:S(2)}, u32[]{:S(2)}) %all-to-all-start.4) | async-done | bytes 524320 | tf_op jit(solution)/shard_map/all_to_all | solution.py:192
  64.2 3.5 %all-to-all-start.2 = ((bf16[8,24,1024]{2,1,0:T(8,128)(2,1)}), bf16[8,24,1024]{2,1,0:T(8,128)(2,1)S(1)}, u32[]{:S(2)}, u32[]{:S(2)}) async-start(bf16[8,24,1024]{2,1,0:T(8,128)(2,1)} %shard_map.86), calls=%async_computation.2 | async-start | bytes 786432 | tf_op jit(solution)/shard_map/all_to_all | solution.py:192
  67.7 2.0 %shard_map.90 = (bf16[3,3,128,128]{3,2,1,0:T(8,128)(2,1)S(1)}, bf16[3,3,128,128]{3,2,1,0:T(8,128)(2,1)S(1)}) custom-call(s32[2]{0:T(128)S(1)} %pad_add_fusion.place_ref, bf16[16,16,512]{2,1,0:T(8,128)(2,1)S(1)} %get-tuple-element.17.feat_ref, bf16[16,24,512]{2,1,0:T(8,128)(2,1)S(1)} %all-to-all-done.blocks_ref.grad_ref), custom_call_target="tpu_custom_call" | custom-call | flops 805306368 | bytes 1310736 | tf_op jit(solution)/shard_map/pallas_call | solution.py:37
  69.8 7.3 %all-to-all-done.2.blocks_ref.grad_ref = bf16[8,24,1024]{2,1,0:T(8,128)(2,1)S(1)} async-done(((bf16[8,24,1024]{2,1,0:T(8,128)(2,1)}), bf16[8,24,1024]{2,1,0:T(8,128)(2,1)S(1)}, u32[]{:S(2)}, u32[]{:S(2)}) %all-to-all-start.2) | async-done | bytes 393248 | tf_op jit(solution)/shard_map/all_to_all | solution.py:192
  77.1 3.3 %shard_map.87 = bf16[8,16,1024]{2,1,0:T(8,128)(2,1)} custom-call(s32[2]{0:T(128)S(1)} %pad_add_fusion.place_ref, bf16[8,24,1024]{2,1,0:T(8,128)(2,1)S(1)} %all-to-all-done.2.blocks_ref.grad_ref, bf16[3,3,128,128]{3,2,1,0:T(8,128)(2,1)S(1)} %bitcast.66, bf16[3,3,128,128]{3,2,1,0:T(8,128)(2,1)S(1)} %collective-permute-done.4.other_ref), custom_call_target="tpu_custom_call" | custom-call | flops 805306368 | bytes 1966096 | tf_op jit(solution)/shard_map/pallas_call | solution.py:37
  80.4 3.4 %all-to-all-start.3 = ((bf16[8,16,1024]{2,1,0:T(8,128)(2,1)}), bf16[8,16,1024]{2,1,0:T(8,128)(2,1)S(1)}, u32[]{:S(2)}, u32[]{:S(2)}) async-start(bf16[8,16,1024]{2,1,0:T(8,128)(2,1)} %shard_map.87), calls=%async_computation.3 | async-start | bytes 524288 | tf_op jit(solution)/shard_map/all_to_all | solution.py:192
  84.6 7.6 %all-to-all-done.3 = bf16[8,16,1024]{2,1,0:T(8,128)(2,1)S(1)} async-done(((bf16[8,16,1024]{2,1,0:T(8,128)(2,1)}), bf16[8,16,1024]{2,1,0:T(8,128)(2,1)S(1)}, u32[]{:S(2)}, u32[]{:S(2)}) %all-to-all-start.3) | async-done | bytes 262176 | tf_op jit(solution)/shard_map/all_to_all | solution.py:192
  92.2 7.5 %all-to-all-start.7 = ((bf16[16,72,128]{2,1,0:T(8,128)(2,1)}), bf16[16,72,128]{2,1,0:T(8,128)(2,1)S(1)}, u32[]{:S(2)}, u32[]{:S(2)}) async-start(bf16[16,72,128]{2,1,0:T(8,128)(2,1)} %bitcast.31), calls=%async_computation.7 | async-start | bytes 589824 | tf_op jit(solution)/shard_map/all_to_all | solution.py:192
  99.7 2.0 %shard_map.88 = (bf16[3,3,128,128]{3,2,1,0:T(8,128)(2,1)S(1)}, bf16[3,3,128,128]{3,2,1,0:T(8,128)(2,1)S(1)}) custom-call(s32[2]{0:T(128)S(1)} %pad_add_fusion.place_ref, bf16[16,16,512]{2,1,0:T(8,128)(2,1)S(1)} %get-tuple-element.18.feat_ref, bf16[8,24,1024]{2,1,0:T(8,128)(2,1)S(1)} %all-to-all-done.2.blocks_ref.grad_ref), custom_call_target="tpu_custom_call" | custom-call | flops 805306368 | bytes 1310736 | tf_op jit(solution)/shard_map/pallas_call | solution.py:37
  104.1 4.9 %all-to-all-done.7.parts_ref = bf16[16,72,128]{2,1,0:T(8,128)(2,1)S(1)} async-done(((bf16[16,72,128]{2,1,0:T(8,128)(2,1)}), bf16[16,72,128]{2,1,0:T(8,128)(2,1)S(1)}, u32[]{:S(2)}, u32[]{:S(2)}) %all-to-all-start.7) | async-done | bytes 294944 | tf_op jit(solution)/shard_map/all_to_all | solution.py:192
  109.0 4.3 %all-to-all-start.5 = ((bf16[16,72,128]{2,1,0:T(8,128)(2,1)}), bf16[16,72,128]{2,1,0:T(8,128)(2,1)S(1)}, u32[]{:S(2)}, u32[]{:S(2)}) async-start(bf16[16,72,128]{2,1,0:T(8,128)(2,1)} %bitcast.29), calls=%async_computation.5 | async-start | bytes 589824 | tf_op jit(solution)/shard_map/all_to_all | solution.py:192
  114.1 9.4 %all-to-all-done.5.parts_ref = bf16[16,72,128]{2,1,0:T(8,128)(2,1)S(1)} async-done(((bf16[16,72,128]{2,1,0:T(8,128)(2,1)}), bf16[16,72,128]{2,1,0:T(8,128)(2,1)S(1)}, u32[]{:S(2)}, u32[]{:S(2)}) %all-to-all-start.5) | async-done | bytes 294944 | tf_op jit(solution)/shard_map/all_to_all | solution.py:192
  123.5 4.4 %all-to-all-start.8 = ((bf16[16,72,128]{2,1,0:T(8,128)(2,1)}), bf16[16,72,128]{2,1,0:T(8,128)(2,1)S(1)}, u32[]{:S(2)}, u32[]{:S(2)}) async-start(bf16[16,72,128]{2,1,0:T(8,128)(2,1)} %shard_map.91), calls=%async_computation.8 | async-start | bytes 589824 | tf_op jit(solution)/shard_map/all_to_all | solution.py:192
  128.7 9.3 %all-to-all-done.8 = bf16[16,72,128]{2,1,0:T(8,128)(2,1)S(1)} async-done(((bf16[16,72,128]{2,1,0:T(8,128)(2,1)}), bf16[16,72,128]{2,1,0:T(8,128)(2,1)S(1)}, u32[]{:S(2)}, u32[]{:S(2)}) %all-to-all-start.8) | async-done | bytes 294944 | tf_op jit(solution)/shard_map/all_to_all | solution.py:192
  138.0 4.4 %all-to-all-start.6 = ((bf16[16,72,128]{2,1,0:T(8,128)(2,1)}), bf16[16,72,128]{2,1,0:T(8,128)(2,1)S(1)}, u32[]{:S(2)}, u32[]{:S(2)}) async-start(bf16[16,72,128]{2,1,0:T(8,128)(2,1)} %shard_map.89), calls=%async_computation.6 | async-start | bytes 589824 | tf_op jit(solution)/shard_map/all_to_all | solution.py:192
  145.5 7.0 %all-to-all-done.6 = bf16[16,72,128]{2,1,0:T(8,128)(2,1)S(1)} async-done(((bf16[16,72,128]{2,1,0:T(8,128)(2,1)}), bf16[16,72,128]{2,1,0:T(8,128)(2,1)S(1)}, u32[]{:S(2)}, u32[]{:S(2)}) %all-to-all-start.6) | async-done | bytes 294944 | tf_op jit(solution)/shard_map/all_to_all | solution.py:192
  (75 shorter events, 20.3 us)
Async XLA Ops:
  1.4 3.1 %copy-start.3 = (bf16[1,4,32,128]{3,2,1,0:T(8,128)(2,1)S(1)}, bf16[1,4,32,128]{3,2,1,0:T(8,128)(2,1)}, u32[]{:S(2)}) copy-start(bf16[1,4,32,128]{3,2,1,0:T(8,128)(2,1)} %param.8) | copy-start | bytes 98308
  1.4 3.1 %copy-start.4 = (bf16[1,4,32,128]{3,2,1,0:T(8,128)(2,1)S(1)}, bf16[1,4,32,128]{3,2,1,0:T(8,128)(2,1)}, u32[]{:S(2)}) copy-start(bf16[1,4,32,128]{3,2,1,0:T(8,128)(2,1)} %param.9) | copy-start | bytes 98308
  2.3 3.7 %collective-permute-start.1 = (bf16[3,512]{1,0:T(4,128)(2,1)S(1)}, bf16[3,512]{1,0:T(4,128)(2,1)S(1)}, u32[]{:S(2)}, u32[]{:S(2)}) collective-permute-start(bf16[3,512]{1,0:T(4,128)(2,1)S(1)} %pad_maximum_fusion.5), channel_id=1, source_target_pairs={{1,0},{2,1},{3,2},{4,3},{5,4},{6,5},{7,6},{8,7},{9,8},{10,9},{11,1... | collective-permute-start | bytes 9224 | tf_op jit(solution)/shard_map/ppermute | solution.py:233
  4.2 6.8 %collective-permute-start = (bf16[3,512]{1,0:T(4,128)(2,1)S(1)}, bf16[3,512]{1,0:T(4,128)(2,1)S(1)}, u32[]{:S(2)}, u32[]{:S(2)}) collective-permute-start(bf16[3,512]{1,0:T(4,128)(2,1)S(1)} %pad_maximum_fusion.4), channel_id=1, source_target_pairs={{0,1},{1,2},{2,3},{3,4},{4,5},{5,6},{6,7},{7,8},{8,9},{9,10},{10,1... | collective-permute-start | bytes 9224 | tf_op jit(solution)/shard_map/ppermute | solution.py:232
  6.5 4.5 %copy-start.8 = (pred[24]{0:T(512)(128)(4,1)S(1)}, pred[24]{0:T(512)(128)(4,1)}, u32[]{:S(2)}) copy-start(pred[24]{0:T(512)(128)(4,1)} %constant.42.clone.1) | copy-start | bytes 76
  12.5 6.9 %copy-start = (bf16[1,3,3,128,128]{4,3,2,1,0:T(8,128)(2,1)S(1)}, bf16[1,3,3,128,128]{4,3,2,1,0:T(8,128)(2,1)}, u32[]{:S(2)}) copy-start(bf16[1,3,3,128,128]{4,3,2,1,0:T(8,128)(2,1)} %param.11) | copy-start | bytes 884740
  12.5 17.6 %all-to-all-start = ((bf16[16,24,512]{2,1,0:T(8,128)(2,1)}), bf16[16,24,512]{2,1,0:T(8,128)(2,1)S(1)}, u32[]{:S(2)}, u32[]{:S(2)}) async-start(bf16[16,24,512]{2,1,0:T(8,128)(2,1)} %bitcast.14), calls=%async_computation | async-start | bytes 786432 | tf_op jit(solution)/shard_map/all_to_all | solution.py:192
  19.4 1.7 %collective-permute-start.2 = (bf16[3,3,128,128]{3,2,1,0:T(8,128)(2,1)S(1)}, bf16[3,3,128,128]{3,2,1,0:T(8,128)(2,1)S(1)}, u32[]{:S(2)}, u32[]{:S(2)}) collective-permute-start(bf16[3,3,128,128]{3,2,1,0:T(8,128)(2,1)S(1)} %bitcast.63), channel_id=1, source_target_pairs={{0,16},{16,0},{1,17},{17,1},{2,18},{18,2},{3,19},{19,3},{4,20},{20... | collective-permute-start | bytes 884744 | tf_op jit(solution)/shard_map/ppermute | solution.py:240
  33.9 3.6 %copy-start.5 = (bf16[1,4,32,128]{3,2,1,0:T(8,128)(2,1)S(1)}, bf16[1,4,32,128]{3,2,1,0:T(8,128)(2,1)}, u32[]{:S(2)}) copy-start(bf16[1,4,32,128]{3,2,1,0:T(8,128)(2,1)} %param.6) | copy-start | bytes 98308
  33.9 13.4 %all-to-all-start.1 = ((bf16[8,24,1024]{2,1,0:T(8,128)(2,1)}), bf16[8,24,1024]{2,1,0:T(8,128)(2,1)S(1)}, u32[]{:S(2)}, u32[]{:S(2)}) async-start(bf16[8,24,1024]{2,1,0:T(8,128)(2,1)} %shard_map.85), calls=%async_computation.1 | async-start | bytes 786432 | tf_op jit(solution)/shard_map/all_to_all | solution.py:192
  48.1 3.7 %copy-start.7 = (bf16[3,512]{1,0:T(4,128)(2,1)S(1)}, bf16[3,512]{1,0:T(4,128)(2,1)}, u32[]{:S(2)}) copy-start(bf16[3,512]{1,0:T(4,128)(2,1)} %copy-done.6) | copy-start | bytes 9220
  48.1 16.0 %all-to-all-start.4 = ((bf16[16,16,1024]{2,1,0:T(8,128)(2,1)}), bf16[16,16,1024]{2,1,0:T(8,128)(2,1)S(1)}, u32[]{:S(2)}, u32[]{:S(2)}) async-start(bf16[16,16,1024]{2,1,0:T(8,128)(2,1)} %bitcast.28), calls=%async_computation.4 | async-start | bytes 1048576 | tf_op jit(solution)/shard_map/all_to_all | solution.py:192
  51.8 1.5 copy-start.1
  52.0 1.3 collective-permute-start.3
  53.3 16.5 %collective-permute-start.4 = (bf16[3,3,128,128]{3,2,1,0:T(8,128)(2,1)S(1)}, bf16[3,3,128,128]{3,2,1,0:T(8,128)(2,1)S(1)}, u32[]{:S(2)}, u32[]{:S(2)}) collective-permute-start(bf16[3,3,128,128]{3,2,1,0:T(8,128)(2,1)S(1)} %bitcast.65), channel_id=1, source_target_pairs={{0,16},{16,0},{1,17},{17,1},{2,18},{18,2},{3,19},{19,3},{4,20},{20... | collective-permute-start | bytes 884744 | tf_op jit(solution)/shard_map/ppermute | solution.py:241
  64.2 12.9 %all-to-all-start.2 = ((bf16[8,24,1024]{2,1,0:T(8,128)(2,1)}), bf16[8,24,1024]{2,1,0:T(8,128)(2,1)S(1)}, u32[]{:S(2)}, u32[]{:S(2)}) async-start(bf16[8,24,1024]{2,1,0:T(8,128)(2,1)} %shard_map.86), calls=%async_computation.2 | async-start | bytes 786432 | tf_op jit(solution)/shard_map/all_to_all | solution.py:192
  69.7 14.1 %collective-permute-start.7 = (bf16[3,3,128,128]{3,2,1,0:T(8,128)(2,1)S(1)}, bf16[3,3,128,128]{3,2,1,0:T(8,128)(2,1)S(1)}, u32[]{:S(2)}, u32[]{:S(2)}) collective-permute-start(bf16[3,3,128,128]{3,2,1,0:T(8,128)(2,1)S(1)} %get-tuple-element.10), channel_id=1, source_target_pairs={{0,16},{16,0},{1,17},{17,1},{2,18},{18,2},{3,19},{19,3},{4,20},{20... | collective-permute-start | bytes 884744 | tf_op jit(solution)/shard_map/ppermute | solution.py:172
  80.4 11.8 %all-to-all-start.3 = ((bf16[8,16,1024]{2,1,0:T(8,128)(2,1)}), bf16[8,16,1024]{2,1,0:T(8,128)(2,1)S(1)}, u32[]{:S(2)}, u32[]{:S(2)}) async-start(bf16[8,16,1024]{2,1,0:T(8,128)(2,1)} %shard_map.87), calls=%async_computation.3 | async-start | bytes 524288 | tf_op jit(solution)/shard_map/all_to_all | solution.py:192
  92.2 16.8 %all-to-all-start.7 = ((bf16[16,72,128]{2,1,0:T(8,128)(2,1)}), bf16[16,72,128]{2,1,0:T(8,128)(2,1)S(1)}, u32[]{:S(2)}, u32[]{:S(2)}) async-start(bf16[16,72,128]{2,1,0:T(8,128)(2,1)} %bitcast.31), calls=%async_computation.7 | async-start | bytes 589824 | tf_op jit(solution)/shard_map/all_to_all | solution.py:192
  101.6 1.7 %collective-permute-start.6 = (bf16[3,3,128,128]{3,2,1,0:T(8,128)(2,1)S(1)}, bf16[3,3,128,128]{3,2,1,0:T(8,128)(2,1)S(1)}, u32[]{:S(2)}, u32[]{:S(2)}) collective-permute-start(bf16[3,3,128,128]{3,2,1,0:T(8,128)(2,1)S(1)} %get-tuple-element.8), channel_id=1, source_target_pairs={{0,16},{16,0},{1,17},{17,1},{2,18},{18,2},{3,19},{19,3},{4,20},{20... | collective-permute-start | bytes 884744 | tf_op jit(solution)/shard_map/ppermute | solution.py:172
  109.0 14.5 %all-to-all-start.5 = ((bf16[16,72,128]{2,1,0:T(8,128)(2,1)}), bf16[16,72,128]{2,1,0:T(8,128)(2,1)S(1)}, u32[]{:S(2)}, u32[]{:S(2)}) async-start(bf16[16,72,128]{2,1,0:T(8,128)(2,1)} %bitcast.29), calls=%async_computation.5 | async-start | bytes 589824 | tf_op jit(solution)/shard_map/all_to_all | solution.py:192
  123.5 14.5 %all-to-all-start.8 = ((bf16[16,72,128]{2,1,0:T(8,128)(2,1)}), bf16[16,72,128]{2,1,0:T(8,128)(2,1)S(1)}, u32[]{:S(2)}, u32[]{:S(2)}) async-start(bf16[16,72,128]{2,1,0:T(8,128)(2,1)} %shard_map.91), calls=%async_computation.8 | async-start | bytes 589824 | tf_op jit(solution)/shard_map/all_to_all | solution.py:192
  138.0 14.4 %all-to-all-start.6 = ((bf16[16,72,128]{2,1,0:T(8,128)(2,1)}), bf16[16,72,128]{2,1,0:T(8,128)(2,1)S(1)}, u32[]{:S(2)}, u32[]{:S(2)}) async-start(bf16[16,72,128]{2,1,0:T(8,128)(2,1)} %shard_map.89), calls=%async_computation.6 | async-start | bytes 589824 | tf_op jit(solution)/shard_map/all_to_all | solution.py:192
  142.7 1.3 collective-permute-start.5
  (3 other events, 2.0 us)

commit v2 on v1

v2 whole, which is shorter than its diff:
```python
import functools

import jax
import jax.numpy as jnp
from jax import lax
from jax.experimental import pallas as pl
from jax.experimental.pallas import tpu as pltpu
from jax.sharding import Mesh
from jax.sharding import PartitionSpec as P

CHIPS = ("rot_x", "rot_y")
CORE = "rot_c"
ROT = (*CHIPS, CORE)
AZ = "az"

ROWS = 4
CHAN = 128
WIDE = ROWS * CHAN
SWAP = [(0, 1), (1, 0)]
VMEM = pl.BlockSpec(memory_space=pltpu.VMEM)
SMEM = pl.BlockSpec(memory_space=pltpu.SMEM)


def slope(pre):
    logistic = 1.0 / (1.0 + jnp.exp(-pre))
    return logistic * (1.0 + pre * (1.0 - logistic))


def params():
    return pltpu.CompilerParams(vmem_limit_bytes=40 * 1024 * 1024)


def call(kernel, out_shape, scratch, flops, *operands):
    n_bytes = sum(a.size * a.dtype.itemsize for a in operands)
    in_specs = [SMEM if a.dtype == jnp.int32 else VMEM for a in operands]
    out_specs = jax.tree.map(lambda _: VMEM, out_shape)
    return pl.pallas_call(
        kernel,
        out_shape=out_shape,
        in_specs=in_specs,
        out_specs=out_specs,
        scratch_shapes=scratch,
        compiler_params=params(),
        cost_estimate=pl.CostEstimate(flops=flops, bytes_accessed=2 * n_bytes, transcendentals=0),
    )(*operands)


def interleave(blocks_ref, rows_ref, orients, width, shift):
    per_block = blocks_ref.shape[2] // WIDE
    for g in range(orients):
        s = (g - shift) % orients
        lanes = slice((s % per_block) * WIDE, (s % per_block + 1) * WIDE)
        rows_ref[:, g, :] = blocks_ref[s // per_block, :width, lanes].astype(jnp.float32)


def band_weights(filt_ref, band_ref, slot):
    zero = jnp.zeros((CHAN, CHAN), jnp.bfloat16)
    for j in range(3):
        for out_row in range(ROWS):
            for in_row in range(ROWS):
                i = out_row - in_row + 1
                piece = filt_ref[i, j] if 0 <= i < 3 else zero
                band_ref[
                    slot,
                    j,
                    out_row * CHAN : (out_row + 1) * CHAN,
                    in_row * CHAN : (in_row + 1) * CHAN,
                ] = piece


def rotation_sums(orients, width, core, blocks_ref, mine_ref, other_ref, rows_0, rows_1, band):
    in_width = rows_0.shape[0]
    band_weights(mine_ref, band, core)
    band_weights(other_ref, band, 1 - core)
    interleave(blocks_ref, rows_0, orients, in_width, 0)
    interleave(blocks_ref, rows_1, orients, in_width, 1)
    total = None
    for slot, rows in ((0, rows_0), (1, rows_1)):
        flat = rows[...].reshape(in_width * orients, WIDE).astype(jnp.bfloat16)
        for j in range(3):
            window = flat[(2 - j) * orients : (2 - j + width) * orients]
            term = lax.dot_general(
                window,
                band[slot, j],
                (((1,), (1,)), ((), ())),
                preferred_element_type=jnp.float32,
            )
            total = term if total is None else total + term
    return total.reshape(width, orients, WIDE)


def conv_two_kernel(
    orients,
    width,
    place_ref,
    blocks_ref,
    mine_ref,
    other_ref,
    feats_ref,
    partner_ref,
    out_ref,
    rows_0,
    rows_1,
    band,
    sums,
):
    chip, core = place_ref[0], place_ref[1]
    total = rotation_sums(
        orients, width, core, blocks_ref, mine_ref, other_ref, rows_0, rows_1, band
    )
    sums[...] = jnp.zeros_like(sums)
    sums[:width] = total
    chips = orients // 2
    ahead = feats_ref.shape[0]
    feats, partner = feats_ref[...], partner_ref[...]
    first = jnp.where(core == 0, feats, partner)
    second = jnp.where(core == 0, partner, feats)
    for pair in range(chips):
        to = lax.rem(pair + chip, chips)
        for half in range(2):
            out_ref[to, ahead:, half * WIDE : (half + 1) * WIDE] = sums[
                :, 2 * pair + half, :
            ].astype(jnp.bfloat16)
        out_ref[pair, :ahead, :WIDE] = first
        out_ref[pair, :ahead, WIDE:] = second


def conv_one_kernel(
    orients, width, place_ref, blocks_ref, mine_ref, other_ref, out_ref, rows_0, rows_1, band, sums
):
    chip, core = place_ref[0], place_ref[1]
    sums[...] = rotation_sums(
        orients, width, core, blocks_ref, mine_ref, other_ref, rows_0, rows_1, band
    )
    chips = orients // 2
    across = out_ref.shape[1]
    for pair in range(chips):
        to = lax.rem(pair + chip, chips)
        other = lax.rem(to + chip, 2)
        step = lax.rem(to // 2 - chip // 2 + across, across)
        for half in range(2):
            out_ref[other, step, :, half * WIDE : (half + 1) * WIDE] = sums[
                :, 2 * pair + half, :
            ].astype(jnp.bfloat16)


def conv(kernel, place, blocks, width, padded, out_shape, *operands):
    orients = 16
    in_width = blocks.shape[1]
    return call(
        functools.partial(kernel, orients, width),
        jax.ShapeDtypeStruct(out_shape, jnp.bfloat16),
        [
            pltpu.VMEM((in_width, orients, WIDE), jnp.float32),
            pltpu.VMEM((in_width, orients, WIDE), jnp.float32),
            pltpu.VMEM((2, 3, WIDE, WIDE), jnp.bfloat16),
            pltpu.VMEM((padded, orients, WIDE), jnp.float32),
        ],
        2 * 6 * width * orients * WIDE * WIDE,
        place,
        blocks,
        *operands,
    )


def filter_kernel(
    orients, width, feat_first, first, place_ref, feat_ref, grad_ref, mine_ref, other_ref, feat_rows, grad_rows
):
    chip, core = place_ref[0], place_ref[1]
    in_width = grad_rows.shape[0]
    interleave(grad_ref, grad_rows, orients, in_width, 0)
    grads = grad_rows[...].reshape(in_width * orients, WIDE).astype(jnp.bfloat16)
    for out_ref, slot in ((other_ref, 1 - core), (mine_ref, core)):
        for g in range(orients):
            near = lax.rem((g + 1) // 2 + chip, orients // 2)
            here = lax.rem(g // 2 + chip, orients // 2)
            low, high = feat_first, feat_first + width
            shift_0 = feat_ref[here, low:high, (g % 2) * WIDE : (g % 2 + 1) * WIDE]
            shift_1 = feat_ref[near, low:high, ((g + 1) % 2) * WIDE : ((g + 1) % 2 + 1) * WIDE]
            feat_rows[:, g, :] = jnp.where(slot == 0, shift_0, shift_1).astype(jnp.float32)
        feats = feat_rows[...].reshape(width * orients, WIDE).astype(jnp.bfloat16)
        for j in range(3):
            window = grads[(first - j) * orients : (first - j + width) * orients]
            product = lax.dot_general(
                feats,
                window,
                (((0,), (0,)), ((), ())),
                preferred_element_type=jnp.float32,
            )
            for i in range(3):
                total = None
                for row in range(ROWS):
                    grad_row = row - i + 1
                    if not 0 <= grad_row < ROWS:
                        continue
                    piece = product[
                        row * CHAN : (row + 1) * CHAN, grad_row * CHAN : (grad_row + 1) * CHAN
                    ]
                    total = piece if total is None else total + piece
                out_ref[i, j] = total.astype(jnp.bfloat16)


def filter_terms(place, feats, feat_first, width, grads, first):
    orients = 2 * feats.shape[0]
    in_width = grads.shape[1]
    bank = jax.ShapeDtypeStruct((3, 3, CHAN, CHAN), jnp.bfloat16)
    mine, other = call(
        functools.partial(filter_kernel, orients, width, feat_first, first),
        (bank, bank),
        [
            pltpu.VMEM((width, orients, WIDE), jnp.float32),
            pltpu.VMEM((in_width, orients, WIDE), jnp.float32),
        ],
        2 * 6 * width * orients * WIDE * WIDE,
        place,
        feats,
        grads,
    )
    return mine, lax.ppermute(other, CORE, SWAP)


def point_kernel(place_ref, parts_ref, pre_ref, partner_ref, out_ref):
    core = place_ref[1]
    ahead = parts_ref.shape[1] - out_ref.shape[1]
    total = parts_ref[0, ahead:].astype(jnp.float32)
    for n in range(1, parts_ref.shape[0]):
        total = total + parts_ref[n, ahead:].astype(jnp.float32)
    mine = slope(pre_ref[...].astype(jnp.float32))
    partner = slope(partner_ref[...].astype(jnp.float32))
    first = total[:, :WIDE] * jnp.where(core == 0, mine, partner)
    second = total[:, WIDE:] * jnp.where(core == 0, partner, mine)
    first, second = first.astype(jnp.bfloat16), second.astype(jnp.bfloat16)
    for n in range(out_ref.shape[0]):
        out_ref[n, :, :WIDE] = first
        out_ref[n, :, WIDE:] = second


def exchange(parts, axes):
    return lax.all_to_all(parts, axes, 0, 0, tiled=True)


def join_kernel(mine_1, theirs_1, mine_2, theirs_2, out_ref):
    size = mine_1.shape[1]
    for first, mine, theirs in ((0, mine_1, theirs_1), (size, mine_2, theirs_2)):
        both = mine[...].astype(jnp.float32) + theirs[...].astype(jnp.float32)
        out_ref[:, first : first + size] = both.astype(jnp.bfloat16)


def reduce_kernel(parts_ref, out_ref):
    total = parts_ref[0].astype(jnp.float32)
    for n in range(1, parts_ref.shape[0]):
        total = total + parts_ref[n].astype(jnp.float32)
    total = total.astype(jnp.bfloat16)
    for n in range(out_ref.shape[0]):
        out_ref[n] = total


def summed_over_az(pairs, scale):
    count = lax.axis_size(AZ)
    banks = [bank.reshape(count, -1, CHAN) for pair in pairs for bank in pair]
    size = banks[0].shape[1]
    shape = jax.ShapeDtypeStruct((count, 2 * size, CHAN), jnp.bfloat16)
    joined = call(join_kernel, shape, [], count * size * CHAN, *banks)
    copies = call(reduce_kernel, shape, [], count * size * CHAN, exchange(joined, AZ))
    whole = exchange(copies, AZ)
    one, two = whole[:, :size], whole[:, size:]
    return tuple(
        (part.astype(jnp.float32) * scale).reshape(1, 3, 3, CHAN, CHAN) for part in (one, two)
    )


def lanes_kernel(
    place_ref, inputs_ref, pre_one_ref, pre_two_ref, cotangent_ref, grad_ref, pre_ref, feats_ref, partner_ref, up_ref, down_ref
):
    core = place_ref[1]
    columns = grad_ref.shape[0]
    half = columns // 2
    for row in range(ROWS):
        lanes = slice(row * CHAN, (row + 1) * CHAN)
        pre = pre_one_ref[0, row]
        wide = pre.astype(jnp.float32)
        grad = cotangent_ref[0, row].astype(jnp.float32) * slope(
            pre_two_ref[0, row].astype(jnp.float32)
        )
        grad_ref[:, lanes] = grad.astype(jnp.bfloat16)
        pre_ref[:, lanes] = pre
        act = (wide / (1.0 + jnp.exp(-wide))).astype(jnp.bfloat16)
        given = inputs_ref[0, row]
        for first, field in ((0, act), (half, given)):
            low, high = field[:half], field[half:]
            feats_ref[first : first + half, lanes] = jnp.where(core == 0, low, high)
            partner_ref[first : first + half, lanes] = jnp.where(core == 0, high, low)
        grad = grad.astype(jnp.bfloat16).astype(jnp.float32)
        pad = jnp.zeros((5, CHAN), jnp.float32)
        up_ref[:, lanes] = jnp.concatenate([grad[-2:], wide[-1:], pad]).astype(jnp.bfloat16)
        down_ref[:, lanes] = jnp.concatenate([grad[:2], wide[:1], pad]).astype(jnp.bfloat16)


def rims_kernel(
    place_ref, grad_ref, pre_ref, low_ref, high_ref, sent_ref, mine_ref, partner_ref, grad_rim, pre_rim
):
    core = place_ref[1]
    columns = grad_ref.shape[0]
    half = columns // 2
    rows = sent_ref.shape[1]
    low, high = low_ref[...].astype(jnp.float32), high_ref[...].astype(jnp.float32)
    grad_rim[...] = jnp.zeros_like(grad_rim)
    grad_rim[:2] = low[:2]
    grad_rim[2 : 2 + columns] = grad_ref[...].astype(jnp.float32)
    grad_rim[2 + columns : 4 + columns] = high[:2]
    pre_rim[...] = jnp.zeros_like(pre_rim)
    pre_rim[:1] = low[2:3]
    pre_rim[1 : 1 + columns] = pre_ref[...].astype(jnp.float32)
    pre_rim[1 + columns : 2 + columns] = high[2:3]
    for n in range(2):
        part = grad_rim[n * half : n * half + rows].astype(jnp.bfloat16)
        for chip in range(sent_ref.shape[0] // 2):
            sent_ref[2 * chip + n] = part
    left = pre_rim[:rows].astype(jnp.bfloat16)
    right = pre_rim[half : half + rows].astype(jnp.bfloat16)
    mine_ref[...] = jnp.where(core == 0, left, right)
    partner_ref[...] = jnp.where(core == 0, right, left)


def shards(inputs, pre_one, pre_two, cotangent, filt_one, filt_two):
    columns = inputs.shape[2]
    half = columns // 2
    chip = lax.axis_index(CHIPS)
    core = lax.axis_index(CORE)
    place = jnp.stack([chip, core]).astype(jnp.int32)
    az_count = lax.axis_size(AZ)
    rot_count = lax.axis_size(ROT)
    chips = lax.axis_size(CHIPS)
    cell_count = rot_count * inputs.shape[1] * columns * az_count
    scale = cell_count ** (-0.5)
    padded = half + 8

    def narrow(*shape):
        return jax.ShapeDtypeStruct(shape, jnp.bfloat16)

    grad_two, pre, feats, feats_away, up, down = call(
        lanes_kernel,
        (
            narrow(columns, WIDE),
            narrow(columns, WIDE),
            narrow(columns, WIDE),
            narrow(columns, WIDE),
            narrow(8, WIDE),
            narrow(8, WIDE),
        ),
        [],
        inputs.size * 20,
        place,
        inputs,
        pre_one,
        pre_two,
        cotangent,
    )
    forward = [(i, (i + 1) % az_count) for i in range(az_count)]
    backward = [(target, source) for source, target in forward]
    low = lax.ppermute(up, AZ, forward)
    high = lax.ppermute(down, AZ, backward)
    sent, pre_here, pre_away = call(
        rims_kernel,
        (narrow(rot_count, padded, WIDE), narrow(padded, WIDE), narrow(padded, WIDE)),
        [pltpu.VMEM((columns + 8, WIDE), jnp.float32), pltpu.VMEM((columns + 8, WIDE), jnp.float32)],
        inputs.size * 20,
        place,
        grad_two,
        pre,
        low,
        high,
    )
    all_grad_two = exchange(sent, ROT)

    other_two = lax.ppermute(filt_two[0], CORE, SWAP)
    other_one = lax.ppermute(filt_one[0], CORE, SWAP)
    feats_partner = lax.ppermute(feats_away, CORE, SWAP)
    pre_partner = lax.ppermute(pre_away, CORE, SWAP)

    shares = conv(
        conv_two_kernel,
        place,
        all_grad_two,
        half + 2,
        padded,
        (chips, padded + columns, 2 * WIDE),
        filt_two[0],
        other_two,
        feats,
        feats_partner,
    )
    arrived = exchange(shares, CHIPS)
    copies = call(
        point_kernel,
        narrow(chips, padded, 2 * WIDE),
        [],
        arrived.size,
        place,
        arrived,
        pre_here,
        pre_partner,
    )
    all_grad_one = exchange(copies, CHIPS)
    pair_two = filter_terms(place, arrived, 0, half, all_grad_two, 3)
    pair_one = filter_terms(place, arrived, half, half, all_grad_one, 2)
    filt_grad_one, filt_grad_two = summed_over_az((pair_one, pair_two), scale)

    along_x = lax.axis_size(CHIPS[0])
    shares = conv(
        conv_one_kernel,
        place,
        all_grad_one,
        half,
        half,
        (2, along_x, half, 2 * WIDE),
        filt_one[0],
        other_one,
    )
    arrived_y = lax.ppermute(shares[1], CHIPS[1], SWAP)
    partial = (shares[0].astype(jnp.float32) + arrived_y.astype(jnp.float32)).astype(jnp.bfloat16)
    total = partial[0].astype(jnp.float32)
    for step in range(1, along_x):
        came = lax.ppermute(
            partial[step], CHIPS[0], [(i, (i + step) % along_x) for i in range(along_x)]
        )
        total = total + came.astype(jnp.float32)
    total = total.astype(jnp.bfloat16)
    left, right = total[:, :WIDE], total[:, WIDE:]
    mine = jnp.where(core == 0, left, right)
    theirs = lax.ppermute(jnp.where(core == 0, right, left), CORE, SWAP)
    whole = jnp.where(core == 0, jnp.concatenate([mine, theirs]), jnp.concatenate([theirs, mine]))
    input_grad = jnp.moveaxis(whole.reshape(columns, ROWS, CHAN), 1, 0)[None]
    return input_grad, filt_grad_one, filt_grad_two


def solution(mesh):
    finer = Mesh(mesh.devices.reshape(4, 2, 2, mesh.shape["az"]), (*ROT, AZ))
    field = P(ROT, None, AZ, None)
    bank = P(ROT, None, None, None, None)
    return jax.shard_map(
        shards,
        mesh=finer,
        in_specs=(field, field, field, field, bank, bank),
        out_specs=(field, bank, bank),
        check_vma=False,
    )
```

time: 155 us -> 121 us (0.78)
  waiting for transfers between devices: 83.6 us -> 62.3 us
  starting transfers between devices: 45.4 us -> 36.4 us
  other arithmetic: 4.59 us -> 1.87 us
  Pallas kernels: 13.4 us -> 15.7 us
  local copies, waits for them, and re-layouts: 5.35 us -> 3.07 us
    all_to_all x9 -> x5, waiting for transfers between devices: 73 us -> 47.3 us  [exchange(): return lax.all_to_all(parts, axes, 0, 0, tiled=True)]
    all_to_all x9 -> x5, starting transfers between devices: 41.7 us -> 28.5 us  [exchange(): return lax.all_to_all(parts, axes, 0, 0, tiled=True)]
    ppermute x6 -> x11, starting transfers between devices: 2.83 us -> 7.09 us  [the longest x3 2.72 us: shards(): lax.ppermute(partial[step], CHIPS[0], [(i, (i + step) % along_x) for i in...]
    ppermute x6 -> x11, waiting for transfers between devices: 9.53 us -> 13.4 us  [the longest x3 4.83 us: shards(): lax.ppermute(partial[step], CHIPS[0], [(i, (i + step) % along_x) for i in...]
    pallas_call x7 -> x9, Pallas kernels: 13.4 us -> 15.7 us  [call(): pl.pallas_call(kernel, out_shape=out_shape, in_specs=in_specs, out_specs=...]
    broadcast_in_dim x2 -> x0, local copies, waits for them, and re-layouts: 1.63 us -> none  [the longest x1 0.85 us: shards(): jnp.broadcast_to(feats[None], (chips, *feats.shape))]
    ppermute x1, waiting for transfers between devices: 0.01 us -> 1.57 us  [shards(): other_one = lax.ppermute(filt_one[0], CORE, SWAP)]
  transfers between devices with their start and end apart: 17 -> 18, of which waited for: 15 -> 15; matrix products, arithmetic and copies ran while one was open for 2% -> 1% of each run, Pallas kernels for 6% -> 6%
where the time goes in v2:
time: 121 us; the launch traced here: 120 us
  waiting for transfers between devices  62.3 us (51%)
  starting transfers between devices  36.4 us (30%)
  Pallas kernels  15.7 us (13%)
  local copies, waits for them, and re-layouts  3.07 us (3%)
  other arithmetic  1.87 us (2%)
    all_to_all x5, waiting for transfers between devices, exchange(): return lax.all_to_all(parts, axes, 0, 0, tiled=True)  47.3 us
    all_to_all x5, starting transfers between devices, exchange(): return lax.all_to_all(parts, axes, 0, 0, tiled=True)  28.5 us
    pallas_call x9, Pallas kernels, call(): pl.pallas_call(kernel, out_shape=out_shape, in_specs=in_specs, out_specs=...  15.7 us
    ppermute x3, waiting for transfers between devices, shards(): lax.ppermute(partial[step], CHIPS[0], [(i, (i + step) % along_x) for i in...  4.83 us
    unnamed x12, local copies, waits for them, and re-layouts  3.04 us
    ppermute x3, starting transfers between devices, shards(): lax.ppermute(partial[step], CHIPS[0], [(i, (i + step) % along_x) for i in...  2.72 us
  transfers between devices with their start and end apart: 18, of which 15 were waited for; matrix products, arithmetic and copies ran while one was open for 1% of the time, Pallas kernels for 6%

profile of v2, /device:TPU:32, one launch (start us, length us, event | category | flops | bytes accessed | tf_op | source)
XLA Modules:
  0.0 120.2 jit_solution(4284004117031723114)
XLA Ops:
  4.4 2.0 %collective-permute-start = (bf16[8,512]{1,0:T(8,128)(2,1)S(1)}, bf16[8,512]{1,0:T(8,128)(2,1)S(1)}, u32[]{:S(2)}, u32[]{:S(2)}) collective-permute-start(bf16[8,512]{1,0:T(8,128)(2,1)S(1)} %get-tuple-element.18), channel_id=1, source_target_pairs={{0,1},{1,2},{2,3},{3,4},{4,5},{5,6},{6,7},{7,8},{8,9},{9,10},{10,1... | collective-permute-start | bytes 24584 | tf_op jit(solution)/shard_map/ppermute | solution.py:361
  6.5 1.6 %collective-permute-done.low_ref = bf16[8,512]{1,0:T(8,128)(2,1)S(1)} collective-permute-done((bf16[8,512]{1,0:T(8,128)(2,1)S(1)}, bf16[8,512]{1,0:T(8,128)(2,1)S(1)}, u32[]{:S(2)}, u32[]{:S(2)}) %collective-permute-start) | collective-permute-done | bytes 8224 | tf_op jit(solution)/shard_map/ppermute | solution.py:361
  8.1 1.9 %collective-permute-done.1.high_ref = bf16[8,512]{1,0:T(8,128)(2,1)S(1)} collective-permute-done((bf16[8,512]{1,0:T(8,128)(2,1)S(1)}, bf16[8,512]{1,0:T(8,128)(2,1)S(1)}, u32[]{:S(2)}, u32[]{:S(2)}) %collective-permute-start.1) | collective-permute-done | bytes 8224 | tf_op jit(solution)/shard_map/ppermute | solution.py:362
  10.0 1.3 %shard_map.86 = (bf16[16,24,512]{2,1,0:T(8,128)(2,1)}, bf16[24,512]{1,0:T(8,128)(2,1)S(1)}, bf16[24,512]{1,0:T(8,128)(2,1)S(1)}) custom-call(s32[2]{0:T(128)S(1)} %pad_add_fusion.place_ref, bf16[32,512]{1,0:T(8,128)(2,1)S(1)} %get-tuple-element.16.grad_ref, bf16[32,512]{1,0:T(8,128)(2,1)S(1)} %get-tuple-element.17.pre_ref, ...), custom_call_target="tpu_custom_call" | custom-call | flops 327680 | bytes 163856 | tf_op jit(solution)/shard_map/pallas_call | solution.py:37
  11.3 7.2 %all-to-all-start = ((bf16[16,24,512]{2,1,0:T(8,128)(2,1)}), bf16[16,24,512]{2,1,0:T(8,128)(2,1)S(1)}, u32[]{:S(2)}, u32[]{:S(2)}) async-start(bf16[16,24,512]{2,1,0:T(8,128)(2,1)} %get-tuple-element.20), calls=%async_computation | async-start | bytes 786432 | tf_op jit(solution)/shard_map/all_to_all | solution.py:239
  20.3 8.9 %all-to-all-done.blocks_ref.grad_ref = bf16[16,24,512]{2,1,0:T(8,128)(2,1)S(1)} async-done(((bf16[16,24,512]{2,1,0:T(8,128)(2,1)}), bf16[16,24,512]{2,1,0:T(8,128)(2,1)S(1)}, u32[]{:S(2)}, u32[]{:S(2)}) %all-to-all-start) | async-done | bytes 393248 | tf_op jit(solution)/shard_map/all_to_all | solution.py:239
  29.2 3.9 %shard_map.87 = bf16[8,56,1024]{2,1,0:T(8,128)(2,1)} custom-call(s32[2]{0:T(128)S(1)} %pad_add_fusion.place_ref, bf16[16,24,512]{2,1,0:T(8,128)(2,1)S(1)} %all-to-all-done.blocks_ref.grad_ref, bf16[3,3,128,128]{3,2,1,0:T(8,128)(2,1)S(1)} %bitcast.47, bf16[3,3,128,128]{3,2,1,0:T(8,128)(2,1)S(1)} %collective-permute-done.2.other_ref, ...), custom_call_target="tpu_custom_call" | custom-call | flops 905969664 | bytes 2097168 | tf_op jit(solution)/shard_map/pallas_call | solution.py:37
  33.2 3.6 %all-to-all-start.1 = ((bf16[8,56,1024]{2,1,0:T(8,128)(2,1)}), bf16[8,56,1024]{2,1,0:T(8,128)(2,1)S(1)}, u32[]{:S(2)}, u32[]{:S(2)}) async-start(bf16[8,56,1024]{2,1,0:T(8,128)(2,1)} %shard_map.87), calls=%async_computation.1 | async-start | bytes 1835008 | tf_op jit(solution)/shard_map/all_to_all | solution.py:239
  38.0 13.3 %all-to-all-done.1.parts_ref.feat_ref = bf16[8,56,1024]{2,1,0:T(8,128)(2,1)S(1)} async-done(((bf16[8,56,1024]{2,1,0:T(8,128)(2,1)}), bf16[8,56,1024]{2,1,0:T(8,128)(2,1)S(1)}, u32[]{:S(2)}, u32[]{:S(2)}) %all-to-all-start.1) | async-done | bytes 917536 | tf_op jit(solution)/shard_map/all_to_all | solution.py:239
  51.3 1.4 %shard_map.88 = bf16[8,24,1024]{2,1,0:T(8,128)(2,1)} custom-call(s32[2]{0:T(128)S(1)} %pad_add_fusion.place_ref, bf16[8,56,1024]{2,1,0:T(8,128)(2,1)S(1)} %all-to-all-done.1.parts_ref.feat_ref, bf16[24,512]{1,0:T(8,128)(2,1)S(1)} %get-tuple-element.23.pre_ref, bf16[24,512]{1,0:T(8,128)(2,1)S(1)} %collective-permute-done.4.partner_ref), custom_call_target="tpu_custom_call" | custom-call | flops 458752 | bytes 1933328 | tf_op jit(solution)/shard_map/pallas_call | solution.py:37
  52.7 4.1 %all-to-all-start.2 = ((bf16[8,24,1024]{2,1,0:T(8,128)(2,1)}), bf16[8,24,1024]{2,1,0:T(8,128)(2,1)S(1)}, u32[]{:S(2)}, u32[]{:S(2)}) async-start(bf16[8,24,1024]{2,1,0:T(8,128)(2,1)} %shard_map.88), calls=%async_computation.2 | async-start | bytes 786432 | tf_op jit(solution)/shard_map/all_to_all | solution.py:239
  56.8 2.0 %shard_map.91 = (bf16[3,3,128,128]{3,2,1,0:T(8,128)(2,1)S(1)}, bf16[3,3,128,128]{3,2,1,0:T(8,128)(2,1)S(1)}) custom-call(s32[2]{0:T(128)S(1)} %pad_add_fusion.place_ref, bf16[8,56,1024]{2,1,0:T(8,128)(2,1)S(1)} %all-to-all-done.1.parts_ref.feat_ref, bf16[16,24,512]{2,1,0:T(8,128)(2,1)S(1)} %all-to-all-done.blocks_ref.grad_ref), custom_call_target="tpu_custom_call" | custom-call | flops 805306368 | bytes 2621456 | tf_op jit(solution)/shard_map/pallas_call | solution.py:37
  58.9 7.4 %all-to-all-done.2.blocks_ref.grad_ref = bf16[8,24,1024]{2,1,0:T(8,128)(2,1)S(1)} async-done(((bf16[8,24,1024]{2,1,0:T(8,128)(2,1)}), bf16[8,24,1024]{2,1,0:T(8,128)(2,1)S(1)}, u32[]{:S(2)}, u32[]{:S(2)}) %all-to-all-start.2) | async-done | bytes 393248 | tf_op jit(solution)/shard_map/all_to_all | solution.py:239
  66.3 2.0 %shard_map.90 = (bf16[3,3,128,128]{3,2,1,0:T(8,128)(2,1)S(1)}, bf16[3,3,128,128]{3,2,1,0:T(8,128)(2,1)S(1)}) custom-call(s32[2]{0:T(128)S(1)} %pad_add_fusion.place_ref, bf16[8,56,1024]{2,1,0:T(8,128)(2,1)S(1)} %all-to-all-done.1.parts_ref.feat_ref, bf16[8,24,1024]{2,1,0:T(8,128)(2,1)S(1)} %all-to-all-done.2.blocks_ref.grad_ref), custom_call_target="tpu_custom_call" | custom-call | flops 805306368 | bytes 2621456 | tf_op jit(solution)/shard_map/pallas_call | solution.py:37
  68.4 1.6 %collective-permute-done.11 = bf16[3,3,128,128]{3,2,1,0:T(8,128)(2,1)S(1)} collective-permute-done((bf16[3,3,128,128]{3,2,1,0:T(8,128)(2,1)S(1)}, bf16[3,3,128,128]{3,2,1,0:T(8,128)(2,1)S(1)}, u32[]{:S(2)}, u32[]{:S(2)}) %collective-permute-start.11) | collective-permute-done | bytes 294944 | tf_op jit(solution)/shard_map/ppermute | solution.py:219
  70.9 8.7 %all-to-all-start.3 = ((bf16[16,144,128]{2,1,0:T(8,128)(2,1)}), bf16[16,144,128]{2,1,0:T(8,128)(2,1)S(1)}, u32[]{:S(2)}, u32[]{:S(2)}) async-start(bf16[16,144,128]{2,1,0:T(8,128)(2,1)} %shard_map.92), calls=%async_computation.3 | async-start | bytes 1179648 | tf_op jit(solution)/shard_map/all_to_all | solution.py:239
  79.9 1.6 %collective-permute-done.5.other_ref = bf16[3,3,128,128]{3,2,1,0:T(8,128)(2,1)S(1)} collective-permute-done((bf16[3,3,128,128]{3,2,1,0:T(8,128)(2,1)S(1)}, bf16[3,3,128,128]{3,2,1,0:T(8,128)(2,1)S(1)}, u32[]{:S(2)}, u32[]{:S(2)}) %collective-permute-start.5) | collective-permute-done | bytes 294944 | tf_op jit(solution)/shard_map/ppermute | solution.py:377
  81.5 2.6 %shard_map.89 = bf16[2,4,16,1024]{3,2,1,0:T(8,128)(2,1)S(1)} custom-call(s32[2]{0:T(128)S(1)} %pad_add_fusion.place_ref, bf16[8,24,1024]{2,1,0:T(8,128)(2,1)S(1)} %all-to-all-done.2.blocks_ref.grad_ref, bf16[3,3,128,128]{3,2,1,0:T(8,128)(2,1)S(1)} %bitcast.49, bf16[3,3,128,128]{3,2,1,0:T(8,128)(2,1)S(1)} %collective-permute-done.5.other_ref), custom_call_target="tpu_custom_call" | custom-call | flops 805306368 | bytes 1966096 | tf_op jit(solution)/shard_map/pallas_call | solution.py:37
  84.1 1.8 %collective-permute-start.6 = (bf16[4,16,1024]{2,1,0:T(8,128)(2,1)S(1)}, bf16[4,16,1024]{2,1,0:T(8,128)(2,1)S(1)}, u32[]{:S(2)}, u32[]{:S(2)}) collective-permute-start(bf16[4,16,1024]{2,1,0:T(8,128)(2,1)S(1)} %slice_bitcast_fusion), channel_id=1, source_target_pairs={{0,32},{32,0},{1,33},{33,1},{2,34},{34,2},{3,35},{35,3},{4,36},{36... | collective-permute-start | bytes 393224 | tf_op jit(solution)/shard_map/ppermute | solution.py:420
  85.9 10.7 %all-to-all-done.3.parts_ref = bf16[16,144,128]{2,1,0:T(8,128)(2,1)S(1)} async-done(((bf16[16,144,128]{2,1,0:T(8,128)(2,1)}), bf16[16,144,128]{2,1,0:T(8,128)(2,1)S(1)}, u32[]{:S(2)}, u32[]{:S(2)}) %all-to-all-start.3) | async-done | bytes 589856 | tf_op jit(solution)/shard_map/all_to_all | solution.py:239
  97.5 5.0 %all-to-all-start.4 = ((bf16[16,144,128]{2,1,0:T(8,128)(2,1)}), bf16[16,144,128]{2,1,0:T(8,128)(2,1)S(1)}, u32[]{:S(2)}, u32[]{:S(2)}) async-start(bf16[16,144,128]{2,1,0:T(8,128)(2,1)} %shard_map.93), calls=%async_computation.4 | async-start | bytes 1179648 | tf_op jit(solution)/shard_map/all_to_all | solution.py:239
  105.2 1.3 %collective-permute-done.9 = bf16[16,1024]{1,0:T(8,128)(2,1)S(1)} collective-permute-done((bf16[16,1024]{1,0:T(8,128)(2,1)S(1)}, bf16[16,1024]{1,0:T(8,128)(2,1)S(1)}, u32[]{:S(2)}, u32[]{:S(2)}) %collective-permute-start.9) | collective-permute-done | bytes 32800 | tf_op jit(solution)/shard_map/ppermute | solution.py:424
  106.5 2.6 %collective-permute-done.8 = bf16[16,1024]{1,0:T(8,128)(2,1)S(1)} collective-permute-done((bf16[16,1024]{1,0:T(8,128)(2,1)S(1)}, bf16[16,1024]{1,0:T(8,128)(2,1)S(1)}, u32[]{:S(2)}, u32[]{:S(2)}) %collective-permute-start.8) | collective-permute-done | bytes 32800 | tf_op jit(solution)/shard_map/ppermute | solution.py:424
  112.0 7.1 %all-to-all-done.4 = bf16[16,144,128]{2,1,0:T(8,128)(2,1)S(1)} async-done(((bf16[16,144,128]{2,1,0:T(8,128)(2,1)}), bf16[16,144,128]{2,1,0:T(8,128)(2,1)S(1)}, u32[]{:S(2)}, u32[]{:S(2)}) %all-to-all-start.4) | async-done | bytes 589856 | tf_op jit(solution)/shard_map/all_to_all | solution.py:239
  (43 shorter events, 15.9 us)
Async XLA Ops:
  0.7 0.8 copy-start
  1.5 0.8 copy-start.1
  2.2 0.8 copy-start.2
  3.0 0.8 copy-start.3
  4.4 3.7 %collective-permute-start = (bf16[8,512]{1,0:T(8,128)(2,1)S(1)}, bf16[8,512]{1,0:T(8,128)(2,1)S(1)}, u32[]{:S(2)}, u32[]{:S(2)}) collective-permute-start(bf16[8,512]{1,0:T(8,128)(2,1)S(1)} %get-tuple-element.18), channel_id=1, source_target_pairs={{0,1},{1,2},{2,3},{3,4},{4,5},{5,6},{6,7},{7,8},{8,9},{9,10},{10,1... | collective-permute-start | bytes 24584 | tf_op jit(solution)/shard_map/ppermute | solution.py:361
  6.4 3.7 %collective-permute-start.1 = (bf16[8,512]{1,0:T(8,128)(2,1)S(1)}, bf16[8,512]{1,0:T(8,128)(2,1)S(1)}, u32[]{:S(2)}, u32[]{:S(2)}) collective-permute-start(bf16[8,512]{1,0:T(8,128)(2,1)S(1)} %get-tuple-element.19), channel_id=1, source_target_pairs={{1,0},{2,1},{3,2},{4,3},{5,4},{6,5},{7,6},{8,7},{9,8},{10,9},{11,1... | collective-permute-start | bytes 24584 | tf_op jit(solution)/shard_map/ppermute | solution.py:362
  11.3 7.2 %copy-start.4 = (bf16[1,3,3,128,128]{4,3,2,1,0:T(8,128)(2,1)S(1)}, bf16[1,3,3,128,128]{4,3,2,1,0:T(8,128)(2,1)}, u32[]{:S(2)}) copy-start(bf16[1,3,3,128,128]{4,3,2,1,0:T(8,128)(2,1)} %param.11) | copy-start | bytes 884740
  11.3 17.9 %all-to-all-start = ((bf16[16,24,512]{2,1,0:T(8,128)(2,1)}), bf16[16,24,512]{2,1,0:T(8,128)(2,1)S(1)}, u32[]{:S(2)}, u32[]{:S(2)}) async-start(bf16[16,24,512]{2,1,0:T(8,128)(2,1)} %get-tuple-element.20), calls=%async_computation | async-start | bytes 786432 | tf_op jit(solution)/shard_map/all_to_all | solution.py:239
  18.5 1.8 %collective-permute-start.2 = (bf16[3,3,128,128]{3,2,1,0:T(8,128)(2,1)S(1)}, bf16[3,3,128,128]{3,2,1,0:T(8,128)(2,1)S(1)}, u32[]{:S(2)}, u32[]{:S(2)}) collective-permute-start(bf16[3,3,128,128]{3,2,1,0:T(8,128)(2,1)S(1)} %bitcast.46), channel_id=1, source_target_pairs={{0,16},{16,0},{1,17},{17,1},{2,18},{18,2},{3,19},{19,3},{4,20},{20... | collective-permute-start | bytes 884744 | tf_op jit(solution)/shard_map/ppermute | solution.py:376
  19.0 1.3 %collective-permute-start.3 = (bf16[32,512]{1,0:T(8,128)(2,1)S(1)}, bf16[32,512]{1,0:T(8,128)(2,1)S(1)}, u32[]{:S(2)}, u32[]{:S(2)}) collective-permute-start(bf16[32,512]{1,0:T(8,128)(2,1)S(1)} %get-tuple-element.22), channel_id=1, source_target_pairs={{0,16},{16,0},{1,17},{17,1},{2,18},{18,2},{3,19},{19,3},{4,20},{20... | collective-permute-start | bytes 98312 | tf_op jit(solution)/shard_map/ppermute | solution.py:378
  33.2 18.1 %all-to-all-start.1 = ((bf16[8,56,1024]{2,1,0:T(8,128)(2,1)}), bf16[8,56,1024]{2,1,0:T(8,128)(2,1)S(1)}, u32[]{:S(2)}, u32[]{:S(2)}) async-start(bf16[8,56,1024]{2,1,0:T(8,128)(2,1)} %shard_map.87), calls=%async_computation.1 | async-start | bytes 1835008 | tf_op jit(solution)/shard_map/all_to_all | solution.py:239
  36.7 1.3 %collective-permute-start.4 = (bf16[24,512]{1,0:T(8,128)(2,1)S(1)}, bf16[24,512]{1,0:T(8,128)(2,1)S(1)}, u32[]{:S(2)}, u32[]{:S(2)}) collective-permute-start(bf16[24,512]{1,0:T(8,128)(2,1)S(1)} %get-tuple-element.24), channel_id=1, source_target_pairs={{0,16},{16,0},{1,17},{17,1},{2,18},{18,2},{3,19},{19,3},{4,20},{20... | collective-permute-start | bytes 73736 | tf_op jit(solution)/shard_map/ppermute | solution.py:379
  52.7 13.6 %all-to-all-start.2 = ((bf16[8,24,1024]{2,1,0:T(8,128)(2,1)}), bf16[8,24,1024]{2,1,0:T(8,128)(2,1)S(1)}, u32[]{:S(2)}, u32[]{:S(2)}) async-start(bf16[8,24,1024]{2,1,0:T(8,128)(2,1)} %shard_map.88), calls=%async_computation.2 | async-start | bytes 786432 | tf_op jit(solution)/shard_map/all_to_all | solution.py:239
  58.8 9.6 %collective-permute-start.12 = (bf16[3,3,128,128]{3,2,1,0:T(8,128)(2,1)S(1)}, bf16[3,3,128,128]{3,2,1,0:T(8,128)(2,1)S(1)}, u32[]{:S(2)}, u32[]{:S(2)}) collective-permute-start(bf16[3,3,128,128]{3,2,1,0:T(8,128)(2,1)S(1)} %get-tuple-element.28), channel_id=1, source_target_pairs={{0,16},{16,0},{1,17},{17,1},{2,18},{18,2},{3,19},{19,3},{4,20},{20... | collective-permute-start | bytes 884744 | tf_op jit(solution)/shard_map/ppermute | solution.py:219
  68.3 1.7 %collective-permute-start.11 = (bf16[3,3,128,128]{3,2,1,0:T(8,128)(2,1)S(1)}, bf16[3,3,128,128]{3,2,1,0:T(8,128)(2,1)S(1)}, u32[]{:S(2)}, u32[]{:S(2)}) collective-permute-start(bf16[3,3,128,128]{3,2,1,0:T(8,128)(2,1)S(1)} %get-tuple-element.26), channel_id=1, source_target_pairs={{0,16},{16,0},{1,17},{17,1},{2,18},{18,2},{3,19},{19,3},{4,20},{20... | collective-permute-start | bytes 884744 | tf_op jit(solution)/shard_map/ppermute | solution.py:219
  70.9 8.7 %copy-start.5 = (bf16[1,3,3,128,128]{4,3,2,1,0:T(8,128)(2,1)S(1)}, bf16[1,3,3,128,128]{4,3,2,1,0:T(8,128)(2,1)}, u32[]{:S(2)}) copy-start(bf16[1,3,3,128,128]{4,3,2,1,0:T(8,128)(2,1)} %param.10) | copy-start | bytes 884740
  70.9 25.7 %all-to-all-start.3 = ((bf16[16,144,128]{2,1,0:T(8,128)(2,1)}), bf16[16,144,128]{2,1,0:T(8,128)(2,1)S(1)}, u32[]{:S(2)}, u32[]{:S(2)}) async-start(bf16[16,144,128]{2,1,0:T(8,128)(2,1)} %shard_map.92), calls=%async_computation.3 | async-start | bytes 1179648 | tf_op jit(solution)/shard_map/all_to_all | solution.py:239
  79.6 1.9 %collective-permute-start.5 = (bf16[3,3,128,128]{3,2,1,0:T(8,128)(2,1)S(1)}, bf16[3,3,128,128]{3,2,1,0:T(8,128)(2,1)S(1)}, u32[]{:S(2)}, u32[]{:S(2)}) collective-permute-start(bf16[3,3,128,128]{3,2,1,0:T(8,128)(2,1)S(1)} %bitcast.48), channel_id=1, source_target_pairs={{0,16},{16,0},{1,17},{17,1},{2,18},{18,2},{3,19},{19,3},{4,20},{20... | collective-permute-start | bytes 884744 | tf_op jit(solution)/shard_map/ppermute | solution.py:377
  84.1 18.4 %collective-permute-start.6 = (bf16[4,16,1024]{2,1,0:T(8,128)(2,1)S(1)}, bf16[4,16,1024]{2,1,0:T(8,128)(2,1)S(1)}, u32[]{:S(2)}, u32[]{:S(2)}) collective-permute-start(bf16[4,16,1024]{2,1,0:T(8,128)(2,1)S(1)} %slice_bitcast_fusion), channel_id=1, source_target_pairs={{0,32},{32,0},{1,33},{33,1},{2,34},{34,2},{3,35},{35,3},{4,36},{36... | collective-permute-start | bytes 393224 | tf_op jit(solution)/shard_map/ppermute | solution.py:420
  97.5 21.6 %all-to-all-start.4 = ((bf16[16,144,128]{2,1,0:T(8,128)(2,1)}), bf16[16,144,128]{2,1,0:T(8,128)(2,1)S(1)}, u32[]{:S(2)}, u32[]{:S(2)}) async-start(bf16[16,144,128]{2,1,0:T(8,128)(2,1)} %shard_map.93), calls=%async_computation.4 | async-start | bytes 1179648 | tf_op jit(solution)/shard_map/all_to_all | solution.py:239
  102.5 4.0 %collective-permute-start.9 = (bf16[16,1024]{1,0:T(8,128)(2,1)S(1)}, bf16[16,1024]{1,0:T(8,128)(2,1)S(1)}, u32[]{:S(2)}, u32[]{:S(2)}) collective-permute-start(bf16[16,1024]{1,0:T(8,128)(2,1)S(1)} %get-tuple-element.32), channel_id=1, source_target_pairs={{0,192},{64,0},{128,64},{192,128},{1,193},{65,1},{129,65},{193,129... | collective-permute-start | bytes 98312 | tf_op jit(solution)/shard_map/ppermute | solution.py:424
  103.7 5.4 %collective-permute-start.8 = (bf16[16,1024]{1,0:T(8,128)(2,1)S(1)}, bf16[16,1024]{1,0:T(8,128)(2,1)S(1)}, u32[]{:S(2)}, u32[]{:S(2)}) collective-permute-start(bf16[16,1024]{1,0:T(8,128)(2,1)S(1)} %get-tuple-element.33), channel_id=1, source_target_pairs={{0,128},{64,192},{128,0},{192,64},{1,129},{65,193},{129,1},{193,65... | collective-permute-start | bytes 98312 | tf_op jit(solution)/shard_map/ppermute | solution.py:424
  105.0 5.1 %collective-permute-start.7 = (bf16[16,1024]{1,0:T(8,128)(2,1)S(1)}, bf16[16,1024]{1,0:T(8,128)(2,1)S(1)}, u32[]{:S(2)}, u32[]{:S(2)}) collective-permute-start(bf16[16,1024]{1,0:T(8,128)(2,1)S(1)} %get-tuple-element.31), channel_id=1, source_target_pairs={{0,64},{64,128},{128,192},{192,0},{1,65},{65,129},{129,193},{193,1... | collective-permute-start | bytes 98312 | tf_op jit(solution)/shard_map/ppermute | solution.py:424
  110.1 1.3 %collective-permute-start.10 = (bf16[16,512]{1,0:T(8,128)(2,1)S(1)}, bf16[16,512]{1,0:T(8,128)(2,1)S(1)}, u32[]{:S(2)}, u32[]{:S(2)}) collective-permute-start(bf16[16,512]{1,0:T(8,128)(2,1)S(1)} %get-tuple-element.35), channel_id=1, source_target_pairs={{0,16},{16,0},{1,17},{17,1},{2,18},{18,2},{3,19},{19,3},{4,20},{20... | collective-permute-start | bytes 49160 | tf_op jit(solution)/shard_map/ppermute | solution.py:431

commit v3 on v2

v3 whole, which is shorter than its diff:
```python
import functools

import jax
import jax.numpy as jnp
from jax import lax
from jax.experimental import pallas as pl
from jax.experimental.pallas import tpu as pltpu
from jax.sharding import Mesh
from jax.sharding import PartitionSpec as P

CHIPS = ("rot_x", "rot_y")
CORE = "rot_c"
ROT = (*CHIPS, CORE)
AZ = "az"

ROWS = 4
CHAN = 128
WIDE = ROWS * CHAN
SWAP = [(0, 1), (1, 0)]
VMEM = pl.BlockSpec(memory_space=pltpu.VMEM)
HBM = pl.BlockSpec(memory_space=pltpu.HBM)


def slope(pre):
    logistic = 1.0 / (1.0 + jnp.exp(-pre))
    return logistic * (1.0 + pre * (1.0 - logistic))


def params(mebibytes):
    return pltpu.CompilerParams(vmem_limit_bytes=mebibytes * 1024 * 1024)


def here():
    return lax.axis_index(CHIPS[0]) * 2 + lax.axis_index(CHIPS[1]), lax.axis_index(CORE)


def call(kernel, out_shape, scratch, flops, *operands, space=VMEM, out_space=VMEM, room=40):
    n_bytes = sum(a.size * a.dtype.itemsize for a in operands)
    in_specs = list(space) if isinstance(space, tuple) else [space] * len(operands)
    out_specs = jax.tree.map(lambda _: out_space, out_shape)
    return pl.pallas_call(
        kernel,
        out_shape=out_shape,
        in_specs=in_specs,
        out_specs=out_specs,
        scratch_shapes=scratch,
        compiler_params=params(room),
        cost_estimate=pl.CostEstimate(flops=flops, bytes_accessed=2 * n_bytes, transcendentals=0),
    )(*operands)


def copy_all(pairs, done):
    copies = [pltpu.make_async_copy(a, b, done.at[n]) for n, (a, b) in enumerate(pairs)]
    for copy in copies:
        copy.start()
    for copy in copies:
        copy.wait()


def interleave(blocks_ref, rows_ref, orients, width, shift):
    per_block = blocks_ref.shape[2] // WIDE
    for g in range(orients):
        s = (g - shift) % orients
        lanes = slice((s % per_block) * WIDE, (s % per_block + 1) * WIDE)
        rows_ref[:, g, :] = blocks_ref[s // per_block, :width, lanes].astype(jnp.float32)


def band_weights(filt_ref, band_ref, slot):
    zero = jnp.zeros((CHAN, CHAN), jnp.bfloat16)
    for j in range(3):
        for out_row in range(ROWS):
            for in_row in range(ROWS):
                i = out_row - in_row + 1
                piece = filt_ref[i, j] if 0 <= i < 3 else zero
                band_ref[
                    slot,
                    j,
                    out_row * CHAN : (out_row + 1) * CHAN,
                    in_row * CHAN : (in_row + 1) * CHAN,
                ] = piece


def bands_kernel(mine_ref, other_ref, band_ref):
    _, core = here()
    band_weights(mine_ref, band_ref, core)
    band_weights(other_ref, band_ref, 1 - core)


def bands(mine, other):
    shape = jax.ShapeDtypeStruct((2, 3, WIDE, WIDE), jnp.bfloat16)
    return call(bands_kernel, shape, [], mine.size, mine, other)


def rotation_sums(orients, width, blocks_ref, band_ref, rows_0, rows_1, band, fetched):
    in_width = rows_0.shape[0]
    copies = [
        pltpu.make_async_copy(band_ref.at[n], band.at[n], fetched.at[n]) for n in range(2)
    ]
    for copy in copies:
        copy.start()
    interleave(blocks_ref, rows_0, orients, in_width, 0)
    interleave(blocks_ref, rows_1, orients, in_width, 1)
    total = None
    for slot, rows in ((0, rows_0), (1, rows_1)):
        copies[slot].wait()
        flat = rows[...].reshape(in_width * orients, WIDE).astype(jnp.bfloat16)
        for j in range(3):
            window = flat[(2 - j) * orients : (2 - j + width) * orients]
            term = lax.dot_general(
                window,
                band[slot, j],
                (((1,), (1,)), ((), ())),
                preferred_element_type=jnp.float32,
            )
            total = term if total is None else total + term
    return total.reshape(width, orients, WIDE)


def conv_two_kernel(orients, width, blocks_ref, band_ref, out_ref, *scratch):
    *rows, sums, held, done = scratch
    chip, _ = here()
    total = rotation_sums(orients, width, blocks_ref, band_ref, *rows)
    sums[width:] = jnp.zeros((sums.shape[0] - width, orients, WIDE), jnp.float32)
    sums[:width] = total
    chips = orients // 2
    copies = []
    for pair in range(chips):
        for half in range(2):
            held[pair, :, half * WIDE : (half + 1) * WIDE] = sums[:, 2 * pair + half, :].astype(
                jnp.bfloat16
            )
        to = lax.rem(pair + chip, chips)
        copies.append(pltpu.make_async_copy(held.at[pair], out_ref.at[to], done.at[pair]))
        copies[-1].start()
    for copy in copies:
        copy.wait()


def conv_one_kernel(orients, width, blocks_ref, band_ref, out_ref, *scratch):
    *rows, sums = scratch
    chip, _ = here()
    sums[...] = rotation_sums(orients, width, blocks_ref, band_ref, *rows)
    chips = orients // 2
    across = out_ref.shape[1]
    for pair in range(chips):
        to = lax.rem(pair + chip, chips)
        other = lax.rem(to + chip, 2)
        step = lax.rem(to // 2 - chip // 2 + across, across)
        for half in range(2):
            out_ref[other, step, :, half * WIDE : (half + 1) * WIDE] = sums[
                :, 2 * pair + half, :
            ].astype(jnp.bfloat16)


def conv(kernel, blocks, band, width, padded, out_shape, staging=(), out_space=VMEM, room=40):
    orients = 16
    in_width = blocks.shape[1]
    return call(
        functools.partial(kernel, orients, width),
        jax.ShapeDtypeStruct(out_shape, jnp.bfloat16),
        [
            pltpu.VMEM((in_width, orients, WIDE), jnp.float32),
            pltpu.VMEM((in_width, orients, WIDE), jnp.float32),
            pltpu.VMEM(band.shape, jnp.bfloat16),
            pltpu.SemaphoreType.DMA((2,)),
            pltpu.VMEM((padded, orients, WIDE), jnp.float32),
            *staging,
        ],
        2 * 6 * width * orients * WIDE * WIDE,
        blocks,
        band,
        space=(VMEM, HBM),
        out_space=out_space,
        room=room,
    )


def filter_kernel(
    orients, width, field, first, own, grad_ref, feat_ref, out_ref, feat_rows, grad_rows, held, done
):
    chip, core = here()
    slot = core if own else 1 - core
    in_width = grad_rows.shape[0]
    columns = pl.ds(pl.multiple_of(core * width, width), width)
    lanes = pl.ds(field * WIDE, WIDE)
    copy = pltpu.make_async_copy(feat_ref.at[:, columns, lanes], held, done)
    copy.start()
    interleave(grad_ref, grad_rows, orients, in_width, 0)
    grads = grad_rows[...].reshape(in_width * orients, WIDE).astype(jnp.bfloat16)
    copy.wait()
    for g in range(orients):
        s = lax.rem(g + 2 * chip + slot, orients)
        feat_rows[:, g, :] = held[s].astype(jnp.float32)
    feats = feat_rows[...].reshape(width * orients, WIDE).astype(jnp.bfloat16)
    for j in range(3):
        window = grads[(first - j) * orients : (first - j + width) * orients]
        product = lax.dot_general(
            feats,
            window,
            (((0,), (0,)), ((), ())),
            preferred_element_type=jnp.float32,
        )
        for i in range(3):
            total = None
            for row in range(ROWS):
                grad_row = row - i + 1
                if not 0 <= grad_row < ROWS:
                    continue
                piece = product[
                    row * CHAN : (row + 1) * CHAN, grad_row * CHAN : (grad_row + 1) * CHAN
                ]
                total = piece if total is None else total + piece
            out_ref[i, j] = total.astype(jnp.bfloat16)


def filter_terms(feats, field, width, grads, first):
    orients = feats.shape[0]
    in_width = grads.shape[1]

    def terms(own):
        return call(
            functools.partial(filter_kernel, orients, width, field, first, own),
            jax.ShapeDtypeStruct((3, 3, CHAN, CHAN), jnp.bfloat16),
            [
                pltpu.VMEM((width, orients, WIDE), jnp.float32),
                pltpu.VMEM((in_width, orients, WIDE), jnp.float32),
                pltpu.VMEM((orients, width, WIDE), jnp.bfloat16),
                pltpu.SemaphoreType.DMA,
            ],
            6 * width * orients * WIDE * WIDE,
            grads,
            feats,
            space=(VMEM, HBM),
            room=52,
        )

    theirs = lax.ppermute(terms(False), CORE, SWAP)
    return terms(True), theirs


def point_kernel(parts_ref, pre_ref, partner_ref, out_ref, held, done):
    _, core = here()
    total = parts_ref[0].astype(jnp.float32)
    for n in range(1, parts_ref.shape[0]):
        total = total + parts_ref[n].astype(jnp.float32)
    mine = slope(pre_ref[...].astype(jnp.float32))
    partner = slope(partner_ref[...].astype(jnp.float32))
    first = total[:, :WIDE] * jnp.where(core == 0, mine, partner)
    second = total[:, WIDE:] * jnp.where(core == 0, partner, mine)
    held[:, :WIDE] = first.astype(jnp.bfloat16)
    held[:, WIDE:] = second.astype(jnp.bfloat16)
    copy_all([(held, out_ref.at[n]) for n in range(out_ref.shape[0])], done)


def exchange(parts, axes):
    return lax.all_to_all(parts, axes, 0, 0, tiled=True)


def join_kernel(mine_1, theirs_1, mine_2, theirs_2, out_ref, held, done):
    size = mine_1.shape[1]
    for first, mine, theirs in ((0, mine_1, theirs_1), (size, mine_2, theirs_2)):
        both = mine[...].astype(jnp.float32) + theirs[...].astype(jnp.float32)
        held[:, first : first + size] = both.astype(jnp.bfloat16)
    copy_all([(held, out_ref)], done)


def reduce_kernel(parts_ref, out_ref, held, done):
    total = parts_ref[0].astype(jnp.float32)
    for n in range(1, parts_ref.shape[0]):
        total = total + parts_ref[n].astype(jnp.float32)
    held[...] = total.astype(jnp.bfloat16)
    copy_all([(held, out_ref.at[n]) for n in range(out_ref.shape[0])], done)


def summed_over_az(pairs, scale):
    count = lax.axis_size(AZ)
    banks = [bank.reshape(count, -1, CHAN) for pair in pairs for bank in pair]
    size = banks[0].shape[1]
    shape = jax.ShapeDtypeStruct((count, 2 * size, CHAN), jnp.bfloat16)
    work = count * size * CHAN
    held = [pltpu.VMEM(shape.shape, jnp.bfloat16), pltpu.SemaphoreType.DMA((1,))]
    joined = call(join_kernel, shape, held, work, *banks, out_space=HBM)
    held = [pltpu.VMEM(shape.shape[1:], jnp.bfloat16), pltpu.SemaphoreType.DMA((count,))]
    copies = call(reduce_kernel, shape, held, work, exchange(joined, AZ), out_space=HBM)
    whole = exchange(copies, AZ)
    one, two = whole[:, :size], whole[:, size:]
    return tuple(
        (part.astype(jnp.float32) * scale).reshape(1, 3, 3, CHAN, CHAN) for part in (one, two)
    )


def lanes_kernel(*refs):
    given, (grad_ref, pre_ref, feats_ref, up_ref, down_ref) = refs[:4], refs[4:9]
    held, done = refs[9:13], refs[13]
    copy_all(zip(given, held), done)
    inputs_ref, pre_one_ref, pre_two_ref, cotangent_ref = held
    for row in range(ROWS):
        lanes = slice(row * CHAN, (row + 1) * CHAN)
        pre = pre_one_ref[0, row]
        wide = pre.astype(jnp.float32)
        grad = cotangent_ref[0, row].astype(jnp.float32) * slope(
            pre_two_ref[0, row].astype(jnp.float32)
        )
        grad = grad.astype(jnp.bfloat16)
        grad_ref[:, lanes] = grad
        pre_ref[:, lanes] = pre
        feats_ref[:, lanes] = (wide / (1.0 + jnp.exp(-wide))).astype(jnp.bfloat16)
        feats_ref[:, WIDE + row * CHAN : WIDE + (row + 1) * CHAN] = inputs_ref[0, row]
        grad = grad.astype(jnp.float32)
        pad = jnp.zeros((5, CHAN), jnp.float32)
        up_ref[:, lanes] = jnp.concatenate([grad[-2:], wide[-1:], pad]).astype(jnp.bfloat16)
        down_ref[:, lanes] = jnp.concatenate([grad[:2], wide[:1], pad]).astype(jnp.bfloat16)


def rims_kernel(grad_ref, low_ref, high_ref, out_ref, grad_rim, held, done):
    columns = grad_ref.shape[0]
    rows = out_ref.shape[1]
    grad_rim[:2] = low_ref[...].astype(jnp.float32)[:2]
    grad_rim[2 : 2 + columns] = grad_ref[...].astype(jnp.float32)
    grad_rim[2 + columns :] = jnp.zeros((grad_rim.shape[0] - 2 - columns, WIDE), jnp.float32)
    grad_rim[2 + columns : 4 + columns] = high_ref[...].astype(jnp.float32)[:2]
    for n in range(2):
        first = n * columns // 2
        held[n] = grad_rim[first : first + rows].astype(jnp.bfloat16)
    copy_all([(held.at[n % 2], out_ref.at[n]) for n in range(out_ref.shape[0])], done)


def pre_kernel(pre_ref, low_ref, high_ref, mine_ref, partner_ref, pre_rim):
    _, core = here()
    columns = pre_ref.shape[0]
    half = columns // 2
    rows = mine_ref.shape[0]
    pre_rim[...] = jnp.zeros_like(pre_rim)
    pre_rim[:1] = low_ref[...].astype(jnp.float32)[2:3]
    pre_rim[1 : 1 + columns] = pre_ref[...].astype(jnp.float32)
    pre_rim[1 + columns : 2 + columns] = high_ref[...].astype(jnp.float32)[2:3]
    left = pre_rim[:rows].astype(jnp.bfloat16)
    right = pre_rim[half : half + rows].astype(jnp.bfloat16)
    mine_ref[...] = jnp.where(core == 0, left, right)
    partner_ref[...] = jnp.where(core == 0, right, left)


def shards(inputs, pre_one, pre_two, cotangent, filt_one, filt_two):
    columns = inputs.shape[2]
    half = columns // 2
    core = lax.axis_index(CORE)
    az_count = lax.axis_size(AZ)
    rot_count = lax.axis_size(ROT)
    chips = lax.axis_size(CHIPS)
    cell_count = rot_count * inputs.shape[1] * columns * az_count
    scale = cell_count ** (-0.5)
    padded = half + 8

    def narrow(*shape):
        return jax.ShapeDtypeStruct(shape, jnp.bfloat16)

    grad_two, pre, feats, up, down = call(
        lanes_kernel,
        (
            narrow(columns, WIDE),
            narrow(columns, WIDE),
            narrow(columns, 2 * WIDE),
            narrow(8, WIDE),
            narrow(8, WIDE),
        ),
        [pltpu.VMEM(inputs.shape, jnp.bfloat16)] * 4 + [pltpu.SemaphoreType.DMA((4,))],
        inputs.size * 20,
        inputs,
        pre_one,
        pre_two,
        cotangent,
        space=HBM,
        room=60,
    )
    all_feats = lax.all_gather(feats, ROT)
    forward = [(i, (i + 1) % az_count) for i in range(az_count)]
    backward = [(target, source) for source, target in forward]
    low = lax.ppermute(up, AZ, forward)
    high = lax.ppermute(down, AZ, backward)
    rim = pltpu.VMEM((columns + 8, WIDE), jnp.float32)
    sent = call(
        rims_kernel,
        narrow(rot_count, padded, WIDE),
        [
            rim,
            pltpu.VMEM((2, padded, WIDE), jnp.bfloat16),
            pltpu.SemaphoreType.DMA((rot_count,)),
        ],
        inputs.size * 20,
        grad_two,
        low,
        high,
        out_space=HBM,
    )
    all_grad_two = exchange(sent, ROT)

    pre_here, pre_away = call(
        pre_kernel,
        (narrow(padded, WIDE), narrow(padded, WIDE)),
        [rim],
        inputs.size,
        pre,
        low,
        high,
    )

    other_two = lax.ppermute(filt_two[0], CORE, SWAP)
    other_one = lax.ppermute(filt_one[0], CORE, SWAP)
    pre_partner = lax.ppermute(pre_away, CORE, SWAP)
    bands_two = bands(filt_two[0], other_two)
    bands_one = bands(filt_one[0], other_one)

    shares = conv(
        conv_two_kernel,
        all_grad_two,
        bands_two,
        half + 2,
        padded,
        (chips, padded, 2 * WIDE),
        [
            pltpu.VMEM((chips, padded, 2 * WIDE), jnp.bfloat16),
            pltpu.SemaphoreType.DMA((chips,)),
        ],
        HBM,
        52,
    )
    arrived = exchange(shares, CHIPS)
    copies = call(
        point_kernel,
        narrow(chips, padded, 2 * WIDE),
        [pltpu.VMEM((padded, 2 * WIDE), jnp.bfloat16), pltpu.SemaphoreType.DMA((chips,))],
        arrived.size,
        arrived,
        pre_here,
        pre_partner,
        out_space=HBM,
    )
    copies, all_feats = lax.optimization_barrier((copies, all_feats))
    all_grad_one = exchange(copies, CHIPS)
    pair_two = filter_terms(all_feats, 0, half, all_grad_two, 3)
    all_grad_one, pair_two = lax.optimization_barrier((all_grad_one, pair_two))
    pair_one = filter_terms(all_feats, 1, half, all_grad_one, 2)
    filt_grad_one, filt_grad_two = summed_over_az((pair_one, pair_two), scale)

    along_x = lax.axis_size(CHIPS[0])
    shares = conv(
        conv_one_kernel,
        all_grad_one,
        bands_one,
        half,
        half,
        (2, along_x, half, 2 * WIDE),
    )
    arrived_y = lax.ppermute(shares[1], CHIPS[1], SWAP)
    partial = (shares[0].astype(jnp.float32) + arrived_y.astype(jnp.float32)).astype(jnp.bfloat16)
    total = partial[0].astype(jnp.float32)
    for step in range(1, along_x):
        came = lax.ppermute(
            partial[step], CHIPS[0], [(i, (i + step) % along_x) for i in range(along_x)]
        )
        total = total + came.astype(jnp.float32)
    total = total.astype(jnp.bfloat16)
    left, right = total[:, :WIDE], total[:, WIDE:]
    mine = jnp.where(core == 0, left, right)
    theirs = lax.ppermute(jnp.where(core == 0, right, left), CORE, SWAP)
    whole = jnp.where(core == 0, jnp.concatenate([mine, theirs]), jnp.concatenate([theirs, mine]))
    input_grad = jnp.moveaxis(whole.reshape(columns, ROWS, CHAN), 1, 0)[None]
    return input_grad, filt_grad_one, filt_grad_two


def solution(mesh):
    finer = Mesh(mesh.devices.reshape(4, 2, 2, mesh.shape["az"]), (*ROT, AZ))
    field = P(ROT, None, AZ, None)
    bank = P(ROT, None, None, None, None)
    return jax.shard_map(
        shards,
        mesh=finer,
        in_specs=(field, field, field, field, bank, bank),
        out_specs=(field, bank, bank),
        check_vma=False,
    )
```

time: 121 us -> 139 us (1.15)
  between operations: 0.81 us -> 14.3 us
  waiting for transfers between devices: 62.3 us -> 63.9 us
  local copies, waits for them, and re-layouts: 3.07 us -> 4.61 us
    all_gather x0 -> x1, waiting for transfers between devices: none -> 11.9 us  [shards(): all_feats = lax.all_gather(feats, ROT)]
    all_to_all x5, waiting for transfers between devices: 47.3 us -> 39.4 us  [exchange(): return lax.all_to_all(parts, axes, 0, 0, tiled=True)]
    ppermute x3, waiting for transfers between devices: 4.83 us -> 2.37 us  [shards(): lax.ppermute(partial[step], CHIPS[0], [(i, (i + step) % along_x) for i in...]
    ppermute x3 -> x2, waiting for transfers between devices: 2.71 us -> 1.13 us  [filter_terms(): theirs = lax.ppermute(terms(False), CORE, SWAP)]
    unnamed x12 -> x14, local copies, waits for them, and re-layouts: 3.04 us -> 4.58 us
    ppermute x1, waiting for transfers between devices: 0.01 us -> 1.47 us  [shards(): other_two = lax.ppermute(filt_two[0], CORE, SWAP)]
    ppermute x3, starting transfers between devices: 2.72 us -> 4.17 us  [shards(): lax.ppermute(partial[step], CHIPS[0], [(i, (i + step) % along_x) for i in...]
    pallas_call x9 -> x14, Pallas kernels: 15.7 us -> 16.3 us  [call(): pl.pallas_call(kernel, out_shape=out_shape, in_specs=in_specs, out_specs=...]
  transfers between devices with their start and end apart: 18 -> 18, of which waited for: 15 -> 17; matrix products, arithmetic and copies ran while one was open for 1% -> 1% of each run, Pallas kernels for 6% -> 9%
where the time goes in v3:
time: 139 us; the launch traced here: 138 us
  waiting for transfers between devices  63.9 us (46%)
  starting transfers between devices  37 us (27%)
  Pallas kernels  16.3 us (12%)
  between operations  14.3 us (10%)
  local copies, waits for them, and re-layouts  4.61 us (3%)
  other arithmetic  1.79 us (1%)
    all_to_all x5, waiting for transfers between devices, exchange(): return lax.all_to_all(parts, axes, 0, 0, tiled=True)  39.4 us
    all_to_all x5, starting transfers between devices, exchange(): return lax.all_to_all(parts, axes, 0, 0, tiled=True)  27.6 us
    pallas_call x14, Pallas kernels, call(): pl.pallas_call(kernel, out_shape=out_shape, in_specs=in_specs, out_specs=...  16.3 us
    all_gather x1, waiting for transfers between devices, shards(): all_feats = lax.all_gather(feats, ROT)  11.9 us
    unnamed x14, local copies, waits for them, and re-layouts  4.58 us
    ppermute x3, starting transfers between devices, shards(): lax.ppermute(partial[step], CHIPS[0], [(i, (i + step) % along_x) for i in...  4.17 us
  transfers between devices with their start and end apart: 18, of which 17 were waited for; matrix products, arithmetic and copies ran while one was open for 1% of the time, Pallas kernels for 9%

profile of v3, /device:TPU:32, one launch (start us, length us, event | category | flops | bytes accessed | tf_op | source)
XLA Modules:
  0.0 137.9 jit_solution(10920654342728679409)
XLA Ops:
  7.2 1.5 %shard_map.85 = (bf16[32,512]{1,0:T(8,128)(2,1)}, bf16[32,512]{1,0:T(8,128)(2,1)}, bf16[32,1024]{1,0:T(8,128)(2,1)}, bf16[8,512]{1,0:T(8,128)(2,1)}, bf16[8,512]{1,0:T(8,128)(2,1)}) custom-call(bf16[1,4,32,128]{3,2,1,0:T(8,128)(2,1)} %refs_0_.1, bf16[1,4,32,128]{3,2,1,0:T(8,128)(2,1)} %refs_1_.1, bf16[1,4,32,128]{3,2,1,0:T(8,128)(2,1)} %refs_2_.1, ...), custom_call_target="tpu_custom_call" | custom-call | flops 327680 | bytes 262144 | tf_op jit(solution)/shard_map/pallas_call | solution.py:41
  8.8 2.0 %collective-permute-start = (bf16[8,512]{1,0:T(8,128)(2,1)}, bf16[8,512]{1,0:T(8,128)(2,1)S(1)}, u32[]{:S(2)}, u32[]{:S(2)}) collective-permute-start(bf16[8,512]{1,0:T(8,128)(2,1)} %get-tuple-element.16), channel_id=1, source_target_pairs={{0,1},{1,2},{2,3},{3,4},{4,5},{5,6},{6,7},{7,8},{8,9},{9,10},{10,1... | collective-permute-start | bytes 24584 | tf_op jit(solution)/shard_map/ppermute | solution.py:378
  10.9 1.8 %collective-permute-done.low_ref = bf16[8,512]{1,0:T(8,128)(2,1)S(1)} collective-permute-done((bf16[8,512]{1,0:T(8,128)(2,1)}, bf16[8,512]{1,0:T(8,128)(2,1)S(1)}, u32[]{:S(2)}, u32[]{:S(2)}) %collective-permute-start) | collective-permute-done | bytes 8224 | tf_op jit(solution)/shard_map/ppermute | solution.py:378
  12.7 1.9 %collective-permute-done.1.high_ref = bf16[8,512]{1,0:T(8,128)(2,1)S(1)} collective-permute-done((bf16[8,512]{1,0:T(8,128)(2,1)}, bf16[8,512]{1,0:T(8,128)(2,1)S(1)}, u32[]{:S(2)}, u32[]{:S(2)}) %collective-permute-start.1) | collective-permute-done | bytes 8224 | tf_op jit(solution)/shard_map/ppermute | solution.py:379
  16.3 7.0 %all-to-all-start = ((bf16[16,24,512]{2,1,0:T(8,128)(2,1)}), bf16[16,24,512]{2,1,0:T(8,128)(2,1)S(1)}, u32[]{:S(2)}, u32[]{:S(2)}) async-start(bf16[16,24,512]{2,1,0:T(8,128)(2,1)} %shard_map.86), calls=%async_computation | async-start | bytes 786432 | tf_op jit(solution)/shard_map/all_to_all | solution.py:256
  23.8 1.5 %collective-permute-done.2.other_ref = bf16[3,3,128,128]{3,2,1,0:T(8,128)(2,1)S(1)} collective-permute-done((bf16[3,3,128,128]{3,2,1,0:T(8,128)(2,1)}, bf16[3,3,128,128]{3,2,1,0:T(8,128)(2,1)S(1)}, u32[]{:S(2)}, u32[]{:S(2)}) %collective-permute-start.2) | collective-permute-done | bytes 294944 | tf_op jit(solution)/shard_map/ppermute | solution.py:407
  26.6 1.6 %copy-done.2 = bf16[2,3,512,512]{3,2,1,0:T(8,128)(2,1)} copy-done((bf16[2,3,512,512]{3,2,1,0:T(8,128)(2,1)}, bf16[2,3,512,512]{3,2,1,0:T(8,128)(2,1)S(1)}, u32[]{:S(2)}) %copy-start.2) | copy-done | bytes 3145752
  28.2 6.2 %all-to-all-done.blocks_ref.grad_ref = bf16[16,24,512]{2,1,0:T(8,128)(2,1)S(1)} async-done(((bf16[16,24,512]{2,1,0:T(8,128)(2,1)}), bf16[16,24,512]{2,1,0:T(8,128)(2,1)S(1)}, u32[]{:S(2)}, u32[]{:S(2)}) %all-to-all-start) | async-done | bytes 393248 | tf_op jit(solution)/shard_map/all_to_all | solution.py:256
  34.4 4.1 %shard_map.88 = bf16[8,24,1024]{2,1,0:T(8,128)(2,1)} custom-call(bf16[16,24,512]{2,1,0:T(8,128)(2,1)S(1)} %all-to-all-done.blocks_ref.grad_ref, bf16[2,3,512,512]{3,2,1,0:T(8,128)(2,1)} %copy-done.2), custom_call_target="tpu_custom_call" | custom-call | flops 905969664 | bytes 7077888 | tf_op jit(solution)/shard_map/pallas_call | solution.py:41
  38.5 3.5 %all-to-all-start.1 = ((bf16[8,24,1024]{2,1,0:T(8,128)(2,1)}), bf16[8,24,1024]{2,1,0:T(8,128)(2,1)S(1)}, u32[]{:S(2)}, u32[]{:S(2)}) async-start(bf16[8,24,1024]{2,1,0:T(8,128)(2,1)} %shard_map.88), calls=%async_computation.1 | async-start | bytes 786432 | tf_op jit(solution)/shard_map/all_to_all | solution.py:256
  43.3 8.5 %all-to-all-done.1.parts_ref = bf16[8,24,1024]{2,1,0:T(8,128)(2,1)S(1)} async-done(((bf16[8,24,1024]{2,1,0:T(8,128)(2,1)}), bf16[8,24,1024]{2,1,0:T(8,128)(2,1)S(1)}, u32[]{:S(2)}, u32[]{:S(2)}) %all-to-all-start.1) | async-done | bytes 393248 | tf_op jit(solution)/shard_map/all_to_all | solution.py:256
  52.7 11.9 %all-gather.3.cloned.1.call-done = bf16[512,1024]{1,0:T(8,128)(2,1)} async-done(((bf16[32,1024]{1,0:T(8,128)(2,1)}), bf16[512,1024]{1,0:T(8,128)(2,1)}) %all-gather.3.cloned.1.call-update) | async-done | bytes 1048592 | tf_op jit(solution)/shard_map/all_gather | solution.py:375
  64.6 3.7 %all-to-all-start.2 = ((bf16[8,24,1024]{2,1,0:T(8,128)(2,1)}), bf16[8,24,1024]{2,1,0:T(8,128)(2,1)S(1)}, u32[]{:S(2)}, u32[]{:S(2)}) async-start(bf16[8,24,1024]{2,1,0:T(8,128)(2,1)} %shard_map.90), calls=%async_computation.2 | async-start | bytes 786432 | tf_op jit(solution)/shard_map/all_to_all | solution.py:256
  68.3 1.2 copy-done
  72.2 6.2 %all-to-all-done.2.blocks_ref.grad_ref = bf16[8,24,1024]{2,1,0:T(8,128)(2,1)S(1)} async-done(((bf16[8,24,1024]{2,1,0:T(8,128)(2,1)}), bf16[8,24,1024]{2,1,0:T(8,128)(2,1)S(1)}, u32[]{:S(2)}, u32[]{:S(2)}) %all-to-all-start.2) | async-done | bytes 393248 | tf_op jit(solution)/shard_map/all_to_all | solution.py:256
  82.0 8.3 %all-to-all-start.3 = ((bf16[16,144,128]{2,1,0:T(8,128)(2,1)}), bf16[16,144,128]{2,1,0:T(8,128)(2,1)S(1)}, u32[]{:S(2)}, u32[]{:S(2)}) async-start(bf16[16,144,128]{2,1,0:T(8,128)(2,1)} %shard_map.97), calls=%async_computation.3 | async-start | bytes 1179648 | tf_op jit(solution)/shard_map/all_to_all | solution.py:256
  90.6 1.6 %collective-permute-done.5.other_ref = bf16[3,3,128,128]{3,2,1,0:T(8,128)(2,1)S(1)} collective-permute-done((bf16[3,3,128,128]{3,2,1,0:T(8,128)(2,1)S(1)}, bf16[3,3,128,128]{3,2,1,0:T(8,128)(2,1)S(1)}, u32[]{:S(2)}, u32[]{:S(2)}) %collective-permute-start.5) | collective-permute-done | bytes 294944 | tf_op jit(solution)/shard_map/ppermute | solution.py:408
  92.6 2.1 %shard_map.94 = bf16[2,4,16,1024]{3,2,1,0:T(8,128)(2,1)S(1)} custom-call(bf16[8,24,1024]{2,1,0:T(8,128)(2,1)S(1)} %all-to-all-done.2.blocks_ref.grad_ref, bf16[2,3,512,512]{3,2,1,0:T(8,128)(2,1)S(1)} %shard_map.93.band_ref), custom_call_target="tpu_custom_call" | custom-call | flops 805306368 | bytes 7077888 | tf_op jit(solution)/shard_map/pallas_call | solution.py:41
  94.7 2.1 %collective-permute-start.6 = (bf16[4,16,1024]{2,1,0:T(8,128)(2,1)S(1)}, bf16[4,16,1024]{2,1,0:T(8,128)(2,1)S(1)}, u32[]{:S(2)}, u32[]{:S(2)}) collective-permute-start(bf16[4,16,1024]{2,1,0:T(8,128)(2,1)S(1)} %slice_bitcast_fusion), channel_id=1, source_target_pairs={{0,32},{32,0},{1,33},{33,1},{2,34},{34,2},{3,35},{35,3},{4,36},{36... | collective-permute-start | bytes 393224 | tf_op jit(solution)/shard_map/ppermute | solution.py:454
  96.8 10.5 %all-to-all-done.3.parts_ref = bf16[16,144,128]{2,1,0:T(8,128)(2,1)S(1)} async-done(((bf16[16,144,128]{2,1,0:T(8,128)(2,1)}), bf16[16,144,128]{2,1,0:T(8,128)(2,1)S(1)}, u32[]{:S(2)}, u32[]{:S(2)}) %all-to-all-start.3) | async-done | bytes 589856 | tf_op jit(solution)/shard_map/all_to_all | solution.py:256
  108.3 5.0 %all-to-all-start.4 = ((bf16[16,144,128]{2,1,0:T(8,128)(2,1)}), bf16[16,144,128]{2,1,0:T(8,128)(2,1)S(1)}, u32[]{:S(2)}, u32[]{:S(2)}) async-start(bf16[16,144,128]{2,1,0:T(8,128)(2,1)} %shard_map.98), calls=%async_computation.4 | async-start | bytes 1179648 | tf_op jit(solution)/shard_map/all_to_all | solution.py:256
  113.8 2.2 %collective-permute-start.8 = (bf16[16,1024]{1,0:T(8,128)(2,1)S(1)}, bf16[16,1024]{1,0:T(8,128)(2,1)S(1)}, u32[]{:S(2)}, u32[]{:S(2)}) collective-permute-start(bf16[16,1024]{1,0:T(8,128)(2,1)S(1)} %get-tuple-element.31), channel_id=1, source_target_pairs={{0,128},{64,192},{128,0},{192,64},{1,129},{65,193},{129,1},{193,65... | collective-permute-start | bytes 98312 | tf_op jit(solution)/shard_map/ppermute | solution.py:458
  116.0 1.5 %collective-permute-start.9 = (bf16[16,1024]{1,0:T(8,128)(2,1)S(1)}, bf16[16,1024]{1,0:T(8,128)(2,1)S(1)}, u32[]{:S(2)}, u32[]{:S(2)}) collective-permute-start(bf16[16,1024]{1,0:T(8,128)(2,1)S(1)} %get-tuple-element.30), channel_id=1, source_target_pairs={{0,192},{64,0},{128,64},{192,128},{1,193},{65,1},{129,65},{193,129... | collective-permute-start | bytes 98312 | tf_op jit(solution)/shard_map/ppermute | solution.py:458
  121.8 8.1 %all-to-all-done.4 = bf16[16,144,128]{2,1,0:T(8,128)(2,1)S(1)} async-done(((bf16[16,144,128]{2,1,0:T(8,128)(2,1)}), bf16[16,144,128]{2,1,0:T(8,128)(2,1)S(1)}, u32[]{:S(2)}, u32[]{:S(2)}) %all-to-all-start.4) | async-done | bytes 589856 | tf_op jit(solution)/shard_map/all_to_all | solution.py:256
  (50 shorter events, 19.6 us)
Async XLA Ops:
  7.2 57.4 %all-gather.3.cloned.1.call-start = ((), (), s32[]{:S(2)}) async-start(), calls=%async_computation.5 | async-start | bytes 1114112 | tf_op jit(solution)/shard_map/all_gather | solution.py:375
  8.8 3.9 %collective-permute-start = (bf16[8,512]{1,0:T(8,128)(2,1)}, bf16[8,512]{1,0:T(8,128)(2,1)S(1)}, u32[]{:S(2)}, u32[]{:S(2)}) collective-permute-start(bf16[8,512]{1,0:T(8,128)(2,1)} %get-tuple-element.16), channel_id=1, source_target_pairs={{0,1},{1,2},{2,3},{3,4},{4,5},{5,6},{6,7},{7,8},{8,9},{9,10},{10,1... | collective-permute-start | bytes 24584 | tf_op jit(solution)/shard_map/ppermute | solution.py:378
  10.8 3.9 %collective-permute-start.1 = (bf16[8,512]{1,0:T(8,128)(2,1)}, bf16[8,512]{1,0:T(8,128)(2,1)S(1)}, u32[]{:S(2)}, u32[]{:S(2)}) collective-permute-start(bf16[8,512]{1,0:T(8,128)(2,1)} %get-tuple-element.17), channel_id=1, source_target_pairs={{1,0},{2,1},{3,2},{4,3},{5,4},{6,5},{7,6},{8,7},{9,8},{10,9},{11,1... | collective-permute-start | bytes 24584 | tf_op jit(solution)/shard_map/ppermute | solution.py:379
  16.3 18.1 %all-to-all-start = ((bf16[16,24,512]{2,1,0:T(8,128)(2,1)}), bf16[16,24,512]{2,1,0:T(8,128)(2,1)S(1)}, u32[]{:S(2)}, u32[]{:S(2)}) async-start(bf16[16,24,512]{2,1,0:T(8,128)(2,1)} %shard_map.86), calls=%async_computation | async-start | bytes 786432 | tf_op jit(solution)/shard_map/all_to_all | solution.py:256
  23.3 1.9 %collective-permute-start.2 = (bf16[3,3,128,128]{3,2,1,0:T(8,128)(2,1)}, bf16[3,3,128,128]{3,2,1,0:T(8,128)(2,1)S(1)}, u32[]{:S(2)}, u32[]{:S(2)}) collective-permute-start(bf16[3,3,128,128]{3,2,1,0:T(8,128)(2,1)} %bitcast.47), channel_id=1, source_target_pairs={{0,16},{16,0},{1,17},{17,1},{2,18},{18,2},{3,19},{19,3},{4,20},{20... | collective-permute-start | bytes 884744 | tf_op jit(solution)/shard_map/ppermute | solution.py:407
  25.2 1.0 copy-start.3
  26.6 1.6 %copy-start.2 = (bf16[2,3,512,512]{3,2,1,0:T(8,128)(2,1)}, bf16[2,3,512,512]{3,2,1,0:T(8,128)(2,1)S(1)}, u32[]{:S(2)}) copy-start(bf16[2,3,512,512]{3,2,1,0:T(8,128)(2,1)S(1)} %shard_map.87.band_ref) | copy-start | bytes 9437188
  28.2 13.7 %copy-start.6 = (bf16[32,512]{1,0:T(8,128)(2,1)S(1)}, bf16[32,512]{1,0:T(8,128)(2,1)}, u32[]{:S(2)}) copy-start(bf16[32,512]{1,0:T(8,128)(2,1)} %get-tuple-element.18.pre_ref) | copy-start | bytes 98308
  38.5 13.3 %all-to-all-start.1 = ((bf16[8,24,1024]{2,1,0:T(8,128)(2,1)}), bf16[8,24,1024]{2,1,0:T(8,128)(2,1)S(1)}, u32[]{:S(2)}, u32[]{:S(2)}) async-start(bf16[8,24,1024]{2,1,0:T(8,128)(2,1)} %shard_map.88), calls=%async_computation.1 | async-start | bytes 786432 | tf_op jit(solution)/shard_map/all_to_all | solution.py:256
  42.0 1.3 collective-permute-start.3
  64.6 13.8 %all-to-all-start.2 = ((bf16[8,24,1024]{2,1,0:T(8,128)(2,1)}), bf16[8,24,1024]{2,1,0:T(8,128)(2,1)S(1)}, u32[]{:S(2)}, u32[]{:S(2)}) async-start(bf16[8,24,1024]{2,1,0:T(8,128)(2,1)} %shard_map.90), calls=%async_computation.2 | async-start | bytes 786432 | tf_op jit(solution)/shard_map/all_to_all | solution.py:256
  68.3 1.2 copy-start
  69.5 8.8 %copy-start.1 = (bf16[512,1024]{1,0:T(8,128)(2,1)S(1)}, bf16[512,1024]{1,0:T(8,128)(2,1)}, u32[]{:S(2)}) copy-start(bf16[512,1024]{1,0:T(8,128)(2,1)} %all-gather.3.cloned.1.call-done) | copy-start | bytes 3145732
  70.5 1.7 %collective-permute-start.4 = (bf16[3,3,128,128]{3,2,1,0:T(8,128)(2,1)S(1)}, bf16[3,3,128,128]{3,2,1,0:T(8,128)(2,1)S(1)}, u32[]{:S(2)}, u32[]{:S(2)}) collective-permute-start(bf16[3,3,128,128]{3,2,1,0:T(8,128)(2,1)S(1)} %shard_map.92), channel_id=1, source_target_pairs={{0,16},{16,0},{1,17},{17,1},{2,18},{18,2},{3,19},{19,3},{4,20},{20... | collective-permute-start | bytes 884744 | tf_op jit(solution)/shard_map/ppermute | solution.py:237
  71.6 18.7 %copy-start.4 = (bf16[1,3,3,128,128]{4,3,2,1,0:T(8,128)(2,1)S(1)}, bf16[1,3,3,128,128]{4,3,2,1,0:T(8,128)(2,1)}, u32[]{:S(2)}) copy-start(bf16[1,3,3,128,128]{4,3,2,1,0:T(8,128)(2,1)} %param.10) | copy-start | bytes 884740
  79.3 1.7 %collective-permute-start.11 = (bf16[3,3,128,128]{3,2,1,0:T(8,128)(2,1)S(1)}, bf16[3,3,128,128]{3,2,1,0:T(8,128)(2,1)S(1)}, u32[]{:S(2)}, u32[]{:S(2)}) collective-permute-start(bf16[3,3,128,128]{3,2,1,0:T(8,128)(2,1)S(1)} %shard_map.96), channel_id=1, source_target_pairs={{0,16},{16,0},{1,17},{17,1},{2,18},{18,2},{3,19},{19,3},{4,20},{20... | collective-permute-start | bytes 884744 | tf_op jit(solution)/shard_map/ppermute | solution.py:237
  82.0 25.3 %all-to-all-start.3 = ((bf16[16,144,128]{2,1,0:T(8,128)(2,1)}), bf16[16,144,128]{2,1,0:T(8,128)(2,1)S(1)}, u32[]{:S(2)}, u32[]{:S(2)}) async-start(bf16[16,144,128]{2,1,0:T(8,128)(2,1)} %shard_map.97), calls=%async_computation.3 | async-start | bytes 1179648 | tf_op jit(solution)/shard_map/all_to_all | solution.py:256
  90.3 1.9 %collective-permute-start.5 = (bf16[3,3,128,128]{3,2,1,0:T(8,128)(2,1)S(1)}, bf16[3,3,128,128]{3,2,1,0:T(8,128)(2,1)S(1)}, u32[]{:S(2)}, u32[]{:S(2)}) collective-permute-start(bf16[3,3,128,128]{3,2,1,0:T(8,128)(2,1)S(1)} %bitcast.49), channel_id=1, source_target_pairs={{0,16},{16,0},{1,17},{17,1},{2,18},{18,2},{3,19},{19,3},{4,20},{20... | collective-permute-start | bytes 884744 | tf_op jit(solution)/shard_map/ppermute | solution.py:408
  94.7 18.6 %collective-permute-start.6 = (bf16[4,16,1024]{2,1,0:T(8,128)(2,1)S(1)}, bf16[4,16,1024]{2,1,0:T(8,128)(2,1)S(1)}, u32[]{:S(2)}, u32[]{:S(2)}) collective-permute-start(bf16[4,16,1024]{2,1,0:T(8,128)(2,1)S(1)} %slice_bitcast_fusion), channel_id=1, source_target_pairs={{0,32},{32,0},{1,33},{33,1},{2,34},{34,2},{3,35},{35,3},{4,36},{36... | collective-permute-start | bytes 393224 | tf_op jit(solution)/shard_map/ppermute | solution.py:454
  108.3 21.6 %all-to-all-start.4 = ((bf16[16,144,128]{2,1,0:T(8,128)(2,1)}), bf16[16,144,128]{2,1,0:T(8,128)(2,1)S(1)}, u32[]{:S(2)}, u32[]{:S(2)}) async-start(bf16[16,144,128]{2,1,0:T(8,128)(2,1)} %shard_map.98), calls=%async_computation.4 | async-start | bytes 1179648 | tf_op jit(solution)/shard_map/all_to_all | solution.py:256
  113.4 5.2 %collective-permute-start.7 = (bf16[16,1024]{1,0:T(8,128)(2,1)S(1)}, bf16[16,1024]{1,0:T(8,128)(2,1)S(1)}, u32[]{:S(2)}, u32[]{:S(2)}) collective-permute-start(bf16[16,1024]{1,0:T(8,128)(2,1)S(1)} %get-tuple-element.29), channel_id=1, source_target_pairs={{0,64},{64,128},{128,192},{192,0},{1,65},{65,129},{129,193},{193,1... | collective-permute-start | bytes 98312 | tf_op jit(solution)/shard_map/ppermute | solution.py:458
  113.8 5.4 %collective-permute-start.8 = (bf16[16,1024]{1,0:T(8,128)(2,1)S(1)}, bf16[16,1024]{1,0:T(8,128)(2,1)S(1)}, u32[]{:S(2)}, u32[]{:S(2)}) collective-permute-start(bf16[16,1024]{1,0:T(8,128)(2,1)S(1)} %get-tuple-element.31), channel_id=1, source_target_pairs={{0,128},{64,192},{128,0},{192,64},{1,129},{65,193},{129,1},{193,65... | collective-permute-start | bytes 98312 | tf_op jit(solution)/shard_map/ppermute | solution.py:458
  116.0 3.9 %collective-permute-start.9 = (bf16[16,1024]{1,0:T(8,128)(2,1)S(1)}, bf16[16,1024]{1,0:T(8,128)(2,1)S(1)}, u32[]{:S(2)}, u32[]{:S(2)}) collective-permute-start(bf16[16,1024]{1,0:T(8,128)(2,1)S(1)} %get-tuple-element.30), channel_id=1, source_target_pairs={{0,192},{64,0},{128,64},{192,128},{1,193},{65,1},{129,65},{193,129... | collective-permute-start | bytes 98312 | tf_op jit(solution)/shard_map/ppermute | solution.py:458
  119.9 1.3 collective-permute-start.10
  (1 other events, 0.8 us)
Sparse Core Ops, SparseCore 0:
  11.3 53.2 all-gather.2

commit v4 on v3

--- a/solution.py
+++ b/solution.py
@@ -176,18 +176,28 @@
 
 
 def filter_kernel(
-    orients, width, field, first, own, grad_ref, feat_ref, out_ref, feat_rows, grad_rows, held, done
+    orients, width, field, first, own, grad_ref, *refs
 ):
+    feat_refs, (out_ref, feat_rows, grad_rows, held, done) = refs[:-5], refs[-5:]
     chip, core = here()
     slot = core if own else 1 - core
     in_width = grad_rows.shape[0]
-    columns = pl.ds(pl.multiple_of(core * width, width), width)
     lanes = pl.ds(field * WIDE, WIDE)
-    copy = pltpu.make_async_copy(feat_ref.at[:, columns, lanes], held, done)
-    copy.start()
+    copies = []
+    for step, feat_ref in enumerate(feat_refs):
+        row = lax.rem(chip // 2 - step + len(feat_refs), len(feat_refs))
+        for y in range(2):
+            for c in range(2):
+                s = (row * 2 + (chip + y) % 2) * 2 + (core + c) % 2
+                copy = pltpu.make_async_copy(
+                    feat_ref.at[y, c, :, lanes], held.at[s], done.at[len(copies)]
+                )
+                copy.start()
+                copies.append(copy)
     interleave(grad_ref, grad_rows, orients, in_width, 0)
     grads = grad_rows[...].reshape(in_width * orients, WIDE).astype(jnp.bfloat16)
-    copy.wait()
+    for copy in copies:
+        copy.wait()
     for g in range(orients):
         s = lax.rem(g + 2 * chip + slot, orients)
         feat_rows[:, g, :] = held[s].astype(jnp.float32)
@@ -214,7 +224,7 @@
 
 
 def filter_terms(feats, field, width, grads, first):
-    orients = feats.shape[0]
+    orients = len(feats) * 4
     in_width = grads.shape[1]
 
     def terms(own):
@@ -225,12 +235,12 @@
                 pltpu.VMEM((width, orients, WIDE), jnp.float32),
                 pltpu.VMEM((in_width, orients, WIDE), jnp.float32),
                 pltpu.VMEM((orients, width, WIDE), jnp.bfloat16),
-                pltpu.SemaphoreType.DMA,
+                pltpu.SemaphoreType.DMA((orients,)),
             ],
             6 * width * orients * WIDE * WIDE,
             grads,
-            feats,
-            space=(VMEM, HBM),
+            *feats,
+            space=(VMEM, *[HBM] * len(feats)),
             room=52,
         )
 
@@ -256,42 +266,128 @@
     return lax.all_to_all(parts, axes, 0, 0, tiled=True)
 
 
-def join_kernel(mine_1, theirs_1, mine_2, theirs_2, out_ref, held, done):
-    size = mine_1.shape[1]
-    for first, mine, theirs in ((0, mine_1, theirs_1), (size, mine_2, theirs_2)):
-        both = mine[...].astype(jnp.float32) + theirs[...].astype(jnp.float32)
-        held[:, first : first + size] = both.astype(jnp.bfloat16)
+def chunks(pair):
+    count = lax.axis_size(AZ)
+    return [bank.reshape(count, -1, CHAN) for bank in pair]
+
+
+def after(array, first):
+    return lax.optimization_barrier((array, first))[0]
+
+
+def halves_kernel(mine, theirs, stay_ref, leave_ref, both_ref):
+    half = stay_ref.shape[0]
+    side = lax.axis_index(AZ) // half
+    both_ref[...] = mine[...].astype(jnp.float32) + theirs[...].astype(jnp.float32)
+    stay_ref[...] = both_ref[pl.ds(side * half, half)].astype(jnp.bfloat16)
+    leave_ref[...] = both_ref[pl.ds((1 - side) * half, half)].astype(jnp.bfloat16)
+
+
+def deal_kernel(stay, came, out_ref):
+    both = stay[...].astype(jnp.float32) + came[...].astype(jnp.float32)
+    lines = both.reshape(-1, CHAN)
+    count, size, _ = out_ref.shape
+    lines = jnp.concatenate([lines, jnp.zeros((count * size - lines.shape[0], CHAN), jnp.float32)])
+    out_ref[...] = lines.reshape(out_ref.shape).astype(jnp.bfloat16)
+
+
+def half_terms(pair):
+    mine, theirs = chunks(pair)
+    count, size, _ = mine.shape
+    half = jax.ShapeDtypeStruct((count // 2, size, CHAN), jnp.bfloat16)
+    both = pltpu.VMEM(mine.shape, jnp.float32)
+    stay, leave = call(halves_kernel, (half, half), [both], mine.size, mine, theirs)
+    came = lax.ppermute(leave, AZ, [(i, (i + count // 2) % count) for i in range(count)])
+    dealt = -(-size // 16) * 8
+    shape = jax.ShapeDtypeStruct((count, dealt, CHAN), jnp.bfloat16)
+    return leave, call(deal_kernel, shape, [], mine.size, stay, came)
+
+
+def join_kernel(mine, theirs, also, out_ref, held, done):
+    size = mine.shape[1]
+    both = mine[...].astype(jnp.float32) + theirs[...].astype(jnp.float32)
+    held[:, :size] = both.astype(jnp.bfloat16)
+    held[:, size:] = also[...]
     copy_all([(held, out_ref)], done)
 
 
-def reduce_kernel(parts_ref, out_ref, held, done):
-    total = parts_ref[0].astype(jnp.float32)
-    for n in range(1, parts_ref.shape[0]):
-        total = total + parts_ref[n].astype(jnp.float32)
-    held[...] = total.astype(jnp.bfloat16)
-    copy_all([(held, out_ref.at[n]) for n in range(out_ref.shape[0])], done)
-
-
-def summed_over_az(pairs, scale):
-    count = lax.axis_size(AZ)
-    banks = [bank.reshape(count, -1, CHAN) for pair in pairs for bank in pair]
-    size = banks[0].shape[1]
-    shape = jax.ShapeDtypeStruct((count, 2 * size, CHAN), jnp.bfloat16)
-    work = count * size * CHAN
+def joined_terms(pair, also):
+    mine, theirs = chunks(pair)
+    count, size, _ = mine.shape
+    shape = jax.ShapeDtypeStruct((count, size + also.shape[1], CHAN), jnp.bfloat16)
     held = [pltpu.VMEM(shape.shape, jnp.bfloat16), pltpu.SemaphoreType.DMA((1,))]
-    joined = call(join_kernel, shape, held, work, *banks, out_space=HBM)
-    held = [pltpu.VMEM(shape.shape[1:], jnp.bfloat16), pltpu.SemaphoreType.DMA((count,))]
-    copies = call(reduce_kernel, shape, held, work, exchange(joined, AZ), out_space=HBM)
-    whole = exchange(copies, AZ)
-    one, two = whole[:, :size], whole[:, size:]
-    return tuple(
-        (part.astype(jnp.float32) * scale).reshape(1, 3, 3, CHAN, CHAN) for part in (one, two)
-    )
+    return call(join_kernel, shape, held, mine.size, mine, theirs, also, out_space=HBM)
+
+
+def reduce_kernel(size, parts_ref, out_ref, held, done):
+    count = parts_ref.shape[0]
+    dealt = parts_ref.shape[1] - size
+    total = [parts_ref[n].astype(jnp.float32) for n in (0, count // 2)]
+    for n in range(1, count // 2):
+        total[0] = total[0] + parts_ref[n].astype(jnp.float32)
+        total[1] = total[1] + parts_ref[count // 2 + n].astype(jnp.float32)
+    held[:size] = (total[0][:size] + total[1][:size]).astype(jnp.bfloat16)
+    held[size : size + dealt] = total[0][size:].astype(jnp.bfloat16)
+    held[size + dealt :] = total[1][size:].astype(jnp.bfloat16)
+    copy_all([(held, out_ref.at[n]) for n in range(count)], done)
+
+
+def finish_kernel(size, scale, whole_ref, one_ref, two_ref, held_one, held_two, done):
+    count = whole_ref.shape[0]
+    dealt = (whole_ref.shape[1] - size) // 2
+    lines = two_ref.shape[1]
+    held_one[...] = whole_ref[:, :size].astype(jnp.float32) * scale
+    first = pltpu.make_async_copy(held_one, one_ref, done.at[0])
+    first.start()
+    for side in range(2):
+        for n in range(count):
+            start, end = n * dealt, min((n + 1) * dealt, lines)
+            if end > start:
+                row = size + side * dealt
+                part = whole_ref[n, row : row + dealt].astype(jnp.float32) * scale
+                held_two[side, start:end] = part[: end - start]
+    second = pltpu.make_async_copy(held_two, two_ref, done.at[1])
+    second.start()
+    first.wait()
+    second.wait()
+
+
+def summed_over_az(joined, size, scale):
+    count, both, _ = joined.shape
+    dealt = both - size
+    held = [pltpu.VMEM((size + 2 * dealt, CHAN), jnp.bfloat16), pltpu.SemaphoreType.DMA((count,))]
+    shape = jax.ShapeDtypeStruct((count, size + 2 * dealt, CHAN), jnp.bfloat16)
+    copies = call(
+        functools.partial(reduce_kernel, size),
+        shape,
+        held,
+        joined.size,
+        exchange(joined, AZ),
+        out_space=HBM,
+    )
+    one = (count, size, CHAN)
+    two = (2, count * size // 2, CHAN)
+    banks = call(
+        functools.partial(finish_kernel, size, scale),
+        (jax.ShapeDtypeStruct(one, jnp.float32), jax.ShapeDtypeStruct(two, jnp.float32)),
+        [
+            pltpu.VMEM(one, jnp.float32),
+            pltpu.VMEM(two, jnp.float32),
+            pltpu.SemaphoreType.DMA((2,)),
+        ],
+        joined.size,
+        exchange(copies, AZ),
+        out_space=HBM,
+        room=52,
+    )
+    return tuple(bank.reshape(1, 3, 3, CHAN, CHAN) for bank in banks)
 
 
 def lanes_kernel(*refs):
-    given, (grad_ref, pre_ref, feats_ref, up_ref, down_ref) = refs[:4], refs[4:9]
-    held, done = refs[9:13], refs[13]
+    given, (grad_ref, pre_ref, feats_ref, away_ref, up_ref, down_ref) = refs[:4], refs[4:10]
+    held, done = refs[10:14], refs[14]
+    _, core = here()
+    half = feats_ref.shape[0]
     copy_all(zip(given, held), done)
     inputs_ref, pre_one_ref, pre_two_ref, cotangent_ref = held
     for row in range(ROWS):
@@ -304,8 +400,12 @@
         grad = grad.astype(jnp.bfloat16)
         grad_ref[:, lanes] = grad
         pre_ref[:, lanes] = pre
-        feats_ref[:, lanes] = (wide / (1.0 + jnp.exp(-wide))).astype(jnp.bfloat16)
-        feats_ref[:, WIDE + row * CHAN : WIDE + (row + 1) * CHAN] = inputs_ref[0, row]
+        act = (wide / (1.0 + jnp.exp(-wide))).astype(jnp.bfloat16)
+        for first, field in ((0, act), (WIDE, inputs_ref[0, row])):
+            low, high = field[:half], field[half:]
+            place = slice(first + row * CHAN, first + (row + 1) * CHAN)
+            feats_ref[:, place] = jnp.where(core == 0, low, high)
+            away_ref[:, place] = jnp.where(core == 0, high, low)
         grad = grad.astype(jnp.float32)
         pad = jnp.zeros((5, CHAN), jnp.float32)
         up_ref[:, lanes] = jnp.concatenate([grad[-2:], wide[-1:], pad]).astype(jnp.bfloat16)
@@ -354,12 +454,13 @@
     def narrow(*shape):
         return jax.ShapeDtypeStruct(shape, jnp.bfloat16)
 
-    grad_two, pre, feats, up, down = call(
+    grad_two, pre, feats, feats_away, up, down = call(
         lanes_kernel,
         (
             narrow(columns, WIDE),
             narrow(columns, WIDE),
-            narrow(columns, 2 * WIDE),
+            narrow(half, 2 * WIDE),
+            narrow(half, 2 * WIDE),
             narrow(8, WIDE),
             narrow(8, WIDE),
         ),
@@ -372,7 +473,6 @@
         space=HBM,
         room=60,
     )
-    all_feats = lax.all_gather(feats, ROT)
     forward = [(i, (i + 1) % az_count) for i in range(az_count)]
     backward = [(target, source) for source, target in forward]
     low = lax.ppermute(up, AZ, forward)
@@ -404,6 +504,13 @@
         high,
     )
 
+    pair = jnp.stack([feats, lax.ppermute(feats_away, CORE, SWAP)])
+    chip_pair = jnp.stack([pair, lax.ppermute(pair, CHIPS[1], SWAP)])
+    along_x = lax.axis_size(CHIPS[0])
+    all_feats = [chip_pair] + [
+        lax.ppermute(chip_pair, CHIPS[0], [(i, (i + step) % along_x) for i in range(along_x)])
+        for step in range(1, along_x)
+    ]
     other_two = lax.ppermute(filt_two[0], CORE, SWAP)
     other_one = lax.ppermute(filt_one[0], CORE, SWAP)
     pre_partner = lax.ppermute(pre_away, CORE, SWAP)
@@ -412,7 +519,7 @@
 
     shares = conv(
         conv_two_kernel,
-        all_grad_two,
+        after(all_grad_two, chip_pair),
         bands_two,
         half + 2,
         padded,
@@ -424,7 +531,9 @@
         HBM,
         52,
     )
-    arrived = exchange(shares, CHIPS)
+    pair_two = filter_terms(all_feats, 0, half, all_grad_two, 3)
+    leave, terms_two = half_terms(pair_two)
+    arrived = after(exchange(shares, CHIPS), leave)
     copies = call(
         point_kernel,
         narrow(chips, padded, 2 * WIDE),
@@ -435,17 +544,13 @@
         pre_partner,
         out_space=HBM,
     )
-    copies, all_feats = lax.optimization_barrier((copies, all_feats))
-    all_grad_one = exchange(copies, CHIPS)
-    pair_two = filter_terms(all_feats, 0, half, all_grad_two, 3)
-    all_grad_one, pair_two = lax.optimization_barrier((all_grad_one, pair_two))
-    pair_one = filter_terms(all_feats, 1, half, all_grad_one, 2)
-    filt_grad_one, filt_grad_two = summed_over_az((pair_one, pair_two), scale)
-
-    along_x = lax.axis_size(CHIPS[0])
+    all_grad_one = after(exchange(copies, CHIPS), terms_two)
+    joined = joined_terms(filter_terms(all_feats, 1, half, all_grad_one, 2), terms_two)
+    filt_grad_one, filt_grad_two = summed_over_az(joined, filt_one.size // CHAN // az_count, scale)
+
     shares = conv(
         conv_one_kernel,
-        all_grad_one,
+        after(all_grad_one, joined),
         bands_one,
         half,
         half,

time: 139 us -> 118 us (0.85)
  waiting for transfers between devices: 63.9 us -> 46.5 us
  between operations: 14.3 us -> 1.07 us
  starting transfers between devices: 37 us -> 46.1 us
  Pallas kernels: 16.3 us -> 18.8 us
    all_to_all x5, waiting for transfers between devices: 39.4 us -> 22.9 us  [exchange(): return lax.all_to_all(parts, axes, 0, 0, tiled=True)]
    ppermute x0 -> x6, waiting for transfers between devices: none -> 12.6 us  [the longest x1 6.31 us: half_terms(): lax.ppermute(leave, AZ, [(i, (i + count // 2) % count) for i in range(cou...]
    all_gather x1 -> x0, waiting for transfers between devices: 11.9 us -> none  [shards(): all_feats = lax.all_gather(feats, ROT)]
    ppermute x0 -> x6, starting transfers between devices: none -> 9.64 us  [the longest x3 4.84 us: shards(): lax.ppermute(chip_pair, CHIPS[0], [(i, (i + step) % along_x) for i in ran...]
    pallas_call x14 -> x17, Pallas kernels: 16.3 us -> 18.8 us  [call(): pl.pallas_call(kernel, out_shape=out_shape, in_specs=in_specs, out_specs=...]
    ppermute x3, waiting for transfers between devices: 2.37 us -> 4.33 us  [shards(): lax.ppermute(partial[step], CHIPS[0], [(i, (i + step) % along_x) for i in...]
    ppermute x1, waiting for transfers between devices: 1.47 us -> 0.01 us  [shards(): other_two = lax.ppermute(filt_two[0], CORE, SWAP)]
    unnamed x14 -> x10, local copies, waits for them, and re-layouts: 4.58 us -> 3.35 us
  transfers between devices with their start and end apart: 18 -> 23, of which waited for: 17 -> 15; matrix products, arithmetic and copies ran while one was open for 1% -> 1% of each run, Pallas kernels for 9% -> 10%
where the time goes in v4:
time: 118 us; the launch traced here: 117 us
  waiting for transfers between devices  46.5 us (39%)
  starting transfers between devices  46.1 us (39%)
  Pallas kernels  18.8 us (16%)
  local copies, waits for them, and re-layouts  3.38 us (3%)
  other arithmetic  1.47 us (1%)
    all_to_all x5, starting transfers between devices, exchange(): return lax.all_to_all(parts, axes, 0, 0, tiled=True)  27.6 us
    all_to_all x5, waiting for transfers between devices, exchange(): return lax.all_to_all(parts, axes, 0, 0, tiled=True)  22.9 us
    pallas_call x17, Pallas kernels, call(): pl.pallas_call(kernel, out_shape=out_shape, in_specs=in_specs, out_specs=...  18.8 us
    ppermute x1, waiting for transfers between devices, half_terms(): lax.ppermute(leave, AZ, [(i, (i + count // 2) % count) for i in range(cou...  6.31 us
    ppermute x1, waiting for transfers between devices, shards(): chip_pair = jnp.stack([pair, lax.ppermute(pair, CHIPS[1], SWAP)])  5.38 us
    ppermute x3, starting transfers between devices, shards(): lax.ppermute(chip_pair, CHIPS[0], [(i, (i + step) % along_x) for i in ran...  4.84 us
    ppermute x3, waiting for transfers between devices, shards(): lax.ppermute(partial[step], CHIPS[0], [(i, (i + step) % along_x) for i in...  4.33 us
    ppermute x1, starting transfers between devices, shards(): chip_pair = jnp.stack([pair, lax.ppermute(pair, CHIPS[1], SWAP)])  3.43 us
  transfers between devices with their start and end apart: 23, of which 15 were waited for; matrix products, arithmetic and copies ran while one was open for 1% of the time, Pallas kernels for 10%

profile of v4, /device:TPU:32, one launch (start us, length us, event | category | flops | bytes accessed | tf_op | source)
XLA Modules:
  0.0 117.3 jit_solution(2204689647073776430)
XLA Ops:
  0.6 1.5 %shard_map.85 = (bf16[32,512]{1,0:T(8,128)(2,1)}, bf16[32,512]{1,0:T(8,128)(2,1)}, bf16[16,1024]{1,0:T(8,128)(2,1)}, bf16[16,1024]{1,0:T(8,128)(2,1)}, bf16[8,512]{1,0:T(8,128)(2,1)}, /*index=5*/bf16[8,512]{1,0:T(8,128)(2,1)}) custom-call(bf16[1,4,32,128]{3,2,1,0:T(8,128)(2,1)} %refs_0_.1, bf16[1,4,32,128]{3,2,1,0:T(8,128)(2,1)} %refs_1_.1, ...), custom_call_target="tpu_custom_call" | custom-call | flops 327680 | bytes 262144 | tf_op jit(solution)/shard_map/pallas_call | solution.py:41
  2.2 2.0 %collective-permute-start = (bf16[8,512]{1,0:T(8,128)(2,1)}, bf16[8,512]{1,0:T(8,128)(2,1)S(1)}, u32[]{:S(2)}, u32[]{:S(2)}) collective-permute-start(bf16[8,512]{1,0:T(8,128)(2,1)} %get-tuple-element.20), channel_id=1, source_target_pairs={{0,1},{1,2},{2,3},{3,4},{4,5},{5,6},{6,7},{7,8},{8,9},{9,10},{10,1... | collective-permute-start | bytes 24584 | tf_op jit(solution)/shard_map/ppermute | solution.py:478
  4.3 1.8 %collective-permute-done.low_ref = bf16[8,512]{1,0:T(8,128)(2,1)S(1)} collective-permute-done((bf16[8,512]{1,0:T(8,128)(2,1)}, bf16[8,512]{1,0:T(8,128)(2,1)S(1)}, u32[]{:S(2)}, u32[]{:S(2)}) %collective-permute-start) | collective-permute-done | bytes 8224 | tf_op jit(solution)/shard_map/ppermute | solution.py:478
  6.1 1.9 %collective-permute-done.1.high_ref = bf16[8,512]{1,0:T(8,128)(2,1)S(1)} collective-permute-done((bf16[8,512]{1,0:T(8,128)(2,1)}, bf16[8,512]{1,0:T(8,128)(2,1)S(1)}, u32[]{:S(2)}, u32[]{:S(2)}) %collective-permute-start.1) | collective-permute-done | bytes 8224 | tf_op jit(solution)/shard_map/ppermute | solution.py:479
  9.7 7.0 %all-to-all-start = ((bf16[16,24,512]{2,1,0:T(8,128)(2,1)}), bf16[16,24,512]{2,1,0:T(8,128)(2,1)S(1)}, u32[]{:S(2)}, u32[]{:S(2)}) async-start(bf16[16,24,512]{2,1,0:T(8,128)(2,1)} %shard_map.86), calls=%async_computation | async-start | bytes 786432 | tf_op jit(solution)/shard_map/all_to_all | solution.py:266
  19.0 3.4 %collective-permute-start.3 = (bf16[2,16,1024]{2,1,0:T(8,128)(2,1)S(1)}, bf16[2,16,1024]{2,1,0:T(8,128)(2,1)S(1)}, u32[]{:S(2)}, u32[]{:S(2)}) collective-permute-start(bf16[2,16,1024]{2,1,0:T(8,128)(2,1)S(1)} %get-tuple-element.39), channel_id=1, source_target_pairs={{0,32},{32,0},{1,33},{33,1},{2,34},{34,2},{3,35},{35,3},{4,36},{36... | collective-permute-start | bytes 196616 | tf_op jit(solution)/shard_map/ppermute | solution.py:508
  22.4 5.4 %collective-permute-done.3 = bf16[2,16,1024]{2,1,0:T(8,128)(2,1)S(1)} collective-permute-done((bf16[2,16,1024]{2,1,0:T(8,128)(2,1)S(1)}, bf16[2,16,1024]{2,1,0:T(8,128)(2,1)S(1)}, u32[]{:S(2)}, u32[]{:S(2)}) %collective-permute-start.3) | collective-permute-done | bytes 65568 | tf_op jit(solution)/shard_map/ppermute | solution.py:508
  28.6 2.6 %collective-permute-start.6 = (bf16[2,2,16,1024]{3,2,1,0:T(8,128)(2,1)S(1)}, bf16[2,2,16,1024]{3,2,1,0:T(8,128)(2,1)S(1)}, u32[]{:S(2)}, u32[]{:S(2)}) collective-permute-start(bf16[2,2,16,1024]{3,2,1,0:T(8,128)(2,1)S(1)} %pad_maximum_fusion.refs_0_), channel_id=1, source_target_pairs={{0,128},{64,192},{128,0},{192,64},{1,129},{65,193},{129,1},{193,65... | collective-permute-start | bytes 393224 | tf_op jit(solution)/shard_map/ppermute | solution.py:511
  34.1 1.6 %copy-done = bf16[2,3,512,512]{3,2,1,0:T(8,128)(2,1)} copy-done((bf16[2,3,512,512]{3,2,1,0:T(8,128)(2,1)}, bf16[2,3,512,512]{3,2,1,0:T(8,128)(2,1)S(1)}, u32[]{:S(2)}) %copy-start) | copy-done | bytes 3145752
  35.7 4.1 %shard_map.88 = bf16[8,24,1024]{2,1,0:T(8,128)(2,1)} custom-call(bf16[16,24,512]{2,1,0:T(8,128)(2,1)S(1)} %all-to-all-done.blocks_ref.grad_ref, bf16[2,3,512,512]{3,2,1,0:T(8,128)(2,1)} %copy-done), custom_call_target="tpu_custom_call" | custom-call | flops 905969664 | bytes 7077888 | tf_op jit(solution)/shard_map/pallas_call | solution.py:41
  39.8 3.6 %all-to-all-start.1 = ((bf16[8,24,1024]{2,1,0:T(8,128)(2,1)}), bf16[8,24,1024]{2,1,0:T(8,128)(2,1)S(1)}, u32[]{:S(2)}, u32[]{:S(2)}) async-start(bf16[8,24,1024]{2,1,0:T(8,128)(2,1)} %shard_map.88), calls=%async_computation.1 | async-start | bytes 786432 | tf_op jit(solution)/shard_map/all_to_all | solution.py:266
  46.9 5.8 %all-to-all-done.1.parts_ref = bf16[8,24,1024]{2,1,0:T(8,128)(2,1)S(1)} async-done(((bf16[8,24,1024]{2,1,0:T(8,128)(2,1)}), bf16[8,24,1024]{2,1,0:T(8,128)(2,1)S(1)}, u32[]{:S(2)}, u32[]{:S(2)}) %all-to-all-start.1) | async-done | bytes 393248 | tf_op jit(solution)/shard_map/all_to_all | solution.py:266
  53.7 3.6 %all-to-all-start.2 = ((bf16[8,24,1024]{2,1,0:T(8,128)(2,1)}), bf16[8,24,1024]{2,1,0:T(8,128)(2,1)S(1)}, u32[]{:S(2)}, u32[]{:S(2)}) async-start(bf16[8,24,1024]{2,1,0:T(8,128)(2,1)} %shard_map.93), calls=%async_computation.2 | async-start | bytes 786432 | tf_op jit(solution)/shard_map/all_to_all | solution.py:266
  58.2 6.3 %collective-permute-done.10.came = bf16[8,72,128]{2,1,0:T(8,128)(2,1)S(1)} collective-permute-done((bf16[8,72,128]{2,1,0:T(8,128)(2,1)S(1)}, bf16[8,72,128]{2,1,0:T(8,128)(2,1)S(1)}, u32[]{:S(2)}, u32[]{:S(2)}) %collective-permute-start.10) | collective-permute-done | bytes 147488 | tf_op jit(solution)/shard_map/ppermute | solution.py:300
  64.6 1.7 %all-to-all-done.2.grad_ref.blocks_ref = bf16[8,24,1024]{2,1,0:T(8,128)(2,1)S(1)} async-done(((bf16[8,24,1024]{2,1,0:T(8,128)(2,1)}), bf16[8,24,1024]{2,1,0:T(8,128)(2,1)S(1)}, u32[]{:S(2)}, u32[]{:S(2)}) %all-to-all-start.2) | async-done | bytes 393248 | tf_op jit(solution)/shard_map/all_to_all | solution.py:266
  70.1 8.6 %all-to-all-start.3 = ((bf16[16,112,128]{2,1,0:T(8,128)(2,1)}), bf16[16,112,128]{2,1,0:T(8,128)(2,1)S(1)}, u32[]{:S(2)}, u32[]{:S(2)}) async-start(bf16[16,112,128]{2,1,0:T(8,128)(2,1)} %shard_map.97), calls=%async_computation.3 | async-start | bytes 917504 | tf_op jit(solution)/shard_map/all_to_all | solution.py:266
  78.7 1.6 %collective-permute-done.12.other_ref = bf16[3,3,128,128]{3,2,1,0:T(8,128)(2,1)S(1)} collective-permute-done((bf16[3,3,128,128]{3,2,1,0:T(8,128)(2,1)S(1)}, bf16[3,3,128,128]{3,2,1,0:T(8,128)(2,1)S(1)}, u32[]{:S(2)}, u32[]{:S(2)}) %collective-permute-start.12) | collective-permute-done | bytes 294944 | tf_op jit(solution)/shard_map/ppermute | solution.py:515
  80.7 2.1 %shard_map.99 = bf16[2,4,16,1024]{3,2,1,0:T(8,128)(2,1)S(1)} custom-call(bf16[8,24,1024]{2,1,0:T(8,128)(2,1)S(1)} %all-to-all-done.2.grad_ref.blocks_ref, bf16[2,3,512,512]{3,2,1,0:T(8,128)(2,1)S(1)} %shard_map.98.band_ref), custom_call_target="tpu_custom_call" | custom-call | flops 805306368 | bytes 7077888 | tf_op jit(solution)/shard_map/pallas_call | solution.py:41
  82.9 2.2 %collective-permute-start.13 = (bf16[4,16,1024]{2,1,0:T(8,128)(2,1)S(1)}, bf16[4,16,1024]{2,1,0:T(8,128)(2,1)S(1)}, u32[]{:S(2)}, u32[]{:S(2)}) collective-permute-start(bf16[4,16,1024]{2,1,0:T(8,128)(2,1)S(1)} %slice_bitcast_fusion), channel_id=1, source_target_pairs={{0,32},{32,0},{1,33},{33,1},{2,34},{34,2},{3,35},{35,3},{4,36},{36... | collective-permute-start | bytes 393224 | tf_op jit(solution)/shard_map/ppermute | solution.py:559
  85.1 7.9 %all-to-all-done.3.parts_ref = bf16[16,112,128]{2,1,0:T(8,128)(2,1)S(1)} async-done(((bf16[16,112,128]{2,1,0:T(8,128)(2,1)}), bf16[16,112,128]{2,1,0:T(8,128)(2,1)S(1)}, u32[]{:S(2)}, u32[]{:S(2)}) %all-to-all-start.3) | async-done | bytes 458784 | tf_op jit(solution)/shard_map/all_to_all | solution.py:266
  94.1 4.9 %all-to-all-start.4 = ((bf16[16,152,128]{2,1,0:T(8,128)(2,1)}), bf16[16,152,128]{2,1,0:T(8,128)(2,1)S(1)}, u32[]{:S(2)}, u32[]{:S(2)}) async-start(bf16[16,152,128]{2,1,0:T(8,128)(2,1)} %shard_map.100), calls=%async_computation.4 | async-start | bytes 1245184 | tf_op jit(solution)/shard_map/all_to_all | solution.py:266
  99.0 1.6 %collective-permute-start.16 = (bf16[16,1024]{1,0:T(8,128)(2,1)S(1)}, bf16[16,1024]{1,0:T(8,128)(2,1)S(1)}, u32[]{:S(2)}, u32[]{:S(2)}) collective-permute-start(bf16[16,1024]{1,0:T(8,128)(2,1)S(1)} %get-tuple-element.36), channel_id=1, source_target_pairs={{0,192},{64,0},{128,64},{192,128},{1,193},{65,1},{129,65},{193,129... | collective-permute-start | bytes 98312 | tf_op jit(solution)/shard_map/ppermute | solution.py:563
  103.0 3.0 %collective-permute-done.15 = bf16[16,1024]{1,0:T(8,128)(2,1)S(1)} collective-permute-done((bf16[16,1024]{1,0:T(8,128)(2,1)S(1)}, bf16[16,1024]{1,0:T(8,128)(2,1)S(1)}, u32[]{:S(2)}, u32[]{:S(2)}) %collective-permute-start.15) | collective-permute-done | bytes 32800 | tf_op jit(solution)/shard_map/ppermute | solution.py:563
  108.6 7.5 %all-to-all-done.4.whole_ref = bf16[16,152,128]{2,1,0:T(8,128)(2,1)S(1)} async-done(((bf16[16,152,128]{2,1,0:T(8,128)(2,1)}), bf16[16,152,128]{2,1,0:T(8,128)(2,1)S(1)}, u32[]{:S(2)}, u32[]{:S(2)}) %all-to-all-start.4) | async-done | bytes 622624 | tf_op jit(solution)/shard_map/all_to_all | solution.py:266
  (59 shorter events, 24.5 us)
Async XLA Ops:
  2.2 3.9 %collective-permute-start = (bf16[8,512]{1,0:T(8,128)(2,1)}, bf16[8,512]{1,0:T(8,128)(2,1)S(1)}, u32[]{:S(2)}, u32[]{:S(2)}) collective-permute-start(bf16[8,512]{1,0:T(8,128)(2,1)} %get-tuple-element.20), channel_id=1, source_target_pairs={{0,1},{1,2},{2,3},{3,4},{4,5},{5,6},{6,7},{7,8},{8,9},{9,10},{10,1... | collective-permute-start | bytes 24584 | tf_op jit(solution)/shard_map/ppermute | solution.py:478
  4.2 3.9 %collective-permute-start.1 = (bf16[8,512]{1,0:T(8,128)(2,1)}, bf16[8,512]{1,0:T(8,128)(2,1)S(1)}, u32[]{:S(2)}, u32[]{:S(2)}) collective-permute-start(bf16[8,512]{1,0:T(8,128)(2,1)} %get-tuple-element.21), channel_id=1, source_target_pairs={{1,0},{2,1},{3,2},{4,3},{5,4},{6,5},{7,6},{8,7},{9,8},{10,9},{11,1... | collective-permute-start | bytes 24584 | tf_op jit(solution)/shard_map/ppermute | solution.py:479
  9.7 26.0 %all-to-all-start = ((bf16[16,24,512]{2,1,0:T(8,128)(2,1)}), bf16[16,24,512]{2,1,0:T(8,128)(2,1)S(1)}, u32[]{:S(2)}, u32[]{:S(2)}) async-start(bf16[16,24,512]{2,1,0:T(8,128)(2,1)} %shard_map.86), calls=%async_computation | async-start | bytes 786432 | tf_op jit(solution)/shard_map/all_to_all | solution.py:266
  16.7 1.5 %collective-permute-start.2 = (bf16[16,1024]{1,0:T(8,128)(2,1)}, bf16[16,1024]{1,0:T(8,128)(2,1)S(1)}, u32[]{:S(2)}, u32[]{:S(2)}) collective-permute-start(bf16[16,1024]{1,0:T(8,128)(2,1)} %get-tuple-element.23), channel_id=1, source_target_pairs={{0,16},{16,0},{1,17},{17,1},{2,18},{18,2},{3,19},{19,3},{4,20},{20... | collective-permute-start | bytes 98312 | tf_op jit(solution)/shard_map/ppermute | solution.py:507
  17.1 15.5 %collective-permute-start.4 = (bf16[3,3,128,128]{3,2,1,0:T(8,128)(2,1)}, bf16[3,3,128,128]{3,2,1,0:T(8,128)(2,1)S(1)}, u32[]{:S(2)}, u32[]{:S(2)}) collective-permute-start(bf16[3,3,128,128]{3,2,1,0:T(8,128)(2,1)} %bitcast.45), channel_id=1, source_target_pairs={{0,16},{16,0},{1,17},{17,1},{2,18},{18,2},{3,19},{19,3},{4,20},{20... | collective-permute-start | bytes 884744 | tf_op jit(solution)/shard_map/ppermute | solution.py:514
  19.0 8.8 %collective-permute-start.3 = (bf16[2,16,1024]{2,1,0:T(8,128)(2,1)S(1)}, bf16[2,16,1024]{2,1,0:T(8,128)(2,1)S(1)}, u32[]{:S(2)}, u32[]{:S(2)}) collective-permute-start(bf16[2,16,1024]{2,1,0:T(8,128)(2,1)S(1)} %get-tuple-element.39), channel_id=1, source_target_pairs={{0,32},{32,0},{1,33},{33,1},{2,34},{34,2},{3,35},{35,3},{4,36},{36... | collective-permute-start | bytes 196616 | tf_op jit(solution)/shard_map/ppermute | solution.py:508
  27.8 15.5 %collective-permute-start.5 = (bf16[2,2,16,1024]{3,2,1,0:T(8,128)(2,1)S(1)}, bf16[2,2,16,1024]{3,2,1,0:T(8,128)(2,1)S(1)}, u32[]{:S(2)}, u32[]{:S(2)}) collective-permute-start(bf16[2,2,16,1024]{3,2,1,0:T(8,128)(2,1)S(1)} %pad_maximum_fusion.refs_0_), channel_id=1, source_target_pairs={{0,64},{64,128},{128,192},{192,0},{1,65},{65,129},{129,193},{193,1... | collective-permute-start | bytes 393224 | tf_op jit(solution)/shard_map/ppermute | solution.py:511
  28.6 14.7 %collective-permute-start.6 = (bf16[2,2,16,1024]{3,2,1,0:T(8,128)(2,1)S(1)}, bf16[2,2,16,1024]{3,2,1,0:T(8,128)(2,1)S(1)}, u32[]{:S(2)}, u32[]{:S(2)}) collective-permute-start(bf16[2,2,16,1024]{3,2,1,0:T(8,128)(2,1)S(1)} %pad_maximum_fusion.refs_0_), channel_id=1, source_target_pairs={{0,128},{64,192},{128,0},{192,64},{1,129},{65,193},{129,1},{193,65... | collective-permute-start | bytes 393224 | tf_op jit(solution)/shard_map/ppermute | solution.py:511
  31.2 12.2 %collective-permute-start.7 = (bf16[2,2,16,1024]{3,2,1,0:T(8,128)(2,1)S(1)}, bf16[2,2,16,1024]{3,2,1,0:T(8,128)(2,1)S(1)}, u32[]{:S(2)}, u32[]{:S(2)}) collective-permute-start(bf16[2,2,16,1024]{3,2,1,0:T(8,128)(2,1)S(1)} %pad_maximum_fusion.refs_0_), channel_id=1, source_target_pairs={{0,192},{64,0},{128,64},{192,128},{1,193},{65,1},{129,65},{193,129... | collective-permute-start | bytes 393224 | tf_op jit(solution)/shard_map/ppermute | solution.py:511
  39.8 13.0 %all-to-all-start.1 = ((bf16[8,24,1024]{2,1,0:T(8,128)(2,1)}), bf16[8,24,1024]{2,1,0:T(8,128)(2,1)S(1)}, u32[]{:S(2)}, u32[]{:S(2)}) async-start(bf16[8,24,1024]{2,1,0:T(8,128)(2,1)} %shard_map.88), calls=%async_computation.1 | async-start | bytes 786432 | tf_op jit(solution)/shard_map/all_to_all | solution.py:266
  44.7 2.0 %collective-permute-start.8 = (bf16[3,3,128,128]{3,2,1,0:T(8,128)(2,1)S(1)}, bf16[3,3,128,128]{3,2,1,0:T(8,128)(2,1)S(1)}, u32[]{:S(2)}, u32[]{:S(2)}) collective-permute-start(bf16[3,3,128,128]{3,2,1,0:T(8,128)(2,1)S(1)} %shard_map.90), channel_id=1, source_target_pairs={{0,16},{16,0},{1,17},{17,1},{2,18},{18,2},{3,19},{19,3},{4,20},{20... | collective-permute-start | bytes 884744 | tf_op jit(solution)/shard_map/ppermute | solution.py:247
  44.9 7.9 %collective-permute-start.9 = (bf16[24,512]{1,0:T(8,128)(2,1)S(1)}, bf16[24,512]{1,0:T(8,128)(2,1)S(1)}, u32[]{:S(2)}, u32[]{:S(2)}) collective-permute-start(bf16[24,512]{1,0:T(8,128)(2,1)S(1)} %get-tuple-element.29), channel_id=1, source_target_pairs={{0,16},{16,0},{1,17},{17,1},{2,18},{18,2},{3,19},{19,3},{4,20},{20... | collective-permute-start | bytes 73736 | tf_op jit(solution)/shard_map/ppermute | solution.py:516
  53.6 25.0 %copy-start.2 = (bf16[1,3,3,128,128]{4,3,2,1,0:T(8,128)(2,1)S(1)}, bf16[1,3,3,128,128]{4,3,2,1,0:T(8,128)(2,1)}, u32[]{:S(2)}) copy-start(bf16[1,3,3,128,128]{4,3,2,1,0:T(8,128)(2,1)} %param.10) | copy-start | bytes 884740
  53.7 12.6 %all-to-all-start.2 = ((bf16[8,24,1024]{2,1,0:T(8,128)(2,1)}), bf16[8,24,1024]{2,1,0:T(8,128)(2,1)S(1)}, u32[]{:S(2)}, u32[]{:S(2)}) async-start(bf16[8,24,1024]{2,1,0:T(8,128)(2,1)} %shard_map.93), calls=%async_computation.2 | async-start | bytes 786432 | tf_op jit(solution)/shard_map/all_to_all | solution.py:266
  57.3 7.3 %collective-permute-start.10 = (bf16[8,72,128]{2,1,0:T(8,128)(2,1)S(1)}, bf16[8,72,128]{2,1,0:T(8,128)(2,1)S(1)}, u32[]{:S(2)}, u32[]{:S(2)}) collective-permute-start(bf16[8,72,128]{2,1,0:T(8,128)(2,1)S(1)} %get-tuple-element.25), channel_id=1, source_target_pairs={{0,8},{1,9},{2,10},{3,11},{4,12},{5,13},{6,14},{7,15},{8,0},{9,1},... | collective-permute-start | bytes 442376 | tf_op jit(solution)/shard_map/ppermute | solution.py:300
  67.5 1.7 %collective-permute-start.11 = (bf16[3,3,128,128]{3,2,1,0:T(8,128)(2,1)S(1)}, bf16[3,3,128,128]{3,2,1,0:T(8,128)(2,1)S(1)}, u32[]{:S(2)}, u32[]{:S(2)}) collective-permute-start(bf16[3,3,128,128]{3,2,1,0:T(8,128)(2,1)S(1)} %shard_map.96), channel_id=1, source_target_pairs={{0,16},{16,0},{1,17},{17,1},{2,18},{18,2},{3,19},{19,3},{4,20},{20... | collective-permute-start | bytes 884744 | tf_op jit(solution)/shard_map/ppermute | solution.py:247
  70.1 23.0 %all-to-all-start.3 = ((bf16[16,112,128]{2,1,0:T(8,128)(2,1)}), bf16[16,112,128]{2,1,0:T(8,128)(2,1)S(1)}, u32[]{:S(2)}, u32[]{:S(2)}) async-start(bf16[16,112,128]{2,1,0:T(8,128)(2,1)} %shard_map.97), calls=%async_computation.3 | async-start | bytes 917504 | tf_op jit(solution)/shard_map/all_to_all | solution.py:266
  78.6 1.7 %collective-permute-start.12 = (bf16[3,3,128,128]{3,2,1,0:T(8,128)(2,1)S(1)}, bf16[3,3,128,128]{3,2,1,0:T(8,128)(2,1)S(1)}, u32[]{:S(2)}, u32[]{:S(2)}) collective-permute-start(bf16[3,3,128,128]{3,2,1,0:T(8,128)(2,1)S(1)} %bitcast.47), channel_id=1, source_target_pairs={{0,16},{16,0},{1,17},{17,1},{2,18},{18,2},{3,19},{19,3},{4,20},{20... | collective-permute-start | bytes 884744 | tf_op jit(solution)/shard_map/ppermute | solution.py:515
  82.9 16.1 %collective-permute-start.13 = (bf16[4,16,1024]{2,1,0:T(8,128)(2,1)S(1)}, bf16[4,16,1024]{2,1,0:T(8,128)(2,1)S(1)}, u32[]{:S(2)}, u32[]{:S(2)}) collective-permute-start(bf16[4,16,1024]{2,1,0:T(8,128)(2,1)S(1)} %slice_bitcast_fusion), channel_id=1, source_target_pairs={{0,32},{32,0},{1,33},{33,1},{2,34},{34,2},{3,35},{35,3},{4,36},{36... | collective-permute-start | bytes 393224 | tf_op jit(solution)/shard_map/ppermute | solution.py:559
  94.1 22.0 %all-to-all-start.4 = ((bf16[16,152,128]{2,1,0:T(8,128)(2,1)}), bf16[16,152,128]{2,1,0:T(8,128)(2,1)S(1)}, u32[]{:S(2)}, u32[]{:S(2)}) async-start(bf16[16,152,128]{2,1,0:T(8,128)(2,1)} %shard_map.100), calls=%async_computation.4 | async-start | bytes 1245184 | tf_op jit(solution)/shard_map/all_to_all | solution.py:266
  99.0 4.0 %collective-permute-start.16 = (bf16[16,1024]{1,0:T(8,128)(2,1)S(1)}, bf16[16,1024]{1,0:T(8,128)(2,1)S(1)}, u32[]{:S(2)}, u32[]{:S(2)}) collective-permute-start(bf16[16,1024]{1,0:T(8,128)(2,1)S(1)} %get-tuple-element.36), channel_id=1, source_target_pairs={{0,192},{64,0},{128,64},{192,128},{1,193},{65,1},{129,65},{193,129... | collective-permute-start | bytes 98312 | tf_op jit(solution)/shard_map/ppermute | solution.py:563
  100.6 5.4 %collective-permute-start.15 = (bf16[16,1024]{1,0:T(8,128)(2,1)S(1)}, bf16[16,1024]{1,0:T(8,128)(2,1)S(1)}, u32[]{:S(2)}, u32[]{:S(2)}) collective-permute-start(bf16[16,1024]{1,0:T(8,128)(2,1)S(1)} %get-tuple-element.37), channel_id=1, source_target_pairs={{0,128},{64,192},{128,0},{192,64},{1,129},{65,193},{129,1},{193,65... | collective-permute-start | bytes 98312 | tf_op jit(solution)/shard_map/ppermute | solution.py:563
  101.6 5.1 %collective-permute-start.14 = (bf16[16,1024]{1,0:T(8,128)(2,1)S(1)}, bf16[16,1024]{1,0:T(8,128)(2,1)S(1)}, u32[]{:S(2)}, u32[]{:S(2)}) collective-permute-start(bf16[16,1024]{1,0:T(8,128)(2,1)S(1)} %get-tuple-element.35), channel_id=1, source_target_pairs={{0,64},{64,128},{128,192},{192,0},{1,65},{65,129},{129,193},{193,1... | collective-permute-start | bytes 98312 | tf_op jit(solution)/shard_map/ppermute | solution.py:563
  106.7 1.3 %collective-permute-start.17 = (bf16[16,512]{1,0:T(8,128)(2,1)S(1)}, bf16[16,512]{1,0:T(8,128)(2,1)S(1)}, u32[]{:S(2)}, u32[]{:S(2)}) collective-permute-start(bf16[16,512]{1,0:T(8,128)(2,1)S(1)} %get-tuple-element.41), channel_id=1, source_target_pairs={{0,16},{16,0},{1,17},{17,1},{2,18},{18,2},{3,19},{19,3},{4,20},{20... | collective-permute-start | bytes 49160 | tf_op jit(solution)/shard_map/ppermute | solution.py:570
  (4 other events, 12.5 us)

commit v5 on v4

--- a/solution.py
+++ b/solution.py
@@ -37,7 +37,9 @@
 def call(kernel, out_shape, scratch, flops, *operands, space=VMEM, out_space=VMEM, room=40):
     n_bytes = sum(a.size * a.dtype.itemsize for a in operands)
     in_specs = list(space) if isinstance(space, tuple) else [space] * len(operands)
-    out_specs = jax.tree.map(lambda _: out_space, out_shape)
+    out_specs = out_space
+    if not isinstance(out_space, tuple):
+        out_specs = jax.tree.map(lambda _: out_space, out_shape)
     return pl.pallas_call(
         kernel,
         out_shape=out_shape,
@@ -57,12 +59,11 @@
         copy.wait()
 
 
-def interleave(blocks_ref, rows_ref, orients, width, shift):
-    per_block = blocks_ref.shape[2] // WIDE
+def interleave(blocks_ref, rows_ref, orients, first, shift):
     for g in range(orients):
         s = (g - shift) % orients
-        lanes = slice((s % per_block) * WIDE, (s % per_block + 1) * WIDE)
-        rows_ref[:, g, :] = blocks_ref[s // per_block, :width, lanes].astype(jnp.float32)
+        lanes = slice((s % 2) * WIDE, (s % 2 + 1) * WIDE)
+        rows_ref[:, g, :] = blocks_ref[s // 2, first:, lanes].astype(jnp.float32)
 
 
 def band_weights(filt_ref, band_ref, slot):
@@ -98,8 +99,9 @@
     ]
     for copy in copies:
         copy.start()
-    interleave(blocks_ref, rows_0, orients, in_width, 0)
-    interleave(blocks_ref, rows_1, orients, in_width, 1)
+    first = blocks_ref.shape[1] - in_width
+    interleave(blocks_ref, rows_0, orients, first, 0)
+    interleave(blocks_ref, rows_1, orients, first, 1)
     total = None
     for slot, rows in ((0, rows_0), (1, rows_1)):
         copies[slot].wait()
@@ -152,9 +154,8 @@
             ].astype(jnp.bfloat16)
 
 
-def conv(kernel, blocks, band, width, padded, out_shape, staging=(), out_space=VMEM, room=40):
-    orients = 16
-    in_width = blocks.shape[1]
+def conv(kernel, blocks, in_width, band, width, padded, out_shape, staging=(), out_space=VMEM, room=40):
+    orients = 2 * blocks.shape[0]
     return call(
         functools.partial(kernel, orients, width),
         jax.ShapeDtypeStruct(out_shape, jnp.bfloat16),
@@ -176,31 +177,28 @@
 
 
 def filter_kernel(
-    orients, width, field, first, own, grad_ref, *refs
+    orients, width, field, first, own, grad_ref, feat_ref, out_ref, feat_rows, grad_rows, held, done
 ):
-    feat_refs, (out_ref, feat_rows, grad_rows, held, done) = refs[:-5], refs[-5:]
     chip, core = here()
     slot = core if own else 1 - core
     in_width = grad_rows.shape[0]
-    lanes = pl.ds(field * WIDE, WIDE)
-    copies = []
-    for step, feat_ref in enumerate(feat_refs):
-        row = lax.rem(chip // 2 - step + len(feat_refs), len(feat_refs))
-        for y in range(2):
-            for c in range(2):
-                s = (row * 2 + (chip + y) % 2) * 2 + (core + c) % 2
-                copy = pltpu.make_async_copy(
-                    feat_ref.at[y, c, :, lanes], held.at[s], done.at[len(copies)]
-                )
-                copy.start()
-                copies.append(copy)
-    interleave(grad_ref, grad_rows, orients, in_width, 0)
+    copies = [
+        pltpu.make_async_copy(
+            feat_ref.at[:, pl.ds(field * width, width), pl.ds(half * WIDE, WIDE)],
+            held.at[:, half],
+            done.at[half],
+        )
+        for half in range(2)
+    ]
+    for copy in copies:
+        copy.start()
+    interleave(grad_ref, grad_rows, orients, grad_ref.shape[1] - in_width, 0)
     grads = grad_rows[...].reshape(in_width * orients, WIDE).astype(jnp.bfloat16)
     for copy in copies:
         copy.wait()
     for g in range(orients):
         s = lax.rem(g + 2 * chip + slot, orients)
-        feat_rows[:, g, :] = held[s].astype(jnp.float32)
+        feat_rows[:, g, :] = held[s // 2, lax.rem(s, 2)].astype(jnp.float32)
     feats = feat_rows[...].reshape(width * orients, WIDE).astype(jnp.bfloat16)
     for j in range(3):
         window = grads[(first - j) * orients : (first - j + width) * orients]
@@ -223,9 +221,8 @@
             out_ref[i, j] = total.astype(jnp.bfloat16)
 
 
-def filter_terms(feats, field, width, grads, first):
-    orients = len(feats) * 4
-    in_width = grads.shape[1]
+def filter_terms(feats, field, width, grads, in_width, first):
+    orients = 2 * feats.shape[0]
 
     def terms(own):
         return call(
@@ -234,13 +231,13 @@
             [
                 pltpu.VMEM((width, orients, WIDE), jnp.float32),
                 pltpu.VMEM((in_width, orients, WIDE), jnp.float32),
-                pltpu.VMEM((orients, width, WIDE), jnp.bfloat16),
-                pltpu.SemaphoreType.DMA((orients,)),
+                pltpu.VMEM((orients // 2, 2, width, WIDE), jnp.bfloat16),
+                pltpu.SemaphoreType.DMA((2,)),
             ],
             6 * width * orients * WIDE * WIDE,
             grads,
-            *feats,
-            space=(VMEM, *[HBM] * len(feats)),
+            feats,
+            space=(VMEM, HBM),
             room=52,
         )
 
@@ -248,17 +245,11 @@
     return terms(True), theirs
 
 
-def point_kernel(parts_ref, pre_ref, partner_ref, out_ref, held, done):
-    _, core = here()
+def point_kernel(parts_ref, pre_ref, out_ref, held, done):
     total = parts_ref[0].astype(jnp.float32)
     for n in range(1, parts_ref.shape[0]):
         total = total + parts_ref[n].astype(jnp.float32)
-    mine = slope(pre_ref[...].astype(jnp.float32))
-    partner = slope(partner_ref[...].astype(jnp.float32))
-    first = total[:, :WIDE] * jnp.where(core == 0, mine, partner)
-    second = total[:, WIDE:] * jnp.where(core == 0, partner, mine)
-    held[:, :WIDE] = first.astype(jnp.bfloat16)
-    held[:, WIDE:] = second.astype(jnp.bfloat16)
+    held[...] = (total * slope(pre_ref[...].astype(jnp.float32))).astype(jnp.bfloat16)
     copy_all([(held, out_ref.at[n]) for n in range(out_ref.shape[0])], done)
 
 
@@ -383,61 +374,66 @@
     return tuple(bank.reshape(1, 3, 3, CHAN, CHAN) for bank in banks)
 
 
+def stacked(act, given, grad, pre, side):
+    half = act.shape[0] // 2
+    zeros = jnp.zeros((8, CHAN), jnp.float32)
+    if side == 0:
+        grad = [zeros[:2], grad[: half + 2], zeros[:4]]
+        pre = [zeros[:1], pre[: half + 1], zeros[:6]]
+    else:
+        grad = [grad[half - 2 :], zeros[:6]]
+        pre = [pre[half - 1 :], zeros[:7]]
+    own = slice(side * half, (side + 1) * half)
+    return jnp.concatenate([act[own], given[own], *grad, *pre])
+
+
 def lanes_kernel(*refs):
-    given, (grad_ref, pre_ref, feats_ref, away_ref, up_ref, down_ref) = refs[:4], refs[4:10]
-    held, done = refs[10:14], refs[14]
+    given, (mine_ref, away_ref, same_ref, cross_ref) = refs[:4], refs[4:8]
+    held, done = refs[8:12], refs[12]
     _, core = here()
-    half = feats_ref.shape[0]
     copy_all(zip(given, held), done)
     inputs_ref, pre_one_ref, pre_two_ref, cotangent_ref = held
     for row in range(ROWS):
         lanes = slice(row * CHAN, (row + 1) * CHAN)
-        pre = pre_one_ref[0, row]
-        wide = pre.astype(jnp.float32)
+        pre = pre_one_ref[0, row].astype(jnp.float32)
         grad = cotangent_ref[0, row].astype(jnp.float32) * slope(
             pre_two_ref[0, row].astype(jnp.float32)
         )
-        grad = grad.astype(jnp.bfloat16)
-        grad_ref[:, lanes] = grad
-        pre_ref[:, lanes] = pre
-        act = (wide / (1.0 + jnp.exp(-wide))).astype(jnp.bfloat16)
-        for first, field in ((0, act), (WIDE, inputs_ref[0, row])):
-            low, high = field[:half], field[half:]
-            place = slice(first + row * CHAN, first + (row + 1) * CHAN)
-            feats_ref[:, place] = jnp.where(core == 0, low, high)
-            away_ref[:, place] = jnp.where(core == 0, high, low)
-        grad = grad.astype(jnp.float32)
+        act = pre / (1.0 + jnp.exp(-pre))
+        fields = (act, inputs_ref[0, row].astype(jnp.float32), grad, pre)
+        left, right = stacked(*fields, 0), stacked(*fields, 1)
+        mine_ref[:, lanes] = jnp.where(core == 0, left, right).astype(jnp.bfloat16)
+        away_ref[:, lanes] = jnp.where(core == 0, right, left).astype(jnp.bfloat16)
         pad = jnp.zeros((5, CHAN), jnp.float32)
-        up_ref[:, lanes] = jnp.concatenate([grad[-2:], wide[-1:], pad]).astype(jnp.bfloat16)
-        down_ref[:, lanes] = jnp.concatenate([grad[:2], wide[:1], pad]).astype(jnp.bfloat16)
-
-
-def rims_kernel(grad_ref, low_ref, high_ref, out_ref, grad_rim, held, done):
-    columns = grad_ref.shape[0]
-    rows = out_ref.shape[1]
-    grad_rim[:2] = low_ref[...].astype(jnp.float32)[:2]
-    grad_rim[2 : 2 + columns] = grad_ref[...].astype(jnp.float32)
-    grad_rim[2 + columns :] = jnp.zeros((grad_rim.shape[0] - 2 - columns, WIDE), jnp.float32)
-    grad_rim[2 + columns : 4 + columns] = high_ref[...].astype(jnp.float32)[:2]
-    for n in range(2):
-        first = n * columns // 2
-        held[n] = grad_rim[first : first + rows].astype(jnp.bfloat16)
-    copy_all([(held.at[n % 2], out_ref.at[n]) for n in range(out_ref.shape[0])], done)
-
-
-def pre_kernel(pre_ref, low_ref, high_ref, mine_ref, partner_ref, pre_rim):
+        low = jnp.concatenate([grad[:2], pre[:1], pad])
+        high = jnp.concatenate([grad[-2:], pre[-1:], pad])
+        same_ref[:, lanes] = jnp.where(core == 0, high, low).astype(jnp.bfloat16)
+        cross_ref[:, lanes] = jnp.where(core == 0, low, high).astype(jnp.bfloat16)
+
+
+def rims_kernel(mine_ref, partner_ref, same_ref, cross_ref, out_ref, pre_ref, held, done):
     _, core = here()
-    columns = pre_ref.shape[0]
-    half = columns // 2
-    rows = mine_ref.shape[0]
-    pre_rim[...] = jnp.zeros_like(pre_rim)
-    pre_rim[:1] = low_ref[...].astype(jnp.float32)[2:3]
-    pre_rim[1 : 1 + columns] = pre_ref[...].astype(jnp.float32)
-    pre_rim[1 + columns : 2 + columns] = high_ref[...].astype(jnp.float32)[2:3]
-    left = pre_rim[:rows].astype(jnp.bfloat16)
-    right = pre_rim[half : half + rows].astype(jnp.bfloat16)
-    mine_ref[...] = jnp.where(core == 0, left, right)
-    partner_ref[...] = jnp.where(core == 0, right, left)
+    ahead = held.shape[0] - pre_ref.shape[0]
+    rows = pre_ref.shape[0]
+    used = rows - 8
+    at = lax.broadcasted_iota(jnp.int32, (rows, WIDE), 0)
+    grad_at = jnp.where(core == 0, 0, used + 2)
+    pre_at = jnp.where(core == 0, 0, used + 1)
+    filled = []
+    for body_ref, edge_ref in ((mine_ref, same_ref), (partner_ref, cross_ref)):
+        body = body_ref[...].astype(jnp.float32)
+        edge = edge_ref[...].astype(jnp.float32)
+        grad = body[ahead : ahead + rows]
+        grad = jnp.where(at == grad_at, edge[0:1], grad)
+        grad = jnp.where(at == grad_at + 1, edge[1:2], grad)
+        pre = jnp.where(at == pre_at, edge[2:3], body[ahead + rows :])
+        filled.append(jnp.concatenate([body[:ahead], grad, pre]).astype(jnp.bfloat16))
+    first = jnp.where(core == 0, filled[0], filled[1])
+    second = jnp.where(core == 0, filled[1], filled[0])
+    for lanes, part in ((slice(0, WIDE), first), (slice(WIDE, 2 * WIDE), second)):
+        held[:, lanes] = part[: ahead + rows]
+        pre_ref[:, lanes] = part[ahead + rows :]
+    copy_all([(held, out_ref.at[n]) for n in range(out_ref.shape[0])], done)
 
 
 def shards(inputs, pre_one, pre_two, cotangent, filt_one, filt_two):
@@ -454,16 +450,10 @@
     def narrow(*shape):
         return jax.ShapeDtypeStruct(shape, jnp.bfloat16)
 
-    grad_two, pre, feats, feats_away, up, down = call(
+    rows = columns + 2 * padded
+    mine, away, same, cross = call(
         lanes_kernel,
-        (
-            narrow(columns, WIDE),
-            narrow(columns, WIDE),
-            narrow(half, 2 * WIDE),
-            narrow(half, 2 * WIDE),
-            narrow(8, WIDE),
-            narrow(8, WIDE),
-        ),
+        (narrow(rows, WIDE), narrow(rows, WIDE), narrow(8, WIDE), narrow(8, WIDE)),
         [pltpu.VMEM(inputs.shape, jnp.bfloat16)] * 4 + [pltpu.SemaphoreType.DMA((4,))],
         inputs.size * 20,
         inputs,
@@ -473,53 +463,37 @@
         space=HBM,
         room=60,
     )
-    forward = [(i, (i + 1) % az_count) for i in range(az_count)]
-    backward = [(target, source) for source, target in forward]
-    low = lax.ppermute(up, AZ, forward)
-    high = lax.ppermute(down, AZ, backward)
-    rim = pltpu.VMEM((columns + 8, WIDE), jnp.float32)
-    sent = call(
+    after_me = [(i, (i + 1) % az_count) for i in range(az_count)]
+    before_me = [(i, (i - 1) % az_count) for i in range(az_count)]
+    place = lambda c, pairs, d: [(c * az_count + i, d * az_count + j) for i, j in pairs]
+    same = lax.ppermute(same, (CORE, AZ), place(0, after_me, 0) + place(1, before_me, 1))
+    cross = lax.ppermute(cross, (CORE, AZ), place(1, after_me, 0) + place(0, before_me, 1))
+    partner = lax.ppermute(away, CORE, SWAP)
+    sent, pre_pair = call(
         rims_kernel,
-        narrow(rot_count, padded, WIDE),
+        (narrow(chips, columns + padded, 2 * WIDE), narrow(padded, 2 * WIDE)),
         [
-            rim,
-            pltpu.VMEM((2, padded, WIDE), jnp.bfloat16),
-            pltpu.SemaphoreType.DMA((rot_count,)),
+            pltpu.VMEM((columns + padded, 2 * WIDE), jnp.bfloat16),
+            pltpu.SemaphoreType.DMA((chips,)),
         ],
         inputs.size * 20,
-        grad_two,
-        low,
-        high,
-        out_space=HBM,
-    )
-    all_grad_two = exchange(sent, ROT)
-
-    pre_here, pre_away = call(
-        pre_kernel,
-        (narrow(padded, WIDE), narrow(padded, WIDE)),
-        [rim],
-        inputs.size,
-        pre,
-        low,
-        high,
-    )
-
-    pair = jnp.stack([feats, lax.ppermute(feats_away, CORE, SWAP)])
-    chip_pair = jnp.stack([pair, lax.ppermute(pair, CHIPS[1], SWAP)])
-    along_x = lax.axis_size(CHIPS[0])
-    all_feats = [chip_pair] + [
-        lax.ppermute(chip_pair, CHIPS[0], [(i, (i + step) % along_x) for i in range(along_x)])
-        for step in range(1, along_x)
-    ]
+        mine,
+        partner,
+        same,
+        cross,
+        out_space=(HBM, VMEM),
+    )
+    first_blocks = exchange(sent, CHIPS)
+
     other_two = lax.ppermute(filt_two[0], CORE, SWAP)
     other_one = lax.ppermute(filt_one[0], CORE, SWAP)
-    pre_partner = lax.ppermute(pre_away, CORE, SWAP)
     bands_two = bands(filt_two[0], other_two)
     bands_one = bands(filt_one[0], other_one)
 
     shares = conv(
         conv_two_kernel,
-        after(all_grad_two, chip_pair),
+        first_blocks,
+        padded,
         bands_two,
         half + 2,
         padded,
@@ -531,7 +505,7 @@
         HBM,
         52,
     )
-    pair_two = filter_terms(all_feats, 0, half, all_grad_two, 3)
+    pair_two = filter_terms(first_blocks, 0, half, first_blocks, padded, 3)
     leave, terms_two = half_terms(pair_two)
     arrived = after(exchange(shares, CHIPS), leave)
     copies = call(
@@ -540,17 +514,19 @@
         [pltpu.VMEM((padded, 2 * WIDE), jnp.bfloat16), pltpu.SemaphoreType.DMA((chips,))],
         arrived.size,
         arrived,
-        pre_here,
-        pre_partner,
+        pre_pair,
         out_space=HBM,
     )
     all_grad_one = after(exchange(copies, CHIPS), terms_two)
-    joined = joined_terms(filter_terms(all_feats, 1, half, all_grad_one, 2), terms_two)
+    joined = joined_terms(filter_terms(first_blocks, 1, half, all_grad_one, padded, 2), terms_two)
     filt_grad_one, filt_grad_two = summed_over_az(joined, filt_one.size // CHAN // az_count, scale)
+
+    along_x = lax.axis_size(CHIPS[0])
 
     shares = conv(
         conv_one_kernel,
         after(all_grad_one, joined),
+        padded,
         bands_one,
         half,
         half,

time: 118 us -> 116 us (0.983)
  starting transfers between devices: 46.1 us -> 42.7 us
  waiting for transfers between devices: 46.5 us -> 49.5 us
    ppermute x8 -> x3, waiting for transfers between devices: 10 us -> 1.58 us  [the longest x1 1.57 us: shards(): lax.ppermute(cross, (CORE, AZ), place(1, after_me, 0) + place(0, before_m...]
    all_to_all x5, waiting for transfers between devices: 22.9 us -> 31 us  [exchange(): return lax.all_to_all(parts, axes, 0, 0, tiled=True)]
    ppermute x8 -> x3, starting transfers between devices: 11.4 us -> 6.89 us  [the longest x1 4.8 us: shards(): lax.ppermute(cross, (CORE, AZ), place(1, after_me, 0) + place(0, before_m...]
    ppermute x1, waiting for transfers between devices: 0.01 us -> 1.78 us  [shards(): other_two = lax.ppermute(filt_two[0], CORE, SWAP)]
    all_to_all x5, starting transfers between devices: 27.6 us -> 29 us  [exchange(): return lax.all_to_all(parts, axes, 0, 0, tiled=True)]
    pallas_call x17 -> x16, Pallas kernels: 18.8 us -> 17.9 us  [call(): pl.pallas_call(kernel, out_shape=out_shape, in_specs=in_specs, out_specs=...]
    unnamed x10 -> x8, local copies, waits for them, and re-layouts: 3.35 us -> 3.48 us
  transfers between devices with their start and end apart: 23 -> 18, of which waited for: 15 -> 15; matrix products, arithmetic and copies ran while one was open for 1% -> 1% of each run, Pallas kernels for 10% -> 6%
where the time goes in v5:
time: 116 us; the launch traced here: 115 us
  waiting for transfers between devices  49.5 us (43%)
  starting transfers between devices  42.7 us (37%)
  Pallas kernels  17.9 us (15%)
  local copies, waits for them, and re-layouts  3.51 us (3%)
    all_to_all x5, waiting for transfers between devices, exchange(): return lax.all_to_all(parts, axes, 0, 0, tiled=True)  31 us
    all_to_all x5, starting transfers between devices, exchange(): return lax.all_to_all(parts, axes, 0, 0, tiled=True)  29 us
    pallas_call x16, Pallas kernels, call(): pl.pallas_call(kernel, out_shape=out_shape, in_specs=in_specs, out_specs=...  17.9 us
    ppermute x1, waiting for transfers between devices, half_terms(): lax.ppermute(leave, AZ, [(i, (i + count // 2) % count) for i in range(cou...  6.65 us
    ppermute x1, starting transfers between devices, shards(): lax.ppermute(cross, (CORE, AZ), place(1, after_me, 0) + place(0, before_m...  4.8 us
    ppermute x3, waiting for transfers between devices, shards(): lax.ppermute(partial[step], CHIPS[0], [(i, (i + step) % along_x) for i in...  4.76 us
    unnamed x8, local copies, waits for them, and re-layouts  3.48 us
    ppermute x3, starting transfers between devices, shards(): lax.ppermute(partial[step], CHIPS[0], [(i, (i + step) % along_x) for i in...  3.2 us
  transfers between devices with their start and end apart: 18, of which 15 were waited for; matrix products, arithmetic and copies ran while one was open for 1% of the time, Pallas kernels for 6%

profile of v5, /device:TPU:32, one launch (start us, length us, event | category | flops | bytes accessed | tf_op | source)
XLA Modules:
  0.0 115.3 jit_solution(13848114695881460824)
XLA Ops:
  0.6 1.6 %shard_map.85 = (bf16[80,512]{1,0:T(8,128)(2,1)}, bf16[80,512]{1,0:T(8,128)(2,1)}, bf16[8,512]{1,0:T(8,128)(2,1)}, bf16[8,512]{1,0:T(8,128)(2,1)}) custom-call(bf16[1,4,32,128]{3,2,1,0:T(8,128)(2,1)} %refs_0_.1, bf16[1,4,32,128]{3,2,1,0:T(8,128)(2,1)} %refs_1_.1, bf16[1,4,32,128]{3,2,1,0:T(8,128)(2,1)} %refs_2_.1, bf16[1,4,32,128]{3,2,1,0:T(8,128)(2,1)} %refs_3_.1), custom_call_target="tpu_custom_call" | custom-call | flops 327680 | bytes 262144 | tf_op jit(solution)/shard_map/pallas_call | solution.py:43
  2.3 2.0 %collective-permute-start.1 = (bf16[8,512]{1,0:T(8,128)(2,1)}, bf16[8,512]{1,0:T(8,128)(2,1)S(1)}, u32[]{:S(2)}, u32[]{:S(2)}) collective-permute-start(bf16[8,512]{1,0:T(8,128)(2,1)} %get-tuple-element.18), channel_id=1, source_target_pairs={{0,1},{1,2},{2,3},{3,4},{4,5},{5,6},{6,7},{7,8},{8,9},{9,10},{10,1... | collective-permute-start | bytes 24584 | tf_op jit(solution)/shard_map/ppermute | solution.py:469
  4.3 4.8 %collective-permute-start.2 = (bf16[8,512]{1,0:T(8,128)(2,1)}, bf16[8,512]{1,0:T(8,128)(2,1)S(1)}, u32[]{:S(2)}, u32[]{:S(2)}) collective-permute-start(bf16[8,512]{1,0:T(8,128)(2,1)} %get-tuple-element.19), channel_id=1, source_target_pairs={{16,1},{17,2},{18,3},{19,4},{20,5},{21,6},{22,7},{23,8},{24,9},{25... | collective-permute-start | bytes 24584 | tf_op jit(solution)/shard_map/ppermute | solution.py:470
  9.1 1.6 %collective-permute-done.2.cross_ref = bf16[8,512]{1,0:T(8,128)(2,1)S(1)} collective-permute-done((bf16[8,512]{1,0:T(8,128)(2,1)}, bf16[8,512]{1,0:T(8,128)(2,1)S(1)}, u32[]{:S(2)}, u32[]{:S(2)}) %collective-permute-start.2) | collective-permute-done | bytes 8224 | tf_op jit(solution)/shard_map/ppermute | solution.py:470
  12.6 6.6 %all-to-all-start = ((bf16[8,56,1024]{2,1,0:T(8,128)(2,1)}), bf16[8,56,1024]{2,1,0:T(8,128)(2,1)S(1)}, u32[]{:S(2)}, u32[]{:S(2)}) async-start(bf16[8,56,1024]{2,1,0:T(8,128)(2,1)} %get-tuple-element.20), calls=%async_computation | async-start | bytes 1835008 | tf_op jit(solution)/shard_map/all_to_all | solution.py:257
  19.3 1.8 %collective-permute-done.3.other_ref = bf16[3,3,128,128]{3,2,1,0:T(8,128)(2,1)S(1)} collective-permute-done((bf16[3,3,128,128]{3,2,1,0:T(8,128)(2,1)}, bf16[3,3,128,128]{3,2,1,0:T(8,128)(2,1)S(1)}, u32[]{:S(2)}, u32[]{:S(2)}) %collective-permute-start.3) | collective-permute-done | bytes 294944 | tf_op jit(solution)/shard_map/ppermute | solution.py:488
  22.5 1.6 %copy-done = bf16[2,3,512,512]{3,2,1,0:T(8,128)(2,1)} copy-done((bf16[2,3,512,512]{3,2,1,0:T(8,128)(2,1)}, bf16[2,3,512,512]{3,2,1,0:T(8,128)(2,1)S(1)}, u32[]{:S(2)}) %copy-start) | copy-done | bytes 3145752
  24.1 7.9 %all-to-all-done.blocks_ref.grad_ref.feat_ref = bf16[8,56,1024]{2,1,0:T(8,128)(2,1)S(1)} async-done(((bf16[8,56,1024]{2,1,0:T(8,128)(2,1)}), bf16[8,56,1024]{2,1,0:T(8,128)(2,1)S(1)}, u32[]{:S(2)}, u32[]{:S(2)}) %all-to-all-start) | async-done | bytes 917536 | tf_op jit(solution)/shard_map/all_to_all | solution.py:257
  32.0 4.1 %shard_map.88 = bf16[8,24,1024]{2,1,0:T(8,128)(2,1)} custom-call(bf16[8,56,1024]{2,1,0:T(8,128)(2,1)S(1)} %all-to-all-done.blocks_ref.grad_ref.feat_ref, bf16[2,3,512,512]{3,2,1,0:T(8,128)(2,1)} %copy-done), custom_call_target="tpu_custom_call" | custom-call | flops 905969664 | bytes 8126464 | tf_op jit(solution)/shard_map/pallas_call | solution.py:43
  36.0 3.9 %all-to-all-start.1 = ((bf16[8,24,1024]{2,1,0:T(8,128)(2,1)}), bf16[8,24,1024]{2,1,0:T(8,128)(2,1)S(1)}, u32[]{:S(2)}, u32[]{:S(2)}) async-start(bf16[8,24,1024]{2,1,0:T(8,128)(2,1)} %shard_map.88), calls=%async_computation.1 | async-start | bytes 786432 | tf_op jit(solution)/shard_map/all_to_all | solution.py:257
  42.8 6.3 %all-to-all-done.1.parts_ref = bf16[8,24,1024]{2,1,0:T(8,128)(2,1)S(1)} async-done(((bf16[8,24,1024]{2,1,0:T(8,128)(2,1)}), bf16[8,24,1024]{2,1,0:T(8,128)(2,1)S(1)}, u32[]{:S(2)}, u32[]{:S(2)}) %all-to-all-start.1) | async-done | bytes 393248 | tf_op jit(solution)/shard_map/all_to_all | solution.py:257
  50.0 3.6 %all-to-all-start.2 = ((bf16[8,24,1024]{2,1,0:T(8,128)(2,1)}), bf16[8,24,1024]{2,1,0:T(8,128)(2,1)S(1)}, u32[]{:S(2)}, u32[]{:S(2)}) async-start(bf16[8,24,1024]{2,1,0:T(8,128)(2,1)} %shard_map.92), calls=%async_computation.2 | async-start | bytes 786432 | tf_op jit(solution)/shard_map/all_to_all | solution.py:257
  54.3 6.7 %collective-permute-done.5.came = bf16[8,72,128]{2,1,0:T(8,128)(2,1)S(1)} collective-permute-done((bf16[8,72,128]{2,1,0:T(8,128)(2,1)S(1)}, bf16[8,72,128]{2,1,0:T(8,128)(2,1)S(1)}, u32[]{:S(2)}, u32[]{:S(2)}) %collective-permute-start.5) | collective-permute-done | bytes 147488 | tf_op jit(solution)/shard_map/ppermute | solution.py:291
  61.0 1.5 %all-to-all-done.2.grad_ref.blocks_ref = bf16[8,24,1024]{2,1,0:T(8,128)(2,1)S(1)} async-done(((bf16[8,24,1024]{2,1,0:T(8,128)(2,1)}), bf16[8,24,1024]{2,1,0:T(8,128)(2,1)S(1)}, u32[]{:S(2)}, u32[]{:S(2)}) %all-to-all-start.2) | async-done | bytes 393248 | tf_op jit(solution)/shard_map/all_to_all | solution.py:257
  66.1 9.9 %all-to-all-start.3 = ((bf16[16,112,128]{2,1,0:T(8,128)(2,1)}), bf16[16,112,128]{2,1,0:T(8,128)(2,1)S(1)}, u32[]{:S(2)}, u32[]{:S(2)}) async-start(bf16[16,112,128]{2,1,0:T(8,128)(2,1)} %shard_map.96), calls=%async_computation.3 | async-start | bytes 917504 | tf_op jit(solution)/shard_map/all_to_all | solution.py:257
  76.4 1.6 %collective-permute-done.7.other_ref = bf16[3,3,128,128]{3,2,1,0:T(8,128)(2,1)S(1)} collective-permute-done((bf16[3,3,128,128]{3,2,1,0:T(8,128)(2,1)S(1)}, bf16[3,3,128,128]{3,2,1,0:T(8,128)(2,1)S(1)}, u32[]{:S(2)}, u32[]{:S(2)}) %collective-permute-start.7) | collective-permute-done | bytes 294944 | tf_op jit(solution)/shard_map/ppermute | solution.py:489
  78.3 2.1 %shard_map.98 = bf16[2,4,16,1024]{3,2,1,0:T(8,128)(2,1)S(1)} custom-call(bf16[8,24,1024]{2,1,0:T(8,128)(2,1)S(1)} %all-to-all-done.2.grad_ref.blocks_ref, bf16[2,3,512,512]{3,2,1,0:T(8,128)(2,1)S(1)} %shard_map.97.band_ref), custom_call_target="tpu_custom_call" | custom-call | flops 805306368 | bytes 7077888 | tf_op jit(solution)/shard_map/pallas_call | solution.py:43
  80.5 2.3 %collective-permute-start.8 = (bf16[4,16,1024]{2,1,0:T(8,128)(2,1)S(1)}, bf16[4,16,1024]{2,1,0:T(8,128)(2,1)S(1)}, u32[]{:S(2)}, u32[]{:S(2)}) collective-permute-start(bf16[4,16,1024]{2,1,0:T(8,128)(2,1)S(1)} %slice_bitcast_fusion), channel_id=1, source_target_pairs={{0,32},{32,0},{1,33},{33,1},{2,34},{34,2},{3,35},{35,3},{4,36},{36... | collective-permute-start | bytes 393224 | tf_op jit(solution)/shard_map/ppermute | solution.py:535
  82.8 7.8 %all-to-all-done.3.parts_ref = bf16[16,112,128]{2,1,0:T(8,128)(2,1)S(1)} async-done(((bf16[16,112,128]{2,1,0:T(8,128)(2,1)}), bf16[16,112,128]{2,1,0:T(8,128)(2,1)S(1)}, u32[]{:S(2)}, u32[]{:S(2)}) %all-to-all-start.3) | async-done | bytes 458784 | tf_op jit(solution)/shard_map/all_to_all | solution.py:257
  91.7 4.9 %all-to-all-start.4 = ((bf16[16,152,128]{2,1,0:T(8,128)(2,1)}), bf16[16,152,128]{2,1,0:T(8,128)(2,1)S(1)}, u32[]{:S(2)}, u32[]{:S(2)}) async-start(bf16[16,152,128]{2,1,0:T(8,128)(2,1)} %shard_map.99), calls=%async_computation.4 | async-start | bytes 1245184 | tf_op jit(solution)/shard_map/all_to_all | solution.py:257
  96.7 1.5 %collective-permute-start.11 = (bf16[16,1024]{1,0:T(8,128)(2,1)S(1)}, bf16[16,1024]{1,0:T(8,128)(2,1)S(1)}, u32[]{:S(2)}, u32[]{:S(2)}) collective-permute-start(bf16[16,1024]{1,0:T(8,128)(2,1)S(1)} %get-tuple-element.30), channel_id=1, source_target_pairs={{0,192},{64,0},{128,64},{192,128},{1,193},{65,1},{129,65},{193,129... | collective-permute-start | bytes 98312 | tf_op jit(solution)/shard_map/ppermute | solution.py:539
  98.2 1.4 %collective-permute-start.10 = (bf16[16,1024]{1,0:T(8,128)(2,1)S(1)}, bf16[16,1024]{1,0:T(8,128)(2,1)S(1)}, u32[]{:S(2)}, u32[]{:S(2)}) collective-permute-start(bf16[16,1024]{1,0:T(8,128)(2,1)S(1)} %get-tuple-element.31), channel_id=1, source_target_pairs={{0,128},{64,192},{128,0},{192,64},{1,129},{65,193},{129,1},{193,65... | collective-permute-start | bytes 98312 | tf_op jit(solution)/shard_map/ppermute | solution.py:539
  100.7 2.9 %collective-permute-done.10 = bf16[16,1024]{1,0:T(8,128)(2,1)S(1)} collective-permute-done((bf16[16,1024]{1,0:T(8,128)(2,1)S(1)}, bf16[16,1024]{1,0:T(8,128)(2,1)S(1)}, u32[]{:S(2)}, u32[]{:S(2)}) %collective-permute-start.10) | collective-permute-done | bytes 32800 | tf_op jit(solution)/shard_map/ppermute | solution.py:539
  106.6 7.5 %all-to-all-done.4.whole_ref = bf16[16,152,128]{2,1,0:T(8,128)(2,1)S(1)} async-done(((bf16[16,152,128]{2,1,0:T(8,128)(2,1)}), bf16[16,152,128]{2,1,0:T(8,128)(2,1)S(1)}, u32[]{:S(2)}, u32[]{:S(2)}) %all-to-all-start.4) | async-done | bytes 622624 | tf_op jit(solution)/shard_map/all_to_all | solution.py:257
  (44 shorter events, 18.5 us)
Async XLA Ops:
  2.2 8.5 %collective-permute-start = (bf16[80,512]{1,0:T(8,128)(2,1)}, bf16[80,512]{1,0:T(8,128)(2,1)S(1)}, u32[]{:S(2)}, u32[]{:S(2)}) collective-permute-start(bf16[80,512]{1,0:T(8,128)(2,1)} %get-tuple-element.17), channel_id=1, source_target_pairs={{0,16},{16,0},{1,17},{17,1},{2,18},{18,2},{3,19},{19,3},{4,20},{20... | collective-permute-start | bytes 245768 | tf_op jit(solution)/shard_map/ppermute | solution.py:471
  2.3 6.8 %collective-permute-start.1 = (bf16[8,512]{1,0:T(8,128)(2,1)}, bf16[8,512]{1,0:T(8,128)(2,1)S(1)}, u32[]{:S(2)}, u32[]{:S(2)}) collective-permute-start(bf16[8,512]{1,0:T(8,128)(2,1)} %get-tuple-element.18), channel_id=1, source_target_pairs={{0,1},{1,2},{2,3},{3,4},{4,5},{5,6},{6,7},{7,8},{8,9},{9,10},{10,1... | collective-permute-start | bytes 24584 | tf_op jit(solution)/shard_map/ppermute | solution.py:469
  4.3 6.4 %collective-permute-start.2 = (bf16[8,512]{1,0:T(8,128)(2,1)}, bf16[8,512]{1,0:T(8,128)(2,1)S(1)}, u32[]{:S(2)}, u32[]{:S(2)}) collective-permute-start(bf16[8,512]{1,0:T(8,128)(2,1)} %get-tuple-element.19), channel_id=1, source_target_pairs={{16,1},{17,2},{18,3},{19,4},{20,5},{21,6},{22,7},{23,8},{24,9},{25... | collective-permute-start | bytes 24584 | tf_op jit(solution)/shard_map/ppermute | solution.py:470
  10.7 0.9 copy-start.3
  12.6 19.3 %all-to-all-start = ((bf16[8,56,1024]{2,1,0:T(8,128)(2,1)}), bf16[8,56,1024]{2,1,0:T(8,128)(2,1)S(1)}, u32[]{:S(2)}, u32[]{:S(2)}) async-start(bf16[8,56,1024]{2,1,0:T(8,128)(2,1)} %get-tuple-element.20), calls=%async_computation | async-start | bytes 1835008 | tf_op jit(solution)/shard_map/all_to_all | solution.py:257
  19.3 1.8 %collective-permute-start.3 = (bf16[3,3,128,128]{3,2,1,0:T(8,128)(2,1)}, bf16[3,3,128,128]{3,2,1,0:T(8,128)(2,1)S(1)}, u32[]{:S(2)}, u32[]{:S(2)}) collective-permute-start(bf16[3,3,128,128]{3,2,1,0:T(8,128)(2,1)} %bitcast.42), channel_id=1, source_target_pairs={{0,16},{16,0},{1,17},{17,1},{2,18},{18,2},{3,19},{19,3},{4,20},{20... | collective-permute-start | bytes 884744 | tf_op jit(solution)/shard_map/ppermute | solution.py:488
  21.1 1.0 copy-start.1
  22.5 1.6 %copy-start = (bf16[2,3,512,512]{3,2,1,0:T(8,128)(2,1)}, bf16[2,3,512,512]{3,2,1,0:T(8,128)(2,1)S(1)}, u32[]{:S(2)}) copy-start(bf16[2,3,512,512]{3,2,1,0:T(8,128)(2,1)S(1)} %shard_map.87.band_ref) | copy-start | bytes 9437188
  36.0 13.0 %all-to-all-start.1 = ((bf16[8,24,1024]{2,1,0:T(8,128)(2,1)}), bf16[8,24,1024]{2,1,0:T(8,128)(2,1)S(1)}, u32[]{:S(2)}, u32[]{:S(2)}) async-start(bf16[8,24,1024]{2,1,0:T(8,128)(2,1)} %shard_map.88), calls=%async_computation.1 | async-start | bytes 786432 | tf_op jit(solution)/shard_map/all_to_all | solution.py:257
  41.0 1.7 %collective-permute-start.4 = (bf16[3,3,128,128]{3,2,1,0:T(8,128)(2,1)S(1)}, bf16[3,3,128,128]{3,2,1,0:T(8,128)(2,1)S(1)}, u32[]{:S(2)}, u32[]{:S(2)}) collective-permute-start(bf16[3,3,128,128]{3,2,1,0:T(8,128)(2,1)S(1)} %shard_map.90), channel_id=1, source_target_pairs={{0,16},{16,0},{1,17},{17,1},{2,18},{18,2},{3,19},{19,3},{4,20},{20... | collective-permute-start | bytes 884744 | tf_op jit(solution)/shard_map/ppermute | solution.py:244
  50.0 26.1 %copy-start.2 = (bf16[1,3,3,128,128]{4,3,2,1,0:T(8,128)(2,1)S(1)}, bf16[1,3,3,128,128]{4,3,2,1,0:T(8,128)(2,1)}, u32[]{:S(2)}) copy-start(bf16[1,3,3,128,128]{4,3,2,1,0:T(8,128)(2,1)} %param.10) | copy-start | bytes 884740
  50.0 12.6 %all-to-all-start.2 = ((bf16[8,24,1024]{2,1,0:T(8,128)(2,1)}), bf16[8,24,1024]{2,1,0:T(8,128)(2,1)S(1)}, u32[]{:S(2)}, u32[]{:S(2)}) async-start(bf16[8,24,1024]{2,1,0:T(8,128)(2,1)} %shard_map.92), calls=%async_computation.2 | async-start | bytes 786432 | tf_op jit(solution)/shard_map/all_to_all | solution.py:257
  53.6 7.4 %collective-permute-start.5 = (bf16[8,72,128]{2,1,0:T(8,128)(2,1)S(1)}, bf16[8,72,128]{2,1,0:T(8,128)(2,1)S(1)}, u32[]{:S(2)}, u32[]{:S(2)}) collective-permute-start(bf16[8,72,128]{2,1,0:T(8,128)(2,1)S(1)} %get-tuple-element.21), channel_id=1, source_target_pairs={{0,8},{1,9},{2,10},{3,11},{4,12},{5,13},{6,14},{7,15},{8,0},{9,1},... | collective-permute-start | bytes 442376 | tf_op jit(solution)/shard_map/ppermute | solution.py:291
  63.6 1.7 %collective-permute-start.6 = (bf16[3,3,128,128]{3,2,1,0:T(8,128)(2,1)S(1)}, bf16[3,3,128,128]{3,2,1,0:T(8,128)(2,1)S(1)}, u32[]{:S(2)}, u32[]{:S(2)}) collective-permute-start(bf16[3,3,128,128]{3,2,1,0:T(8,128)(2,1)S(1)} %shard_map.95), channel_id=1, source_target_pairs={{0,16},{16,0},{1,17},{17,1},{2,18},{18,2},{3,19},{19,3},{4,20},{20... | collective-permute-start | bytes 884744 | tf_op jit(solution)/shard_map/ppermute | solution.py:244
  66.1 24.6 %all-to-all-start.3 = ((bf16[16,112,128]{2,1,0:T(8,128)(2,1)}), bf16[16,112,128]{2,1,0:T(8,128)(2,1)S(1)}, u32[]{:S(2)}, u32[]{:S(2)}) async-start(bf16[16,112,128]{2,1,0:T(8,128)(2,1)} %shard_map.96), calls=%async_computation.3 | async-start | bytes 917504 | tf_op jit(solution)/shard_map/all_to_all | solution.py:257
  76.1 1.9 %collective-permute-start.7 = (bf16[3,3,128,128]{3,2,1,0:T(8,128)(2,1)S(1)}, bf16[3,3,128,128]{3,2,1,0:T(8,128)(2,1)S(1)}, u32[]{:S(2)}, u32[]{:S(2)}) collective-permute-start(bf16[3,3,128,128]{3,2,1,0:T(8,128)(2,1)S(1)} %bitcast.44), channel_id=1, source_target_pairs={{0,16},{16,0},{1,17},{17,1},{2,18},{18,2},{3,19},{19,3},{4,20},{20... | collective-permute-start | bytes 884744 | tf_op jit(solution)/shard_map/ppermute | solution.py:489
  80.5 16.1 %collective-permute-start.8 = (bf16[4,16,1024]{2,1,0:T(8,128)(2,1)S(1)}, bf16[4,16,1024]{2,1,0:T(8,128)(2,1)S(1)}, u32[]{:S(2)}, u32[]{:S(2)}) collective-permute-start(bf16[4,16,1024]{2,1,0:T(8,128)(2,1)S(1)} %slice_bitcast_fusion), channel_id=1, source_target_pairs={{0,32},{32,0},{1,33},{33,1},{2,34},{34,2},{3,35},{35,3},{4,36},{36... | collective-permute-start | bytes 393224 | tf_op jit(solution)/shard_map/ppermute | solution.py:535
  91.7 22.4 %all-to-all-start.4 = ((bf16[16,152,128]{2,1,0:T(8,128)(2,1)}), bf16[16,152,128]{2,1,0:T(8,128)(2,1)S(1)}, u32[]{:S(2)}, u32[]{:S(2)}) async-start(bf16[16,152,128]{2,1,0:T(8,128)(2,1)} %shard_map.99), calls=%async_computation.4 | async-start | bytes 1245184 | tf_op jit(solution)/shard_map/all_to_all | solution.py:257
  96.7 4.0 %collective-permute-start.11 = (bf16[16,1024]{1,0:T(8,128)(2,1)S(1)}, bf16[16,1024]{1,0:T(8,128)(2,1)S(1)}, u32[]{:S(2)}, u32[]{:S(2)}) collective-permute-start(bf16[16,1024]{1,0:T(8,128)(2,1)S(1)} %get-tuple-element.30), channel_id=1, source_target_pairs={{0,192},{64,0},{128,64},{192,128},{1,193},{65,1},{129,65},{193,129... | collective-permute-start | bytes 98312 | tf_op jit(solution)/shard_map/ppermute | solution.py:539
  98.2 5.4 %collective-permute-start.10 = (bf16[16,1024]{1,0:T(8,128)(2,1)S(1)}, bf16[16,1024]{1,0:T(8,128)(2,1)S(1)}, u32[]{:S(2)}, u32[]{:S(2)}) collective-permute-start(bf16[16,1024]{1,0:T(8,128)(2,1)S(1)} %get-tuple-element.31), channel_id=1, source_target_pairs={{0,128},{64,192},{128,0},{192,64},{1,129},{65,193},{129,1},{193,65... | collective-permute-start | bytes 98312 | tf_op jit(solution)/shard_map/ppermute | solution.py:539
  99.5 5.1 %collective-permute-start.9 = (bf16[16,1024]{1,0:T(8,128)(2,1)S(1)}, bf16[16,1024]{1,0:T(8,128)(2,1)S(1)}, u32[]{:S(2)}, u32[]{:S(2)}) collective-permute-start(bf16[16,1024]{1,0:T(8,128)(2,1)S(1)} %get-tuple-element.29), channel_id=1, source_target_pairs={{0,64},{64,128},{128,192},{192,0},{1,65},{65,129},{129,193},{193,1... | collective-permute-start | bytes 98312 | tf_op jit(solution)/shard_map/ppermute | solution.py:539
  104.7 1.3 %collective-permute-start.12 = (bf16[16,512]{1,0:T(8,128)(2,1)S(1)}, bf16[16,512]{1,0:T(8,128)(2,1)S(1)}, u32[]{:S(2)}, u32[]{:S(2)}) collective-permute-start(bf16[16,512]{1,0:T(8,128)(2,1)S(1)} %get-tuple-element.33), channel_id=1, source_target_pairs={{0,16},{16,0},{1,17},{17,1},{2,18},{18,2},{3,19},{19,3},{4,20},{20... | collective-permute-start | bytes 49160 | tf_op jit(solution)/shard_map/ppermute | solution.py:546

commit v6 on v5

--- a/solution.py
+++ b/solution.py
@@ -81,30 +81,16 @@
                 ] = piece
 
 
-def bands_kernel(mine_ref, other_ref, band_ref):
+def rotation_sums(orients, width, blocks_ref, mine_ref, other_ref, rows_0, rows_1, band):
+    in_width = rows_0.shape[0]
     _, core = here()
-    band_weights(mine_ref, band_ref, core)
-    band_weights(other_ref, band_ref, 1 - core)
-
-
-def bands(mine, other):
-    shape = jax.ShapeDtypeStruct((2, 3, WIDE, WIDE), jnp.bfloat16)
-    return call(bands_kernel, shape, [], mine.size, mine, other)
-
-
-def rotation_sums(orients, width, blocks_ref, band_ref, rows_0, rows_1, band, fetched):
-    in_width = rows_0.shape[0]
-    copies = [
-        pltpu.make_async_copy(band_ref.at[n], band.at[n], fetched.at[n]) for n in range(2)
-    ]
-    for copy in copies:
-        copy.start()
+    band_weights(mine_ref, band, core)
+    band_weights(other_ref, band, 1 - core)
     first = blocks_ref.shape[1] - in_width
     interleave(blocks_ref, rows_0, orients, first, 0)
     interleave(blocks_ref, rows_1, orients, first, 1)
     total = None
     for slot, rows in ((0, rows_0), (1, rows_1)):
-        copies[slot].wait()
         flat = rows[...].reshape(in_width * orients, WIDE).astype(jnp.bfloat16)
         for j in range(3):
             window = flat[(2 - j) * orients : (2 - j + width) * orients]
@@ -118,10 +104,10 @@
     return total.reshape(width, orients, WIDE)
 
 
-def conv_two_kernel(orients, width, blocks_ref, band_ref, out_ref, *scratch):
+def conv_two_kernel(orients, width, blocks_ref, mine_ref, other_ref, out_ref, *scratch):
     *rows, sums, held, done = scratch
     chip, _ = here()
-    total = rotation_sums(orients, width, blocks_ref, band_ref, *rows)
+    total = rotation_sums(orients, width, blocks_ref, mine_ref, other_ref, *rows)
     sums[width:] = jnp.zeros((sums.shape[0] - width, orients, WIDE), jnp.float32)
     sums[:width] = total
     chips = orients // 2
@@ -138,10 +124,10 @@
         copy.wait()
 
 
-def conv_one_kernel(orients, width, blocks_ref, band_ref, out_ref, *scratch):
+def conv_one_kernel(orients, width, blocks_ref, mine_ref, other_ref, out_ref, *scratch):
     *rows, sums = scratch
     chip, _ = here()
-    sums[...] = rotation_sums(orients, width, blocks_ref, band_ref, *rows)
+    sums[...] = rotation_sums(orients, width, blocks_ref, mine_ref, other_ref, *rows)
     chips = orients // 2
     across = out_ref.shape[1]
     for pair in range(chips):
@@ -154,7 +140,7 @@
             ].astype(jnp.bfloat16)
 
 
-def conv(kernel, blocks, in_width, band, width, padded, out_shape, staging=(), out_space=VMEM, room=40):
+def conv(kernel, blocks, in_width, mine, other, width, padded, out_shape, staging=(), out_space=VMEM, room=40):
     orients = 2 * blocks.shape[0]
     return call(
         functools.partial(kernel, orients, width),
@@ -162,15 +148,14 @@
         [
             pltpu.VMEM((in_width, orients, WIDE), jnp.float32),
             pltpu.VMEM((in_width, orients, WIDE), jnp.float32),
-            pltpu.VMEM(band.shape, jnp.bfloat16),
-            pltpu.SemaphoreType.DMA((2,)),
+            pltpu.VMEM((2, 3, WIDE, WIDE), jnp.bfloat16),
             pltpu.VMEM((padded, orients, WIDE), jnp.float32),
             *staging,
         ],
         2 * 6 * width * orients * WIDE * WIDE,
         blocks,
-        band,
-        space=(VMEM, HBM),
+        mine,
+        other,
         out_space=out_space,
         room=room,
     )
@@ -483,18 +468,16 @@
         cross,
         out_space=(HBM, VMEM),
     )
-    first_blocks = exchange(sent, CHIPS)
-
     other_two = lax.ppermute(filt_two[0], CORE, SWAP)
     other_one = lax.ppermute(filt_one[0], CORE, SWAP)
-    bands_two = bands(filt_two[0], other_two)
-    bands_one = bands(filt_one[0], other_one)
+    first_blocks = exchange(after(sent, (other_two, other_one)), CHIPS)
 
     shares = conv(
         conv_two_kernel,
         first_blocks,
         padded,
-        bands_two,
+        filt_two[0],
+        other_two,
         half + 2,
         padded,
         (chips, padded, 2 * WIDE),
@@ -527,7 +510,8 @@
         conv_one_kernel,
         after(all_grad_one, joined),
         padded,
-        bands_one,
+        filt_one[0],
+        other_one,
         half,
         half,
         (2, along_x, half, 2 * WIDE),

time: 116 us -> 115 us (level)
  blocking collectives: 0 us -> 19.9 us
  waiting for transfers between devices: 49.5 us -> 39.2 us
  starting transfers between devices: 42.7 us -> 36.5 us
  local copies, waits for them, and re-layouts: 3.51 us -> 0.93 us
  Pallas kernels: 17.9 us -> 16.6 us
    all_to_all x0 -> x1, blocking collectives: none -> 19.9 us  [exchange(): return lax.all_to_all(parts, axes, 0, 0, tiled=True)]
    all_to_all x5 -> x4, starting transfers between devices: 29 us -> 21.4 us  [exchange(): return lax.all_to_all(parts, axes, 0, 0, tiled=True)]
    all_to_all x5 -> x4, waiting for transfers between devices: 31 us -> 25.1 us  [exchange(): return lax.all_to_all(parts, axes, 0, 0, tiled=True)]
    unnamed x8 -> x6, local copies, waits for them, and re-layouts: 3.48 us -> 0.9 us
    ppermute x1, waiting for transfers between devices: 1.78 us -> 0.01 us  [shards(): other_two = lax.ppermute(filt_two[0], CORE, SWAP)]
    ppermute x1, waiting for transfers between devices: 1.57 us -> 0.01 us  [shards(): other_one = lax.ppermute(filt_one[0], CORE, SWAP)]
    pallas_call x16 -> x14, Pallas kernels: 17.9 us -> 16.6 us  [call(): pl.pallas_call(kernel, out_shape=out_shape, in_specs=in_specs, out_specs=...]
  transfers between devices with their start and end apart: 18 -> 17, of which waited for: 15 -> 11; matrix products, arithmetic and copies ran while one was open for 1% -> 1% of each run, Pallas kernels for 6% -> 8%
where the time goes in v6:
time: 115 us
  waiting for transfers between devices  39.2 us (34%)
  starting transfers between devices  36.5 us (32%)
  blocking collectives  19.9 us (17%)
  Pallas kernels  16.6 us (14%)
    all_to_all x4, waiting for transfers between devices, exchange(): return lax.all_to_all(parts, axes, 0, 0, tiled=True)  25.1 us
    all_to_all x4, starting transfers between devices, exchange(): return lax.all_to_all(parts, axes, 0, 0, tiled=True)  21.4 us
    all_to_all x1, blocking collectives, exchange(): return lax.all_to_all(parts, axes, 0, 0, tiled=True)  19.9 us
    pallas_call x14, Pallas kernels, call(): pl.pallas_call(kernel, out_shape=out_shape, in_specs=in_specs, out_specs=...  16.6 us
    ppermute x1, waiting for transfers between devices, half_terms(): lax.ppermute(leave, AZ, [(i, (i + count // 2) % count) for i in range(cou...  5.65 us
    ppermute x1, starting transfers between devices, shards(): lax.ppermute(cross, (CORE, AZ), place(1, after_me, 0) + place(0, before_m...  4.79 us
    ppermute x3, waiting for transfers between devices, shards(): lax.ppermute(partial[step], CHIPS[0], [(i, (i + step) % along_x) for i in...  4.72 us
    ppermute x3, starting transfers between devices, shards(): lax.ppermute(partial[step], CHIPS[0], [(i, (i + step) % along_x) for i in...  4.01 us
  transfers between devices with their start and end apart: 17, of which 11 were waited for; matrix products, arithmetic and copies ran while one was open for 1% of the time, Pallas kernels for 8%

profile of v6, /device:TPU:32, one launch (start us, length us, event | category | flops | bytes accessed | tf_op | source)
XLA Modules:
  0.0 114.8 jit_solution(2809697356799275776)
XLA Ops:
  1.2 1.6 %shard_map.85 = (bf16[80,512]{1,0:T(8,128)(2,1)}, bf16[80,512]{1,0:T(8,128)(2,1)}, bf16[8,512]{1,0:T(8,128)(2,1)}, bf16[8,512]{1,0:T(8,128)(2,1)}) custom-call(bf16[1,4,32,128]{3,2,1,0:T(8,128)(2,1)} %refs_0_.1, bf16[1,4,32,128]{3,2,1,0:T(8,128)(2,1)} %refs_1_.1, bf16[1,4,32,128]{3,2,1,0:T(8,128)(2,1)} %refs_2_.1, bf16[1,4,32,128]{3,2,1,0:T(8,128)(2,1)} %refs_3_.1), custom_call_target="tpu_custom_call" | custom-call | flops 327680 | bytes 262144 | tf_op jit(solution)/shard_map/pallas_call | solution.py:43
  3.0 1.9 %collective-permute-start.1 = (bf16[8,512]{1,0:T(8,128)(2,1)}, bf16[8,512]{1,0:T(8,128)(2,1)S(1)}, u32[]{:S(2)}, u32[]{:S(2)}) collective-permute-start(bf16[8,512]{1,0:T(8,128)(2,1)} %get-tuple-element.19), channel_id=1, source_target_pairs={{0,1},{1,2},{2,3},{3,4},{4,5},{5,6},{6,7},{7,8},{8,9},{9,10},{10,1... | collective-permute-start | bytes 24584 | tf_op jit(solution)/shard_map/ppermute | solution.py:454
  4.9 4.8 %collective-permute-start.2 = (bf16[8,512]{1,0:T(8,128)(2,1)}, bf16[8,512]{1,0:T(8,128)(2,1)S(1)}, u32[]{:S(2)}, u32[]{:S(2)}) collective-permute-start(bf16[8,512]{1,0:T(8,128)(2,1)} %get-tuple-element.20), channel_id=1, source_target_pairs={{16,1},{17,2},{18,3},{19,4},{20,5},{21,6},{22,7},{23,8},{24,9},{25... | collective-permute-start | bytes 24584 | tf_op jit(solution)/shard_map/ppermute | solution.py:455
  9.7 1.6 %collective-permute-done.2.cross_ref = bf16[8,512]{1,0:T(8,128)(2,1)S(1)} collective-permute-done((bf16[8,512]{1,0:T(8,128)(2,1)}, bf16[8,512]{1,0:T(8,128)(2,1)S(1)}, u32[]{:S(2)}, u32[]{:S(2)}) %collective-permute-start.2) | collective-permute-done | bytes 8224 | tf_op jit(solution)/shard_map/ppermute | solution.py:455
  12.2 1.3 %shard_map.86 = (bf16[8,56,1024]{2,1,0:T(8,128)(2,1)S(1)}, bf16[24,1024]{1,0:T(8,128)(2,1)S(1)}) custom-call(bf16[80,512]{1,0:T(8,128)(2,1)S(1)} %copy-done, bf16[80,512]{1,0:T(8,128)(2,1)S(1)} %collective-permute-done.partner_ref, bf16[8,512]{1,0:T(8,128)(2,1)S(1)} %collective-permute-done.1.same_ref, bf16[8,512]{1,0:T(8,128)(2,1)S(1)} %collective-permute-done.2.cross_ref), custom_call_target="tpu_custom_call" | custom-call | flops 327680 | bytes 360448 | tf_op jit(solution)/shard_map/pallas_call | solution.py:43
  13.5 19.9 %all_to_all.25.blocks_ref.grad_ref.feat_ref = bf16[8,56,1024]{2,1,0:T(8,128)(2,1)S(1)} all-to-all(bf16[8,56,1024]{2,1,0:T(8,128)(2,1)S(1)} %get-tuple-element.22), channel_id=1, replica_groups=mesh['rot_x'=4,'rot_y'=2,'rot_c'=2,'az'=16] {'rot_x','rot_y'}, dimensions={0} | all-to-all | bytes 1835008 | tf_op jit(solution)/shard_map/all_to_all | solution.py:242
  33.4 3.3 %shard_map.87 = bf16[8,24,1024]{2,1,0:T(8,128)(2,1)} custom-call(bf16[8,56,1024]{2,1,0:T(8,128)(2,1)S(1)} %all_to_all.25.blocks_ref.grad_ref.feat_ref, bf16[3,3,128,128]{3,2,1,0:T(8,128)(2,1)S(1)} %bitcast.45, bf16[3,3,128,128]{3,2,1,0:T(8,128)(2,1)S(1)} %collective-permute-done.3.other_ref), custom_call_target="tpu_custom_call" | custom-call | flops 905969664 | bytes 3014656 | tf_op jit(solution)/shard_map/pallas_call | solution.py:43
  36.7 3.5 %all-to-all-start.1 = ((bf16[8,24,1024]{2,1,0:T(8,128)(2,1)}), bf16[8,24,1024]{2,1,0:T(8,128)(2,1)S(1)}, u32[]{:S(2)}, u32[]{:S(2)}) async-start(bf16[8,24,1024]{2,1,0:T(8,128)(2,1)} %shard_map.87), calls=%async_computation.1 | async-start | bytes 786432 | tf_op jit(solution)/shard_map/all_to_all | solution.py:242
  41.3 1.1 shard_map.88
  43.0 6.0 %all-to-all-done.1.parts_ref = bf16[8,24,1024]{2,1,0:T(8,128)(2,1)S(1)} async-done(((bf16[8,24,1024]{2,1,0:T(8,128)(2,1)}), bf16[8,24,1024]{2,1,0:T(8,128)(2,1)S(1)}, u32[]{:S(2)}, u32[]{:S(2)}) %all-to-all-start.1) | async-done | bytes 393248 | tf_op jit(solution)/shard_map/all_to_all | solution.py:242
  49.9 3.5 %all-to-all-start.2 = ((bf16[8,24,1024]{2,1,0:T(8,128)(2,1)}), bf16[8,24,1024]{2,1,0:T(8,128)(2,1)S(1)}, u32[]{:S(2)}, u32[]{:S(2)}) async-start(bf16[8,24,1024]{2,1,0:T(8,128)(2,1)} %shard_map.91), calls=%async_computation.2 | async-start | bytes 786432 | tf_op jit(solution)/shard_map/all_to_all | solution.py:242
  54.2 5.7 %collective-permute-done.6.came = bf16[8,72,128]{2,1,0:T(8,128)(2,1)S(1)} collective-permute-done((bf16[8,72,128]{2,1,0:T(8,128)(2,1)S(1)}, bf16[8,72,128]{2,1,0:T(8,128)(2,1)S(1)}, u32[]{:S(2)}, u32[]{:S(2)}) %collective-permute-start.6) | collective-permute-done | bytes 147488 | tf_op jit(solution)/shard_map/ppermute | solution.py:276
  59.9 2.5 %all-to-all-done.2.grad_ref.blocks_ref = bf16[8,24,1024]{2,1,0:T(8,128)(2,1)S(1)} async-done(((bf16[8,24,1024]{2,1,0:T(8,128)(2,1)}), bf16[8,24,1024]{2,1,0:T(8,128)(2,1)S(1)}, u32[]{:S(2)}, u32[]{:S(2)}) %all-to-all-start.2) | async-done | bytes 393248 | tf_op jit(solution)/shard_map/all_to_all | solution.py:242
  66.0 9.5 %all-to-all-start.3 = ((bf16[16,112,128]{2,1,0:T(8,128)(2,1)}), bf16[16,112,128]{2,1,0:T(8,128)(2,1)S(1)}, u32[]{:S(2)}, u32[]{:S(2)}) async-start(bf16[16,112,128]{2,1,0:T(8,128)(2,1)} %shard_map.95), calls=%async_computation.3 | async-start | bytes 917504 | tf_op jit(solution)/shard_map/all_to_all | solution.py:242
  75.5 2.2 %shard_map.96 = bf16[2,4,16,1024]{3,2,1,0:T(8,128)(2,1)S(1)} custom-call(bf16[8,24,1024]{2,1,0:T(8,128)(2,1)S(1)} %all-to-all-done.2.grad_ref.blocks_ref, bf16[3,3,128,128]{3,2,1,0:T(8,128)(2,1)S(1)} %bitcast.47, bf16[3,3,128,128]{3,2,1,0:T(8,128)(2,1)S(1)} %collective-permute-done.4.other_ref), custom_call_target="tpu_custom_call" | custom-call | flops 805306368 | bytes 1966080 | tf_op jit(solution)/shard_map/pallas_call | solution.py:43
  77.7 2.6 %collective-permute-start.8 = (bf16[4,16,1024]{2,1,0:T(8,128)(2,1)S(1)}, bf16[4,16,1024]{2,1,0:T(8,128)(2,1)S(1)}, u32[]{:S(2)}, u32[]{:S(2)}) collective-permute-start(bf16[4,16,1024]{2,1,0:T(8,128)(2,1)S(1)} %slice_bitcast_fusion), channel_id=1, source_target_pairs={{0,32},{32,0},{1,33},{33,1},{2,34},{34,2},{3,35},{35,3},{4,36},{36... | collective-permute-start | bytes 393224 | tf_op jit(solution)/shard_map/ppermute | solution.py:519
  80.3 9.8 %all-to-all-done.3.parts_ref = bf16[16,112,128]{2,1,0:T(8,128)(2,1)S(1)} async-done(((bf16[16,112,128]{2,1,0:T(8,128)(2,1)}), bf16[16,112,128]{2,1,0:T(8,128)(2,1)S(1)}, u32[]{:S(2)}, u32[]{:S(2)}) %all-to-all-start.3) | async-done | bytes 458784 | tf_op jit(solution)/shard_map/all_to_all | solution.py:242
  91.2 4.9 %all-to-all-start.4 = ((bf16[16,152,128]{2,1,0:T(8,128)(2,1)}), bf16[16,152,128]{2,1,0:T(8,128)(2,1)S(1)}, u32[]{:S(2)}, u32[]{:S(2)}) async-start(bf16[16,152,128]{2,1,0:T(8,128)(2,1)} %shard_map.97), calls=%async_computation.4 | async-start | bytes 1245184 | tf_op jit(solution)/shard_map/all_to_all | solution.py:242
  97.2 2.3 %collective-permute-start.11 = (bf16[16,1024]{1,0:T(8,128)(2,1)S(1)}, bf16[16,1024]{1,0:T(8,128)(2,1)S(1)}, u32[]{:S(2)}, u32[]{:S(2)}) collective-permute-start(bf16[16,1024]{1,0:T(8,128)(2,1)S(1)} %get-tuple-element.32), channel_id=1, source_target_pairs={{0,192},{64,0},{128,64},{192,128},{1,193},{65,1},{129,65},{193,129... | collective-permute-start | bytes 98312 | tf_op jit(solution)/shard_map/ppermute | solution.py:523
  100.2 1.2 %collective-permute-done.9 = bf16[16,1024]{1,0:T(8,128)(2,1)S(1)} collective-permute-done((bf16[16,1024]{1,0:T(8,128)(2,1)S(1)}, bf16[16,1024]{1,0:T(8,128)(2,1)S(1)}, u32[]{:S(2)}, u32[]{:S(2)}) %collective-permute-start.9) | collective-permute-done | bytes 32800 | tf_op jit(solution)/shard_map/ppermute | solution.py:523
  101.3 3.5 %collective-permute-done.10 = bf16[16,1024]{1,0:T(8,128)(2,1)S(1)} collective-permute-done((bf16[16,1024]{1,0:T(8,128)(2,1)S(1)}, bf16[16,1024]{1,0:T(8,128)(2,1)S(1)}, u32[]{:S(2)}, u32[]{:S(2)}) %collective-permute-start.10) | collective-permute-done | bytes 32800 | tf_op jit(solution)/shard_map/ppermute | solution.py:523
  105.0 1.2 %collective-permute-done.12 = bf16[16,512]{1,0:T(8,128)(2,1)S(1)} collective-permute-done((bf16[16,512]{1,0:T(8,128)(2,1)S(1)}, bf16[16,512]{1,0:T(8,128)(2,1)S(1)}, u32[]{:S(2)}, u32[]{:S(2)}) %collective-permute-start.12) | collective-permute-done | bytes 16416 | tf_op jit(solution)/shard_map/ppermute | solution.py:530
  106.8 6.7 %all-to-all-done.4.whole_ref = bf16[16,152,128]{2,1,0:T(8,128)(2,1)S(1)} async-done(((bf16[16,152,128]{2,1,0:T(8,128)(2,1)}), bf16[16,152,128]{2,1,0:T(8,128)(2,1)S(1)}, u32[]{:S(2)}, u32[]{:S(2)}) %all-to-all-start.4) | async-done | bytes 622624 | tf_op jit(solution)/shard_map/all_to_all | solution.py:242
  113.5 1.1 shard_map.98
  (39 shorter events, 12.3 us)
Async XLA Ops:
  0.6 12.9 %collective-permute-start.4 = (bf16[3,3,128,128]{3,2,1,0:T(8,128)(2,1)}, bf16[3,3,128,128]{3,2,1,0:T(8,128)(2,1)S(1)}, u32[]{:S(2)}, u32[]{:S(2)}) collective-permute-start(bf16[3,3,128,128]{3,2,1,0:T(8,128)(2,1)} %bitcast.46), channel_id=1, source_target_pairs={{0,16},{16,0},{1,17},{17,1},{2,18},{18,2},{3,19},{19,3},{4,20},{20... | collective-permute-start | bytes 884744 | tf_op jit(solution)/shard_map/ppermute | solution.py:472
  0.7 12.8 %collective-permute-start.3 = (bf16[3,3,128,128]{3,2,1,0:T(8,128)(2,1)}, bf16[3,3,128,128]{3,2,1,0:T(8,128)(2,1)S(1)}, u32[]{:S(2)}, u32[]{:S(2)}) collective-permute-start(bf16[3,3,128,128]{3,2,1,0:T(8,128)(2,1)} %bitcast.44), channel_id=1, source_target_pairs={{0,16},{16,0},{1,17},{17,1},{2,18},{18,2},{3,19},{19,3},{4,20},{20... | collective-permute-start | bytes 884744 | tf_op jit(solution)/shard_map/ppermute | solution.py:471
  2.8 8.5 %collective-permute-start = (bf16[80,512]{1,0:T(8,128)(2,1)}, bf16[80,512]{1,0:T(8,128)(2,1)S(1)}, u32[]{:S(2)}, u32[]{:S(2)}) collective-permute-start(bf16[80,512]{1,0:T(8,128)(2,1)} %get-tuple-element.18), channel_id=1, source_target_pairs={{0,16},{16,0},{1,17},{17,1},{2,18},{18,2},{3,19},{19,3},{4,20},{20... | collective-permute-start | bytes 245768 | tf_op jit(solution)/shard_map/ppermute | solution.py:456
  3.0 6.7 %collective-permute-start.1 = (bf16[8,512]{1,0:T(8,128)(2,1)}, bf16[8,512]{1,0:T(8,128)(2,1)S(1)}, u32[]{:S(2)}, u32[]{:S(2)}) collective-permute-start(bf16[8,512]{1,0:T(8,128)(2,1)} %get-tuple-element.19), channel_id=1, source_target_pairs={{0,1},{1,2},{2,3},{3,4},{4,5},{5,6},{6,7},{7,8},{8,9},{9,10},{10,1... | collective-permute-start | bytes 24584 | tf_op jit(solution)/shard_map/ppermute | solution.py:454
  4.9 6.4 %collective-permute-start.2 = (bf16[8,512]{1,0:T(8,128)(2,1)}, bf16[8,512]{1,0:T(8,128)(2,1)S(1)}, u32[]{:S(2)}, u32[]{:S(2)}) collective-permute-start(bf16[8,512]{1,0:T(8,128)(2,1)} %get-tuple-element.20), channel_id=1, source_target_pairs={{16,1},{17,2},{18,3},{19,4},{20,5},{21,6},{22,7},{23,8},{24,9},{25... | collective-permute-start | bytes 24584 | tf_op jit(solution)/shard_map/ppermute | solution.py:455
  11.3 0.9 copy-start
  13.5 19.9 %copy-start.1 = (bf16[1,3,3,128,128]{4,3,2,1,0:T(8,128)(2,1)S(1)}, bf16[1,3,3,128,128]{4,3,2,1,0:T(8,128)(2,1)}, u32[]{:S(2)}) copy-start(bf16[1,3,3,128,128]{4,3,2,1,0:T(8,128)(2,1)} %param.11) | copy-start | bytes 884740
  36.7 12.4 %all-to-all-start.1 = ((bf16[8,24,1024]{2,1,0:T(8,128)(2,1)}), bf16[8,24,1024]{2,1,0:T(8,128)(2,1)S(1)}, u32[]{:S(2)}, u32[]{:S(2)}) async-start(bf16[8,24,1024]{2,1,0:T(8,128)(2,1)} %shard_map.87), calls=%async_computation.1 | async-start | bytes 786432 | tf_op jit(solution)/shard_map/all_to_all | solution.py:242
  41.2 1.7 %collective-permute-start.5 = (bf16[3,3,128,128]{3,2,1,0:T(8,128)(2,1)S(1)}, bf16[3,3,128,128]{3,2,1,0:T(8,128)(2,1)S(1)}, u32[]{:S(2)}, u32[]{:S(2)}) collective-permute-start(bf16[3,3,128,128]{3,2,1,0:T(8,128)(2,1)S(1)} %shard_map.89), channel_id=1, source_target_pairs={{0,16},{16,0},{1,17},{17,1},{2,18},{18,2},{3,19},{19,3},{4,20},{20... | collective-permute-start | bytes 884744 | tf_op jit(solution)/shard_map/ppermute | solution.py:229
  49.9 12.4 %all-to-all-start.2 = ((bf16[8,24,1024]{2,1,0:T(8,128)(2,1)}), bf16[8,24,1024]{2,1,0:T(8,128)(2,1)S(1)}, u32[]{:S(2)}, u32[]{:S(2)}) async-start(bf16[8,24,1024]{2,1,0:T(8,128)(2,1)} %shard_map.91), calls=%async_computation.2 | async-start | bytes 786432 | tf_op jit(solution)/shard_map/all_to_all | solution.py:242
  53.4 6.4 %collective-permute-start.6 = (bf16[8,72,128]{2,1,0:T(8,128)(2,1)S(1)}, bf16[8,72,128]{2,1,0:T(8,128)(2,1)S(1)}, u32[]{:S(2)}, u32[]{:S(2)}) collective-permute-start(bf16[8,72,128]{2,1,0:T(8,128)(2,1)S(1)} %get-tuple-element.23), channel_id=1, source_target_pairs={{0,8},{1,9},{2,10},{3,11},{4,12},{5,13},{6,14},{7,15},{8,0},{9,1},... | collective-permute-start | bytes 442376 | tf_op jit(solution)/shard_map/ppermute | solution.py:276
  63.4 1.7 %collective-permute-start.7 = (bf16[3,3,128,128]{3,2,1,0:T(8,128)(2,1)S(1)}, bf16[3,3,128,128]{3,2,1,0:T(8,128)(2,1)S(1)}, u32[]{:S(2)}, u32[]{:S(2)}) collective-permute-start(bf16[3,3,128,128]{3,2,1,0:T(8,128)(2,1)S(1)} %shard_map.94), channel_id=1, source_target_pairs={{0,16},{16,0},{1,17},{17,1},{2,18},{18,2},{3,19},{19,3},{4,20},{20... | collective-permute-start | bytes 884744 | tf_op jit(solution)/shard_map/ppermute | solution.py:229
  66.0 9.6 %copy-start.2 = (bf16[1,3,3,128,128]{4,3,2,1,0:T(8,128)(2,1)S(1)}, bf16[1,3,3,128,128]{4,3,2,1,0:T(8,128)(2,1)}, u32[]{:S(2)}) copy-start(bf16[1,3,3,128,128]{4,3,2,1,0:T(8,128)(2,1)} %param.10) | copy-start | bytes 884740
  66.0 24.2 %all-to-all-start.3 = ((bf16[16,112,128]{2,1,0:T(8,128)(2,1)}), bf16[16,112,128]{2,1,0:T(8,128)(2,1)S(1)}, u32[]{:S(2)}, u32[]{:S(2)}) async-start(bf16[16,112,128]{2,1,0:T(8,128)(2,1)} %shard_map.95), calls=%async_computation.3 | async-start | bytes 917504 | tf_op jit(solution)/shard_map/all_to_all | solution.py:242
  77.7 18.3 %collective-permute-start.8 = (bf16[4,16,1024]{2,1,0:T(8,128)(2,1)S(1)}, bf16[4,16,1024]{2,1,0:T(8,128)(2,1)S(1)}, u32[]{:S(2)}, u32[]{:S(2)}) collective-permute-start(bf16[4,16,1024]{2,1,0:T(8,128)(2,1)S(1)} %slice_bitcast_fusion), channel_id=1, source_target_pairs={{0,32},{32,0},{1,33},{33,1},{2,34},{34,2},{3,35},{35,3},{4,36},{36... | collective-permute-start | bytes 393224 | tf_op jit(solution)/shard_map/ppermute | solution.py:519
  91.2 22.4 %all-to-all-start.4 = ((bf16[16,152,128]{2,1,0:T(8,128)(2,1)}), bf16[16,152,128]{2,1,0:T(8,128)(2,1)S(1)}, u32[]{:S(2)}, u32[]{:S(2)}) async-start(bf16[16,152,128]{2,1,0:T(8,128)(2,1)} %shard_map.97), calls=%async_computation.4 | async-start | bytes 1245184 | tf_op jit(solution)/shard_map/all_to_all | solution.py:242
  96.1 5.2 %collective-permute-start.9 = (bf16[16,1024]{1,0:T(8,128)(2,1)S(1)}, bf16[16,1024]{1,0:T(8,128)(2,1)S(1)}, u32[]{:S(2)}, u32[]{:S(2)}) collective-permute-start(bf16[16,1024]{1,0:T(8,128)(2,1)S(1)} %get-tuple-element.31), channel_id=1, source_target_pairs={{0,64},{64,128},{128,192},{192,0},{1,65},{65,129},{129,193},{193,1... | collective-permute-start | bytes 98312 | tf_op jit(solution)/shard_map/ppermute | solution.py:523
  97.2 4.2 %collective-permute-start.11 = (bf16[16,1024]{1,0:T(8,128)(2,1)S(1)}, bf16[16,1024]{1,0:T(8,128)(2,1)S(1)}, u32[]{:S(2)}, u32[]{:S(2)}) collective-permute-start(bf16[16,1024]{1,0:T(8,128)(2,1)S(1)} %get-tuple-element.32), channel_id=1, source_target_pairs={{0,192},{64,0},{128,64},{192,128},{1,193},{65,1},{129,65},{193,129... | collective-permute-start | bytes 98312 | tf_op jit(solution)/shard_map/ppermute | solution.py:523
  99.5 5.4 %collective-permute-start.10 = (bf16[16,1024]{1,0:T(8,128)(2,1)S(1)}, bf16[16,1024]{1,0:T(8,128)(2,1)S(1)}, u32[]{:S(2)}, u32[]{:S(2)}) collective-permute-start(bf16[16,1024]{1,0:T(8,128)(2,1)S(1)} %get-tuple-element.33), channel_id=1, source_target_pairs={{0,128},{64,192},{128,0},{192,64},{1,129},{65,193},{129,1},{193,65... | collective-permute-start | bytes 98312 | tf_op jit(solution)/shard_map/ppermute | solution.py:523
  104.9 1.3 %collective-permute-start.12 = (bf16[16,512]{1,0:T(8,128)(2,1)S(1)}, bf16[16,512]{1,0:T(8,128)(2,1)S(1)}, u32[]{:S(2)}, u32[]{:S(2)}) collective-permute-start(bf16[16,512]{1,0:T(8,128)(2,1)S(1)} %get-tuple-element.35), channel_id=1, source_target_pairs={{0,16},{16,0},{1,17},{17,1},{2,18},{18,2},{3,19},{19,3},{4,20},{20... | collective-permute-start | bytes 49160 | tf_op jit(solution)/shard_map/ppermute | solution.py:530

commit v7 on v6

--- a/solution.py
+++ b/solution.py
@@ -251,32 +251,15 @@
     return lax.optimization_barrier((array, first))[0]
 
 
-def halves_kernel(mine, theirs, stay_ref, leave_ref, both_ref):
-    half = stay_ref.shape[0]
-    side = lax.axis_index(AZ) // half
-    both_ref[...] = mine[...].astype(jnp.float32) + theirs[...].astype(jnp.float32)
-    stay_ref[...] = both_ref[pl.ds(side * half, half)].astype(jnp.bfloat16)
-    leave_ref[...] = both_ref[pl.ds((1 - side) * half, half)].astype(jnp.bfloat16)
-
-
-def deal_kernel(stay, came, out_ref):
-    both = stay[...].astype(jnp.float32) + came[...].astype(jnp.float32)
-    lines = both.reshape(-1, CHAN)
-    count, size, _ = out_ref.shape
-    lines = jnp.concatenate([lines, jnp.zeros((count * size - lines.shape[0], CHAN), jnp.float32)])
-    out_ref[...] = lines.reshape(out_ref.shape).astype(jnp.bfloat16)
-
-
-def half_terms(pair):
+def both_kernel(mine, theirs, out_ref):
+    both = mine[...].astype(jnp.float32) + theirs[...].astype(jnp.float32)
+    out_ref[...] = both.astype(jnp.bfloat16)
+
+
+def both_cores(pair):
     mine, theirs = chunks(pair)
-    count, size, _ = mine.shape
-    half = jax.ShapeDtypeStruct((count // 2, size, CHAN), jnp.bfloat16)
-    both = pltpu.VMEM(mine.shape, jnp.float32)
-    stay, leave = call(halves_kernel, (half, half), [both], mine.size, mine, theirs)
-    came = lax.ppermute(leave, AZ, [(i, (i + count // 2) % count) for i in range(count)])
-    dealt = -(-size // 16) * 8
-    shape = jax.ShapeDtypeStruct((count, dealt, CHAN), jnp.bfloat16)
-    return leave, call(deal_kernel, shape, [], mine.size, stay, came)
+    shape = jax.ShapeDtypeStruct(mine.shape, jnp.bfloat16)
+    return call(both_kernel, shape, [], mine.size, mine, theirs)
 
 
 def join_kernel(mine, theirs, also, out_ref, held, done):
@@ -295,62 +278,35 @@
     return call(join_kernel, shape, held, mine.size, mine, theirs, also, out_space=HBM)
 
 
-def reduce_kernel(size, parts_ref, out_ref, held, done):
-    count = parts_ref.shape[0]
-    dealt = parts_ref.shape[1] - size
-    total = [parts_ref[n].astype(jnp.float32) for n in (0, count // 2)]
-    for n in range(1, count // 2):
-        total[0] = total[0] + parts_ref[n].astype(jnp.float32)
-        total[1] = total[1] + parts_ref[count // 2 + n].astype(jnp.float32)
-    held[:size] = (total[0][:size] + total[1][:size]).astype(jnp.bfloat16)
-    held[size : size + dealt] = total[0][size:].astype(jnp.bfloat16)
-    held[size + dealt :] = total[1][size:].astype(jnp.bfloat16)
-    copy_all([(held, out_ref.at[n]) for n in range(count)], done)
-
-
-def finish_kernel(size, scale, whole_ref, one_ref, two_ref, held_one, held_two, done):
-    count = whole_ref.shape[0]
-    dealt = (whole_ref.shape[1] - size) // 2
-    lines = two_ref.shape[1]
-    held_one[...] = whole_ref[:, :size].astype(jnp.float32) * scale
-    first = pltpu.make_async_copy(held_one, one_ref, done.at[0])
-    first.start()
-    for side in range(2):
-        for n in range(count):
-            start, end = n * dealt, min((n + 1) * dealt, lines)
-            if end > start:
-                row = size + side * dealt
-                part = whole_ref[n, row : row + dealt].astype(jnp.float32) * scale
-                held_two[side, start:end] = part[: end - start]
-    second = pltpu.make_async_copy(held_two, two_ref, done.at[1])
-    second.start()
-    first.wait()
-    second.wait()
-
-
-def summed_over_az(joined, size, scale):
+def reduce_kernel(parts_ref, out_ref, held, done):
+    total = parts_ref[0].astype(jnp.float32)
+    for n in range(1, parts_ref.shape[0]):
+        total = total + parts_ref[n].astype(jnp.float32)
+    held[...] = total.astype(jnp.bfloat16)
+    copy_all([(held, out_ref.at[n]) for n in range(out_ref.shape[0])], done)
+
+
+def finish_kernel(scale, whole_ref, one_ref, two_ref, held, done):
+    size = one_ref.shape[1]
+    copies = []
+    for n, out_ref in enumerate((one_ref, two_ref)):
+        held[n] = whole_ref[:, n * size : (n + 1) * size].astype(jnp.float32) * scale
+        copies.append(pltpu.make_async_copy(held.at[n], out_ref, done.at[n]))
+        copies[n].start()
+    for copy in copies:
+        copy.wait()
+
+
+def summed_over_az(joined, scale):
     count, both, _ = joined.shape
-    dealt = both - size
-    held = [pltpu.VMEM((size + 2 * dealt, CHAN), jnp.bfloat16), pltpu.SemaphoreType.DMA((count,))]
-    shape = jax.ShapeDtypeStruct((count, size + 2 * dealt, CHAN), jnp.bfloat16)
-    copies = call(
-        functools.partial(reduce_kernel, size),
-        shape,
-        held,
-        joined.size,
-        exchange(joined, AZ),
-        out_space=HBM,
-    )
-    one = (count, size, CHAN)
-    two = (2, count * size // 2, CHAN)
+    held = [pltpu.VMEM((both, CHAN), jnp.bfloat16), pltpu.SemaphoreType.DMA((count,))]
+    shape = jax.ShapeDtypeStruct(joined.shape, jnp.bfloat16)
+    copies = call(reduce_kernel, shape, held, joined.size, exchange(joined, AZ), out_space=HBM)
+    bank = jax.ShapeDtypeStruct((count, both // 2, CHAN), jnp.float32)
     banks = call(
-        functools.partial(finish_kernel, size, scale),
-        (jax.ShapeDtypeStruct(one, jnp.float32), jax.ShapeDtypeStruct(two, jnp.float32)),
-        [
-            pltpu.VMEM(one, jnp.float32),
-            pltpu.VMEM(two, jnp.float32),
-            pltpu.SemaphoreType.DMA((2,)),
-        ],
+        functools.partial(finish_kernel, scale),
+        (bank, bank),
+        [pltpu.VMEM((2, *bank.shape), jnp.float32), pltpu.SemaphoreType.DMA((2,))],
         joined.size,
         exchange(copies, AZ),
         out_space=HBM,
@@ -489,8 +445,8 @@
         52,
     )
     pair_two = filter_terms(first_blocks, 0, half, first_blocks, padded, 3)
-    leave, terms_two = half_terms(pair_two)
-    arrived = after(exchange(shares, CHIPS), leave)
+    terms_two = both_cores(pair_two)
+    arrived = after(exchange(shares, CHIPS), terms_two)
     copies = call(
         point_kernel,
         narrow(chips, padded, 2 * WIDE),
@@ -500,9 +456,9 @@
         pre_pair,
         out_space=HBM,
     )
-    all_grad_one = after(exchange(copies, CHIPS), terms_two)
+    all_grad_one = exchange(copies, CHIPS)
     joined = joined_terms(filter_terms(first_blocks, 1, half, all_grad_one, padded, 2), terms_two)
-    filt_grad_one, filt_grad_two = summed_over_az(joined, filt_one.size // CHAN // az_count, scale)
+    filt_grad_one, filt_grad_two = summed_over_az(joined, scale)
 
     along_x = lax.axis_size(CHIPS[0])
 

time: 115 us -> 117 us (1.017)
  blocking collectives: 19.9 us -> 32.2 us
  starting transfers between devices: 36.5 us -> 30.3 us
  waiting for transfers between devices: 39.2 us -> 34.9 us
    all_to_all x1 -> x2, blocking collectives: 19.9 us -> 32.2 us  [exchange(): return lax.all_to_all(parts, axes, 0, 0, tiled=True)]
    ppermute x1 -> x0, waiting for transfers between devices: 5.65 us -> none  [half_terms(): lax.ppermute(leave, AZ, [(i, (i + count // 2) % count) for i in range(cou...]
    all_to_all x4 -> x3, starting transfers between devices: 21.4 us -> 17.8 us  [exchange(): return lax.all_to_all(parts, axes, 0, 0, tiled=True)]
    ppermute x1, starting transfers between devices: 2.57 us -> 1.12 us  [shards(): arrived_y = lax.ppermute(shares[1], CHIPS[1], SWAP)]
    all_to_all x4 -> x3, waiting for transfers between devices: 25.1 us -> 26 us  [exchange(): return lax.all_to_all(parts, axes, 0, 0, tiled=True)]
    pallas_call x14 -> x13, Pallas kernels: 16.6 us -> 16.3 us  [call(): pl.pallas_call(kernel, out_shape=out_shape, in_specs=in_specs, out_specs=...]
  transfers between devices with their start and end apart: 17 -> 15, of which waited for: 11 -> 9; matrix products, arithmetic and copies ran while one was open for 1% -> 1% of each run, Pallas kernels for 8% -> 8%
where the time goes in v7:
time: 117 us; the launch traced here: 116 us
  waiting for transfers between devices  34.9 us (30%)
  blocking collectives  32.2 us (28%)
  starting transfers between devices  30.3 us (26%)
  Pallas kernels  16.3 us (14%)
    all_to_all x2, blocking collectives, exchange(): return lax.all_to_all(parts, axes, 0, 0, tiled=True)  32.2 us
    all_to_all x3, waiting for transfers between devices, exchange(): return lax.all_to_all(parts, axes, 0, 0, tiled=True)  26 us
    all_to_all x3, starting transfers between devices, exchange(): return lax.all_to_all(parts, axes, 0, 0, tiled=True)  17.8 us
    pallas_call x13, Pallas kernels, call(): pl.pallas_call(kernel, out_shape=out_shape, in_specs=in_specs, out_specs=...  16.3 us
    ppermute x3, waiting for transfers between devices, shards(): lax.ppermute(partial[step], CHIPS[0], [(i, (i + step) % along_x) for i in...  5.17 us
    ppermute x1, starting transfers between devices, shards(): lax.ppermute(cross, (CORE, AZ), place(1, after_me, 0) + place(0, before_m...  4.79 us
    ppermute x3, starting transfers between devices, shards(): lax.ppermute(partial[step], CHIPS[0], [(i, (i + step) % along_x) for i in...  3.56 us
  transfers between devices with their start and end apart: 15, of which 9 were waited for; matrix products, arithmetic and copies ran while one was open for 1% of the time, Pallas kernels for 8%

profile of v7, /device:TPU:32, one launch (start us, length us, event | category | flops | bytes accessed | tf_op | source)
XLA Modules:
  0.0 116.3 jit_solution(15003989028808923508)
XLA Ops:
  1.2 1.6 %shard_map.85 = (bf16[80,512]{1,0:T(8,128)(2,1)}, bf16[80,512]{1,0:T(8,128)(2,1)}, bf16[8,512]{1,0:T(8,128)(2,1)}, bf16[8,512]{1,0:T(8,128)(2,1)}) custom-call(bf16[1,4,32,128]{3,2,1,0:T(8,128)(2,1)} %refs_0_.1, bf16[1,4,32,128]{3,2,1,0:T(8,128)(2,1)} %refs_1_.1, bf16[1,4,32,128]{3,2,1,0:T(8,128)(2,1)} %refs_2_.1, bf16[1,4,32,128]{3,2,1,0:T(8,128)(2,1)} %refs_3_.1), custom_call_target="tpu_custom_call" | custom-call | flops 327680 | bytes 262144 | tf_op jit(solution)/shard_map/pallas_call | solution.py:43
  3.0 1.9 %collective-permute-start.1 = (bf16[8,512]{1,0:T(8,128)(2,1)}, bf16[8,512]{1,0:T(8,128)(2,1)S(1)}, u32[]{:S(2)}, u32[]{:S(2)}) collective-permute-start(bf16[8,512]{1,0:T(8,128)(2,1)} %get-tuple-element.16), channel_id=1, source_target_pairs={{0,1},{1,2},{2,3},{3,4},{4,5},{5,6},{6,7},{7,8},{8,9},{9,10},{10,1... | collective-permute-start | bytes 24584 | tf_op jit(solution)/shard_map/ppermute | solution.py:410
  4.9 4.8 %collective-permute-start.2 = (bf16[8,512]{1,0:T(8,128)(2,1)}, bf16[8,512]{1,0:T(8,128)(2,1)S(1)}, u32[]{:S(2)}, u32[]{:S(2)}) collective-permute-start(bf16[8,512]{1,0:T(8,128)(2,1)} %get-tuple-element.17), channel_id=1, source_target_pairs={{16,1},{17,2},{18,3},{19,4},{20,5},{21,6},{22,7},{23,8},{24,9},{25... | collective-permute-start | bytes 24584 | tf_op jit(solution)/shard_map/ppermute | solution.py:411
  9.7 1.6 %collective-permute-done.2.cross_ref = bf16[8,512]{1,0:T(8,128)(2,1)S(1)} collective-permute-done((bf16[8,512]{1,0:T(8,128)(2,1)}, bf16[8,512]{1,0:T(8,128)(2,1)S(1)}, u32[]{:S(2)}, u32[]{:S(2)}) %collective-permute-start.2) | collective-permute-done | bytes 8224 | tf_op jit(solution)/shard_map/ppermute | solution.py:411
  12.2 1.3 %shard_map.86 = (bf16[8,56,1024]{2,1,0:T(8,128)(2,1)S(1)}, bf16[24,1024]{1,0:T(8,128)(2,1)S(1)}) custom-call(bf16[80,512]{1,0:T(8,128)(2,1)S(1)} %copy-done, bf16[80,512]{1,0:T(8,128)(2,1)S(1)} %collective-permute-done.partner_ref, bf16[8,512]{1,0:T(8,128)(2,1)S(1)} %collective-permute-done.1.same_ref, bf16[8,512]{1,0:T(8,128)(2,1)S(1)} %collective-permute-done.2.cross_ref), custom_call_target="tpu_custom_call" | custom-call | flops 327680 | bytes 360448 | tf_op jit(solution)/shard_map/pallas_call | solution.py:43
  13.5 19.9 %all_to_all.25.blocks_ref.grad_ref.feat_ref = bf16[8,56,1024]{2,1,0:T(8,128)(2,1)S(1)} all-to-all(bf16[8,56,1024]{2,1,0:T(8,128)(2,1)S(1)} %get-tuple-element.19), channel_id=1, replica_groups=mesh['rot_x'=4,'rot_y'=2,'rot_c'=2,'az'=16] {'rot_x','rot_y'}, dimensions={0} | all-to-all | bytes 1835008 | tf_op jit(solution)/shard_map/all_to_all | solution.py:242
  33.4 3.3 %shard_map.87 = bf16[8,24,1024]{2,1,0:T(8,128)(2,1)} custom-call(bf16[8,56,1024]{2,1,0:T(8,128)(2,1)S(1)} %all_to_all.25.blocks_ref.grad_ref.feat_ref, bf16[3,3,128,128]{3,2,1,0:T(8,128)(2,1)S(1)} %bitcast.45, bf16[3,3,128,128]{3,2,1,0:T(8,128)(2,1)S(1)} %collective-permute-done.3.other_ref), custom_call_target="tpu_custom_call" | custom-call | flops 905969664 | bytes 3014656 | tf_op jit(solution)/shard_map/pallas_call | solution.py:43
  36.7 3.5 %all-to-all-start.1 = ((bf16[8,24,1024]{2,1,0:T(8,128)(2,1)}), bf16[8,24,1024]{2,1,0:T(8,128)(2,1)S(1)}, u32[]{:S(2)}, u32[]{:S(2)}) async-start(bf16[8,24,1024]{2,1,0:T(8,128)(2,1)} %shard_map.87), calls=%async_computation.1 | async-start | bytes 786432 | tf_op jit(solution)/shard_map/all_to_all | solution.py:242
  40.1 1.1 shard_map.89
  41.3 1.1 shard_map.88
  43.0 6.1 %all-to-all-done.1.parts_ref = bf16[8,24,1024]{2,1,0:T(8,128)(2,1)S(1)} async-done(((bf16[8,24,1024]{2,1,0:T(8,128)(2,1)}), bf16[8,24,1024]{2,1,0:T(8,128)(2,1)S(1)}, u32[]{:S(2)}, u32[]{:S(2)}) %all-to-all-start.1) | async-done | bytes 393248 | tf_op jit(solution)/shard_map/all_to_all | solution.py:242
  49.7 12.3 %all_to_all.26.grad_ref.blocks_ref = bf16[8,24,1024]{2,1,0:T(8,128)(2,1)S(1)} all-to-all(bf16[8,24,1024]{2,1,0:T(8,128)(2,1)S(1)} %shard_map.91), channel_id=1, replica_groups=mesh['rot_x'=4,'rot_y'=2,'rot_c'=2,'az'=16] {'rot_x','rot_y'}, dimensions={0} | all-to-all | bytes 786432 | tf_op jit(solution)/shard_map/all_to_all | solution.py:242
  63.2 1.1 shard_map.92
  65.7 9.3 %all-to-all-start.3 = ((bf16[16,144,128]{2,1,0:T(8,128)(2,1)}), bf16[16,144,128]{2,1,0:T(8,128)(2,1)S(1)}, u32[]{:S(2)}, u32[]{:S(2)}) async-start(bf16[16,144,128]{2,1,0:T(8,128)(2,1)} %shard_map.94), calls=%async_computation.3 | async-start | bytes 1179648 | tf_op jit(solution)/shard_map/all_to_all | solution.py:242
  75.0 2.2 %shard_map.95 = bf16[2,4,16,1024]{3,2,1,0:T(8,128)(2,1)S(1)} custom-call(bf16[8,24,1024]{2,1,0:T(8,128)(2,1)S(1)} %all_to_all.26.grad_ref.blocks_ref, bf16[3,3,128,128]{3,2,1,0:T(8,128)(2,1)S(1)} %bitcast.47, bf16[3,3,128,128]{3,2,1,0:T(8,128)(2,1)S(1)} %collective-permute-done.4.other_ref), custom_call_target="tpu_custom_call" | custom-call | flops 805306368 | bytes 1966080 | tf_op jit(solution)/shard_map/pallas_call | solution.py:43
  77.2 1.1 collective-permute-start.7
  78.3 13.9 %all-to-all-done.3.parts_ref = bf16[16,144,128]{2,1,0:T(8,128)(2,1)S(1)} async-done(((bf16[16,144,128]{2,1,0:T(8,128)(2,1)}), bf16[16,144,128]{2,1,0:T(8,128)(2,1)S(1)}, u32[]{:S(2)}, u32[]{:S(2)}) %all-to-all-start.3) | async-done | bytes 589856 | tf_op jit(solution)/shard_map/all_to_all | solution.py:242
  93.3 5.1 %all-to-all-start.4 = ((bf16[16,144,128]{2,1,0:T(8,128)(2,1)}), bf16[16,144,128]{2,1,0:T(8,128)(2,1)S(1)}, u32[]{:S(2)}, u32[]{:S(2)}) async-start(bf16[16,144,128]{2,1,0:T(8,128)(2,1)} %shard_map.96), calls=%async_computation.4 | async-start | bytes 1179648 | tf_op jit(solution)/shard_map/all_to_all | solution.py:242
  99.0 2.7 %collective-permute-start.10 = (bf16[16,1024]{1,0:T(8,128)(2,1)S(1)}, bf16[16,1024]{1,0:T(8,128)(2,1)S(1)}, u32[]{:S(2)}, u32[]{:S(2)}) collective-permute-start(bf16[16,1024]{1,0:T(8,128)(2,1)S(1)} %get-tuple-element.26), channel_id=1, source_target_pairs={{0,192},{64,0},{128,64},{192,128},{1,193},{65,1},{129,65},{193,129... | collective-permute-start | bytes 98312 | tf_op jit(solution)/shard_map/ppermute | solution.py:479
  102.0 1.6 %collective-permute-done.8 = bf16[16,1024]{1,0:T(8,128)(2,1)S(1)} collective-permute-done((bf16[16,1024]{1,0:T(8,128)(2,1)S(1)}, bf16[16,1024]{1,0:T(8,128)(2,1)S(1)}, u32[]{:S(2)}, u32[]{:S(2)}) %collective-permute-start.8) | collective-permute-done | bytes 32800 | tf_op jit(solution)/shard_map/ppermute | solution.py:479
  103.6 3.5 %collective-permute-done.9 = bf16[16,1024]{1,0:T(8,128)(2,1)S(1)} collective-permute-done((bf16[16,1024]{1,0:T(8,128)(2,1)S(1)}, bf16[16,1024]{1,0:T(8,128)(2,1)S(1)}, u32[]{:S(2)}, u32[]{:S(2)}) %collective-permute-start.9) | collective-permute-done | bytes 32800 | tf_op jit(solution)/shard_map/ppermute | solution.py:479
  107.3 1.2 collective-permute-done.11
  109.1 6.0 %all-to-all-done.4.whole_ref = bf16[16,144,128]{2,1,0:T(8,128)(2,1)S(1)} async-done(((bf16[16,144,128]{2,1,0:T(8,128)(2,1)}), bf16[16,144,128]{2,1,0:T(8,128)(2,1)S(1)}, u32[]{:S(2)}, u32[]{:S(2)}) %all-to-all-start.4) | async-done | bytes 589856 | tf_op jit(solution)/shard_map/all_to_all | solution.py:242
  115.1 1.1 shard_map.97
  (35 shorter events, 8.2 us)
Async XLA Ops:
  0.6 12.9 %collective-permute-start.4 = (bf16[3,3,128,128]{3,2,1,0:T(8,128)(2,1)}, bf16[3,3,128,128]{3,2,1,0:T(8,128)(2,1)S(1)}, u32[]{:S(2)}, u32[]{:S(2)}) collective-permute-start(bf16[3,3,128,128]{3,2,1,0:T(8,128)(2,1)} %bitcast.46), channel_id=1, source_target_pairs={{0,16},{16,0},{1,17},{17,1},{2,18},{18,2},{3,19},{19,3},{4,20},{20... | collective-permute-start | bytes 884744 | tf_op jit(solution)/shard_map/ppermute | solution.py:428
  0.7 12.8 %collective-permute-start.3 = (bf16[3,3,128,128]{3,2,1,0:T(8,128)(2,1)}, bf16[3,3,128,128]{3,2,1,0:T(8,128)(2,1)S(1)}, u32[]{:S(2)}, u32[]{:S(2)}) collective-permute-start(bf16[3,3,128,128]{3,2,1,0:T(8,128)(2,1)} %bitcast.44), channel_id=1, source_target_pairs={{0,16},{16,0},{1,17},{17,1},{2,18},{18,2},{3,19},{19,3},{4,20},{20... | collective-permute-start | bytes 884744 | tf_op jit(solution)/shard_map/ppermute | solution.py:427
  2.8 8.5 %collective-permute-start = (bf16[80,512]{1,0:T(8,128)(2,1)}, bf16[80,512]{1,0:T(8,128)(2,1)S(1)}, u32[]{:S(2)}, u32[]{:S(2)}) collective-permute-start(bf16[80,512]{1,0:T(8,128)(2,1)} %get-tuple-element.15), channel_id=1, source_target_pairs={{0,16},{16,0},{1,17},{17,1},{2,18},{18,2},{3,19},{19,3},{4,20},{20... | collective-permute-start | bytes 245768 | tf_op jit(solution)/shard_map/ppermute | solution.py:412
  3.0 6.7 %collective-permute-start.1 = (bf16[8,512]{1,0:T(8,128)(2,1)}, bf16[8,512]{1,0:T(8,128)(2,1)S(1)}, u32[]{:S(2)}, u32[]{:S(2)}) collective-permute-start(bf16[8,512]{1,0:T(8,128)(2,1)} %get-tuple-element.16), channel_id=1, source_target_pairs={{0,1},{1,2},{2,3},{3,4},{4,5},{5,6},{6,7},{7,8},{8,9},{9,10},{10,1... | collective-permute-start | bytes 24584 | tf_op jit(solution)/shard_map/ppermute | solution.py:410
  4.9 6.4 %collective-permute-start.2 = (bf16[8,512]{1,0:T(8,128)(2,1)}, bf16[8,512]{1,0:T(8,128)(2,1)S(1)}, u32[]{:S(2)}, u32[]{:S(2)}) collective-permute-start(bf16[8,512]{1,0:T(8,128)(2,1)} %get-tuple-element.17), channel_id=1, source_target_pairs={{16,1},{17,2},{18,3},{19,4},{20,5},{21,6},{22,7},{23,8},{24,9},{25... | collective-permute-start | bytes 24584 | tf_op jit(solution)/shard_map/ppermute | solution.py:411
  11.3 0.9 copy-start
  13.5 19.9 %copy-start.1 = (bf16[1,3,3,128,128]{4,3,2,1,0:T(8,128)(2,1)S(1)}, bf16[1,3,3,128,128]{4,3,2,1,0:T(8,128)(2,1)}, u32[]{:S(2)}) copy-start(bf16[1,3,3,128,128]{4,3,2,1,0:T(8,128)(2,1)} %param.11) | copy-start | bytes 884740
  36.7 12.4 %all-to-all-start.1 = ((bf16[8,24,1024]{2,1,0:T(8,128)(2,1)}), bf16[8,24,1024]{2,1,0:T(8,128)(2,1)S(1)}, u32[]{:S(2)}, u32[]{:S(2)}) async-start(bf16[8,24,1024]{2,1,0:T(8,128)(2,1)} %shard_map.87), calls=%async_computation.1 | async-start | bytes 786432 | tf_op jit(solution)/shard_map/all_to_all | solution.py:242
  41.2 1.7 %collective-permute-start.5 = (bf16[3,3,128,128]{3,2,1,0:T(8,128)(2,1)S(1)}, bf16[3,3,128,128]{3,2,1,0:T(8,128)(2,1)S(1)}, u32[]{:S(2)}, u32[]{:S(2)}) collective-permute-start(bf16[3,3,128,128]{3,2,1,0:T(8,128)(2,1)S(1)} %shard_map.89), channel_id=1, source_target_pairs={{0,16},{16,0},{1,17},{17,1},{2,18},{18,2},{3,19},{19,3},{4,20},{20... | collective-permute-start | bytes 884744 | tf_op jit(solution)/shard_map/ppermute | solution.py:229
  63.1 1.7 %collective-permute-start.6 = (bf16[3,3,128,128]{3,2,1,0:T(8,128)(2,1)S(1)}, bf16[3,3,128,128]{3,2,1,0:T(8,128)(2,1)S(1)}, u32[]{:S(2)}, u32[]{:S(2)}) collective-permute-start(bf16[3,3,128,128]{3,2,1,0:T(8,128)(2,1)S(1)} %shard_map.93), channel_id=1, source_target_pairs={{0,16},{16,0},{1,17},{17,1},{2,18},{18,2},{3,19},{19,3},{4,20},{20... | collective-permute-start | bytes 884744 | tf_op jit(solution)/shard_map/ppermute | solution.py:229
  65.7 9.3 %copy-start.2 = (bf16[1,3,3,128,128]{4,3,2,1,0:T(8,128)(2,1)S(1)}, bf16[1,3,3,128,128]{4,3,2,1,0:T(8,128)(2,1)}, u32[]{:S(2)}) copy-start(bf16[1,3,3,128,128]{4,3,2,1,0:T(8,128)(2,1)} %param.10) | copy-start | bytes 884740
  65.7 26.5 %all-to-all-start.3 = ((bf16[16,144,128]{2,1,0:T(8,128)(2,1)}), bf16[16,144,128]{2,1,0:T(8,128)(2,1)S(1)}, u32[]{:S(2)}, u32[]{:S(2)}) async-start(bf16[16,144,128]{2,1,0:T(8,128)(2,1)} %shard_map.94), calls=%async_computation.3 | async-start | bytes 1179648 | tf_op jit(solution)/shard_map/all_to_all | solution.py:242
  77.2 21.1 %collective-permute-start.7 = (bf16[4,16,1024]{2,1,0:T(8,128)(2,1)S(1)}, bf16[4,16,1024]{2,1,0:T(8,128)(2,1)S(1)}, u32[]{:S(2)}, u32[]{:S(2)}) collective-permute-start(bf16[4,16,1024]{2,1,0:T(8,128)(2,1)S(1)} %slice_bitcast_fusion), channel_id=1, source_target_pairs={{0,32},{32,0},{1,33},{33,1},{2,34},{34,2},{3,35},{35,3},{4,36},{36... | collective-permute-start | bytes 393224 | tf_op jit(solution)/shard_map/ppermute | solution.py:475
  93.3 21.8 %all-to-all-start.4 = ((bf16[16,144,128]{2,1,0:T(8,128)(2,1)}), bf16[16,144,128]{2,1,0:T(8,128)(2,1)S(1)}, u32[]{:S(2)}, u32[]{:S(2)}) async-start(bf16[16,144,128]{2,1,0:T(8,128)(2,1)} %shard_map.96), calls=%async_computation.4 | async-start | bytes 1179648 | tf_op jit(solution)/shard_map/all_to_all | solution.py:242
  98.4 5.2 %collective-permute-start.8 = (bf16[16,1024]{1,0:T(8,128)(2,1)S(1)}, bf16[16,1024]{1,0:T(8,128)(2,1)S(1)}, u32[]{:S(2)}, u32[]{:S(2)}) collective-permute-start(bf16[16,1024]{1,0:T(8,128)(2,1)S(1)} %get-tuple-element.25), channel_id=1, source_target_pairs={{0,64},{64,128},{128,192},{192,0},{1,65},{65,129},{129,193},{193,1... | collective-permute-start | bytes 98312 | tf_op jit(solution)/shard_map/ppermute | solution.py:479
  99.0 4.6 %collective-permute-start.10 = (bf16[16,1024]{1,0:T(8,128)(2,1)S(1)}, bf16[16,1024]{1,0:T(8,128)(2,1)S(1)}, u32[]{:S(2)}, u32[]{:S(2)}) collective-permute-start(bf16[16,1024]{1,0:T(8,128)(2,1)S(1)} %get-tuple-element.26), channel_id=1, source_target_pairs={{0,192},{64,0},{128,64},{192,128},{1,193},{65,1},{129,65},{193,129... | collective-permute-start | bytes 98312 | tf_op jit(solution)/shard_map/ppermute | solution.py:479
  101.7 5.4 %collective-permute-start.9 = (bf16[16,1024]{1,0:T(8,128)(2,1)S(1)}, bf16[16,1024]{1,0:T(8,128)(2,1)S(1)}, u32[]{:S(2)}, u32[]{:S(2)}) collective-permute-start(bf16[16,1024]{1,0:T(8,128)(2,1)S(1)} %get-tuple-element.27), channel_id=1, source_target_pairs={{0,128},{64,192},{128,0},{192,64},{1,129},{65,193},{129,1},{193,65... | collective-permute-start | bytes 98312 | tf_op jit(solution)/shard_map/ppermute | solution.py:479
  107.2 1.3 %collective-permute-start.11 = (bf16[16,512]{1,0:T(8,128)(2,1)S(1)}, bf16[16,512]{1,0:T(8,128)(2,1)S(1)}, u32[]{:S(2)}, u32[]{:S(2)}) collective-permute-start(bf16[16,512]{1,0:T(8,128)(2,1)S(1)} %get-tuple-element.29), channel_id=1, source_target_pairs={{0,16},{16,0},{1,17},{17,1},{2,18},{18,2},{3,19},{19,3},{4,20},{20... | collective-permute-start | bytes 49160 | tf_op jit(solution)/shard_map/ppermute | solution.py:486

commit v8 on v6

--- a/solution.py
+++ b/solution.py
@@ -162,28 +162,29 @@
 
 
 def filter_kernel(
-    orients, width, field, first, own, grad_ref, feat_ref, out_ref, feat_rows, grad_rows, held, done
+    orients, width, field, first, own, grad_ref, *refs
 ):
+    feat_refs, (out_ref, feat_rows, grad_rows, held, done) = refs[:-5], refs[-5:]
     chip, core = here()
     slot = core if own else 1 - core
     in_width = grad_rows.shape[0]
-    copies = [
-        pltpu.make_async_copy(
-            feat_ref.at[:, pl.ds(field * width, width), pl.ds(half * WIDE, WIDE)],
-            held.at[:, half],
-            done.at[half],
-        )
-        for half in range(2)
-    ]
-    for copy in copies:
-        copy.start()
+    part = pl.ds(field * width, width)
+    copies = []
+    for step, feat_ref in enumerate(feat_refs):
+        row = lax.rem(chip // 2 - step + len(feat_refs), len(feat_refs))
+        for y in range(2):
+            for c in range(2):
+                s = (row * 2 + lax.rem(chip + y, 2)) * 2 + lax.rem(core + c, 2)
+                source = feat_ref.at[y, c, part]
+                copies.append(pltpu.make_async_copy(source, held.at[s], done.at[len(copies)]))
+                copies[-1].start()
     interleave(grad_ref, grad_rows, orients, grad_ref.shape[1] - in_width, 0)
     grads = grad_rows[...].reshape(in_width * orients, WIDE).astype(jnp.bfloat16)
     for copy in copies:
         copy.wait()
     for g in range(orients):
         s = lax.rem(g + 2 * chip + slot, orients)
-        feat_rows[:, g, :] = held[s // 2, lax.rem(s, 2)].astype(jnp.float32)
+        feat_rows[:, g, :] = held[s].astype(jnp.float32)
     feats = feat_rows[...].reshape(width * orients, WIDE).astype(jnp.bfloat16)
     for j in range(3):
         window = grads[(first - j) * orients : (first - j + width) * orients]
@@ -207,7 +208,7 @@
 
 
 def filter_terms(feats, field, width, grads, in_width, first):
-    orients = 2 * feats.shape[0]
+    orients = 4 * len(feats)
 
     def terms(own):
         return call(
@@ -216,13 +217,13 @@
             [
                 pltpu.VMEM((width, orients, WIDE), jnp.float32),
                 pltpu.VMEM((in_width, orients, WIDE), jnp.float32),
-                pltpu.VMEM((orients // 2, 2, width, WIDE), jnp.bfloat16),
-                pltpu.SemaphoreType.DMA((2,)),
+                pltpu.VMEM((orients, width, WIDE), jnp.bfloat16),
+                pltpu.SemaphoreType.DMA((orients,)),
             ],
             6 * width * orients * WIDE * WIDE,
             grads,
-            feats,
-            space=(VMEM, HBM),
+            *feats,
+            space=(VMEM, *[HBM] * len(feats)),
             room=52,
         )
 
@@ -263,8 +264,8 @@
     both = stay[...].astype(jnp.float32) + came[...].astype(jnp.float32)
     lines = both.reshape(-1, CHAN)
     count, size, _ = out_ref.shape
-    lines = jnp.concatenate([lines, jnp.zeros((count * size - lines.shape[0], CHAN), jnp.float32)])
-    out_ref[...] = lines.reshape(out_ref.shape).astype(jnp.bfloat16)
+    for n in range(count):
+        out_ref[n] = lines[n * size : (n + 1) * size].astype(jnp.bfloat16)
 
 
 def half_terms(pair):
@@ -274,8 +275,7 @@
     both = pltpu.VMEM(mine.shape, jnp.float32)
     stay, leave = call(halves_kernel, (half, half), [both], mine.size, mine, theirs)
     came = lax.ppermute(leave, AZ, [(i, (i + count // 2) % count) for i in range(count)])
-    dealt = -(-size // 16) * 8
-    shape = jax.ShapeDtypeStruct((count, dealt, CHAN), jnp.bfloat16)
+    shape = jax.ShapeDtypeStruct((count, size // 2, CHAN), jnp.bfloat16)
     return leave, call(deal_kernel, shape, [], mine.size, stay, came)
 
 
@@ -297,31 +297,25 @@
 
 def reduce_kernel(size, parts_ref, out_ref, held, done):
     count = parts_ref.shape[0]
-    dealt = parts_ref.shape[1] - size
     total = [parts_ref[n].astype(jnp.float32) for n in (0, count // 2)]
     for n in range(1, count // 2):
         total[0] = total[0] + parts_ref[n].astype(jnp.float32)
         total[1] = total[1] + parts_ref[count // 2 + n].astype(jnp.float32)
-    held[:size] = (total[0][:size] + total[1][:size]).astype(jnp.bfloat16)
-    held[size : size + dealt] = total[0][size:].astype(jnp.bfloat16)
-    held[size + dealt :] = total[1][size:].astype(jnp.bfloat16)
+    whole = [total[0][:size] + total[1][:size], total[0][size:], total[1][size:]]
+    held[...] = jnp.concatenate(whole).astype(jnp.bfloat16)
     copy_all([(held, out_ref.at[n]) for n in range(count)], done)
 
 
 def finish_kernel(size, scale, whole_ref, one_ref, two_ref, held_one, held_two, done):
     count = whole_ref.shape[0]
     dealt = (whole_ref.shape[1] - size) // 2
-    lines = two_ref.shape[1]
     held_one[...] = whole_ref[:, :size].astype(jnp.float32) * scale
     first = pltpu.make_async_copy(held_one, one_ref, done.at[0])
     first.start()
     for side in range(2):
         for n in range(count):
-            start, end = n * dealt, min((n + 1) * dealt, lines)
-            if end > start:
-                row = size + side * dealt
-                part = whole_ref[n, row : row + dealt].astype(jnp.float32) * scale
-                held_two[side, start:end] = part[: end - start]
+            part = whole_ref[n, size:].astype(jnp.float32) * scale
+            held_two[side, n * dealt : (n + 1) * dealt] = part[side * dealt : (side + 1) * dealt]
     second = pltpu.make_async_copy(held_two, two_ref, done.at[1])
     second.start()
     first.wait()
@@ -369,12 +363,12 @@
         grad = [grad[half - 2 :], zeros[:6]]
         pre = [pre[half - 1 :], zeros[:7]]
     own = slice(side * half, (side + 1) * half)
-    return jnp.concatenate([act[own], given[own], *grad, *pre])
+    return jnp.concatenate([act[own], given[own]]), jnp.concatenate([*grad, *pre])
 
 
 def lanes_kernel(*refs):
-    given, (mine_ref, away_ref, same_ref, cross_ref) = refs[:4], refs[4:8]
-    held, done = refs[8:12], refs[12]
+    given, (same_ref, cross_ref), sides = refs[:4], refs[4:6], refs[6:10]
+    held, done = refs[10:14], refs[14]
     _, core = here()
     copy_all(zip(given, held), done)
     inputs_ref, pre_one_ref, pre_two_ref, cotangent_ref = held
@@ -386,9 +380,10 @@
         )
         act = pre / (1.0 + jnp.exp(-pre))
         fields = (act, inputs_ref[0, row].astype(jnp.float32), grad, pre)
-        left, right = stacked(*fields, 0), stacked(*fields, 1)
-        mine_ref[:, lanes] = jnp.where(core == 0, left, right).astype(jnp.bfloat16)
-        away_ref[:, lanes] = jnp.where(core == 0, right, left).astype(jnp.bfloat16)
+        for n, (left, right) in enumerate(zip(stacked(*fields, 0), stacked(*fields, 1))):
+            mine_ref, away_ref = sides[2 * n : 2 * n + 2]
+            mine_ref[:, lanes] = jnp.where(core == 0, left, right).astype(jnp.bfloat16)
+            away_ref[:, lanes] = jnp.where(core == 0, right, left).astype(jnp.bfloat16)
         pad = jnp.zeros((5, CHAN), jnp.float32)
         low = jnp.concatenate([grad[:2], pre[:1], pad])
         high = jnp.concatenate([grad[-2:], pre[-1:], pad])
@@ -398,7 +393,6 @@
 
 def rims_kernel(mine_ref, partner_ref, same_ref, cross_ref, out_ref, pre_ref, held, done):
     _, core = here()
-    ahead = held.shape[0] - pre_ref.shape[0]
     rows = pre_ref.shape[0]
     used = rows - 8
     at = lax.broadcasted_iota(jnp.int32, (rows, WIDE), 0)
@@ -408,16 +402,16 @@
     for body_ref, edge_ref in ((mine_ref, same_ref), (partner_ref, cross_ref)):
         body = body_ref[...].astype(jnp.float32)
         edge = edge_ref[...].astype(jnp.float32)
-        grad = body[ahead : ahead + rows]
+        grad = body[:rows]
         grad = jnp.where(at == grad_at, edge[0:1], grad)
         grad = jnp.where(at == grad_at + 1, edge[1:2], grad)
-        pre = jnp.where(at == pre_at, edge[2:3], body[ahead + rows :])
-        filled.append(jnp.concatenate([body[:ahead], grad, pre]).astype(jnp.bfloat16))
+        pre = jnp.where(at == pre_at, edge[2:3], body[rows:])
+        filled.append(jnp.concatenate([grad, pre]).astype(jnp.bfloat16))
     first = jnp.where(core == 0, filled[0], filled[1])
     second = jnp.where(core == 0, filled[1], filled[0])
     for lanes, part in ((slice(0, WIDE), first), (slice(WIDE, 2 * WIDE), second)):
-        held[:, lanes] = part[: ahead + rows]
-        pre_ref[:, lanes] = part[ahead + rows :]
+        held[:, lanes] = part[:rows]
+        pre_ref[:, lanes] = part[rows:]
     copy_all([(held, out_ref.at[n]) for n in range(out_ref.shape[0])], done)
 
 
@@ -435,10 +429,10 @@
     def narrow(*shape):
         return jax.ShapeDtypeStruct(shape, jnp.bfloat16)
 
-    rows = columns + 2 * padded
-    mine, away, same, cross = call(
+    edge, block, rims = narrow(8, WIDE), narrow(columns, WIDE), narrow(2 * padded, WIDE)
+    same, cross, feats, feats_away, mine, away = call(
         lanes_kernel,
-        (narrow(rows, WIDE), narrow(rows, WIDE), narrow(8, WIDE), narrow(8, WIDE)),
+        (edge, edge, block, block, rims, rims),
         [pltpu.VMEM(inputs.shape, jnp.bfloat16)] * 4 + [pltpu.SemaphoreType.DMA((4,))],
         inputs.size * 20,
         inputs,
@@ -454,11 +448,13 @@
     same = lax.ppermute(same, (CORE, AZ), place(0, after_me, 0) + place(1, before_me, 1))
     cross = lax.ppermute(cross, (CORE, AZ), place(1, after_me, 0) + place(0, before_me, 1))
     partner = lax.ppermute(away, CORE, SWAP)
+    pair = [feats, lax.ppermute(feats_away, CORE, SWAP)]
+    along_y = [lax.ppermute(part, CHIPS[1], SWAP) for part in pair]
     sent, pre_pair = call(
         rims_kernel,
-        (narrow(chips, columns + padded, 2 * WIDE), narrow(padded, 2 * WIDE)),
+        (narrow(chips, padded, 2 * WIDE), narrow(padded, 2 * WIDE)),
         [
-            pltpu.VMEM((columns + padded, 2 * WIDE), jnp.bfloat16),
+            pltpu.VMEM((padded, 2 * WIDE), jnp.bfloat16),
             pltpu.SemaphoreType.DMA((chips,)),
         ],
         inputs.size * 20,
@@ -470,7 +466,15 @@
     )
     other_two = lax.ppermute(filt_two[0], CORE, SWAP)
     other_one = lax.ppermute(filt_one[0], CORE, SWAP)
-    first_blocks = exchange(after(sent, (other_two, other_one)), CHIPS)
+    first_blocks = exchange(after(sent, (other_two, other_one, along_y)), CHIPS)
+
+    along_x = lax.axis_size(CHIPS[0])
+    near = jnp.stack([jnp.stack(pair), jnp.stack(along_y)])
+    all_feats = [near] + [
+        lax.ppermute(near, CHIPS[0], [(i, (i + step) % along_x) for i in range(along_x)])
+        for step in range(1, along_x)
+    ]
+    first_blocks = after(first_blocks, near)
 
     shares = conv(
         conv_two_kernel,
@@ -488,7 +492,7 @@
         HBM,
         52,
     )
-    pair_two = filter_terms(first_blocks, 0, half, first_blocks, padded, 3)
+    pair_two = filter_terms(all_feats, 0, half, first_blocks, padded, 3)
     leave, terms_two = half_terms(pair_two)
     arrived = after(exchange(shares, CHIPS), leave)
     copies = call(
@@ -501,10 +505,8 @@
         out_space=HBM,
     )
     all_grad_one = after(exchange(copies, CHIPS), terms_two)
-    joined = joined_terms(filter_terms(first_blocks, 1, half, all_grad_one, padded, 2), terms_two)
+    joined = joined_terms(filter_terms(all_feats, 1, half, all_grad_one, padded, 2), terms_two)
     filt_grad_one, filt_grad_two = summed_over_az(joined, filt_one.size // CHAN // az_count, scale)
-
-    along_x = lax.axis_size(CHIPS[0])
 
     shares = conv(
         conv_one_kernel,

time: 115 us -> 117 us (1.017)
  blocking collectives: 19.9 us -> 0 us
  starting transfers between devices: 36.5 us -> 49 us
  waiting for transfers between devices: 39.2 us -> 46.5 us
  Pallas kernels: 16.6 us -> 17.8 us
    all_to_all x1 -> x0, blocking collectives: 19.9 us -> none  [exchange(): return lax.all_to_all(parts, axes, 0, 0, tiled=True)]
    ppermute x0 -> x6, starting transfers between devices: none -> 8.73 us  [the longest x3 5.01 us: shards(): lax.ppermute(near, CHIPS[0], [(i, (i + step) % along_x) for i in range(al...]
    all_to_all x4 -> x5, starting transfers between devices: 21.4 us -> 25.1 us  [exchange(): return lax.all_to_all(parts, axes, 0, 0, tiled=True)]
    ppermute x0 -> x6, waiting for transfers between devices: none -> 3.16 us  [the longest x2 3.15 us: shards(): along_y = [lax.ppermute(part, CHIPS[1], SWAP) for part in pair]]
    all_to_all x4 -> x5, waiting for transfers between devices: 25.1 us -> 27.4 us  [exchange(): return lax.all_to_all(parts, axes, 0, 0, tiled=True)]
    ppermute x1, waiting for transfers between devices: 0.01 us -> 1.89 us  [shards(): lax.ppermute(same, (CORE, AZ), place(0, after_me, 0) + place(1, before_me...]
    pallas_call x14, Pallas kernels: 16.6 us -> 17.8 us  [call(): pl.pallas_call(kernel, out_shape=out_shape, in_specs=in_specs, out_specs=...]
    ppermute x1, waiting for transfers between devices: 5.65 us -> 6.87 us  [half_terms(): lax.ppermute(leave, AZ, [(i, (i + count // 2) % count) for i in range(cou...]
  transfers between devices with their start and end apart: 17 -> 24, of which waited for: 11 -> 13; matrix products, arithmetic and copies ran while one was open for 1% -> 1% of each run, Pallas kernels for 8% -> 12%
where the time goes in v8:
time: 117 us; the launch traced here: 116 us
  starting transfers between devices  49 us (42%)
  waiting for transfers between devices  46.5 us (40%)
  Pallas kernels  17.8 us (15%)
    all_to_all x5, waiting for transfers between devices, exchange(): return lax.all_to_all(parts, axes, 0, 0, tiled=True)  27.4 us
    all_to_all x5, starting transfers between devices, exchange(): return lax.all_to_all(parts, axes, 0, 0, tiled=True)  25.1 us
    pallas_call x14, Pallas kernels, call(): pl.pallas_call(kernel, out_shape=out_shape, in_specs=in_specs, out_specs=...  17.8 us
    ppermute x1, waiting for transfers between devices, half_terms(): lax.ppermute(leave, AZ, [(i, (i + count // 2) % count) for i in range(cou...  6.87 us
    ppermute x3, starting transfers between devices, shards(): lax.ppermute(near, CHIPS[0], [(i, (i + step) % along_x) for i in range(al...  5.01 us
    ppermute x3, starting transfers between devices, shards(): lax.ppermute(partial[step], CHIPS[0], [(i, (i + step) % along_x) for i in...  4.37 us
    ppermute x3, waiting for transfers between devices, shards(): lax.ppermute(partial[step], CHIPS[0], [(i, (i + step) % along_x) for i in...  4.36 us
    ppermute x1, starting transfers between devices, shards(): lax.ppermute(cross, (CORE, AZ), place(1, after_me, 0) + place(0, before_m...  3.85 us
  transfers between devices with their start and end apart: 24, of which 13 were waited for; matrix products, arithmetic and copies ran while one was open for 1% of the time, Pallas kernels for 12%

profile of v8, /device:TPU:32, one launch (start us, length us, event | category | flops | bytes accessed | tf_op | source)
XLA Modules:
  0.0 116.0 jit_solution(18379101882808499297)
XLA Ops:
  1.2 1.6 %shard_map.85 = (bf16[8,512]{1,0:T(8,128)(2,1)}, bf16[8,512]{1,0:T(8,128)(2,1)}, bf16[32,512]{1,0:T(8,128)(2,1)}, bf16[32,512]{1,0:T(8,128)(2,1)}, bf16[48,512]{1,0:T(8,128)(2,1)}, /*index=5*/bf16[48,512]{1,0:T(8,128)(2,1)}) custom-call(bf16[1,4,32,128]{3,2,1,0:T(8,128)(2,1)} %refs_0_.1, bf16[1,4,32,128]{3,2,1,0:T(8,128)(2,1)} %refs_1_.1, ...), custom_call_target="tpu_custom_call" | custom-call | flops 327680 | bytes 262144 | tf_op jit(solution)/shard_map/pallas_call | solution.py:43
  3.0 1.9 %collective-permute-start.1 = (bf16[8,512]{1,0:T(8,128)(2,1)}, bf16[8,512]{1,0:T(8,128)(2,1)S(1)}, u32[]{:S(2)}, u32[]{:S(2)}) collective-permute-start(bf16[8,512]{1,0:T(8,128)(2,1)} %get-tuple-element.22), channel_id=1, source_target_pairs={{0,1},{1,2},{2,3},{3,4},{4,5},{5,6},{6,7},{7,8},{8,9},{9,10},{10,1... | collective-permute-start | bytes 24584 | tf_op jit(solution)/shard_map/ppermute | solution.py:448
  5.0 1.9 %collective-permute-done.1.same_ref = bf16[8,512]{1,0:T(8,128)(2,1)S(1)} collective-permute-done((bf16[8,512]{1,0:T(8,128)(2,1)}, bf16[8,512]{1,0:T(8,128)(2,1)S(1)}, u32[]{:S(2)}, u32[]{:S(2)}) %collective-permute-start.1) | collective-permute-done | bytes 8224 | tf_op jit(solution)/shard_map/ppermute | solution.py:448
  6.9 3.9 %collective-permute-start.2 = (bf16[8,512]{1,0:T(8,128)(2,1)}, bf16[8,512]{1,0:T(8,128)(2,1)S(1)}, u32[]{:S(2)}, u32[]{:S(2)}) collective-permute-start(bf16[8,512]{1,0:T(8,128)(2,1)} %get-tuple-element.23), channel_id=1, source_target_pairs={{16,1},{17,2},{18,3},{19,4},{20,5},{21,6},{22,7},{23,8},{24,9},{25... | collective-permute-start | bytes 24584 | tf_op jit(solution)/shard_map/ppermute | solution.py:449
  10.7 1.6 %collective-permute-done.2.cross_ref = bf16[8,512]{1,0:T(8,128)(2,1)S(1)} collective-permute-done((bf16[8,512]{1,0:T(8,128)(2,1)}, bf16[8,512]{1,0:T(8,128)(2,1)S(1)}, u32[]{:S(2)}, u32[]{:S(2)}) %collective-permute-start.2) | collective-permute-done | bytes 8224 | tf_op jit(solution)/shard_map/ppermute | solution.py:449
  12.3 2.9 %collective-permute-start.5 = (bf16[32,512]{1,0:T(8,128)(2,1)}, bf16[32,512]{1,0:T(8,128)(2,1)S(1)}, u32[]{:S(2)}, u32[]{:S(2)}) collective-permute-start(bf16[32,512]{1,0:T(8,128)(2,1)} %get-tuple-element.25), channel_id=1, source_target_pairs={{0,32},{32,0},{1,33},{33,1},{2,34},{34,2},{3,35},{35,3},{4,36},{36... | collective-permute-start | bytes 98312 | tf_op jit(solution)/shard_map/ppermute | solution.py:452
  18.2 2.5 %collective-permute-done.7 = bf16[32,512]{1,0:T(8,128)(2,1)S(1)} collective-permute-done((bf16[32,512]{1,0:T(8,128)(2,1)S(1)}, bf16[32,512]{1,0:T(8,128)(2,1)S(1)}, u32[]{:S(2)}, u32[]{:S(2)}) %collective-permute-start.7) | collective-permute-done | bytes 32800 | tf_op jit(solution)/shard_map/ppermute | solution.py:452
  20.6 4.5 %all-to-all-start = ((bf16[8,24,1024]{2,1,0:T(8,128)(2,1)}), bf16[8,24,1024]{2,1,0:T(8,128)(2,1)S(1)}, u32[]{:S(2)}, u32[]{:S(2)}) async-start(bf16[8,24,1024]{2,1,0:T(8,128)(2,1)} %get-tuple-element.27), calls=%async_computation | async-start | bytes 786432 | tf_op jit(solution)/shard_map/all_to_all | solution.py:243
  25.2 3.3 %collective-permute-start.10 = (bf16[2,2,32,512]{3,2,1,0:T(8,128)(2,1)S(1)}, bf16[2,2,32,512]{3,2,1,0:T(8,128)(2,1)S(1)}, u32[]{:S(2)}, u32[]{:S(2)}) collective-permute-start(bf16[2,2,32,512]{3,2,1,0:T(8,128)(2,1)S(1)} %pad_maximum_fusion.refs_0_), channel_id=1, source_target_pairs={{0,192},{64,0},{128,64},{192,128},{1,193},{65,1},{129,65},{193,129... | collective-permute-start | bytes 393224 | tf_op jit(solution)/shard_map/ppermute | solution.py:474
  30.2 5.5 %all-to-all-done.blocks_ref.grad_ref = bf16[8,24,1024]{2,1,0:T(8,128)(2,1)S(1)} async-done(((bf16[8,24,1024]{2,1,0:T(8,128)(2,1)}), bf16[8,24,1024]{2,1,0:T(8,128)(2,1)S(1)}, u32[]{:S(2)}, u32[]{:S(2)}) %all-to-all-start) | async-done | bytes 393248 | tf_op jit(solution)/shard_map/all_to_all | solution.py:243
  35.7 3.3 %shard_map.87 = bf16[8,24,1024]{2,1,0:T(8,128)(2,1)} custom-call(bf16[8,24,1024]{2,1,0:T(8,128)(2,1)S(1)} %all-to-all-done.blocks_ref.grad_ref, bf16[3,3,128,128]{3,2,1,0:T(8,128)(2,1)S(1)} %bitcast.53, bf16[3,3,128,128]{3,2,1,0:T(8,128)(2,1)S(1)} %collective-permute-done.3.other_ref), custom_call_target="tpu_custom_call" | custom-call | flops 905969664 | bytes 1966080 | tf_op jit(solution)/shard_map/pallas_call | solution.py:43
  39.0 3.5 %all-to-all-start.1 = ((bf16[8,24,1024]{2,1,0:T(8,128)(2,1)}), bf16[8,24,1024]{2,1,0:T(8,128)(2,1)S(1)}, u32[]{:S(2)}, u32[]{:S(2)}) async-start(bf16[8,24,1024]{2,1,0:T(8,128)(2,1)} %shard_map.87), calls=%async_computation.1 | async-start | bytes 786432 | tf_op jit(solution)/shard_map/all_to_all | solution.py:243
  42.5 1.5 %shard_map.89 = bf16[3,3,128,128]{3,2,1,0:T(8,128)(2,1)S(1)} custom-call(bf16[8,24,1024]{2,1,0:T(8,128)(2,1)S(1)} %all-to-all-done.blocks_ref.grad_ref, bf16[2,2,32,512]{3,2,1,0:T(8,128)(2,1)S(1)} %pad_maximum_fusion.refs_0_, bf16[2,2,32,512]{3,2,1,0:T(8,128)(2,1)S(1)} %collective-permute-done.8.refs_1_, ...), custom_call_target="tpu_custom_call" | custom-call | flops 402653184 | bytes 1835008 | tf_op jit(solution)/shard_map/pallas_call | solution.py:43
  46.0 5.4 %all-to-all-done.1.parts_ref = bf16[8,24,1024]{2,1,0:T(8,128)(2,1)S(1)} async-done(((bf16[8,24,1024]{2,1,0:T(8,128)(2,1)}), bf16[8,24,1024]{2,1,0:T(8,128)(2,1)S(1)}, u32[]{:S(2)}, u32[]{:S(2)}) %all-to-all-start.1) | async-done | bytes 393248 | tf_op jit(solution)/shard_map/all_to_all | solution.py:243
  52.3 3.5 %all-to-all-start.2 = ((bf16[8,24,1024]{2,1,0:T(8,128)(2,1)}), bf16[8,24,1024]{2,1,0:T(8,128)(2,1)S(1)}, u32[]{:S(2)}, u32[]{:S(2)}) async-start(bf16[8,24,1024]{2,1,0:T(8,128)(2,1)} %shard_map.91), calls=%async_computation.2 | async-start | bytes 786432 | tf_op jit(solution)/shard_map/all_to_all | solution.py:243
  56.7 6.9 %collective-permute-done.12.came = bf16[8,72,128]{2,1,0:T(8,128)(2,1)S(1)} collective-permute-done((bf16[8,72,128]{2,1,0:T(8,128)(2,1)S(1)}, bf16[8,72,128]{2,1,0:T(8,128)(2,1)S(1)}, u32[]{:S(2)}, u32[]{:S(2)}) %collective-permute-start.12) | collective-permute-done | bytes 147488 | tf_op jit(solution)/shard_map/ppermute | solution.py:277
  68.8 8.8 %all-to-all-start.3 = ((bf16[16,108,128]{2,1,0:T(8,128)(2,1)}), bf16[16,108,128]{2,1,0:T(8,128)(2,1)S(1)}, u32[]{:S(2)}, u32[]{:S(2)}) async-start(bf16[16,108,128]{2,1,0:T(8,128)(2,1)} %shard_map.95), calls=%async_computation.3 | async-start | bytes 917504 | tf_op jit(solution)/shard_map/all_to_all | solution.py:243
  77.6 2.2 %shard_map.96 = bf16[2,4,16,1024]{3,2,1,0:T(8,128)(2,1)S(1)} custom-call(bf16[8,24,1024]{2,1,0:T(8,128)(2,1)S(1)} %all-to-all-done.2.grad_ref.blocks_ref, bf16[3,3,128,128]{3,2,1,0:T(8,128)(2,1)S(1)} %bitcast.55, bf16[3,3,128,128]{3,2,1,0:T(8,128)(2,1)S(1)} %collective-permute-done.4.other_ref), custom_call_target="tpu_custom_call" | custom-call | flops 805306368 | bytes 1966080 | tf_op jit(solution)/shard_map/pallas_call | solution.py:43
  79.8 3.0 %collective-permute-start.14 = (bf16[4,16,1024]{2,1,0:T(8,128)(2,1)S(1)}, bf16[4,16,1024]{2,1,0:T(8,128)(2,1)S(1)}, u32[]{:S(2)}, u32[]{:S(2)}) collective-permute-start(bf16[4,16,1024]{2,1,0:T(8,128)(2,1)S(1)} %slice_bitcast_fusion), channel_id=1, source_target_pairs={{0,32},{32,0},{1,33},{33,1},{2,34},{34,2},{3,35},{35,3},{4,36},{36... | collective-permute-start | bytes 393224 | tf_op jit(solution)/shard_map/ppermute | solution.py:521
  82.8 9.5 %all-to-all-done.3.parts_ref = bf16[16,108,128]{2,1,0:T(8,128)(2,1)S(1)} async-done(((bf16[16,108,128]{2,1,0:T(8,128)(2,1)}), bf16[16,108,128]{2,1,0:T(8,128)(2,1)S(1)}, u32[]{:S(2)}, u32[]{:S(2)}) %all-to-all-start.3) | async-done | bytes 442400 | tf_op jit(solution)/shard_map/all_to_all | solution.py:243
  93.2 4.8 %all-to-all-start.4 = ((bf16[16,144,128]{2,1,0:T(8,128)(2,1)}), bf16[16,144,128]{2,1,0:T(8,128)(2,1)S(1)}, u32[]{:S(2)}, u32[]{:S(2)}) async-start(bf16[16,144,128]{2,1,0:T(8,128)(2,1)} %shard_map.97), calls=%async_computation.4 | async-start | bytes 1179648 | tf_op jit(solution)/shard_map/all_to_all | solution.py:243
  98.9 2.6 %collective-permute-start.17 = (bf16[16,1024]{1,0:T(8,128)(2,1)S(1)}, bf16[16,1024]{1,0:T(8,128)(2,1)S(1)}, u32[]{:S(2)}, u32[]{:S(2)}) collective-permute-start(bf16[16,1024]{1,0:T(8,128)(2,1)S(1)} %get-tuple-element.38), channel_id=1, source_target_pairs={{0,192},{64,0},{128,64},{192,128},{1,193},{65,1},{129,65},{193,129... | collective-permute-start | bytes 98312 | tf_op jit(solution)/shard_map/ppermute | solution.py:525
  103.3 3.5 %collective-permute-done.16 = bf16[16,1024]{1,0:T(8,128)(2,1)S(1)} collective-permute-done((bf16[16,1024]{1,0:T(8,128)(2,1)S(1)}, bf16[16,1024]{1,0:T(8,128)(2,1)S(1)}, u32[]{:S(2)}, u32[]{:S(2)}) %collective-permute-start.16) | collective-permute-done | bytes 32800 | tf_op jit(solution)/shard_map/ppermute | solution.py:525
  108.8 6.0 %all-to-all-done.4.whole_ref = bf16[16,144,128]{2,1,0:T(8,128)(2,1)S(1)} async-done(((bf16[16,144,128]{2,1,0:T(8,128)(2,1)}), bf16[16,144,128]{2,1,0:T(8,128)(2,1)S(1)}, u32[]{:S(2)}, u32[]{:S(2)}) %all-to-all-start.4) | async-done | bytes 589856 | tf_op jit(solution)/shard_map/all_to_all | solution.py:243
  (57 shorter events, 21.2 us)
Async XLA Ops:
  0.6 20.0 %collective-permute-start.4 = (bf16[3,3,128,128]{3,2,1,0:T(8,128)(2,1)}, bf16[3,3,128,128]{3,2,1,0:T(8,128)(2,1)S(1)}, u32[]{:S(2)}, u32[]{:S(2)}) collective-permute-start(bf16[3,3,128,128]{3,2,1,0:T(8,128)(2,1)} %bitcast.54), channel_id=1, source_target_pairs={{0,16},{16,0},{1,17},{17,1},{2,18},{18,2},{3,19},{19,3},{4,20},{20... | collective-permute-start | bytes 884744 | tf_op jit(solution)/shard_map/ppermute | solution.py:468
  0.7 19.9 %collective-permute-start.3 = (bf16[3,3,128,128]{3,2,1,0:T(8,128)(2,1)}, bf16[3,3,128,128]{3,2,1,0:T(8,128)(2,1)S(1)}, u32[]{:S(2)}, u32[]{:S(2)}) collective-permute-start(bf16[3,3,128,128]{3,2,1,0:T(8,128)(2,1)} %bitcast.52), channel_id=1, source_target_pairs={{0,16},{16,0},{1,17},{17,1},{2,18},{18,2},{3,19},{19,3},{4,20},{20... | collective-permute-start | bytes 884744 | tf_op jit(solution)/shard_map/ppermute | solution.py:467
  2.8 12.4 %collective-permute-start.6 = (bf16[32,512]{1,0:T(8,128)(2,1)}, bf16[32,512]{1,0:T(8,128)(2,1)S(1)}, u32[]{:S(2)}, u32[]{:S(2)}) collective-permute-start(bf16[32,512]{1,0:T(8,128)(2,1)} %get-tuple-element.26), channel_id=1, source_target_pairs={{0,16},{16,0},{1,17},{17,1},{2,18},{18,2},{3,19},{19,3},{4,20},{20... | collective-permute-start | bytes 98312 | tf_op jit(solution)/shard_map/ppermute | solution.py:451
  3.0 3.9 %collective-permute-start.1 = (bf16[8,512]{1,0:T(8,128)(2,1)}, bf16[8,512]{1,0:T(8,128)(2,1)S(1)}, u32[]{:S(2)}, u32[]{:S(2)}) collective-permute-start(bf16[8,512]{1,0:T(8,128)(2,1)} %get-tuple-element.22), channel_id=1, source_target_pairs={{0,1},{1,2},{2,3},{3,4},{4,5},{5,6},{6,7},{7,8},{8,9},{9,10},{10,1... | collective-permute-start | bytes 24584 | tf_op jit(solution)/shard_map/ppermute | solution.py:448
  4.9 10.9 %collective-permute-start = (bf16[48,512]{1,0:T(8,128)(2,1)}, bf16[48,512]{1,0:T(8,128)(2,1)S(1)}, u32[]{:S(2)}, u32[]{:S(2)}) collective-permute-start(bf16[48,512]{1,0:T(8,128)(2,1)} %get-tuple-element.21), channel_id=1, source_target_pairs={{0,16},{16,0},{1,17},{17,1},{2,18},{18,2},{3,19},{19,3},{4,20},{20... | collective-permute-start | bytes 147464 | tf_op jit(solution)/shard_map/ppermute | solution.py:450
  6.9 5.4 %collective-permute-start.2 = (bf16[8,512]{1,0:T(8,128)(2,1)}, bf16[8,512]{1,0:T(8,128)(2,1)S(1)}, u32[]{:S(2)}, u32[]{:S(2)}) collective-permute-start(bf16[8,512]{1,0:T(8,128)(2,1)} %get-tuple-element.23), channel_id=1, source_target_pairs={{16,1},{17,2},{18,3},{19,4},{20,5},{21,6},{22,7},{23,8},{24,9},{25... | collective-permute-start | bytes 24584 | tf_op jit(solution)/shard_map/ppermute | solution.py:449
  12.3 5.9 %collective-permute-start.5 = (bf16[32,512]{1,0:T(8,128)(2,1)}, bf16[32,512]{1,0:T(8,128)(2,1)S(1)}, u32[]{:S(2)}, u32[]{:S(2)}) collective-permute-start(bf16[32,512]{1,0:T(8,128)(2,1)} %get-tuple-element.25), channel_id=1, source_target_pairs={{0,32},{32,0},{1,33},{33,1},{2,34},{34,2},{3,35},{35,3},{4,36},{36... | collective-permute-start | bytes 98312 | tf_op jit(solution)/shard_map/ppermute | solution.py:452
  15.2 5.4 %collective-permute-start.7 = (bf16[32,512]{1,0:T(8,128)(2,1)S(1)}, bf16[32,512]{1,0:T(8,128)(2,1)S(1)}, u32[]{:S(2)}, u32[]{:S(2)}) collective-permute-start(bf16[32,512]{1,0:T(8,128)(2,1)S(1)} %collective-permute-done.6), channel_id=1, source_target_pairs={{0,32},{32,0},{1,33},{33,1},{2,34},{34,2},{3,35},{35,3},{4,36},{36... | collective-permute-start | bytes 98312 | tf_op jit(solution)/shard_map/ppermute | solution.py:452
  20.6 15.1 %all-to-all-start = ((bf16[8,24,1024]{2,1,0:T(8,128)(2,1)}), bf16[8,24,1024]{2,1,0:T(8,128)(2,1)S(1)}, u32[]{:S(2)}, u32[]{:S(2)}) async-start(bf16[8,24,1024]{2,1,0:T(8,128)(2,1)} %get-tuple-element.27), calls=%async_computation | async-start | bytes 786432 | tf_op jit(solution)/shard_map/all_to_all | solution.py:243
  25.2 17.3 %collective-permute-start.10 = (bf16[2,2,32,512]{3,2,1,0:T(8,128)(2,1)S(1)}, bf16[2,2,32,512]{3,2,1,0:T(8,128)(2,1)S(1)}, u32[]{:S(2)}, u32[]{:S(2)}) collective-permute-start(bf16[2,2,32,512]{3,2,1,0:T(8,128)(2,1)S(1)} %pad_maximum_fusion.refs_0_), channel_id=1, source_target_pairs={{0,192},{64,0},{128,64},{192,128},{1,193},{65,1},{129,65},{193,129... | collective-permute-start | bytes 393224 | tf_op jit(solution)/shard_map/ppermute | solution.py:474
  28.5 14.0 %collective-permute-start.9 = (bf16[2,2,32,512]{3,2,1,0:T(8,128)(2,1)S(1)}, bf16[2,2,32,512]{3,2,1,0:T(8,128)(2,1)S(1)}, u32[]{:S(2)}, u32[]{:S(2)}) collective-permute-start(bf16[2,2,32,512]{3,2,1,0:T(8,128)(2,1)S(1)} %pad_maximum_fusion.refs_0_), channel_id=1, source_target_pairs={{0,128},{64,192},{128,0},{192,64},{1,129},{65,193},{129,1},{193,65... | collective-permute-start | bytes 393224 | tf_op jit(solution)/shard_map/ppermute | solution.py:474
  29.4 13.1 %collective-permute-start.8 = (bf16[2,2,32,512]{3,2,1,0:T(8,128)(2,1)S(1)}, bf16[2,2,32,512]{3,2,1,0:T(8,128)(2,1)S(1)}, u32[]{:S(2)}, u32[]{:S(2)}) collective-permute-start(bf16[2,2,32,512]{3,2,1,0:T(8,128)(2,1)S(1)} %pad_maximum_fusion.refs_0_), channel_id=1, source_target_pairs={{0,64},{64,128},{128,192},{192,0},{1,65},{65,129},{129,193},{193,1... | collective-permute-start | bytes 393224 | tf_op jit(solution)/shard_map/ppermute | solution.py:474
  39.0 12.4 %all-to-all-start.1 = ((bf16[8,24,1024]{2,1,0:T(8,128)(2,1)}), bf16[8,24,1024]{2,1,0:T(8,128)(2,1)S(1)}, u32[]{:S(2)}, u32[]{:S(2)}) async-start(bf16[8,24,1024]{2,1,0:T(8,128)(2,1)} %shard_map.87), calls=%async_computation.1 | async-start | bytes 786432 | tf_op jit(solution)/shard_map/all_to_all | solution.py:243
  44.0 1.9 %collective-permute-start.11 = (bf16[3,3,128,128]{3,2,1,0:T(8,128)(2,1)S(1)}, bf16[3,3,128,128]{3,2,1,0:T(8,128)(2,1)S(1)}, u32[]{:S(2)}, u32[]{:S(2)}) collective-permute-start(bf16[3,3,128,128]{3,2,1,0:T(8,128)(2,1)S(1)} %shard_map.89), channel_id=1, source_target_pairs={{0,16},{16,0},{1,17},{17,1},{2,18},{18,2},{3,19},{19,3},{4,20},{20... | collective-permute-start | bytes 884744 | tf_op jit(solution)/shard_map/ppermute | solution.py:230
  52.3 12.5 %all-to-all-start.2 = ((bf16[8,24,1024]{2,1,0:T(8,128)(2,1)}), bf16[8,24,1024]{2,1,0:T(8,128)(2,1)S(1)}, u32[]{:S(2)}, u32[]{:S(2)}) async-start(bf16[8,24,1024]{2,1,0:T(8,128)(2,1)} %shard_map.91), calls=%async_computation.2 | async-start | bytes 786432 | tf_op jit(solution)/shard_map/all_to_all | solution.py:243
  55.7 7.9 %collective-permute-start.12 = (bf16[8,72,128]{2,1,0:T(8,128)(2,1)S(1)}, bf16[8,72,128]{2,1,0:T(8,128)(2,1)S(1)}, u32[]{:S(2)}, u32[]{:S(2)}) collective-permute-start(bf16[8,72,128]{2,1,0:T(8,128)(2,1)S(1)} %get-tuple-element.29), channel_id=1, source_target_pairs={{0,8},{1,9},{2,10},{3,11},{4,12},{5,13},{6,14},{7,15},{8,0},{9,1},... | collective-permute-start | bytes 442376 | tf_op jit(solution)/shard_map/ppermute | solution.py:277
  66.2 1.7 %collective-permute-start.13 = (bf16[3,3,128,128]{3,2,1,0:T(8,128)(2,1)S(1)}, bf16[3,3,128,128]{3,2,1,0:T(8,128)(2,1)S(1)}, u32[]{:S(2)}, u32[]{:S(2)}) collective-permute-start(bf16[3,3,128,128]{3,2,1,0:T(8,128)(2,1)S(1)} %shard_map.94), channel_id=1, source_target_pairs={{0,16},{16,0},{1,17},{17,1},{2,18},{18,2},{3,19},{19,3},{4,20},{20... | collective-permute-start | bytes 884744 | tf_op jit(solution)/shard_map/ppermute | solution.py:230
  68.8 23.5 %all-to-all-start.3 = ((bf16[16,108,128]{2,1,0:T(8,128)(2,1)}), bf16[16,108,128]{2,1,0:T(8,128)(2,1)S(1)}, u32[]{:S(2)}, u32[]{:S(2)}) async-start(bf16[16,108,128]{2,1,0:T(8,128)(2,1)} %shard_map.95), calls=%async_computation.3 | async-start | bytes 917504 | tf_op jit(solution)/shard_map/all_to_all | solution.py:243
  79.8 18.3 %collective-permute-start.14 = (bf16[4,16,1024]{2,1,0:T(8,128)(2,1)S(1)}, bf16[4,16,1024]{2,1,0:T(8,128)(2,1)S(1)}, u32[]{:S(2)}, u32[]{:S(2)}) collective-permute-start(bf16[4,16,1024]{2,1,0:T(8,128)(2,1)S(1)} %slice_bitcast_fusion), channel_id=1, source_target_pairs={{0,32},{32,0},{1,33},{33,1},{2,34},{34,2},{3,35},{35,3},{4,36},{36... | collective-permute-start | bytes 393224 | tf_op jit(solution)/shard_map/ppermute | solution.py:521
  93.2 21.5 %all-to-all-start.4 = ((bf16[16,144,128]{2,1,0:T(8,128)(2,1)}), bf16[16,144,128]{2,1,0:T(8,128)(2,1)S(1)}, u32[]{:S(2)}, u32[]{:S(2)}) async-start(bf16[16,144,128]{2,1,0:T(8,128)(2,1)} %shard_map.97), calls=%async_computation.4 | async-start | bytes 1179648 | tf_op jit(solution)/shard_map/all_to_all | solution.py:243
  98.1 5.2 %collective-permute-start.15 = (bf16[16,1024]{1,0:T(8,128)(2,1)S(1)}, bf16[16,1024]{1,0:T(8,128)(2,1)S(1)}, u32[]{:S(2)}, u32[]{:S(2)}) collective-permute-start(bf16[16,1024]{1,0:T(8,128)(2,1)S(1)} %get-tuple-element.37), channel_id=1, source_target_pairs={{0,64},{64,128},{128,192},{192,0},{1,65},{65,129},{129,193},{193,1... | collective-permute-start | bytes 98312 | tf_op jit(solution)/shard_map/ppermute | solution.py:525
  98.9 4.5 %collective-permute-start.17 = (bf16[16,1024]{1,0:T(8,128)(2,1)S(1)}, bf16[16,1024]{1,0:T(8,128)(2,1)S(1)}, u32[]{:S(2)}, u32[]{:S(2)}) collective-permute-start(bf16[16,1024]{1,0:T(8,128)(2,1)S(1)} %get-tuple-element.38), channel_id=1, source_target_pairs={{0,192},{64,0},{128,64},{192,128},{1,193},{65,1},{129,65},{193,129... | collective-permute-start | bytes 98312 | tf_op jit(solution)/shard_map/ppermute | solution.py:525
  101.4 5.4 %collective-permute-start.16 = (bf16[16,1024]{1,0:T(8,128)(2,1)S(1)}, bf16[16,1024]{1,0:T(8,128)(2,1)S(1)}, u32[]{:S(2)}, u32[]{:S(2)}) collective-permute-start(bf16[16,1024]{1,0:T(8,128)(2,1)S(1)} %get-tuple-element.39), channel_id=1, source_target_pairs={{0,128},{64,192},{128,0},{192,64},{1,129},{65,193},{129,1},{193,65... | collective-permute-start | bytes 98312 | tf_op jit(solution)/shard_map/ppermute | solution.py:525
  106.9 1.3 %collective-permute-start.18 = (bf16[16,512]{1,0:T(8,128)(2,1)S(1)}, bf16[16,512]{1,0:T(8,128)(2,1)S(1)}, u32[]{:S(2)}, u32[]{:S(2)}) collective-permute-start(bf16[16,512]{1,0:T(8,128)(2,1)S(1)} %get-tuple-element.41), channel_id=1, source_target_pairs={{0,16},{16,0},{1,17},{17,1},{2,18},{18,2},{3,19},{19,3},{4,20},{20... | collective-permute-start | bytes 49160 | tf_op jit(solution)/shard_map/ppermute | solution.py:532
  (4 other events, 24.8 us)

commit v9 on v6

--- a/solution.py
+++ b/solution.py
@@ -263,8 +263,8 @@
     both = stay[...].astype(jnp.float32) + came[...].astype(jnp.float32)
     lines = both.reshape(-1, CHAN)
     count, size, _ = out_ref.shape
-    lines = jnp.concatenate([lines, jnp.zeros((count * size - lines.shape[0], CHAN), jnp.float32)])
-    out_ref[...] = lines.reshape(out_ref.shape).astype(jnp.bfloat16)
+    for n in range(count):
+        out_ref[n] = lines[n * size : (n + 1) * size].astype(jnp.bfloat16)
 
 
 def half_terms(pair):
@@ -274,8 +274,7 @@
     both = pltpu.VMEM(mine.shape, jnp.float32)
     stay, leave = call(halves_kernel, (half, half), [both], mine.size, mine, theirs)
     came = lax.ppermute(leave, AZ, [(i, (i + count // 2) % count) for i in range(count)])
-    dealt = -(-size // 16) * 8
-    shape = jax.ShapeDtypeStruct((count, dealt, CHAN), jnp.bfloat16)
+    shape = jax.ShapeDtypeStruct((count, size // 2, CHAN), jnp.bfloat16)
     return leave, call(deal_kernel, shape, [], mine.size, stay, came)
 
 
@@ -297,31 +296,25 @@
 
 def reduce_kernel(size, parts_ref, out_ref, held, done):
     count = parts_ref.shape[0]
-    dealt = parts_ref.shape[1] - size
     total = [parts_ref[n].astype(jnp.float32) for n in (0, count // 2)]
     for n in range(1, count // 2):
         total[0] = total[0] + parts_ref[n].astype(jnp.float32)
         total[1] = total[1] + parts_ref[count // 2 + n].astype(jnp.float32)
-    held[:size] = (total[0][:size] + total[1][:size]).astype(jnp.bfloat16)
-    held[size : size + dealt] = total[0][size:].astype(jnp.bfloat16)
-    held[size + dealt :] = total[1][size:].astype(jnp.bfloat16)
+    whole = [total[0][:size] + total[1][:size], total[0][size:], total[1][size:]]
+    held[...] = jnp.concatenate(whole).astype(jnp.bfloat16)
     copy_all([(held, out_ref.at[n]) for n in range(count)], done)
 
 
 def finish_kernel(size, scale, whole_ref, one_ref, two_ref, held_one, held_two, done):
     count = whole_ref.shape[0]
     dealt = (whole_ref.shape[1] - size) // 2
-    lines = two_ref.shape[1]
     held_one[...] = whole_ref[:, :size].astype(jnp.float32) * scale
     first = pltpu.make_async_copy(held_one, one_ref, done.at[0])
     first.start()
     for side in range(2):
         for n in range(count):
-            start, end = n * dealt, min((n + 1) * dealt, lines)
-            if end > start:
-                row = size + side * dealt
-                part = whole_ref[n, row : row + dealt].astype(jnp.float32) * scale
-                held_two[side, start:end] = part[: end - start]
+            part = whole_ref[n, size:].astype(jnp.float32) * scale
+            held_two[side, n * dealt : (n + 1) * dealt] = part[side * dealt : (side + 1) * dealt]
     second = pltpu.make_async_copy(held_two, two_ref, done.at[1])
     second.start()
     first.wait()
@@ -454,6 +447,7 @@
     same = lax.ppermute(same, (CORE, AZ), place(0, after_me, 0) + place(1, before_me, 1))
     cross = lax.ppermute(cross, (CORE, AZ), place(1, after_me, 0) + place(0, before_me, 1))
     partner = lax.ppermute(away, CORE, SWAP)
+    mine = mine + lax.shift_right_logical(core, 1).astype(mine.dtype)
     sent, pre_pair = call(
         rims_kernel,
         (narrow(chips, columns + padded, 2 * WIDE), narrow(padded, 2 * WIDE)),

time: 115 us -> 113 us (0.983)
  starting transfers between devices: 36.5 us -> 33 us
  blocking collectives: 19.9 us -> 22.4 us
  waiting for transfers between devices: 39.2 us -> 38 us
    all_to_all x1, blocking collectives: 19.9 us -> 22.4 us  [exchange(): return lax.all_to_all(parts, axes, 0, 0, tiled=True)]
    all_to_all x4, starting transfers between devices: 21.4 us -> 18.8 us  [exchange(): return lax.all_to_all(parts, axes, 0, 0, tiled=True)]
where the time goes in v9:
time: 113 us
  waiting for transfers between devices  38 us (34%)
  starting transfers between devices  33 us (29%)
  blocking collectives  22.4 us (20%)
  Pallas kernels  16.6 us (15%)
  other arithmetic  1.59 us (1%)
    all_to_all x4, waiting for transfers between devices, exchange(): return lax.all_to_all(parts, axes, 0, 0, tiled=True)  24 us
    all_to_all x1, blocking collectives, exchange(): return lax.all_to_all(parts, axes, 0, 0, tiled=True)  22.4 us
    all_to_all x4, starting transfers between devices, exchange(): return lax.all_to_all(parts, axes, 0, 0, tiled=True)  18.8 us
    pallas_call x14, Pallas kernels, call(): pl.pallas_call(kernel, out_shape=out_shape, in_specs=in_specs, out_specs=...  16.6 us
    ppermute x1, waiting for transfers between devices, half_terms(): lax.ppermute(leave, AZ, [(i, (i + count // 2) % count) for i in range(cou...  6.48 us
    ppermute x3, waiting for transfers between devices, shards(): lax.ppermute(partial[step], CHIPS[0], [(i, (i + step) % along_x) for i in...  4.71 us
    ppermute x1, starting transfers between devices, shards(): lax.ppermute(cross, (CORE, AZ), place(1, after_me, 0) + place(0, before_m...  4.48 us
    ppermute x3, starting transfers between devices, shards(): lax.ppermute(partial[step], CHIPS[0], [(i, (i + step) % along_x) for i in...  4.02 us
  transfers between devices with their start and end apart: 17, of which 11 were waited for; matrix products, arithmetic and copies ran while one was open for 1% of the time, Pallas kernels for 8%

profile of v9, /device:TPU:32, one launch (start us, length us, event | category | flops | bytes accessed | tf_op | source)
XLA Modules:
  0.0 112.7 jit_solution(582107172162530507)
XLA Ops:
  1.2 1.6 %shard_map.85 = (bf16[80,512]{1,0:T(8,128)(2,1)}, bf16[80,512]{1,0:T(8,128)(2,1)}, bf16[8,512]{1,0:T(8,128)(2,1)}, bf16[8,512]{1,0:T(8,128)(2,1)}) custom-call(bf16[1,4,32,128]{3,2,1,0:T(8,128)(2,1)} %refs_0_.1, bf16[1,4,32,128]{3,2,1,0:T(8,128)(2,1)} %refs_1_.1, bf16[1,4,32,128]{3,2,1,0:T(8,128)(2,1)} %refs_2_.1, bf16[1,4,32,128]{3,2,1,0:T(8,128)(2,1)} %refs_3_.1), custom_call_target="tpu_custom_call" | custom-call | flops 327680 | bytes 262144 | tf_op jit(solution)/shard_map/pallas_call | solution.py:43
  2.8 2.0 %collective-permute-start.1 = (bf16[8,512]{1,0:T(8,128)(2,1)}, bf16[8,512]{1,0:T(8,128)(2,1)S(1)}, u32[]{:S(2)}, u32[]{:S(2)}) collective-permute-start(bf16[8,512]{1,0:T(8,128)(2,1)} %get-tuple-element.19), channel_id=1, source_target_pairs={{0,1},{1,2},{2,3},{3,4},{4,5},{5,6},{6,7},{7,8},{8,9},{9,10},{10,1... | collective-permute-start | bytes 24584 | tf_op jit(solution)/shard_map/ppermute | solution.py:447
  4.8 4.5 %collective-permute-start.2 = (bf16[8,512]{1,0:T(8,128)(2,1)}, bf16[8,512]{1,0:T(8,128)(2,1)S(1)}, u32[]{:S(2)}, u32[]{:S(2)}) collective-permute-start(bf16[8,512]{1,0:T(8,128)(2,1)} %get-tuple-element.20), channel_id=1, source_target_pairs={{16,1},{17,2},{18,3},{19,4},{20,5},{21,6},{22,7},{23,8},{24,9},{25... | collective-permute-start | bytes 24584 | tf_op jit(solution)/shard_map/ppermute | solution.py:448
  10.9 1.3 %shard_map.86 = (bf16[8,56,1024]{2,1,0:T(8,128)(2,1)S(1)}, bf16[24,1024]{1,0:T(8,128)(2,1)S(1)}) custom-call(bf16[80,512]{1,0:T(8,128)(2,1)S(1)} %broadcast_add_fusion.mine_ref, bf16[80,512]{1,0:T(8,128)(2,1)S(1)} %collective-permute-done.partner_ref, bf16[8,512]{1,0:T(8,128)(2,1)S(1)} %collective-permute-done.1.same_ref, ...), custom_call_target="tpu_custom_call" | custom-call | flops 327680 | bytes 360448 | tf_op jit(solution)/shard_map/pallas_call | solution.py:43
  12.2 22.4 %all_to_all.25.blocks_ref.grad_ref.feat_ref = bf16[8,56,1024]{2,1,0:T(8,128)(2,1)S(1)} all-to-all(bf16[8,56,1024]{2,1,0:T(8,128)(2,1)S(1)} %get-tuple-element.22), channel_id=1, replica_groups=mesh['rot_x'=4,'rot_y'=2,'rot_c'=2,'az'=16] {'rot_x','rot_y'}, dimensions={0} | all-to-all | bytes 1835008 | tf_op jit(solution)/shard_map/all_to_all | solution.py:242
  34.7 3.3 %shard_map.87 = bf16[8,24,1024]{2,1,0:T(8,128)(2,1)} custom-call(bf16[8,56,1024]{2,1,0:T(8,128)(2,1)S(1)} %all_to_all.25.blocks_ref.grad_ref.feat_ref, bf16[3,3,128,128]{3,2,1,0:T(8,128)(2,1)S(1)} %bitcast.45, bf16[3,3,128,128]{3,2,1,0:T(8,128)(2,1)S(1)} %collective-permute-done.3.other_ref), custom_call_target="tpu_custom_call" | custom-call | flops 905969664 | bytes 3014656 | tf_op jit(solution)/shard_map/pallas_call | solution.py:43
  37.9 3.5 %all-to-all-start.1 = ((bf16[8,24,1024]{2,1,0:T(8,128)(2,1)}), bf16[8,24,1024]{2,1,0:T(8,128)(2,1)S(1)}, u32[]{:S(2)}, u32[]{:S(2)}) async-start(bf16[8,24,1024]{2,1,0:T(8,128)(2,1)} %shard_map.87), calls=%async_computation.1 | async-start | bytes 786432 | tf_op jit(solution)/shard_map/all_to_all | solution.py:242
  41.4 1.1 shard_map.89
  42.6 1.1 shard_map.88
  44.3 6.0 %all-to-all-done.1.parts_ref = bf16[8,24,1024]{2,1,0:T(8,128)(2,1)S(1)} async-done(((bf16[8,24,1024]{2,1,0:T(8,128)(2,1)}), bf16[8,24,1024]{2,1,0:T(8,128)(2,1)S(1)}, u32[]{:S(2)}, u32[]{:S(2)}) %all-to-all-start.1) | async-done | bytes 393248 | tf_op jit(solution)/shard_map/all_to_all | solution.py:242
  51.2 3.5 %all-to-all-start.2 = ((bf16[8,24,1024]{2,1,0:T(8,128)(2,1)}), bf16[8,24,1024]{2,1,0:T(8,128)(2,1)S(1)}, u32[]{:S(2)}, u32[]{:S(2)}) async-start(bf16[8,24,1024]{2,1,0:T(8,128)(2,1)} %shard_map.91), calls=%async_computation.2 | async-start | bytes 786432 | tf_op jit(solution)/shard_map/all_to_all | solution.py:242
  54.9 6.5 %collective-permute-done.6.came = bf16[8,72,128]{2,1,0:T(8,128)(2,1)S(1)} collective-permute-done((bf16[8,72,128]{2,1,0:T(8,128)(2,1)S(1)}, bf16[8,72,128]{2,1,0:T(8,128)(2,1)S(1)}, u32[]{:S(2)}, u32[]{:S(2)}) %collective-permute-start.6) | collective-permute-done | bytes 147488 | tf_op jit(solution)/shard_map/ppermute | solution.py:276
  61.4 2.2 %all-to-all-done.2.grad_ref.blocks_ref = bf16[8,24,1024]{2,1,0:T(8,128)(2,1)S(1)} async-done(((bf16[8,24,1024]{2,1,0:T(8,128)(2,1)}), bf16[8,24,1024]{2,1,0:T(8,128)(2,1)S(1)}, u32[]{:S(2)}, u32[]{:S(2)}) %all-to-all-start.2) | async-done | bytes 393248 | tf_op jit(solution)/shard_map/all_to_all | solution.py:242
  67.2 7.0 %all-to-all-start.3 = ((bf16[16,108,128]{2,1,0:T(8,128)(2,1)}), bf16[16,108,128]{2,1,0:T(8,128)(2,1)S(1)}, u32[]{:S(2)}, u32[]{:S(2)}) async-start(bf16[16,108,128]{2,1,0:T(8,128)(2,1)} %shard_map.95), calls=%async_computation.3 | async-start | bytes 917504 | tf_op jit(solution)/shard_map/all_to_all | solution.py:242
  74.2 2.2 %shard_map.96 = bf16[2,4,16,1024]{3,2,1,0:T(8,128)(2,1)S(1)} custom-call(bf16[8,24,1024]{2,1,0:T(8,128)(2,1)S(1)} %all-to-all-done.2.grad_ref.blocks_ref, bf16[3,3,128,128]{3,2,1,0:T(8,128)(2,1)S(1)} %bitcast.47, bf16[3,3,128,128]{3,2,1,0:T(8,128)(2,1)S(1)} %collective-permute-done.4.other_ref), custom_call_target="tpu_custom_call" | custom-call | flops 805306368 | bytes 1966080 | tf_op jit(solution)/shard_map/pallas_call | solution.py:43
  76.4 2.6 %collective-permute-start.8 = (bf16[4,16,1024]{2,1,0:T(8,128)(2,1)S(1)}, bf16[4,16,1024]{2,1,0:T(8,128)(2,1)S(1)}, u32[]{:S(2)}, u32[]{:S(2)}) collective-permute-start(bf16[4,16,1024]{2,1,0:T(8,128)(2,1)S(1)} %slice_bitcast_fusion), channel_id=1, source_target_pairs={{0,32},{32,0},{1,33},{33,1},{2,34},{34,2},{3,35},{35,3},{4,36},{36... | collective-permute-start | bytes 393224 | tf_op jit(solution)/shard_map/ppermute | solution.py:513
  79.0 9.8 %all-to-all-done.3.parts_ref = bf16[16,108,128]{2,1,0:T(8,128)(2,1)S(1)} async-done(((bf16[16,108,128]{2,1,0:T(8,128)(2,1)}), bf16[16,108,128]{2,1,0:T(8,128)(2,1)S(1)}, u32[]{:S(2)}, u32[]{:S(2)}) %all-to-all-start.3) | async-done | bytes 442400 | tf_op jit(solution)/shard_map/all_to_all | solution.py:242
  89.8 4.9 %all-to-all-start.4 = ((bf16[16,144,128]{2,1,0:T(8,128)(2,1)}), bf16[16,144,128]{2,1,0:T(8,128)(2,1)S(1)}, u32[]{:S(2)}, u32[]{:S(2)}) async-start(bf16[16,144,128]{2,1,0:T(8,128)(2,1)} %shard_map.97), calls=%async_computation.4 | async-start | bytes 1179648 | tf_op jit(solution)/shard_map/all_to_all | solution.py:242
  95.8 2.3 %collective-permute-start.11 = (bf16[16,1024]{1,0:T(8,128)(2,1)S(1)}, bf16[16,1024]{1,0:T(8,128)(2,1)S(1)}, u32[]{:S(2)}, u32[]{:S(2)}) collective-permute-start(bf16[16,1024]{1,0:T(8,128)(2,1)S(1)} %get-tuple-element.32), channel_id=1, source_target_pairs={{0,192},{64,0},{128,64},{192,128},{1,193},{65,1},{129,65},{193,129... | collective-permute-start | bytes 98312 | tf_op jit(solution)/shard_map/ppermute | solution.py:517
  98.8 1.2 %collective-permute-done.9 = bf16[16,1024]{1,0:T(8,128)(2,1)S(1)} collective-permute-done((bf16[16,1024]{1,0:T(8,128)(2,1)S(1)}, bf16[16,1024]{1,0:T(8,128)(2,1)S(1)}, u32[]{:S(2)}, u32[]{:S(2)}) %collective-permute-start.9) | collective-permute-done | bytes 32800 | tf_op jit(solution)/shard_map/ppermute | solution.py:517
  100.0 3.5 %collective-permute-done.10 = bf16[16,1024]{1,0:T(8,128)(2,1)S(1)} collective-permute-done((bf16[16,1024]{1,0:T(8,128)(2,1)S(1)}, bf16[16,1024]{1,0:T(8,128)(2,1)S(1)}, u32[]{:S(2)}, u32[]{:S(2)}) %collective-permute-start.10) | collective-permute-done | bytes 32800 | tf_op jit(solution)/shard_map/ppermute | solution.py:517
  103.7 1.2 %collective-permute-done.12 = bf16[16,512]{1,0:T(8,128)(2,1)S(1)} collective-permute-done((bf16[16,512]{1,0:T(8,128)(2,1)S(1)}, bf16[16,512]{1,0:T(8,128)(2,1)S(1)}, u32[]{:S(2)}, u32[]{:S(2)}) %collective-permute-start.12) | collective-permute-done | bytes 16416 | tf_op jit(solution)/shard_map/ppermute | solution.py:524
  105.5 6.0 %all-to-all-done.4.whole_ref = bf16[16,144,128]{2,1,0:T(8,128)(2,1)S(1)} async-done(((bf16[16,144,128]{2,1,0:T(8,128)(2,1)}), bf16[16,144,128]{2,1,0:T(8,128)(2,1)S(1)}, u32[]{:S(2)}, u32[]{:S(2)}) %all-to-all-start.4) | async-done | bytes 589856 | tf_op jit(solution)/shard_map/all_to_all | solution.py:242
  111.4 1.1 shard_map.98
  (38 shorter events, 11.2 us)
Async XLA Ops:
  0.6 11.6 %collective-permute-start.4 = (bf16[3,3,128,128]{3,2,1,0:T(8,128)(2,1)}, bf16[3,3,128,128]{3,2,1,0:T(8,128)(2,1)S(1)}, u32[]{:S(2)}, u32[]{:S(2)}) collective-permute-start(bf16[3,3,128,128]{3,2,1,0:T(8,128)(2,1)} %bitcast.46), channel_id=1, source_target_pairs={{0,16},{16,0},{1,17},{17,1},{2,18},{18,2},{3,19},{19,3},{4,20},{20... | collective-permute-start | bytes 884744 | tf_op jit(solution)/shard_map/ppermute | solution.py:466
  0.7 11.5 %collective-permute-start.3 = (bf16[3,3,128,128]{3,2,1,0:T(8,128)(2,1)}, bf16[3,3,128,128]{3,2,1,0:T(8,128)(2,1)S(1)}, u32[]{:S(2)}, u32[]{:S(2)}) collective-permute-start(bf16[3,3,128,128]{3,2,1,0:T(8,128)(2,1)} %bitcast.44), channel_id=1, source_target_pairs={{0,16},{16,0},{1,17},{17,1},{2,18},{18,2},{3,19},{19,3},{4,20},{20... | collective-permute-start | bytes 884744 | tf_op jit(solution)/shard_map/ppermute | solution.py:465
  2.8 7.4 %collective-permute-start.1 = (bf16[8,512]{1,0:T(8,128)(2,1)}, bf16[8,512]{1,0:T(8,128)(2,1)S(1)}, u32[]{:S(2)}, u32[]{:S(2)}) collective-permute-start(bf16[8,512]{1,0:T(8,128)(2,1)} %get-tuple-element.19), channel_id=1, source_target_pairs={{0,1},{1,2},{2,3},{3,4},{4,5},{5,6},{6,7},{7,8},{8,9},{9,10},{10,1... | collective-permute-start | bytes 24584 | tf_op jit(solution)/shard_map/ppermute | solution.py:447
  4.8 6.1 %collective-permute-start.2 = (bf16[8,512]{1,0:T(8,128)(2,1)}, bf16[8,512]{1,0:T(8,128)(2,1)S(1)}, u32[]{:S(2)}, u32[]{:S(2)}) collective-permute-start(bf16[8,512]{1,0:T(8,128)(2,1)} %get-tuple-element.20), channel_id=1, source_target_pairs={{16,1},{17,2},{18,3},{19,4},{20,5},{21,6},{22,7},{23,8},{24,9},{25... | collective-permute-start | bytes 24584 | tf_op jit(solution)/shard_map/ppermute | solution.py:448
  9.3 1.6 %collective-permute-start = (bf16[80,512]{1,0:T(8,128)(2,1)}, bf16[80,512]{1,0:T(8,128)(2,1)S(1)}, u32[]{:S(2)}, u32[]{:S(2)}) collective-permute-start(bf16[80,512]{1,0:T(8,128)(2,1)} %get-tuple-element.18), channel_id=1, source_target_pairs={{0,16},{16,0},{1,17},{17,1},{2,18},{18,2},{3,19},{19,3},{4,20},{20... | collective-permute-start | bytes 245768 | tf_op jit(solution)/shard_map/ppermute | solution.py:449
  12.2 22.4 %copy-start = (bf16[1,3,3,128,128]{4,3,2,1,0:T(8,128)(2,1)S(1)}, bf16[1,3,3,128,128]{4,3,2,1,0:T(8,128)(2,1)}, u32[]{:S(2)}) copy-start(bf16[1,3,3,128,128]{4,3,2,1,0:T(8,128)(2,1)} %param.11) | copy-start | bytes 884740
  37.9 12.4 %all-to-all-start.1 = ((bf16[8,24,1024]{2,1,0:T(8,128)(2,1)}), bf16[8,24,1024]{2,1,0:T(8,128)(2,1)S(1)}, u32[]{:S(2)}, u32[]{:S(2)}) async-start(bf16[8,24,1024]{2,1,0:T(8,128)(2,1)} %shard_map.87), calls=%async_computation.1 | async-start | bytes 786432 | tf_op jit(solution)/shard_map/all_to_all | solution.py:242
  42.5 1.7 %collective-permute-start.5 = (bf16[3,3,128,128]{3,2,1,0:T(8,128)(2,1)S(1)}, bf16[3,3,128,128]{3,2,1,0:T(8,128)(2,1)S(1)}, u32[]{:S(2)}, u32[]{:S(2)}) collective-permute-start(bf16[3,3,128,128]{3,2,1,0:T(8,128)(2,1)S(1)} %shard_map.89), channel_id=1, source_target_pairs={{0,16},{16,0},{1,17},{17,1},{2,18},{18,2},{3,19},{19,3},{4,20},{20... | collective-permute-start | bytes 884744 | tf_op jit(solution)/shard_map/ppermute | solution.py:229
  51.2 12.4 %all-to-all-start.2 = ((bf16[8,24,1024]{2,1,0:T(8,128)(2,1)}), bf16[8,24,1024]{2,1,0:T(8,128)(2,1)S(1)}, u32[]{:S(2)}, u32[]{:S(2)}) async-start(bf16[8,24,1024]{2,1,0:T(8,128)(2,1)} %shard_map.91), calls=%async_computation.2 | async-start | bytes 786432 | tf_op jit(solution)/shard_map/all_to_all | solution.py:242
  54.7 6.7 %collective-permute-start.6 = (bf16[8,72,128]{2,1,0:T(8,128)(2,1)S(1)}, bf16[8,72,128]{2,1,0:T(8,128)(2,1)S(1)}, u32[]{:S(2)}, u32[]{:S(2)}) collective-permute-start(bf16[8,72,128]{2,1,0:T(8,128)(2,1)S(1)} %get-tuple-element.23), channel_id=1, source_target_pairs={{0,8},{1,9},{2,10},{3,11},{4,12},{5,13},{6,14},{7,15},{8,0},{9,1},... | collective-permute-start | bytes 442376 | tf_op jit(solution)/shard_map/ppermute | solution.py:276
  64.7 1.7 %collective-permute-start.7 = (bf16[3,3,128,128]{3,2,1,0:T(8,128)(2,1)S(1)}, bf16[3,3,128,128]{3,2,1,0:T(8,128)(2,1)S(1)}, u32[]{:S(2)}, u32[]{:S(2)}) collective-permute-start(bf16[3,3,128,128]{3,2,1,0:T(8,128)(2,1)S(1)} %shard_map.94), channel_id=1, source_target_pairs={{0,16},{16,0},{1,17},{17,1},{2,18},{18,2},{3,19},{19,3},{4,20},{20... | collective-permute-start | bytes 884744 | tf_op jit(solution)/shard_map/ppermute | solution.py:229
  67.2 7.0 %copy-start.1 = (bf16[1,3,3,128,128]{4,3,2,1,0:T(8,128)(2,1)S(1)}, bf16[1,3,3,128,128]{4,3,2,1,0:T(8,128)(2,1)}, u32[]{:S(2)}) copy-start(bf16[1,3,3,128,128]{4,3,2,1,0:T(8,128)(2,1)} %param.10) | copy-start | bytes 884740
  67.2 21.6 %all-to-all-start.3 = ((bf16[16,108,128]{2,1,0:T(8,128)(2,1)}), bf16[16,108,128]{2,1,0:T(8,128)(2,1)S(1)}, u32[]{:S(2)}, u32[]{:S(2)}) async-start(bf16[16,108,128]{2,1,0:T(8,128)(2,1)} %shard_map.95), calls=%async_computation.3 | async-start | bytes 917504 | tf_op jit(solution)/shard_map/all_to_all | solution.py:242
  76.4 18.3 %collective-permute-start.8 = (bf16[4,16,1024]{2,1,0:T(8,128)(2,1)S(1)}, bf16[4,16,1024]{2,1,0:T(8,128)(2,1)S(1)}, u32[]{:S(2)}, u32[]{:S(2)}) collective-permute-start(bf16[4,16,1024]{2,1,0:T(8,128)(2,1)S(1)} %slice_bitcast_fusion), channel_id=1, source_target_pairs={{0,32},{32,0},{1,33},{33,1},{2,34},{34,2},{3,35},{35,3},{4,36},{36... | collective-permute-start | bytes 393224 | tf_op jit(solution)/shard_map/ppermute | solution.py:513
  89.8 21.6 %all-to-all-start.4 = ((bf16[16,144,128]{2,1,0:T(8,128)(2,1)}), bf16[16,144,128]{2,1,0:T(8,128)(2,1)S(1)}, u32[]{:S(2)}, u32[]{:S(2)}) async-start(bf16[16,144,128]{2,1,0:T(8,128)(2,1)} %shard_map.97), calls=%async_computation.4 | async-start | bytes 1179648 | tf_op jit(solution)/shard_map/all_to_all | solution.py:242
  94.8 5.2 %collective-permute-start.9 = (bf16[16,1024]{1,0:T(8,128)(2,1)S(1)}, bf16[16,1024]{1,0:T(8,128)(2,1)S(1)}, u32[]{:S(2)}, u32[]{:S(2)}) collective-permute-start(bf16[16,1024]{1,0:T(8,128)(2,1)S(1)} %get-tuple-element.31), channel_id=1, source_target_pairs={{0,64},{64,128},{128,192},{192,0},{1,65},{65,129},{129,193},{193,1... | collective-permute-start | bytes 98312 | tf_op jit(solution)/shard_map/ppermute | solution.py:517
  95.8 4.2 %collective-permute-start.11 = (bf16[16,1024]{1,0:T(8,128)(2,1)S(1)}, bf16[16,1024]{1,0:T(8,128)(2,1)S(1)}, u32[]{:S(2)}, u32[]{:S(2)}) collective-permute-start(bf16[16,1024]{1,0:T(8,128)(2,1)S(1)} %get-tuple-element.32), channel_id=1, source_target_pairs={{0,192},{64,0},{128,64},{192,128},{1,193},{65,1},{129,65},{193,129... | collective-permute-start | bytes 98312 | tf_op jit(solution)/shard_map/ppermute | solution.py:517
  98.1 5.4 %collective-permute-start.10 = (bf16[16,1024]{1,0:T(8,128)(2,1)S(1)}, bf16[16,1024]{1,0:T(8,128)(2,1)S(1)}, u32[]{:S(2)}, u32[]{:S(2)}) collective-permute-start(bf16[16,1024]{1,0:T(8,128)(2,1)S(1)} %get-tuple-element.33), channel_id=1, source_target_pairs={{0,128},{64,192},{128,0},{192,64},{1,129},{65,193},{129,1},{193,65... | collective-permute-start | bytes 98312 | tf_op jit(solution)/shard_map/ppermute | solution.py:517
  103.6 1.3 %collective-permute-start.12 = (bf16[16,512]{1,0:T(8,128)(2,1)S(1)}, bf16[16,512]{1,0:T(8,128)(2,1)S(1)}, u32[]{:S(2)}, u32[]{:S(2)}) collective-permute-start(bf16[16,512]{1,0:T(8,128)(2,1)S(1)} %get-tuple-element.35), channel_id=1, source_target_pairs={{0,16},{16,0},{1,17},{17,1},{2,18},{18,2},{3,19},{19,3},{4,20},{20... | collective-permute-start | bytes 49160 | tf_op jit(solution)/shard_map/ppermute | solution.py:524

commit v10 on v9

--- a/solution.py
+++ b/solution.py
@@ -59,11 +59,25 @@
         copy.wait()
 
 
-def interleave(blocks_ref, rows_ref, orients, first, shift):
-    for g in range(orients):
-        s = (g - shift) % orients
-        lanes = slice((s % 2) * WIDE, (s % 2 + 1) * WIDE)
-        rows_ref[:, g, :] = blocks_ref[s // 2, first:, lanes].astype(jnp.float32)
+def lanes_of(row):
+    return slice(row * CHAN, (row + 1) * CHAN)
+
+
+def interleave(blocks_ref, rows_ref, stage):
+    in_width, orients, _ = rows_ref.shape
+    lines = blocks_ref.shape[2] == CHAN
+    for n in range(orients // 2):
+        if lines:
+            stage[n] = blocks_ref[n].astype(jnp.float32).reshape(stage.shape[1:])
+        for half in range(2):
+            g = 2 * n + half
+            if not lines:
+                lanes = slice(half * WIDE, (half + 1) * WIDE)
+                first = blocks_ref.shape[1] - in_width
+                rows_ref[:, g, :] = blocks_ref[n, first:, lanes].astype(jnp.float32)
+                continue
+            for row in range(ROWS):
+                rows_ref[:, g, lanes_of(row)] = stage[n, :, half * ROWS + row, :]
 
 
 def band_weights(filt_ref, band_ref, slot):
@@ -81,14 +95,14 @@
                 ] = piece
 
 
-def rotation_sums(orients, width, blocks_ref, mine_ref, other_ref, rows_0, rows_1, band):
+def rotation_sums(orients, width, blocks_ref, mine_ref, other_ref, rows_0, rows_1, band, stage):
     in_width = rows_0.shape[0]
     _, core = here()
     band_weights(mine_ref, band, core)
     band_weights(other_ref, band, 1 - core)
-    first = blocks_ref.shape[1] - in_width
-    interleave(blocks_ref, rows_0, orients, first, 0)
-    interleave(blocks_ref, rows_1, orients, first, 1)
+    interleave(blocks_ref, rows_0, stage)
+    for g in range(orients):
+        rows_1[:, g, :] = rows_0[:, (g - 1) % orients, :]
     total = None
     for slot, rows in ((0, rows_0), (1, rows_1)):
         flat = rows[...].reshape(in_width * orients, WIDE).astype(jnp.bfloat16)
@@ -105,18 +119,16 @@
 
 
 def conv_two_kernel(orients, width, blocks_ref, mine_ref, other_ref, out_ref, *scratch):
-    *rows, sums, held, done = scratch
+    *rows, stage, sums, held, done = scratch
     chip, _ = here()
-    total = rotation_sums(orients, width, blocks_ref, mine_ref, other_ref, *rows)
-    sums[width:] = jnp.zeros((sums.shape[0] - width, orients, WIDE), jnp.float32)
-    sums[:width] = total
+    sums[...] = rotation_sums(orients, width, blocks_ref, mine_ref, other_ref, *rows, stage)
     chips = orients // 2
     copies = []
     for pair in range(chips):
         for half in range(2):
-            held[pair, :, half * WIDE : (half + 1) * WIDE] = sums[:, 2 * pair + half, :].astype(
-                jnp.bfloat16
-            )
+            for row in range(ROWS):
+                stage[pair, :, half * ROWS + row, :] = sums[:, 2 * pair + half, lanes_of(row)]
+        held[pair] = stage[pair].reshape(held.shape[1:]).astype(jnp.bfloat16)
         to = lax.rem(pair + chip, chips)
         copies.append(pltpu.make_async_copy(held.at[pair], out_ref.at[to], done.at[pair]))
         copies[-1].start()
@@ -125,9 +137,9 @@
 
 
 def conv_one_kernel(orients, width, blocks_ref, mine_ref, other_ref, out_ref, *scratch):
-    *rows, sums = scratch
+    *rows, stage, sums = scratch
     chip, _ = here()
-    sums[...] = rotation_sums(orients, width, blocks_ref, mine_ref, other_ref, *rows)
+    sums[...] = rotation_sums(orients, width, blocks_ref, mine_ref, other_ref, *rows, stage)
     chips = orients // 2
     across = out_ref.shape[1]
     for pair in range(chips):
@@ -140,7 +152,7 @@
             ].astype(jnp.bfloat16)
 
 
-def conv(kernel, blocks, in_width, mine, other, width, padded, out_shape, staging=(), out_space=VMEM, room=40):
+def conv(kernel, blocks, in_width, lined, mine, other, width, padded, out_shape, staging=(), out_space=VMEM, room=40):
     orients = 2 * blocks.shape[0]
     return call(
         functools.partial(kernel, orients, width),
@@ -149,6 +161,7 @@
             pltpu.VMEM((in_width, orients, WIDE), jnp.float32),
             pltpu.VMEM((in_width, orients, WIDE), jnp.float32),
             pltpu.VMEM((2, 3, WIDE, WIDE), jnp.bfloat16),
+            pltpu.VMEM((orients // 2, lined, 2 * ROWS, CHAN), jnp.float32),
             pltpu.VMEM((padded, orients, WIDE), jnp.float32),
             *staging,
         ],
@@ -162,7 +175,7 @@
 
 
 def filter_kernel(
-    orients, width, field, first, own, grad_ref, feat_ref, out_ref, feat_rows, grad_rows, held, done
+    orients, width, field, first, own, grad_ref, feat_ref, out_ref, feat_rows, grad_rows, stage, held, done
 ):
     chip, core = here()
     slot = core if own else 1 - core
@@ -177,7 +190,7 @@
     ]
     for copy in copies:
         copy.start()
-    interleave(grad_ref, grad_rows, orients, grad_ref.shape[1] - in_width, 0)
+    interleave(grad_ref, grad_rows, stage)
     grads = grad_rows[...].reshape(in_width * orients, WIDE).astype(jnp.bfloat16)
     for copy in copies:
         copy.wait()
@@ -216,6 +229,7 @@
             [
                 pltpu.VMEM((width, orients, WIDE), jnp.float32),
                 pltpu.VMEM((in_width, orients, WIDE), jnp.float32),
+                pltpu.VMEM((orients // 2, in_width, 2 * ROWS, CHAN), jnp.float32),
                 pltpu.VMEM((orients // 2, 2, width, WIDE), jnp.bfloat16),
                 pltpu.SemaphoreType.DMA((2,)),
             ],
@@ -275,7 +289,7 @@
     stay, leave = call(halves_kernel, (half, half), [both], mine.size, mine, theirs)
     came = lax.ppermute(leave, AZ, [(i, (i + count // 2) % count) for i in range(count)])
     shape = jax.ShapeDtypeStruct((count, size // 2, CHAN), jnp.bfloat16)
-    return leave, call(deal_kernel, shape, [], mine.size, stay, came)
+    return call(deal_kernel, shape, [], mine.size, stay, came)
 
 
 def join_kernel(mine, theirs, also, out_ref, held, done):
@@ -389,10 +403,10 @@
         cross_ref[:, lanes] = jnp.where(core == 0, low, high).astype(jnp.bfloat16)
 
 
-def rims_kernel(mine_ref, partner_ref, same_ref, cross_ref, out_ref, pre_ref, held, done):
+def rims_kernel(mine_ref, partner_ref, same_ref, cross_ref, out_ref, pre_ref, held, stage, done):
     _, core = here()
-    ahead = held.shape[0] - pre_ref.shape[0]
-    rows = pre_ref.shape[0]
+    rows = mine_ref.shape[0] - held.shape[0]
+    ahead = held.shape[0] - rows
     used = rows - 8
     at = lax.broadcasted_iota(jnp.int32, (rows, WIDE), 0)
     grad_at = jnp.where(core == 0, 0, used + 2)
@@ -408,9 +422,12 @@
         filled.append(jnp.concatenate([body[:ahead], grad, pre]).astype(jnp.bfloat16))
     first = jnp.where(core == 0, filled[0], filled[1])
     second = jnp.where(core == 0, filled[1], filled[0])
-    for lanes, part in ((slice(0, WIDE), first), (slice(WIDE, 2 * WIDE), second)):
-        held[:, lanes] = part[: ahead + rows]
-        pre_ref[:, lanes] = part[ahead + rows :]
+    for half, part in enumerate((first, second)):
+        held[:, half * WIDE : (half + 1) * WIDE] = part[: ahead + rows]
+        pre = part[ahead + rows :].astype(jnp.float32)[: stage.shape[0]]
+        for row in range(ROWS):
+            stage[:, half * ROWS + row, :] = pre[:, lanes_of(row)]
+    pre_ref[...] = stage[...].reshape(pre_ref.shape).astype(jnp.bfloat16)
     copy_all([(held, out_ref.at[n]) for n in range(out_ref.shape[0])], done)
 
 
@@ -424,6 +441,7 @@
     cell_count = rot_count * inputs.shape[1] * columns * az_count
     scale = cell_count ** (-0.5)
     padded = half + 8
+    lined = half + 2
 
     def narrow(*shape):
         return jax.ShapeDtypeStruct(shape, jnp.bfloat16)
@@ -450,9 +468,10 @@
     mine = mine + lax.shift_right_logical(core, 1).astype(mine.dtype)
     sent, pre_pair = call(
         rims_kernel,
-        (narrow(chips, columns + padded, 2 * WIDE), narrow(padded, 2 * WIDE)),
+        (narrow(chips, columns + padded, 2 * WIDE), narrow(lined * 2 * ROWS, CHAN)),
         [
             pltpu.VMEM((columns + padded, 2 * WIDE), jnp.bfloat16),
+            pltpu.VMEM((lined, 2 * ROWS, CHAN), jnp.float32),
             pltpu.SemaphoreType.DMA((chips,)),
         ],
         inputs.size * 20,
@@ -463,47 +482,51 @@
         out_space=(HBM, VMEM),
     )
     other_two = lax.ppermute(filt_two[0], CORE, SWAP)
-    other_one = lax.ppermute(filt_one[0], CORE, SWAP)
-    first_blocks = exchange(after(sent, (other_two, other_one)), CHIPS)
+    first_blocks = exchange(after(sent, other_two), CHIPS)
 
     shares = conv(
         conv_two_kernel,
         first_blocks,
         padded,
+        lined,
         filt_two[0],
         other_two,
-        half + 2,
-        padded,
-        (chips, padded, 2 * WIDE),
+        lined,
+        lined,
+        (chips, lined * 2 * ROWS, CHAN),
         [
-            pltpu.VMEM((chips, padded, 2 * WIDE), jnp.bfloat16),
+            pltpu.VMEM((chips, lined * 2 * ROWS, CHAN), jnp.bfloat16),
             pltpu.SemaphoreType.DMA((chips,)),
         ],
         HBM,
         52,
     )
-    pair_two = filter_terms(first_blocks, 0, half, first_blocks, padded, 3)
-    leave, terms_two = half_terms(pair_two)
-    arrived = after(exchange(shares, CHIPS), leave)
+    late_blocks = after(first_blocks, shares)
+    pair_two = filter_terms(late_blocks, 0, half, late_blocks, padded, 3)
+    terms_two = half_terms(pair_two)
+    arrived = after(exchange(shares, CHIPS), pair_two[0])
     copies = call(
         point_kernel,
-        narrow(chips, padded, 2 * WIDE),
-        [pltpu.VMEM((padded, 2 * WIDE), jnp.bfloat16), pltpu.SemaphoreType.DMA((chips,))],
+        narrow(chips, *pre_pair.shape),
+        [pltpu.VMEM(pre_pair.shape, jnp.bfloat16), pltpu.SemaphoreType.DMA((chips,))],
         arrived.size,
         arrived,
         pre_pair,
         out_space=HBM,
     )
     all_grad_one = after(exchange(copies, CHIPS), terms_two)
-    joined = joined_terms(filter_terms(first_blocks, 1, half, all_grad_one, padded, 2), terms_two)
+    joined = joined_terms(filter_terms(first_blocks, 1, half, all_grad_one, lined, 2), terms_two)
     filt_grad_one, filt_grad_two = summed_over_az(joined, filt_one.size // CHAN // az_count, scale)
 
     along_x = lax.axis_size(CHIPS[0])
+
+    other_one = lax.ppermute(after(filt_one[0], joined), CORE, SWAP)
 
     shares = conv(
         conv_one_kernel,
         after(all_grad_one, joined),
-        padded,
+        lined,
+        lined,
         filt_one[0],
         other_one,
         half,

time: 113 us -> 112 us (level)
  starting transfers between devices: 33 us -> 31.5 us
    ppermute x1, waiting for transfers between devices: 0.01 us -> 1.39 us  [shards(): other_one = lax.ppermute(after(filt_one[0], joined), CORE, SWAP)]
    all_to_all x4, starting transfers between devices: 18.8 us -> 17.5 us  [exchange(): return lax.all_to_all(parts, axes, 0, 0, tiled=True)]
  transfers between devices with their start and end apart: 17 -> 17, of which waited for: 11 -> 10; matrix products, arithmetic and copies ran while one was open for 1% -> 1% of each run, Pallas kernels for 8% -> 10%
where the time goes in v10:
time: 112 us; the launch traced here: 111 us
  waiting for transfers between devices  37.2 us (33%)
  starting transfers between devices  31.5 us (28%)
  blocking collectives  22.4 us (20%)
  Pallas kernels  17.3 us (15%)
  other arithmetic  1.59 us (1%)
    all_to_all x4, waiting for transfers between devices, exchange(): return lax.all_to_all(parts, axes, 0, 0, tiled=True)  23.1 us
    all_to_all x1, blocking collectives, exchange(): return lax.all_to_all(parts, axes, 0, 0, tiled=True)  22.4 us
    all_to_all x4, starting transfers between devices, exchange(): return lax.all_to_all(parts, axes, 0, 0, tiled=True)  17.5 us
    pallas_call x14, Pallas kernels, call(): pl.pallas_call(kernel, out_shape=out_shape, in_specs=in_specs, out_specs=...  17.3 us
    ppermute x1, waiting for transfers between devices, half_terms(): lax.ppermute(leave, AZ, [(i, (i + count // 2) % count) for i in range(cou...  5.79 us
    ppermute x3, waiting for transfers between devices, shards(): lax.ppermute(partial[step], CHIPS[0], [(i, (i + step) % along_x) for i in...  5 us
    ppermute x1, starting transfers between devices, shards(): lax.ppermute(cross, (CORE, AZ), place(1, after_me, 0) + place(0, before_m...  4.87 us
    ppermute x3, starting transfers between devices, shards(): lax.ppermute(partial[step], CHIPS[0], [(i, (i + step) % along_x) for i in...  3.73 us
  transfers between devices with their start and end apart: 17, of which 10 were waited for; matrix products, arithmetic and copies ran while one was open for 1% of the time, Pallas kernels for 10%

profile of v10, /device:TPU:32, one launch (start us, length us, event | category | flops | bytes accessed | tf_op | source)
XLA Modules:
  0.0 111.1 jit_solution(17640482920982197333)
XLA Ops:
  0.7 1.6 %shard_map.85 = (bf16[80,512]{1,0:T(8,128)(2,1)}, bf16[80,512]{1,0:T(8,128)(2,1)}, bf16[8,512]{1,0:T(8,128)(2,1)}, bf16[8,512]{1,0:T(8,128)(2,1)}) custom-call(bf16[1,4,32,128]{3,2,1,0:T(8,128)(2,1)} %refs_0_.1, bf16[1,4,32,128]{3,2,1,0:T(8,128)(2,1)} %refs_1_.1, bf16[1,4,32,128]{3,2,1,0:T(8,128)(2,1)} %refs_2_.1, bf16[1,4,32,128]{3,2,1,0:T(8,128)(2,1)} %refs_3_.1), custom_call_target="tpu_custom_call" | custom-call | flops 327680 | bytes 262144 | tf_op jit(solution)/shard_map/pallas_call | solution.py:43
  2.3 2.0 %collective-permute-start.1 = (bf16[8,512]{1,0:T(8,128)(2,1)}, bf16[8,512]{1,0:T(8,128)(2,1)S(1)}, u32[]{:S(2)}, u32[]{:S(2)}) collective-permute-start(bf16[8,512]{1,0:T(8,128)(2,1)} %get-tuple-element.21), channel_id=1, source_target_pairs={{0,1},{1,2},{2,3},{3,4},{4,5},{5,6},{6,7},{7,8},{8,9},{9,10},{10,1... | collective-permute-start | bytes 24584 | tf_op jit(solution)/shard_map/ppermute | solution.py:465
  4.3 4.9 %collective-permute-start.2 = (bf16[8,512]{1,0:T(8,128)(2,1)}, bf16[8,512]{1,0:T(8,128)(2,1)S(1)}, u32[]{:S(2)}, u32[]{:S(2)}) collective-permute-start(bf16[8,512]{1,0:T(8,128)(2,1)} %get-tuple-element.22), channel_id=1, source_target_pairs={{16,1},{17,2},{18,3},{19,4},{20,5},{21,6},{22,7},{23,8},{24,9},{25... | collective-permute-start | bytes 24584 | tf_op jit(solution)/shard_map/ppermute | solution.py:466
  10.8 1.4 %shard_map.86 = (bf16[8,56,1024]{2,1,0:T(8,128)(2,1)S(1)}, bf16[144,128]{1,0:T(8,128)(2,1)S(1)}) custom-call(bf16[80,512]{1,0:T(8,128)(2,1)S(1)} %broadcast_add_fusion.mine_ref, bf16[80,512]{1,0:T(8,128)(2,1)S(1)} %collective-permute-done.partner_ref, bf16[8,512]{1,0:T(8,128)(2,1)S(1)} %collective-permute-done.1.same_ref, ...), custom_call_target="tpu_custom_call" | custom-call | flops 327680 | bytes 360448 | tf_op jit(solution)/shard_map/pallas_call | solution.py:43
  12.2 22.4 %all_to_all.25.blocks_ref.grad_ref.feat_ref = bf16[8,56,1024]{2,1,0:T(8,128)(2,1)S(1)} all-to-all(bf16[8,56,1024]{2,1,0:T(8,128)(2,1)S(1)} %get-tuple-element.24), channel_id=1, replica_groups=mesh['rot_x'=4,'rot_y'=2,'rot_c'=2,'az'=16] {'rot_x','rot_y'}, dimensions={0} | all-to-all | bytes 1835008 | tf_op jit(solution)/shard_map/all_to_all | solution.py:256
  34.6 2.9 %shard_map.87 = bf16[8,144,128]{2,1,0:T(8,128)(2,1)} custom-call(bf16[8,56,1024]{2,1,0:T(8,128)(2,1)S(1)} %all_to_all.25.blocks_ref.grad_ref.feat_ref, bf16[3,3,128,128]{3,2,1,0:T(8,128)(2,1)S(1)} %bitcast.45, bf16[3,3,128,128]{3,2,1,0:T(8,128)(2,1)S(1)} %collective-permute-done.3.other_ref), custom_call_target="tpu_custom_call" | custom-call | flops 905969664 | bytes 3014656 | tf_op jit(solution)/shard_map/pallas_call | solution.py:43
  37.5 3.4 %all-to-all-start.1 = ((bf16[8,144,128]{2,1,0:T(8,128)(2,1)}), bf16[8,144,128]{2,1,0:T(8,128)(2,1)S(1)}, u32[]{:S(2)}, u32[]{:S(2)}) async-start(bf16[8,144,128]{2,1,0:T(8,128)(2,1)} %shard_map.87), calls=%async_computation.1 | async-start | bytes 589824 | tf_op jit(solution)/shard_map/all_to_all | solution.py:256
  43.1 6.3 %all-to-all-done.1.parts_ref = bf16[8,144,128]{2,1,0:T(8,128)(2,1)S(1)} async-done(((bf16[8,144,128]{2,1,0:T(8,128)(2,1)}), bf16[8,144,128]{2,1,0:T(8,128)(2,1)S(1)}, u32[]{:S(2)}, u32[]{:S(2)}) %all-to-all-start.1) | async-done | bytes 294944 | tf_op jit(solution)/shard_map/all_to_all | solution.py:256
  50.3 3.4 %all-to-all-start.2 = ((bf16[8,144,128]{2,1,0:T(8,128)(2,1)}), bf16[8,144,128]{2,1,0:T(8,128)(2,1)S(1)}, u32[]{:S(2)}, u32[]{:S(2)}) async-start(bf16[8,144,128]{2,1,0:T(8,128)(2,1)} %shard_map.89), calls=%async_computation.2 | async-start | bytes 589824 | tf_op jit(solution)/shard_map/all_to_all | solution.py:256
  54.1 5.8 %collective-permute-done.5.came = bf16[8,72,128]{2,1,0:T(8,128)(2,1)S(1)} collective-permute-done((bf16[8,72,128]{2,1,0:T(8,128)(2,1)S(1)}, bf16[8,72,128]{2,1,0:T(8,128)(2,1)S(1)}, u32[]{:S(2)}, u32[]{:S(2)}) %collective-permute-start.5) | collective-permute-done | bytes 147488 | tf_op jit(solution)/shard_map/ppermute | solution.py:290
  59.9 2.3 %all-to-all-done.2.grad_ref.blocks_ref = bf16[8,144,128]{2,1,0:T(8,128)(2,1)S(1)} async-done(((bf16[8,144,128]{2,1,0:T(8,128)(2,1)}), bf16[8,144,128]{2,1,0:T(8,128)(2,1)S(1)}, u32[]{:S(2)}, u32[]{:S(2)}) %all-to-all-start.2) | async-done | bytes 294944 | tf_op jit(solution)/shard_map/all_to_all | solution.py:256
  62.3 1.5 %shard_map.94 = bf16[3,3,128,128]{3,2,1,0:T(8,128)(2,1)S(1)} custom-call(bf16[8,144,128]{2,1,0:T(8,128)(2,1)S(1)} %all-to-all-done.2.grad_ref.blocks_ref, bf16[8,56,1024]{2,1,0:T(8,128)(2,1)S(1)} %all_to_all.25.blocks_ref.grad_ref.feat_ref), custom_call_target="tpu_custom_call" | custom-call | flops 402653184 | bytes 2424832 | tf_op jit(solution)/shard_map/pallas_call | solution.py:43
  63.9 1.5 %shard_map.93 = bf16[3,3,128,128]{3,2,1,0:T(8,128)(2,1)S(1)} custom-call(bf16[8,144,128]{2,1,0:T(8,128)(2,1)S(1)} %all-to-all-done.2.grad_ref.blocks_ref, bf16[8,56,1024]{2,1,0:T(8,128)(2,1)S(1)} %all_to_all.25.blocks_ref.grad_ref.feat_ref), custom_call_target="tpu_custom_call" | custom-call | flops 402653184 | bytes 2424832 | tf_op jit(solution)/shard_map/pallas_call | solution.py:43
  66.3 5.9 %all-to-all-start.3 = ((bf16[16,108,128]{2,1,0:T(8,128)(2,1)}), bf16[16,108,128]{2,1,0:T(8,128)(2,1)S(1)}, u32[]{:S(2)}, u32[]{:S(2)}) async-start(bf16[16,108,128]{2,1,0:T(8,128)(2,1)} %shard_map.95), calls=%async_computation.3 | async-start | bytes 917504 | tf_op jit(solution)/shard_map/all_to_all | solution.py:256
  72.7 1.4 %collective-permute-done.7.other_ref = bf16[3,3,128,128]{3,2,1,0:T(8,128)(2,1)S(1)} collective-permute-done((bf16[3,3,128,128]{3,2,1,0:T(8,128)(2,1)S(1)}, bf16[3,3,128,128]{3,2,1,0:T(8,128)(2,1)S(1)}, u32[]{:S(2)}, u32[]{:S(2)}) %collective-permute-start.7) | collective-permute-done | bytes 294944 | tf_op jit(solution)/shard_map/ppermute | solution.py:523
  74.1 2.4 %shard_map.96 = bf16[2,4,16,1024]{3,2,1,0:T(8,128)(2,1)S(1)} custom-call(bf16[8,144,128]{2,1,0:T(8,128)(2,1)S(1)} %all-to-all-done.2.grad_ref.blocks_ref, bf16[3,3,128,128]{3,2,1,0:T(8,128)(2,1)S(1)} %bitcast.47, bf16[3,3,128,128]{3,2,1,0:T(8,128)(2,1)S(1)} %collective-permute-done.7.other_ref), custom_call_target="tpu_custom_call" | custom-call | flops 805306368 | bytes 1769472 | tf_op jit(solution)/shard_map/pallas_call | solution.py:43
  76.5 2.3 %collective-permute-start.8 = (bf16[4,16,1024]{2,1,0:T(8,128)(2,1)S(1)}, bf16[4,16,1024]{2,1,0:T(8,128)(2,1)S(1)}, u32[]{:S(2)}, u32[]{:S(2)}) collective-permute-start(bf16[4,16,1024]{2,1,0:T(8,128)(2,1)S(1)} %slice_bitcast_fusion), channel_id=1, source_target_pairs={{0,32},{32,0},{1,33},{33,1},{2,34},{34,2},{3,35},{35,3},{4,36},{36... | collective-permute-start | bytes 393224 | tf_op jit(solution)/shard_map/ppermute | solution.py:536
  78.8 8.6 %all-to-all-done.3.parts_ref = bf16[16,108,128]{2,1,0:T(8,128)(2,1)S(1)} async-done(((bf16[16,108,128]{2,1,0:T(8,128)(2,1)}), bf16[16,108,128]{2,1,0:T(8,128)(2,1)S(1)}, u32[]{:S(2)}, u32[]{:S(2)}) %all-to-all-start.3) | async-done | bytes 442400 | tf_op jit(solution)/shard_map/all_to_all | solution.py:256
  88.4 4.7 %all-to-all-start.4 = ((bf16[16,144,128]{2,1,0:T(8,128)(2,1)}), bf16[16,144,128]{2,1,0:T(8,128)(2,1)S(1)}, u32[]{:S(2)}, u32[]{:S(2)}) async-start(bf16[16,144,128]{2,1,0:T(8,128)(2,1)} %shard_map.97), calls=%async_computation.4 | async-start | bytes 1179648 | tf_op jit(solution)/shard_map/all_to_all | solution.py:256
  93.5 3.0 %collective-permute-start.11 = (bf16[16,1024]{1,0:T(8,128)(2,1)S(1)}, bf16[16,1024]{1,0:T(8,128)(2,1)S(1)}, u32[]{:S(2)}, u32[]{:S(2)}) collective-permute-start(bf16[16,1024]{1,0:T(8,128)(2,1)S(1)} %get-tuple-element.36), channel_id=1, source_target_pairs={{0,192},{64,0},{128,64},{192,128},{1,193},{65,1},{129,65},{193,129... | collective-permute-start | bytes 98312 | tf_op jit(solution)/shard_map/ppermute | solution.py:540
  96.9 1.5 %collective-permute-done.9 = bf16[16,1024]{1,0:T(8,128)(2,1)S(1)} collective-permute-done((bf16[16,1024]{1,0:T(8,128)(2,1)S(1)}, bf16[16,1024]{1,0:T(8,128)(2,1)S(1)}, u32[]{:S(2)}, u32[]{:S(2)}) %collective-permute-start.9) | collective-permute-done | bytes 32800 | tf_op jit(solution)/shard_map/ppermute | solution.py:540
  98.4 3.5 %collective-permute-done.10 = bf16[16,1024]{1,0:T(8,128)(2,1)S(1)} collective-permute-done((bf16[16,1024]{1,0:T(8,128)(2,1)S(1)}, bf16[16,1024]{1,0:T(8,128)(2,1)S(1)}, u32[]{:S(2)}, u32[]{:S(2)}) %collective-permute-start.10) | collective-permute-done | bytes 32800 | tf_op jit(solution)/shard_map/ppermute | solution.py:540
  102.1 1.2 %collective-permute-done.12 = bf16[16,512]{1,0:T(8,128)(2,1)S(1)} collective-permute-done((bf16[16,512]{1,0:T(8,128)(2,1)S(1)}, bf16[16,512]{1,0:T(8,128)(2,1)S(1)}, u32[]{:S(2)}, u32[]{:S(2)}) %collective-permute-start.12) | collective-permute-done | bytes 16416 | tf_op jit(solution)/shard_map/ppermute | solution.py:547
  103.9 6.0 %all-to-all-done.4.whole_ref = bf16[16,144,128]{2,1,0:T(8,128)(2,1)S(1)} async-done(((bf16[16,144,128]{2,1,0:T(8,128)(2,1)}), bf16[16,144,128]{2,1,0:T(8,128)(2,1)S(1)}, u32[]{:S(2)}, u32[]{:S(2)}) %all-to-all-start.4) | async-done | bytes 589856 | tf_op jit(solution)/shard_map/all_to_all | solution.py:256
  (38 shorter events, 10.2 us)
Async XLA Ops:
  0.6 11.5 %collective-permute-start.3 = (bf16[3,3,128,128]{3,2,1,0:T(8,128)(2,1)}, bf16[3,3,128,128]{3,2,1,0:T(8,128)(2,1)S(1)}, u32[]{:S(2)}, u32[]{:S(2)}) collective-permute-start(bf16[3,3,128,128]{3,2,1,0:T(8,128)(2,1)} %bitcast.44), channel_id=1, source_target_pairs={{0,16},{16,0},{1,17},{17,1},{2,18},{18,2},{3,19},{19,3},{4,20},{20... | collective-permute-start | bytes 884744 | tf_op jit(solution)/shard_map/ppermute | solution.py:484
  2.3 7.8 %collective-permute-start.1 = (bf16[8,512]{1,0:T(8,128)(2,1)}, bf16[8,512]{1,0:T(8,128)(2,1)S(1)}, u32[]{:S(2)}, u32[]{:S(2)}) collective-permute-start(bf16[8,512]{1,0:T(8,128)(2,1)} %get-tuple-element.21), channel_id=1, source_target_pairs={{0,1},{1,2},{2,3},{3,4},{4,5},{5,6},{6,7},{7,8},{8,9},{9,10},{10,1... | collective-permute-start | bytes 24584 | tf_op jit(solution)/shard_map/ppermute | solution.py:465
  4.3 6.5 %collective-permute-start.2 = (bf16[8,512]{1,0:T(8,128)(2,1)}, bf16[8,512]{1,0:T(8,128)(2,1)S(1)}, u32[]{:S(2)}, u32[]{:S(2)}) collective-permute-start(bf16[8,512]{1,0:T(8,128)(2,1)} %get-tuple-element.22), channel_id=1, source_target_pairs={{16,1},{17,2},{18,3},{19,4},{20,5},{21,6},{22,7},{23,8},{24,9},{25... | collective-permute-start | bytes 24584 | tf_op jit(solution)/shard_map/ppermute | solution.py:466
  9.2 1.6 %collective-permute-start = (bf16[80,512]{1,0:T(8,128)(2,1)}, bf16[80,512]{1,0:T(8,128)(2,1)S(1)}, u32[]{:S(2)}, u32[]{:S(2)}) collective-permute-start(bf16[80,512]{1,0:T(8,128)(2,1)} %get-tuple-element.20), channel_id=1, source_target_pairs={{0,16},{16,0},{1,17},{17,1},{2,18},{18,2},{3,19},{19,3},{4,20},{20... | collective-permute-start | bytes 245768 | tf_op jit(solution)/shard_map/ppermute | solution.py:467
  12.2 22.4 %copy-start = (bf16[1,3,3,128,128]{4,3,2,1,0:T(8,128)(2,1)S(1)}, bf16[1,3,3,128,128]{4,3,2,1,0:T(8,128)(2,1)}, u32[]{:S(2)}) copy-start(bf16[1,3,3,128,128]{4,3,2,1,0:T(8,128)(2,1)} %param.11) | copy-start | bytes 884740
  37.5 11.9 %all-to-all-start.1 = ((bf16[8,144,128]{2,1,0:T(8,128)(2,1)}), bf16[8,144,128]{2,1,0:T(8,128)(2,1)S(1)}, u32[]{:S(2)}, u32[]{:S(2)}) async-start(bf16[8,144,128]{2,1,0:T(8,128)(2,1)} %shard_map.87), calls=%async_computation.1 | async-start | bytes 589824 | tf_op jit(solution)/shard_map/all_to_all | solution.py:256
  42.0 11.7 %collective-permute-start.4 = (bf16[3,3,128,128]{3,2,1,0:T(8,128)(2,1)S(1)}, bf16[3,3,128,128]{3,2,1,0:T(8,128)(2,1)S(1)}, u32[]{:S(2)}, u32[]{:S(2)}) collective-permute-start(bf16[3,3,128,128]{3,2,1,0:T(8,128)(2,1)S(1)} %shard_map.90), channel_id=1, source_target_pairs={{0,16},{16,0},{1,17},{17,1},{2,18},{18,2},{3,19},{19,3},{4,20},{20... | collective-permute-start | bytes 884744 | tf_op jit(solution)/shard_map/ppermute | solution.py:243
  50.3 12.0 %all-to-all-start.2 = ((bf16[8,144,128]{2,1,0:T(8,128)(2,1)}), bf16[8,144,128]{2,1,0:T(8,128)(2,1)S(1)}, u32[]{:S(2)}, u32[]{:S(2)}) async-start(bf16[8,144,128]{2,1,0:T(8,128)(2,1)} %shard_map.89), calls=%async_computation.2 | async-start | bytes 589824 | tf_op jit(solution)/shard_map/all_to_all | solution.py:256
  53.8 6.0 %collective-permute-start.5 = (bf16[8,72,128]{2,1,0:T(8,128)(2,1)S(1)}, bf16[8,72,128]{2,1,0:T(8,128)(2,1)S(1)}, u32[]{:S(2)}, u32[]{:S(2)}) collective-permute-start(bf16[8,72,128]{2,1,0:T(8,128)(2,1)S(1)} %get-tuple-element.29), channel_id=1, source_target_pairs={{0,8},{1,9},{2,10},{3,11},{4,12},{5,13},{6,14},{7,15},{8,0},{9,1},... | collective-permute-start | bytes 442376 | tf_op jit(solution)/shard_map/ppermute | solution.py:290
  63.8 1.7 %collective-permute-start.6 = (bf16[3,3,128,128]{3,2,1,0:T(8,128)(2,1)S(1)}, bf16[3,3,128,128]{3,2,1,0:T(8,128)(2,1)S(1)}, u32[]{:S(2)}, u32[]{:S(2)}) collective-permute-start(bf16[3,3,128,128]{3,2,1,0:T(8,128)(2,1)S(1)} %shard_map.94), channel_id=1, source_target_pairs={{0,16},{16,0},{1,17},{17,1},{2,18},{18,2},{3,19},{19,3},{4,20},{20... | collective-permute-start | bytes 884744 | tf_op jit(solution)/shard_map/ppermute | solution.py:243
  66.3 5.9 %copy-start.1 = (bf16[1,3,3,128,128]{4,3,2,1,0:T(8,128)(2,1)S(1)}, bf16[1,3,3,128,128]{4,3,2,1,0:T(8,128)(2,1)}, u32[]{:S(2)}) copy-start(bf16[1,3,3,128,128]{4,3,2,1,0:T(8,128)(2,1)} %param.10) | copy-start | bytes 884740
  66.3 21.0 %all-to-all-start.3 = ((bf16[16,108,128]{2,1,0:T(8,128)(2,1)}), bf16[16,108,128]{2,1,0:T(8,128)(2,1)S(1)}, u32[]{:S(2)}, u32[]{:S(2)}) async-start(bf16[16,108,128]{2,1,0:T(8,128)(2,1)} %shard_map.95), calls=%async_computation.3 | async-start | bytes 917504 | tf_op jit(solution)/shard_map/all_to_all | solution.py:256
  72.3 1.9 %collective-permute-start.7 = (bf16[3,3,128,128]{3,2,1,0:T(8,128)(2,1)S(1)}, bf16[3,3,128,128]{3,2,1,0:T(8,128)(2,1)S(1)}, u32[]{:S(2)}, u32[]{:S(2)}) collective-permute-start(bf16[3,3,128,128]{3,2,1,0:T(8,128)(2,1)S(1)} %bitcast.46), channel_id=1, source_target_pairs={{0,16},{16,0},{1,17},{17,1},{2,18},{18,2},{3,19},{19,3},{4,20},{20... | collective-permute-start | bytes 884744 | tf_op jit(solution)/shard_map/ppermute | solution.py:523
  76.5 16.6 %collective-permute-start.8 = (bf16[4,16,1024]{2,1,0:T(8,128)(2,1)S(1)}, bf16[4,16,1024]{2,1,0:T(8,128)(2,1)S(1)}, u32[]{:S(2)}, u32[]{:S(2)}) collective-permute-start(bf16[4,16,1024]{2,1,0:T(8,128)(2,1)S(1)} %slice_bitcast_fusion), channel_id=1, source_target_pairs={{0,32},{32,0},{1,33},{33,1},{2,34},{34,2},{3,35},{35,3},{4,36},{36... | collective-permute-start | bytes 393224 | tf_op jit(solution)/shard_map/ppermute | solution.py:536
  88.4 21.5 %all-to-all-start.4 = ((bf16[16,144,128]{2,1,0:T(8,128)(2,1)}), bf16[16,144,128]{2,1,0:T(8,128)(2,1)S(1)}, u32[]{:S(2)}, u32[]{:S(2)}) async-start(bf16[16,144,128]{2,1,0:T(8,128)(2,1)} %shard_map.97), calls=%async_computation.4 | async-start | bytes 1179648 | tf_op jit(solution)/shard_map/all_to_all | solution.py:256
  93.2 5.2 %collective-permute-start.9 = (bf16[16,1024]{1,0:T(8,128)(2,1)S(1)}, bf16[16,1024]{1,0:T(8,128)(2,1)S(1)}, u32[]{:S(2)}, u32[]{:S(2)}) collective-permute-start(bf16[16,1024]{1,0:T(8,128)(2,1)S(1)} %get-tuple-element.35), channel_id=1, source_target_pairs={{0,64},{64,128},{128,192},{192,0},{1,65},{65,129},{129,193},{193,1... | collective-permute-start | bytes 98312 | tf_op jit(solution)/shard_map/ppermute | solution.py:540
  93.5 4.8 %collective-permute-start.11 = (bf16[16,1024]{1,0:T(8,128)(2,1)S(1)}, bf16[16,1024]{1,0:T(8,128)(2,1)S(1)}, u32[]{:S(2)}, u32[]{:S(2)}) collective-permute-start(bf16[16,1024]{1,0:T(8,128)(2,1)S(1)} %get-tuple-element.36), channel_id=1, source_target_pairs={{0,192},{64,0},{128,64},{192,128},{1,193},{65,1},{129,65},{193,129... | collective-permute-start | bytes 98312 | tf_op jit(solution)/shard_map/ppermute | solution.py:540
  96.5 5.4 %collective-permute-start.10 = (bf16[16,1024]{1,0:T(8,128)(2,1)S(1)}, bf16[16,1024]{1,0:T(8,128)(2,1)S(1)}, u32[]{:S(2)}, u32[]{:S(2)}) collective-permute-start(bf16[16,1024]{1,0:T(8,128)(2,1)S(1)} %get-tuple-element.37), channel_id=1, source_target_pairs={{0,128},{64,192},{128,0},{192,64},{1,129},{65,193},{129,1},{193,65... | collective-permute-start | bytes 98312 | tf_op jit(solution)/shard_map/ppermute | solution.py:540
  102.0 1.3 %collective-permute-start.12 = (bf16[16,512]{1,0:T(8,128)(2,1)S(1)}, bf16[16,512]{1,0:T(8,128)(2,1)S(1)}, u32[]{:S(2)}, u32[]{:S(2)}) collective-permute-start(bf16[16,512]{1,0:T(8,128)(2,1)S(1)} %get-tuple-element.39), channel_id=1, source_target_pairs={{0,16},{16,0},{1,17},{17,1},{2,18},{18,2},{3,19},{19,3},{4,20},{20... | collective-permute-start | bytes 49160 | tf_op jit(solution)/shard_map/ppermute | solution.py:547

commit v11 on v10

--- a/solution.py
+++ b/solution.py
@@ -175,8 +175,9 @@
 
 
 def filter_kernel(
-    orients, width, field, first, own, grad_ref, feat_ref, out_ref, feat_rows, grad_rows, stage, held, done
+    orients, width, field, first, own, grad_ref, feat_ref, *refs
 ):
+    (out_ref, *rows_ref), (feat_rows, grad_rows, stage, held, done) = refs[:-5], refs[-5:]
     chip, core = here()
     slot = core if own else 1 - core
     in_width = grad_rows.shape[0]
@@ -190,8 +191,12 @@
     ]
     for copy in copies:
         copy.start()
-    interleave(grad_ref, grad_rows, stage)
-    grads = grad_rows[...].reshape(in_width * orients, WIDE).astype(jnp.bfloat16)
+    if own:
+        grads = grad_ref[...]
+    else:
+        interleave(grad_ref, grad_rows, stage)
+        grads = grad_rows[...].reshape(in_width * orients, WIDE).astype(jnp.bfloat16)
+        rows_ref[0][...] = grads
     for copy in copies:
         copy.wait()
     for g in range(orients):
@@ -222,10 +227,12 @@
 def filter_terms(feats, field, width, grads, in_width, first):
     orients = 2 * feats.shape[0]
 
-    def terms(own):
+    def terms(own, grads):
+        bank = jax.ShapeDtypeStruct((3, 3, CHAN, CHAN), jnp.bfloat16)
+        rows = jax.ShapeDtypeStruct((in_width * orients, WIDE), jnp.bfloat16)
         return call(
             functools.partial(filter_kernel, orients, width, field, first, own),
-            jax.ShapeDtypeStruct((3, 3, CHAN, CHAN), jnp.bfloat16),
+            bank if own else (bank, rows),
             [
                 pltpu.VMEM((width, orients, WIDE), jnp.float32),
                 pltpu.VMEM((in_width, orients, WIDE), jnp.float32),
@@ -240,8 +247,8 @@
             room=52,
         )
 
-    theirs = lax.ppermute(terms(False), CORE, SWAP)
-    return terms(True), theirs
+    other, rows = terms(False, grads)
+    return terms(True, rows), lax.ppermute(other, CORE, SWAP)
 
 
 def point_kernel(parts_ref, pre_ref, out_ref, held, done):

time: 112 us -> 111 us (level)
  transfers between devices with their start and end apart: 17 -> 17, of which waited for: 10 -> 11; matrix products, arithmetic and copies ran while one was open for 1% -> 1% of each run, Pallas kernels for 10% -> 9%
where the time goes in v11:
time: 111 us
  waiting for transfers between devices  37.6 us (34%)
  starting transfers between devices  31.5 us (28%)
  blocking collectives  22.4 us (20%)
  Pallas kernels  16.6 us (15%)
  other arithmetic  1.59 us (1%)
    all_to_all x4, waiting for transfers between devices, exchange(): return lax.all_to_all(parts, axes, 0, 0, tiled=True)  22.7 us
    all_to_all x1, blocking collectives, exchange(): return lax.all_to_all(parts, axes, 0, 0, tiled=True)  22.4 us
    all_to_all x4, starting transfers between devices, exchange(): return lax.all_to_all(parts, axes, 0, 0, tiled=True)  17.7 us
    pallas_call x14, Pallas kernels, call(): pl.pallas_call(kernel, out_shape=out_shape, in_specs=in_specs, out_specs=...  16.6 us
    ppermute x1, waiting for transfers between devices, half_terms(): lax.ppermute(leave, AZ, [(i, (i + count // 2) % count) for i in range(cou...  5.79 us
    ppermute x3, waiting for transfers between devices, shards(): lax.ppermute(partial[step], CHIPS[0], [(i, (i + step) % along_x) for i in...  5 us
    ppermute x1, starting transfers between devices, shards(): lax.ppermute(cross, (CORE, AZ), place(1, after_me, 0) + place(0, before_m...  4.87 us
    ppermute x3, starting transfers between devices, shards(): lax.ppermute(partial[step], CHIPS[0], [(i, (i + step) % along_x) for i in...  3.73 us
  transfers between devices with their start and end apart: 17, of which 11 were waited for; matrix products, arithmetic and copies ran while one was open for 1% of the time, Pallas kernels for 9%

profile of v11, /device:TPU:32, one launch (start us, length us, event | category | flops | bytes accessed | tf_op | source)
XLA Modules:
  0.0 110.7 jit_solution(3472898504486363456)
XLA Ops:
  0.7 1.6 %shard_map.85 = (bf16[80,512]{1,0:T(8,128)(2,1)}, bf16[80,512]{1,0:T(8,128)(2,1)}, bf16[8,512]{1,0:T(8,128)(2,1)}, bf16[8,512]{1,0:T(8,128)(2,1)}) custom-call(bf16[1,4,32,128]{3,2,1,0:T(8,128)(2,1)} %refs_0_.1, bf16[1,4,32,128]{3,2,1,0:T(8,128)(2,1)} %refs_1_.1, bf16[1,4,32,128]{3,2,1,0:T(8,128)(2,1)} %refs_2_.1, bf16[1,4,32,128]{3,2,1,0:T(8,128)(2,1)} %refs_3_.1), custom_call_target="tpu_custom_call" | custom-call | flops 327680 | bytes 262144 | tf_op jit(solution)/shard_map/pallas_call | solution.py:43
  2.3 2.0 %collective-permute-start.1 = (bf16[8,512]{1,0:T(8,128)(2,1)}, bf16[8,512]{1,0:T(8,128)(2,1)S(1)}, u32[]{:S(2)}, u32[]{:S(2)}) collective-permute-start(bf16[8,512]{1,0:T(8,128)(2,1)} %get-tuple-element.25), channel_id=1, source_target_pairs={{0,1},{1,2},{2,3},{3,4},{4,5},{5,6},{6,7},{7,8},{8,9},{9,10},{10,1... | collective-permute-start | bytes 24584 | tf_op jit(solution)/shard_map/ppermute | solution.py:472
  4.3 4.9 %collective-permute-start.2 = (bf16[8,512]{1,0:T(8,128)(2,1)}, bf16[8,512]{1,0:T(8,128)(2,1)S(1)}, u32[]{:S(2)}, u32[]{:S(2)}) collective-permute-start(bf16[8,512]{1,0:T(8,128)(2,1)} %get-tuple-element.26), channel_id=1, source_target_pairs={{16,1},{17,2},{18,3},{19,4},{20,5},{21,6},{22,7},{23,8},{24,9},{25... | collective-permute-start | bytes 24584 | tf_op jit(solution)/shard_map/ppermute | solution.py:473
  10.8 1.4 %shard_map.86 = (bf16[8,56,1024]{2,1,0:T(8,128)(2,1)S(1)}, bf16[144,128]{1,0:T(8,128)(2,1)S(1)}) custom-call(bf16[80,512]{1,0:T(8,128)(2,1)S(1)} %broadcast_add_fusion.mine_ref, bf16[80,512]{1,0:T(8,128)(2,1)S(1)} %collective-permute-done.partner_ref, bf16[8,512]{1,0:T(8,128)(2,1)S(1)} %collective-permute-done.1.same_ref, ...), custom_call_target="tpu_custom_call" | custom-call | flops 327680 | bytes 360448 | tf_op jit(solution)/shard_map/pallas_call | solution.py:43
  12.2 22.4 %all_to_all.25.blocks_ref.grad_ref.feat_ref = bf16[8,56,1024]{2,1,0:T(8,128)(2,1)S(1)} all-to-all(bf16[8,56,1024]{2,1,0:T(8,128)(2,1)S(1)} %get-tuple-element.28), channel_id=1, replica_groups=mesh['rot_x'=4,'rot_y'=2,'rot_c'=2,'az'=16] {'rot_x','rot_y'}, dimensions={0} | all-to-all | bytes 1835008 | tf_op jit(solution)/shard_map/all_to_all | solution.py:263
  34.6 2.9 %shard_map.87 = bf16[8,144,128]{2,1,0:T(8,128)(2,1)} custom-call(bf16[8,56,1024]{2,1,0:T(8,128)(2,1)S(1)} %all_to_all.25.blocks_ref.grad_ref.feat_ref, bf16[3,3,128,128]{3,2,1,0:T(8,128)(2,1)S(1)} %bitcast.45, bf16[3,3,128,128]{3,2,1,0:T(8,128)(2,1)S(1)} %collective-permute-done.3.other_ref), custom_call_target="tpu_custom_call" | custom-call | flops 905969664 | bytes 3014656 | tf_op jit(solution)/shard_map/pallas_call | solution.py:43
  37.5 3.4 %all-to-all-start.1 = ((bf16[8,144,128]{2,1,0:T(8,128)(2,1)}), bf16[8,144,128]{2,1,0:T(8,128)(2,1)S(1)}, u32[]{:S(2)}, u32[]{:S(2)}) async-start(bf16[8,144,128]{2,1,0:T(8,128)(2,1)} %shard_map.87), calls=%async_computation.1 | async-start | bytes 589824 | tf_op jit(solution)/shard_map/all_to_all | solution.py:263
  40.9 1.2 %shard_map.88 = (bf16[3,3,128,128]{3,2,1,0:T(8,128)(2,1)S(1)}, bf16[384,512]{1,0:T(8,128)(2,1)S(1)}) custom-call(bf16[8,56,1024]{2,1,0:T(8,128)(2,1)S(1)} %all_to_all.25.blocks_ref.grad_ref.feat_ref, bf16[8,56,1024]{2,1,0:T(8,128)(2,1)S(1)} %all_to_all.25.blocks_ref.grad_ref.feat_ref), custom_call_target="tpu_custom_call" | custom-call | flops 402653184 | bytes 3670016 | tf_op jit(solution)/shard_map/pallas_call | solution.py:43
  43.1 6.3 %all-to-all-done.1.parts_ref = bf16[8,144,128]{2,1,0:T(8,128)(2,1)S(1)} async-done(((bf16[8,144,128]{2,1,0:T(8,128)(2,1)}), bf16[8,144,128]{2,1,0:T(8,128)(2,1)S(1)}, u32[]{:S(2)}, u32[]{:S(2)}) %all-to-all-start.1) | async-done | bytes 294944 | tf_op jit(solution)/shard_map/all_to_all | solution.py:263
  50.3 3.4 %all-to-all-start.2 = ((bf16[8,144,128]{2,1,0:T(8,128)(2,1)}), bf16[8,144,128]{2,1,0:T(8,128)(2,1)S(1)}, u32[]{:S(2)}, u32[]{:S(2)}) async-start(bf16[8,144,128]{2,1,0:T(8,128)(2,1)} %shard_map.90), calls=%async_computation.2 | async-start | bytes 589824 | tf_op jit(solution)/shard_map/all_to_all | solution.py:263
  54.1 5.8 %collective-permute-done.5.came = bf16[8,72,128]{2,1,0:T(8,128)(2,1)S(1)} collective-permute-done((bf16[8,72,128]{2,1,0:T(8,128)(2,1)S(1)}, bf16[8,72,128]{2,1,0:T(8,128)(2,1)S(1)}, u32[]{:S(2)}, u32[]{:S(2)}) %collective-permute-start.5) | collective-permute-done | bytes 147488 | tf_op jit(solution)/shard_map/ppermute | solution.py:297
  59.9 2.3 %all-to-all-done.2.grad_ref.blocks_ref = bf16[8,144,128]{2,1,0:T(8,128)(2,1)S(1)} async-done(((bf16[8,144,128]{2,1,0:T(8,128)(2,1)}), bf16[8,144,128]{2,1,0:T(8,128)(2,1)S(1)}, u32[]{:S(2)}, u32[]{:S(2)}) %all-to-all-start.2) | async-done | bytes 294944 | tf_op jit(solution)/shard_map/all_to_all | solution.py:263
  62.3 1.5 %shard_map.93 = (bf16[3,3,128,128]{3,2,1,0:T(8,128)(2,1)S(1)}, bf16[288,512]{1,0:T(8,128)(2,1)S(1)}) custom-call(bf16[8,144,128]{2,1,0:T(8,128)(2,1)S(1)} %all-to-all-done.2.grad_ref.blocks_ref, bf16[8,56,1024]{2,1,0:T(8,128)(2,1)S(1)} %all_to_all.25.blocks_ref.grad_ref.feat_ref), custom_call_target="tpu_custom_call" | custom-call | flops 402653184 | bytes 2424832 | tf_op jit(solution)/shard_map/pallas_call | solution.py:43
  66.3 5.9 %all-to-all-start.3 = ((bf16[16,108,128]{2,1,0:T(8,128)(2,1)}), bf16[16,108,128]{2,1,0:T(8,128)(2,1)S(1)}, u32[]{:S(2)}, u32[]{:S(2)}) async-start(bf16[16,108,128]{2,1,0:T(8,128)(2,1)} %shard_map.95), calls=%async_computation.3 | async-start | bytes 917504 | tf_op jit(solution)/shard_map/all_to_all | solution.py:263
  72.6 1.6 %collective-permute-done.7.other_ref = bf16[3,3,128,128]{3,2,1,0:T(8,128)(2,1)S(1)} collective-permute-done((bf16[3,3,128,128]{3,2,1,0:T(8,128)(2,1)S(1)}, bf16[3,3,128,128]{3,2,1,0:T(8,128)(2,1)S(1)}, u32[]{:S(2)}, u32[]{:S(2)}) %collective-permute-start.7) | collective-permute-done | bytes 294944 | tf_op jit(solution)/shard_map/ppermute | solution.py:530
  74.1 2.4 %shard_map.96 = bf16[2,4,16,1024]{3,2,1,0:T(8,128)(2,1)S(1)} custom-call(bf16[8,144,128]{2,1,0:T(8,128)(2,1)S(1)} %all-to-all-done.2.grad_ref.blocks_ref, bf16[3,3,128,128]{3,2,1,0:T(8,128)(2,1)S(1)} %bitcast.47, bf16[3,3,128,128]{3,2,1,0:T(8,128)(2,1)S(1)} %collective-permute-done.7.other_ref), custom_call_target="tpu_custom_call" | custom-call | flops 805306368 | bytes 1769472 | tf_op jit(solution)/shard_map/pallas_call | solution.py:43
  76.5 2.3 %collective-permute-start.8 = (bf16[4,16,1024]{2,1,0:T(8,128)(2,1)S(1)}, bf16[4,16,1024]{2,1,0:T(8,128)(2,1)S(1)}, u32[]{:S(2)}, u32[]{:S(2)}) collective-permute-start(bf16[4,16,1024]{2,1,0:T(8,128)(2,1)S(1)} %slice_bitcast_fusion), channel_id=1, source_target_pairs={{0,32},{32,0},{1,33},{33,1},{2,34},{34,2},{3,35},{35,3},{4,36},{36... | collective-permute-start | bytes 393224 | tf_op jit(solution)/shard_map/ppermute | solution.py:543
  78.8 8.1 %all-to-all-done.3.parts_ref = bf16[16,108,128]{2,1,0:T(8,128)(2,1)S(1)} async-done(((bf16[16,108,128]{2,1,0:T(8,128)(2,1)}), bf16[16,108,128]{2,1,0:T(8,128)(2,1)S(1)}, u32[]{:S(2)}, u32[]{:S(2)}) %all-to-all-start.3) | async-done | bytes 442400 | tf_op jit(solution)/shard_map/all_to_all | solution.py:263
  87.9 4.9 %all-to-all-start.4 = ((bf16[16,144,128]{2,1,0:T(8,128)(2,1)}), bf16[16,144,128]{2,1,0:T(8,128)(2,1)S(1)}, u32[]{:S(2)}, u32[]{:S(2)}) async-start(bf16[16,144,128]{2,1,0:T(8,128)(2,1)} %shard_map.97), calls=%async_computation.4 | async-start | bytes 1179648 | tf_op jit(solution)/shard_map/all_to_all | solution.py:263
  93.2 3.0 %collective-permute-start.11 = (bf16[16,1024]{1,0:T(8,128)(2,1)S(1)}, bf16[16,1024]{1,0:T(8,128)(2,1)S(1)}, u32[]{:S(2)}, u32[]{:S(2)}) collective-permute-start(bf16[16,1024]{1,0:T(8,128)(2,1)S(1)} %get-tuple-element.44), channel_id=1, source_target_pairs={{0,192},{64,0},{128,64},{192,128},{1,193},{65,1},{129,65},{193,129... | collective-permute-start | bytes 98312 | tf_op jit(solution)/shard_map/ppermute | solution.py:547
  96.6 1.5 %collective-permute-done.9 = bf16[16,1024]{1,0:T(8,128)(2,1)S(1)} collective-permute-done((bf16[16,1024]{1,0:T(8,128)(2,1)S(1)}, bf16[16,1024]{1,0:T(8,128)(2,1)S(1)}, u32[]{:S(2)}, u32[]{:S(2)}) %collective-permute-start.9) | collective-permute-done | bytes 32800 | tf_op jit(solution)/shard_map/ppermute | solution.py:547
  98.1 3.5 %collective-permute-done.10 = bf16[16,1024]{1,0:T(8,128)(2,1)S(1)} collective-permute-done((bf16[16,1024]{1,0:T(8,128)(2,1)S(1)}, bf16[16,1024]{1,0:T(8,128)(2,1)S(1)}, u32[]{:S(2)}, u32[]{:S(2)}) %collective-permute-start.10) | collective-permute-done | bytes 32800 | tf_op jit(solution)/shard_map/ppermute | solution.py:547
  101.7 1.2 %collective-permute-done.12 = bf16[16,512]{1,0:T(8,128)(2,1)S(1)} collective-permute-done((bf16[16,512]{1,0:T(8,128)(2,1)S(1)}, bf16[16,512]{1,0:T(8,128)(2,1)S(1)}, u32[]{:S(2)}, u32[]{:S(2)}) %collective-permute-start.12) | collective-permute-done | bytes 16416 | tf_op jit(solution)/shard_map/ppermute | solution.py:554
  103.5 6.0 %all-to-all-done.4.whole_ref = bf16[16,144,128]{2,1,0:T(8,128)(2,1)S(1)} async-done(((bf16[16,144,128]{2,1,0:T(8,128)(2,1)}), bf16[16,144,128]{2,1,0:T(8,128)(2,1)S(1)}, u32[]{:S(2)}, u32[]{:S(2)}) %all-to-all-start.4) | async-done | bytes 589856 | tf_op jit(solution)/shard_map/all_to_all | solution.py:263
  (38 shorter events, 10.4 us)
Async XLA Ops:
  0.6 11.5 %collective-permute-start.3 = (bf16[3,3,128,128]{3,2,1,0:T(8,128)(2,1)}, bf16[3,3,128,128]{3,2,1,0:T(8,128)(2,1)S(1)}, u32[]{:S(2)}, u32[]{:S(2)}) collective-permute-start(bf16[3,3,128,128]{3,2,1,0:T(8,128)(2,1)} %bitcast.44), channel_id=1, source_target_pairs={{0,16},{16,0},{1,17},{17,1},{2,18},{18,2},{3,19},{19,3},{4,20},{20... | collective-permute-start | bytes 884744 | tf_op jit(solution)/shard_map/ppermute | solution.py:491
  2.3 7.8 %collective-permute-start.1 = (bf16[8,512]{1,0:T(8,128)(2,1)}, bf16[8,512]{1,0:T(8,128)(2,1)S(1)}, u32[]{:S(2)}, u32[]{:S(2)}) collective-permute-start(bf16[8,512]{1,0:T(8,128)(2,1)} %get-tuple-element.25), channel_id=1, source_target_pairs={{0,1},{1,2},{2,3},{3,4},{4,5},{5,6},{6,7},{7,8},{8,9},{9,10},{10,1... | collective-permute-start | bytes 24584 | tf_op jit(solution)/shard_map/ppermute | solution.py:472
  4.3 6.5 %collective-permute-start.2 = (bf16[8,512]{1,0:T(8,128)(2,1)}, bf16[8,512]{1,0:T(8,128)(2,1)S(1)}, u32[]{:S(2)}, u32[]{:S(2)}) collective-permute-start(bf16[8,512]{1,0:T(8,128)(2,1)} %get-tuple-element.26), channel_id=1, source_target_pairs={{16,1},{17,2},{18,3},{19,4},{20,5},{21,6},{22,7},{23,8},{24,9},{25... | collective-permute-start | bytes 24584 | tf_op jit(solution)/shard_map/ppermute | solution.py:473
  9.2 1.6 %collective-permute-start = (bf16[80,512]{1,0:T(8,128)(2,1)}, bf16[80,512]{1,0:T(8,128)(2,1)S(1)}, u32[]{:S(2)}, u32[]{:S(2)}) collective-permute-start(bf16[80,512]{1,0:T(8,128)(2,1)} %get-tuple-element.24), channel_id=1, source_target_pairs={{0,16},{16,0},{1,17},{17,1},{2,18},{18,2},{3,19},{19,3},{4,20},{20... | collective-permute-start | bytes 245768 | tf_op jit(solution)/shard_map/ppermute | solution.py:474
  12.2 22.4 %copy-start = (bf16[1,3,3,128,128]{4,3,2,1,0:T(8,128)(2,1)S(1)}, bf16[1,3,3,128,128]{4,3,2,1,0:T(8,128)(2,1)}, u32[]{:S(2)}) copy-start(bf16[1,3,3,128,128]{4,3,2,1,0:T(8,128)(2,1)} %param.11) | copy-start | bytes 884740
  37.5 11.9 %all-to-all-start.1 = ((bf16[8,144,128]{2,1,0:T(8,128)(2,1)}), bf16[8,144,128]{2,1,0:T(8,128)(2,1)S(1)}, u32[]{:S(2)}, u32[]{:S(2)}) async-start(bf16[8,144,128]{2,1,0:T(8,128)(2,1)} %shard_map.87), calls=%async_computation.1 | async-start | bytes 589824 | tf_op jit(solution)/shard_map/all_to_all | solution.py:263
  42.1 11.6 %collective-permute-start.4 = (bf16[3,3,128,128]{3,2,1,0:T(8,128)(2,1)S(1)}, bf16[3,3,128,128]{3,2,1,0:T(8,128)(2,1)S(1)}, u32[]{:S(2)}, u32[]{:S(2)}) collective-permute-start(bf16[3,3,128,128]{3,2,1,0:T(8,128)(2,1)S(1)} %get-tuple-element.33), channel_id=1, source_target_pairs={{0,16},{16,0},{1,17},{17,1},{2,18},{18,2},{3,19},{19,3},{4,20},{20... | collective-permute-start | bytes 884744 | tf_op jit(solution)/shard_map/ppermute | solution.py:251
  50.3 12.0 %all-to-all-start.2 = ((bf16[8,144,128]{2,1,0:T(8,128)(2,1)}), bf16[8,144,128]{2,1,0:T(8,128)(2,1)S(1)}, u32[]{:S(2)}, u32[]{:S(2)}) async-start(bf16[8,144,128]{2,1,0:T(8,128)(2,1)} %shard_map.90), calls=%async_computation.2 | async-start | bytes 589824 | tf_op jit(solution)/shard_map/all_to_all | solution.py:263
  53.8 6.0 %collective-permute-start.5 = (bf16[8,72,128]{2,1,0:T(8,128)(2,1)S(1)}, bf16[8,72,128]{2,1,0:T(8,128)(2,1)S(1)}, u32[]{:S(2)}, u32[]{:S(2)}) collective-permute-start(bf16[8,72,128]{2,1,0:T(8,128)(2,1)S(1)} %get-tuple-element.35), channel_id=1, source_target_pairs={{0,8},{1,9},{2,10},{3,11},{4,12},{5,13},{6,14},{7,15},{8,0},{9,1},... | collective-permute-start | bytes 442376 | tf_op jit(solution)/shard_map/ppermute | solution.py:297
  63.8 1.7 %collective-permute-start.6 = (bf16[3,3,128,128]{3,2,1,0:T(8,128)(2,1)S(1)}, bf16[3,3,128,128]{3,2,1,0:T(8,128)(2,1)S(1)}, u32[]{:S(2)}, u32[]{:S(2)}) collective-permute-start(bf16[3,3,128,128]{3,2,1,0:T(8,128)(2,1)S(1)} %get-tuple-element.38), channel_id=1, source_target_pairs={{0,16},{16,0},{1,17},{17,1},{2,18},{18,2},{3,19},{19,3},{4,20},{20... | collective-permute-start | bytes 884744 | tf_op jit(solution)/shard_map/ppermute | solution.py:251
  66.3 5.9 %copy-start.1 = (bf16[1,3,3,128,128]{4,3,2,1,0:T(8,128)(2,1)S(1)}, bf16[1,3,3,128,128]{4,3,2,1,0:T(8,128)(2,1)}, u32[]{:S(2)}) copy-start(bf16[1,3,3,128,128]{4,3,2,1,0:T(8,128)(2,1)} %param.10) | copy-start | bytes 884740
  66.3 20.5 %all-to-all-start.3 = ((bf16[16,108,128]{2,1,0:T(8,128)(2,1)}), bf16[16,108,128]{2,1,0:T(8,128)(2,1)S(1)}, u32[]{:S(2)}, u32[]{:S(2)}) async-start(bf16[16,108,128]{2,1,0:T(8,128)(2,1)} %shard_map.95), calls=%async_computation.3 | async-start | bytes 917504 | tf_op jit(solution)/shard_map/all_to_all | solution.py:263
  72.3 1.9 %collective-permute-start.7 = (bf16[3,3,128,128]{3,2,1,0:T(8,128)(2,1)S(1)}, bf16[3,3,128,128]{3,2,1,0:T(8,128)(2,1)S(1)}, u32[]{:S(2)}, u32[]{:S(2)}) collective-permute-start(bf16[3,3,128,128]{3,2,1,0:T(8,128)(2,1)S(1)} %bitcast.46), channel_id=1, source_target_pairs={{0,16},{16,0},{1,17},{17,1},{2,18},{18,2},{3,19},{19,3},{4,20},{20... | collective-permute-start | bytes 884744 | tf_op jit(solution)/shard_map/ppermute | solution.py:530
  76.5 16.3 %collective-permute-start.8 = (bf16[4,16,1024]{2,1,0:T(8,128)(2,1)S(1)}, bf16[4,16,1024]{2,1,0:T(8,128)(2,1)S(1)}, u32[]{:S(2)}, u32[]{:S(2)}) collective-permute-start(bf16[4,16,1024]{2,1,0:T(8,128)(2,1)S(1)} %slice_bitcast_fusion), channel_id=1, source_target_pairs={{0,32},{32,0},{1,33},{33,1},{2,34},{34,2},{3,35},{35,3},{4,36},{36... | collective-permute-start | bytes 393224 | tf_op jit(solution)/shard_map/ppermute | solution.py:543
  87.9 21.6 %all-to-all-start.4 = ((bf16[16,144,128]{2,1,0:T(8,128)(2,1)}), bf16[16,144,128]{2,1,0:T(8,128)(2,1)S(1)}, u32[]{:S(2)}, u32[]{:S(2)}) async-start(bf16[16,144,128]{2,1,0:T(8,128)(2,1)} %shard_map.97), calls=%async_computation.4 | async-start | bytes 1179648 | tf_op jit(solution)/shard_map/all_to_all | solution.py:263
  92.9 5.2 %collective-permute-start.9 = (bf16[16,1024]{1,0:T(8,128)(2,1)S(1)}, bf16[16,1024]{1,0:T(8,128)(2,1)S(1)}, u32[]{:S(2)}, u32[]{:S(2)}) collective-permute-start(bf16[16,1024]{1,0:T(8,128)(2,1)S(1)} %get-tuple-element.43), channel_id=1, source_target_pairs={{0,64},{64,128},{128,192},{192,0},{1,65},{65,129},{129,193},{193,1... | collective-permute-start | bytes 98312 | tf_op jit(solution)/shard_map/ppermute | solution.py:547
  93.2 4.8 %collective-permute-start.11 = (bf16[16,1024]{1,0:T(8,128)(2,1)S(1)}, bf16[16,1024]{1,0:T(8,128)(2,1)S(1)}, u32[]{:S(2)}, u32[]{:S(2)}) collective-permute-start(bf16[16,1024]{1,0:T(8,128)(2,1)S(1)} %get-tuple-element.44), channel_id=1, source_target_pairs={{0,192},{64,0},{128,64},{192,128},{1,193},{65,1},{129,65},{193,129... | collective-permute-start | bytes 98312 | tf_op jit(solution)/shard_map/ppermute | solution.py:547
  96.2 5.4 %collective-permute-start.10 = (bf16[16,1024]{1,0:T(8,128)(2,1)S(1)}, bf16[16,1024]{1,0:T(8,128)(2,1)S(1)}, u32[]{:S(2)}, u32[]{:S(2)}) collective-permute-start(bf16[16,1024]{1,0:T(8,128)(2,1)S(1)} %get-tuple-element.45), channel_id=1, source_target_pairs={{0,128},{64,192},{128,0},{192,64},{1,129},{65,193},{129,1},{193,65... | collective-permute-start | bytes 98312 | tf_op jit(solution)/shard_map/ppermute | solution.py:547
  101.6 1.3 %collective-permute-start.12 = (bf16[16,512]{1,0:T(8,128)(2,1)S(1)}, bf16[16,512]{1,0:T(8,128)(2,1)S(1)}, u32[]{:S(2)}, u32[]{:S(2)}) collective-permute-start(bf16[16,512]{1,0:T(8,128)(2,1)S(1)} %get-tuple-element.47), channel_id=1, source_target_pairs={{0,16},{16,0},{1,17},{17,1},{2,18},{18,2},{3,19},{19,3},{4,20},{20... | collective-permute-start | bytes 49160 | tf_op jit(solution)/shard_map/ppermute | solution.py:554
